TPU v7x, 32 devices: a whole 2x2x4 slice. The times are simulated.
32 devices in a mesh: rep: 2 (over y), seq: 4 (over z), ch: 4 (over x, core).
Axes of the slice: x: 2, y: 2, z: 4, core: 2. Of those that a mesh axis runs over, the one named last changes fastest.
Arguments:
- key_proj: bfloat16 [4096, 4096], P(('rep', 'seq'), 'ch'), parts along dimension 0, may hold values from -6 to 6
- value_proj: bfloat16 [4096, 4096], P(('rep', 'seq'), 'ch'), parts along dimension 0, may hold values from -6 to 6
- query_proj: bfloat16 [4096, 4096], P(('rep', 'seq'), 'ch'), parts along dimension 0, may hold values from -6 to 6
- filters: bfloat16 [256, 2048], P('ch', 'seq'), may hold values from -3 to 3
- sources: int32 [8], P('rep'), parts along dimension 0, may hold values from 0 to 15, as said below
- owner: int32 [32], P('rep'), parts along dimension 0, may hold values from 0 to 3, as said below
Outputs:
- conv_out: bfloat16 [4096, 4096], P(('rep', 'seq'), 'ch'), parts along dimension 0
There are 2 independent parts, one for each index of `rep`. A program takes and returns all parts, laid end to end along the dimension named above; an argument that names none is the same for every part. Nothing has to cross between parts.
Inputs may be any that keep to these rules, and one draw needn't show every extreme that they name: `sources`: four distinct stretch numbers in increasing order; the first is 0 and the last 15. owner[k] is the index along seq of the shard holding stretch k; every shard holds exactly 4 stretches, stored one after another in increasing stretch number.
All inputs are finite; a program needn't handle non-finite values.
Results may differ from a plain program's by a relative error of at most 0.0049.
Values may be sent and summed in bfloat16 or wider, within the bound.
No kernel may reach another device: no remote copies, remote signals or barrier semaphores. Data moves between devices by JAX's collectives and lax.ppermute only.
A program may use at most 64 MiB of HBM per device.

v0:
```python
import functools

import jax
import jax.numpy as jnp
from jax import lax
from jax.experimental import pallas as pl
from jax.experimental.pallas import tpu as pltpu
from jax.sharding import PartitionSpec as P

GROUP_CH = 16
STRETCH = 128
WIN = 4
SENT = WIN - 1
LANES = 128
BLOCKS = LANES // GROUP_CH
SPAN = 2 * STRETCH
VMEM_LIMIT = 40 * 1024 * 1024
GATE_LIMIT = 62 * 1024 * 1024

SMEM_SPEC = pl.BlockSpec(memory_space=pltpu.SMEM)
ANY_SPEC = pl.BlockSpec(memory_space=pl.ANY)
HBM_SPEC = pl.BlockSpec(memory_space=pltpu.HBM)
VMEM_SPEC = pl.BlockSpec(memory_space=pltpu.VMEM)
NT = (((1,), (1,)), ((), ()))


def params(limit=VMEM_LIMIT):
    return pltpu.CompilerParams(vmem_limit_bytes=limit)


def lane_block(shape):
    return lax.broadcasted_iota(jnp.int32, shape, 1) // GROUP_CH


def block_transpose(tiles):
    block = lane_block(tiles[0].shape)
    tiles = list(tiles)
    for distance in (4, 2, 1):
        low = (block & distance) == 0
        for first in range(BLOCKS):
            if first & distance:
                continue
            a, b = tiles[first], tiles[first + distance]
            shift = GROUP_CH * distance
            tiles[first] = jnp.where(low, a, pltpu.roll(b, shift, 1))
            tiles[first + distance] = jnp.where(low, pltpu.roll(a, LANES - shift, 1), b)
    return tiles


def gate_kernel(size, parts, fill, sources_in, owner_in, key, value, *refs):
    sends = refs[:parts]
    last, meta, sources, owner, rows, sems, small = refs[parts:]
    stretch_count = owner.shape[0]
    slots = key.shape[0] // STRETCH
    channels = key.shape[1]
    width = channels // parts
    me = lax.axis_index("seq")
    copies = [
        pltpu.make_async_copy(sources_in, sources, small.at[0]),
        pltpu.make_async_copy(owner_in, owner, small.at[1]),
    ]
    for copy in copies:
        copy.start()

    def fetch(w, start):
        span = pl.ds(start, STRETCH)
        return (
            pltpu.make_async_copy(key.at[span], rows.at[w, 0], sems.at[w, 0]),
            pltpu.make_async_copy(value.at[span], rows.at[w, 1], sems.at[w, 1]),
        )

    for copy in fetch(SENT, (slots - 1) * STRETCH):
        copy.start()
    for copy in copies:
        copy.wait()
    for w in range(SENT):
        stretch = sources[w]
        holder = owner[stretch]
        meta[w] = holder

        @pl.when(holder == me)
        def _(w=w, stretch=stretch, holder=holder):
            def count(k, total):
                return total + jnp.where((owner[k] == holder) & (k < stretch), 1, 0)

            slot = lax.fori_loop(0, stretch_count, count, 0)
            for copy in fetch(w, pl.multiple_of(slot * STRETCH, STRETCH)):
                copy.start()

    def target(k, slot):
        mine = owner[k] == me

        @pl.when(mine)
        def _():
            for w in range(WIN):
                lag_block = jnp.maximum(k - sources[w], -1)
                meta[SENT + slot * WIN + w] = (stretch_count - 1 - lag_block) * STRETCH

        return slot + jnp.where(mine, 1, 0)

    lax.fori_loop(0, stretch_count, target, 0)
    tail = SENT + slots * WIN
    meta[tail] = me
    for shift in range(parts):
        meta[tail + 1 + shift] = lax.rem(me + size - shift, size) if parts > 1 else 0

    def product(w, columns):
        rows_k = rows[w, 0, :, columns].astype(jnp.float32)
        rows_v = rows[w, 1, :, columns].astype(jnp.float32)
        return (rows_k * rows_v).astype(jnp.bfloat16).T

    for copy in fetch(SENT, 0):
        copy.wait()
    for start in range(0, channels, LANES):
        last[pl.ds(start, LANES), :] = product(SENT, pl.ds(start, LANES))
    for w in range(SENT):
        mine = owner[sources[w]] == me

        @pl.when(mine)
        def _(w=w):
            for copy in fetch(w, 0):
                copy.wait()
            for shift in range(parts):
                base = lax.rem(me + shift, parts) * width
                for start in range(0, width, LANES):
                    columns = pl.ds(pl.multiple_of(base + start, LANES), LANES)
                    sends[shift][w, pl.ds(start, LANES), :] = product(w, columns)

        if fill:

            @pl.when(jnp.logical_not(mine))
            def _(w=w):
                for send in sends:
                    send[w] = jnp.zeros(send.shape[1:], send.dtype)


def gate(size, parts, fill, sources, owner, key_proj, value_proj):
    row_count, channels = key_proj.shape
    slots = row_count // STRETCH
    send = jax.ShapeDtypeStruct((SENT, channels // parts, STRETCH), jnp.bfloat16)
    *sends, last, meta = pl.pallas_call(
        functools.partial(gate_kernel, size, parts, fill),
        in_specs=[HBM_SPEC] * 4,
        out_specs=[VMEM_SPEC] * (parts + 1) + [SMEM_SPEC],
        out_shape=[send] * parts
        + [
            jax.ShapeDtypeStruct((channels, STRETCH), jnp.bfloat16),
            jax.ShapeDtypeStruct((SENT + slots * WIN + 1 + parts,), jnp.int32),
        ],
        scratch_shapes=[
            pltpu.SMEM(sources.shape, jnp.int32),
            pltpu.SMEM(owner.shape, jnp.int32),
            pltpu.VMEM((WIN, 2, STRETCH, channels), jnp.bfloat16),
            pltpu.SemaphoreType.DMA((WIN, 2)),
            pltpu.SemaphoreType.DMA((2,)),
        ],
        compiler_params=params(GATE_LIMIT),
        name="gate",
    )(sources, owner, key_proj, value_proj)
    return sends, last, meta


def merge_kernel(size, slots, meta, *refs):
    parts, out = refs[:-1], refs[-1]
    me = meta[SENT + slots * WIN]
    for w in range(SENT):
        shift = lax.rem(me + size - meta[w], size)
        for k in range(size):

            @pl.when(shift == k)
            def _(w=w, k=k):
                out[w] = parts[k][w]


def merge(size, slots, meta, parts):
    return pl.pallas_call(
        functools.partial(merge_kernel, size, slots),
        in_specs=[SMEM_SPEC] + [VMEM_SPEC] * size,
        out_specs=VMEM_SPEC,
        out_shape=jax.ShapeDtypeStruct(parts[0].shape, parts[0].dtype),
        compiler_params=params(),
        name="merge",
    )(meta, *parts)


def lags_kernel(size, *refs):
    received = refs[:size]
    out, blocks, reverse, sems = refs[size:]
    group_count, part = received[0].shape
    lag_count = size * part
    padded = out.shape[2]
    step = pl.program_id(0)

    @pl.when(step == 0)
    def _():
        me = lax.axis_index("seq")
        copies = [
            pltpu.make_async_copy(
                received[shift], blocks.at[lax.rem(me + size - shift, size)], sems.at[shift]
            )
            for shift in range(size)
        ]
        for copy in copies:
            copy.start()
        for copy in copies:
            copy.wait()
        row = lax.broadcasted_iota(jnp.int32, (LANES, LANES), 0)
        column = lax.broadcasted_iota(jnp.int32, (LANES, LANES), 1)
        flip = jnp.where(row + column == LANES - 1, 1.0, 0.0).astype(jnp.bfloat16)
        for start in range(0, lag_count, LANES):
            piece = blocks[start // part, :, pl.ds(start % part, LANES)]
            reverse[:, pl.ds(lag_count - LANES - start, LANES)] = jnp.dot(
                piece, flip, preferred_element_type=jnp.float32
            )
        reverse[:, pl.ds(lag_count, padded - lag_count)] = jnp.zeros(
            (group_count, padded - lag_count), jnp.float32
        )

    row = lax.broadcasted_iota(jnp.int32, (GROUP_CH, LANES), 0)
    column = lax.broadcasted_iota(jnp.int32, (GROUP_CH, LANES), 1)
    inside = column > row
    tile_rows = pl.ds(pl.multiple_of(step * BLOCKS, BLOCKS), BLOCKS)
    before = [jnp.zeros((GROUP_CH, LANES), jnp.float32)] * BLOCKS
    for start in range(0, padded, LANES):
        tile = reverse[tile_rows, pl.ds(start, LANES)]
        for g in range(BLOCKS):
            spread = jnp.broadcast_to(tile[g : g + 1, :], (GROUP_CH, LANES))
            rolled = pltpu.roll(spread, 1, 1, stride=1, stride_axis=0)
            out[g, :, pl.ds(start, LANES)] = jnp.where(inside, rolled, before[g]).astype(jnp.bfloat16)
            before[g] = rolled


def lags(size, received):
    group_count, part = received[0].shape
    padded = size * part + SPAN
    return pl.pallas_call(
        functools.partial(lags_kernel, size),
        grid=(group_count // BLOCKS,),
        in_specs=[ANY_SPEC] * size,
        out_specs=pl.BlockSpec((BLOCKS, GROUP_CH, padded), lambda i: (i, 0, 0)),
        out_shape=jax.ShapeDtypeStruct((group_count, GROUP_CH, padded), jnp.bfloat16),
        scratch_shapes=[
            pltpu.VMEM((size, group_count, part), jnp.bfloat16),
            pltpu.VMEM((group_count, padded), jnp.float32),
            pltpu.SemaphoreType.DMA((size,)),
        ],
        compiler_params=params(),
        name="lags",
    )(*received)


def spread_rows(tile, spans, base):
    lane = lax.broadcasted_iota(jnp.int32, tile.shape, 1)
    zero = jnp.zeros(tile.shape, tile.dtype)
    for i1 in range(BLOCKS):
        shift = GROUP_CH * i1
        if i1 == 0:
            low, high = zero, tile
        else:
            moved = pltpu.roll(tile, LANES - shift, 1)
            early = lane < LANES - shift
            low, high = jnp.where(early, zero, moved), jnp.where(early, moved, zero)
        rows = pl.ds(shift, GROUP_CH)
        for g in range(BLOCKS):
            part = slice(g * GROUP_CH, (g + 1) * GROUP_CH)
            spans[g, rows, pl.ds(base, LANES)] = low[part]
            spans[g, rows, pl.ds(base + LANES, LANES)] = high[part]


def window(meta, shifted, group, slot, w):
    start = pl.multiple_of(meta[SENT + slot * WIN + w], STRETCH)
    return shifted[group, :, pl.ds(start, SPAN)]


def last_kernel(slots, meta, last, shifted, out, spans):
    for start in range(0, last.shape[0], LANES):
        spread_rows(last[pl.ds(start, LANES), :], spans, 0)
        results = [
            lax.dot_general(
                window(meta, shifted, start // GROUP_CH + g, slots - 1, SENT),
                spans[g],
                NT,
                preferred_element_type=jnp.float32,
            )
            for g in range(BLOCKS)
        ]
        for m, tile in enumerate(block_transpose(results)):
            out[pl.ds(m * GROUP_CH, GROUP_CH), pl.ds(start, LANES)] = tile


def last_term(slots, meta, last, shifted):
    return pl.pallas_call(
        functools.partial(last_kernel, slots),
        in_specs=[SMEM_SPEC, VMEM_SPEC, VMEM_SPEC],
        out_specs=VMEM_SPEC,
        out_shape=jax.ShapeDtypeStruct((STRETCH, last.shape[0]), jnp.float32),
        scratch_shapes=[pltpu.VMEM((BLOCKS, LANES, SPAN), jnp.bfloat16)],
        compiler_params=params(),
        name="last_term",
    )(meta, last, shifted)


def conv_kernel(shift, slots, meta, pieces, shifted, term, query, *refs):
    out, gates, result, spans, sems = refs[-5:]
    width = pieces.shape[1]
    row_count = query.shape[0]
    base = pl.multiple_of(meta[SENT + slots * WIN + 1 + shift] * width, width)
    fetch = pltpu.make_async_copy(query.at[:, pl.ds(base, width)], gates, sems.at[0])
    fetch.start()
    for start in range(0, width, LANES):
        columns = pl.ds(start, LANES)
        for w in range(SENT):
            spread_rows(pieces[w, columns, :], spans, w * SPAN)
        results = []
        for g in range(BLOCKS):
            group = base // GROUP_CH + (start // GROUP_CH + g)
            filter_rows = jnp.concatenate(
                [
                    jnp.concatenate([window(meta, shifted, group, slot, w) for w in range(SENT)], axis=1)
                    for slot in range(slots)
                ],
                axis=0,
            )
            results.append(
                lax.dot_general(filter_rows, spans[g], NT, preferred_element_type=jnp.float32)
            )
        if start == 0:
            fetch.wait()
        for slot in range(slots):
            tiles = [value[slot * GROUP_CH : (slot + 1) * GROUP_CH] for value in results]
            for m, tile in enumerate(block_transpose(tiles)):
                place = pl.ds(slot * STRETCH + m * GROUP_CH, GROUP_CH)
                if slot == slots - 1:
                    tile = tile + term[
                        pl.ds(m * GROUP_CH, GROUP_CH), pl.ds(pl.multiple_of(base + start, LANES), LANES)
                    ]
                result[place, columns] = (gates[place, columns].astype(jnp.float32) * tile).astype(
                    jnp.bfloat16
                )
    store = pltpu.make_async_copy(result, out.at[:, pl.ds(base, width)], sems.at[1])
    store.start()
    store.wait()


def conv(shift, meta, pieces, shifted, term, query_proj, before):
    row_count = query_proj.shape[0]
    slots = row_count // STRETCH
    width = pieces.shape[1]
    operands = [meta, pieces, shifted, term, query_proj]
    in_specs = [SMEM_SPEC, VMEM_SPEC, VMEM_SPEC, VMEM_SPEC, HBM_SPEC]
    aliases = {}
    if before is not None:
        aliases = {len(operands): 0}
        operands.append(before)
        in_specs.append(HBM_SPEC)
    return pl.pallas_call(
        functools.partial(conv_kernel, shift, slots),
        in_specs=in_specs,
        out_specs=HBM_SPEC,
        out_shape=jax.ShapeDtypeStruct(query_proj.shape, jnp.bfloat16),
        input_output_aliases=aliases,
        scratch_shapes=[
            pltpu.VMEM((row_count, width), jnp.bfloat16),
            pltpu.VMEM((row_count, width), jnp.bfloat16),
            pltpu.VMEM((BLOCKS, LANES, SENT * SPAN), jnp.bfloat16),
            pltpu.SemaphoreType.DMA((2,)),
        ],
        compiler_params=params(),
        name="conv",
    )(*operands)


def shards(size, key_proj, value_proj, query_proj, filters, sources, owner):
    row_count, channels = key_proj.shape
    slots = row_count // STRETCH
    by_parts = channels % (size * LANES) == 0
    parts = size if by_parts else 1

    def shifted_by(value, shift):
        return lax.ppermute(value, "seq", [(z, (z + shift) % size) for z in range(size)])

    filter_parts = [filters] + [shifted_by(filters, shift) for shift in range(1, size)]
    sends, last, meta = gate(size, parts, not by_parts, sources, owner, key_proj, value_proj)
    shifted = lags(size, filter_parts)
    term = last_term(slots, meta, last, shifted)
    if by_parts:
        scattered = [sends[0]] + [shifted_by(sends[shift], shift) for shift in range(1, size)]
        term, *scattered = lax.optimization_barrier((term, *scattered))
        merged = merge(size, slots, meta, scattered)
        gathered = [merged] + [shifted_by(merged, shift) for shift in range(1, size)]
    else:
        gathered = [lax.psum(sends[0], "seq")]
    out = None
    for shift, pieces in enumerate(gathered):
        out = conv(shift, meta, pieces, shifted, term, query_proj, out)
    return out


def solution(mesh):
    return jax.shard_map(
        functools.partial(shards, mesh.shape["seq"]),
        mesh=mesh,
        in_specs=(
            P(("rep", "seq"), "ch"),
            P(("rep", "seq"), "ch"),
            P(("rep", "seq"), "ch"),
            P("ch", "seq"),
            P("rep"),
            P("rep"),
        ),
        out_specs=P(("rep", "seq"), "ch"),
        check_vma=False,
    )
```

profile of v0, /device:TPU:20, one launch (start us, length us, event | category | flops | bytes accessed | tf_op | source)
XLA Modules:
  0.0 63.1 jit_solution(13108481146716803031)
XLA Ops:
  0.0 3.2 %gate.1 = (bf16[3,256,128]{2,1,0:T(8,128)(2,1)}, bf16[3,256,128]{2,1,0:T(8,128)(2,1)}, bf16[3,256,128]{2,1,0:T(8,128)(2,1)}, bf16[3,256,128]{2,1,0:T(8,128)(2,1)}, bf16[1024,128]{1,0:T(8,128)(2,1)}, /*index=5*/s32[24]{0:T(128)}) custom-call(s32[4]{0:T(128)} %sources_in.1, s32[16]{0:T(128)} %owner_in.1, bf16[512,1024]{1,0:T(8,128)(2,1)} %key.1, ...), custom_call_target="tpu_custom_call" | custom-call | tf_op jit(solution)/shard_map/gate/pallas_call | solution.py:141
  3.3 0.0 copy-start.1
  3.3 1.8 %collective-permute-start.3 = (bf16[3,256,128]{2,1,0:T(8,128)(2,1)}, bf16[3,256,128]{2,1,0:T(8,128)(2,1)S(1)}, u32[]{:S(2)}, u32[]{:S(2)}) collective-permute-start(bf16[3,256,128]{2,1,0:T(8,128)(2,1)} %get-tuple-element.19), channel_id=1, source_target_pairs={{0,4},{4,8},{8,12},{12,0},{1,5},{5,9},{9,13},{13,1},{2,6},{6,10},{... | collective-permute-start | bytes 589832 | tf_op jit(solution)/shard_map/ppermute | solution.py:380
  5.1 1.5 %collective-permute-start.5 = (bf16[3,256,128]{2,1,0:T(8,128)(2,1)}, bf16[3,256,128]{2,1,0:T(8,128)(2,1)S(1)}, u32[]{:S(2)}, u32[]{:S(2)}) collective-permute-start(bf16[3,256,128]{2,1,0:T(8,128)(2,1)} %get-tuple-element.21), channel_id=1, source_target_pairs={{0,12},{4,0},{8,4},{12,8},{1,13},{5,1},{9,5},{13,9},{2,14},{6,2},{... | collective-permute-start | bytes 589832 | tf_op jit(solution)/shard_map/ppermute | solution.py:380
  6.6 0.5 collective-permute-start
  7.1 2.9 %collective-permute-start.1 = (bf16[64,512]{1,0:T(8,128)(2,1)}, bf16[64,512]{1,0:T(8,128)(2,1)S(1)}, u32[]{:S(2)}, u32[]{:S(2)}) collective-permute-start(bf16[64,512]{1,0:T(8,128)(2,1)} %refs_0_.1), channel_id=1, source_target_pairs={{0,8},{4,12},{8,0},{12,4},{1,9},{5,13},{9,1},{13,5},{2,10},{6,14},... | collective-permute-start | bytes 196616 | tf_op jit(solution)/shard_map/ppermute | solution.py:380
  10.0 17.7 %collective-permute-done.refs_1_ = bf16[64,512]{1,0:T(8,128)(2,1)S(1)} collective-permute-done((bf16[64,512]{1,0:T(8,128)(2,1)}, bf16[64,512]{1,0:T(8,128)(2,1)S(1)}, u32[]{:S(2)}, u32[]{:S(2)}) %collective-permute-start) | collective-permute-done | bytes 65568 | tf_op jit(solution)/shard_map/ppermute | solution.py:380
  27.7 0.0 collective-permute-start.2
  27.7 0.0 collective-permute-done.1.refs_2_
  27.7 4.5 %collective-permute-done.2.refs_3_ = bf16[64,512]{1,0:T(8,128)(2,1)S(1)} collective-permute-done((bf16[64,512]{1,0:T(8,128)(2,1)}, bf16[64,512]{1,0:T(8,128)(2,1)S(1)}, u32[]{:S(2)}, u32[]{:S(2)}) %collective-permute-start.2) | collective-permute-done | bytes 65568 | tf_op jit(solution)/shard_map/ppermute | solution.py:380
  32.2 0.8 %copy-done.3 = bf16[64,512]{1,0:T(8,128)(2,1)S(1)} copy-done((bf16[64,512]{1,0:T(8,128)(2,1)S(1)}, bf16[64,512]{1,0:T(8,128)(2,1)}, u32[]{:S(2)}) %copy-start.3) | copy-done | bytes 65560
  33.0 2.5 %lags.1.shifted = bf16[64,16,2304]{2,1,0:T(8,128)(2,1)S(1)} custom-call(bf16[64,512]{1,0:T(8,128)(2,1)S(1)} %copy-done.3, bf16[64,512]{1,0:T(8,128)(2,1)S(1)} %collective-permute-done.refs_1_, bf16[64,512]{1,0:T(8,128)(2,1)S(1)} %collective-permute-done.1.refs_2_, bf16[64,512]{1,0:T(8,128)(2,1)S(1)} %collective-permute-done.2.refs_3_), custom_call_target="tpu_custom_call" | custom-call | tf_op jit(solution)/shard_map/lags/pallas_call | solution.py:236
  35.6 2.3 %last_term.1.term = f32[128,1024]{1,0:T(8,128)S(1)} custom-call(s32[24]{0:T(128)S(1)} %copy-done.4, bf16[1024,128]{1,0:T(8,128)(2,1)S(1)} %copy-done.1, bf16[64,16,2304]{2,1,0:T(8,128)(2,1)S(1)} %lags.1.shifted), custom_call_target="tpu_custom_call" | custom-call | tf_op jit(solution)/shard_map/last_term/pallas_call | solution.py:292
  37.9 0.0 collective-permute-done.3.refs_1_
  37.9 0.0 collective-permute-done.5.refs_3_
  37.9 0.6 merge.1.pieces
  38.5 0.1 collective-permute-start.8
  38.6 1.4 %collective-permute-start.7 = (bf16[3,256,128]{2,1,0:T(8,128)(2,1)S(1)}, bf16[3,256,128]{2,1,0:T(8,128)(2,1)S(1)}, u32[]{:S(2)}, u32[]{:S(2)}) collective-permute-start(bf16[3,256,128]{2,1,0:T(8,128)(2,1)S(1)} %merge.1.pieces), channel_id=1, source_target_pairs={{0,8},{4,12},{8,0},{12,4},{1,9},{5,13},{9,1},{13,5},{2,10},{6,14},... | collective-permute-start | bytes 589832 | tf_op jit(solution)/shard_map/ppermute | solution.py:380
  40.0 0.6 collective-permute-start.6
  40.6 3.4 %conv.4.refs_0_ = bf16[512,1024]{1,0:T(8,128)(2,1)} custom-call(s32[24]{0:T(128)S(1)} %copy-done.4, bf16[3,256,128]{2,1,0:T(8,128)(2,1)S(1)} %merge.1.pieces, bf16[64,16,2304]{2,1,0:T(8,128)(2,1)S(1)} %lags.1.shifted, f32[128,1024]{1,0:T(8,128)S(1)} %last_term.1.term, bf16[512,1024]{1,0:T(8,128)(2,1)S(1)} %copy-done), custom_call_target="tpu_custom_call" | custom-call | tf_op jit(solution)/shard_map/conv/pallas_call | solution.py:356
  44.1 8.7 %collective-permute-done.8.pieces = bf16[3,256,128]{2,1,0:T(8,128)(2,1)S(1)} collective-permute-done((bf16[3,256,128]{2,1,0:T(8,128)(2,1)S(1)}, bf16[3,256,128]{2,1,0:T(8,128)(2,1)S(1)}, u32[]{:S(2)}, u32[]{:S(2)}) %collective-permute-start.8) | collective-permute-done | bytes 196640 | tf_op jit(solution)/shard_map/ppermute | solution.py:380
  52.7 3.4 %conv.5.refs_0_ = bf16[512,1024]{1,0:T(8,128)(2,1)} custom-call(s32[24]{0:T(128)S(1)} %copy-done.4, bf16[3,256,128]{2,1,0:T(8,128)(2,1)S(1)} %collective-permute-done.8.pieces, bf16[64,16,2304]{2,1,0:T(8,128)(2,1)S(1)} %lags.1.shifted, f32[128,1024]{1,0:T(8,128)S(1)} %last_term.1.term, ...), custom_call_target="tpu_custom_call", output_to_operand_aliasing={{}: (5, {})} | custom-call | tf_op jit(solution)/shard_map/conv/pallas_call | solution.py:356
  56.2 3.5 %conv.6.refs_0_ = bf16[512,1024]{1,0:T(8,128)(2,1)} custom-call(s32[24]{0:T(128)S(1)} %copy-done.4, bf16[3,256,128]{2,1,0:T(8,128)(2,1)S(1)} %collective-permute-done.7.pieces, bf16[64,16,2304]{2,1,0:T(8,128)(2,1)S(1)} %lags.1.shifted, f32[128,1024]{1,0:T(8,128)S(1)} %last_term.1.term, ...), custom_call_target="tpu_custom_call", output_to_operand_aliasing={{}: (5, {})} | custom-call | tf_op jit(solution)/shard_map/conv/pallas_call | solution.py:356
  59.7 3.5 %conv.7 = bf16[512,1024]{1,0:T(8,128)(2,1)} custom-call(s32[24]{0:T(128)S(1)} %copy-done.4, bf16[3,256,128]{2,1,0:T(8,128)(2,1)S(1)} %collective-permute-done.6.pieces, bf16[64,16,2304]{2,1,0:T(8,128)(2,1)S(1)} %lags.1.shifted, f32[128,1024]{1,0:T(8,128)S(1)} %last_term.1.term, bf16[512,1024]{1,0:T(8,128)(2,1)S(1)} %copy-done, ...), custom_call_target="tpu_custom_call", output_to_operand_aliasing={{}: (5, {})} | custom-call | tf_op jit(solution)/shard_map/conv/pallas_call | solution.py:356
  (12 shorter events, 0.0 us)
Async XLA Ops:
  3.3 32.3 %copy-start.1 = (bf16[1024,128]{1,0:T(8,128)(2,1)S(1)}, bf16[1024,128]{1,0:T(8,128)(2,1)}, u32[]{:S(2)}) copy-start(bf16[1024,128]{1,0:T(8,128)(2,1)} %get-tuple-element.17.last) | copy-start | bytes 786436
  3.3 34.6 %collective-permute-start.3 = (bf16[3,256,128]{2,1,0:T(8,128)(2,1)}, bf16[3,256,128]{2,1,0:T(8,128)(2,1)S(1)}, u32[]{:S(2)}, u32[]{:S(2)}) collective-permute-start(bf16[3,256,128]{2,1,0:T(8,128)(2,1)} %get-tuple-element.19), channel_id=1, source_target_pairs={{0,4},{4,8},{8,12},{12,0},{1,5},{5,9},{9,13},{13,1},{2,6},{6,10},{... | collective-permute-start | bytes 589832 | tf_op jit(solution)/shard_map/ppermute | solution.py:380
  5.1 32.8 %collective-permute-start.4 = (bf16[3,256,128]{2,1,0:T(8,128)(2,1)}, bf16[3,256,128]{2,1,0:T(8,128)(2,1)S(1)}, u32[]{:S(2)}, u32[]{:S(2)}) collective-permute-start(bf16[3,256,128]{2,1,0:T(8,128)(2,1)} %get-tuple-element.20), channel_id=1, source_target_pairs={{0,8},{4,12},{8,0},{12,4},{1,9},{5,13},{9,1},{13,5},{2,10},{6,14},... | collective-permute-start | bytes 589832 | tf_op jit(solution)/shard_map/ppermute | solution.py:380
  5.1 32.8 %copy-start.2 = (bf16[3,256,128]{2,1,0:T(8,128)(2,1)S(1)}, bf16[3,256,128]{2,1,0:T(8,128)(2,1)}, u32[]{:S(2)}) copy-start(bf16[3,256,128]{2,1,0:T(8,128)(2,1)} %get-tuple-element.22.refs_0_) | copy-start | bytes 589828
  5.1 35.5 %copy-start = (bf16[512,1024]{1,0:T(8,128)(2,1)S(1)}, bf16[512,1024]{1,0:T(8,128)(2,1)}, u32[]{:S(2)}) copy-start(bf16[512,1024]{1,0:T(8,128)(2,1)} %query.7) | copy-start | bytes 3145732
  5.1 32.8 %collective-permute-start.5 = (bf16[3,256,128]{2,1,0:T(8,128)(2,1)}, bf16[3,256,128]{2,1,0:T(8,128)(2,1)S(1)}, u32[]{:S(2)}, u32[]{:S(2)}) collective-permute-start(bf16[3,256,128]{2,1,0:T(8,128)(2,1)} %get-tuple-element.21), channel_id=1, source_target_pairs={{0,12},{4,0},{8,4},{12,8},{1,13},{5,1},{9,5},{13,9},{2,14},{6,2},{... | collective-permute-start | bytes 589832 | tf_op jit(solution)/shard_map/ppermute | solution.py:380
  6.6 21.1 %collective-permute-start = (bf16[64,512]{1,0:T(8,128)(2,1)}, bf16[64,512]{1,0:T(8,128)(2,1)S(1)}, u32[]{:S(2)}, u32[]{:S(2)}) collective-permute-start(bf16[64,512]{1,0:T(8,128)(2,1)} %refs_0_.1), channel_id=1, source_target_pairs={{0,4},{4,8},{8,12},{12,0},{1,5},{5,9},{9,13},{13,1},{2,6},{6,10},{... | collective-permute-start | bytes 196616 | tf_op jit(solution)/shard_map/ppermute | solution.py:380
  7.1 20.6 %collective-permute-start.1 = (bf16[64,512]{1,0:T(8,128)(2,1)}, bf16[64,512]{1,0:T(8,128)(2,1)S(1)}, u32[]{:S(2)}, u32[]{:S(2)}) collective-permute-start(bf16[64,512]{1,0:T(8,128)(2,1)} %refs_0_.1), channel_id=1, source_target_pairs={{0,8},{4,12},{8,0},{12,4},{1,9},{5,13},{9,1},{13,5},{2,10},{6,14},... | collective-permute-start | bytes 196616 | tf_op jit(solution)/shard_map/ppermute | solution.py:380
  27.7 4.5 %collective-permute-start.2 = (bf16[64,512]{1,0:T(8,128)(2,1)}, bf16[64,512]{1,0:T(8,128)(2,1)S(1)}, u32[]{:S(2)}, u32[]{:S(2)}) collective-permute-start(bf16[64,512]{1,0:T(8,128)(2,1)} %refs_0_.1), channel_id=1, source_target_pairs={{0,12},{4,0},{8,4},{12,8},{1,13},{5,1},{9,5},{13,9},{2,14},{6,2},{... | collective-permute-start | bytes 196616 | tf_op jit(solution)/shard_map/ppermute | solution.py:380
  32.2 0.8 %copy-start.3 = (bf16[64,512]{1,0:T(8,128)(2,1)S(1)}, bf16[64,512]{1,0:T(8,128)(2,1)}, u32[]{:S(2)}) copy-start(bf16[64,512]{1,0:T(8,128)(2,1)} %refs_0_.1) | copy-start | bytes 196612
  33.0 2.5 %copy-start.4 = (s32[24]{0:T(128)S(1)}, s32[24]{0:T(128)}, u32[]{:S(2)}) copy-start(s32[24]{0:T(128)} %get-tuple-element.16.meta) | copy-start | bytes 292
  38.5 14.2 %collective-permute-start.8 = (bf16[3,256,128]{2,1,0:T(8,128)(2,1)S(1)}, bf16[3,256,128]{2,1,0:T(8,128)(2,1)S(1)}, u32[]{:S(2)}, u32[]{:S(2)}) collective-permute-start(bf16[3,256,128]{2,1,0:T(8,128)(2,1)S(1)} %merge.1.pieces), channel_id=1, source_target_pairs={{0,4},{4,8},{8,12},{12,0},{1,5},{5,9},{9,13},{13,1},{2,6},{6,10},{... | collective-permute-start | bytes 589832 | tf_op jit(solution)/shard_map/ppermute | solution.py:380
  38.6 17.6 %collective-permute-start.7 = (bf16[3,256,128]{2,1,0:T(8,128)(2,1)S(1)}, bf16[3,256,128]{2,1,0:T(8,128)(2,1)S(1)}, u32[]{:S(2)}, u32[]{:S(2)}) collective-permute-start(bf16[3,256,128]{2,1,0:T(8,128)(2,1)S(1)} %merge.1.pieces), channel_id=1, source_target_pairs={{0,8},{4,12},{8,0},{12,4},{1,9},{5,13},{9,1},{13,5},{2,10},{6,14},... | collective-permute-start | bytes 589832 | tf_op jit(solution)/shard_map/ppermute | solution.py:380
  40.0 19.6 %collective-permute-start.6 = (bf16[3,256,128]{2,1,0:T(8,128)(2,1)S(1)}, bf16[3,256,128]{2,1,0:T(8,128)(2,1)S(1)}, u32[]{:S(2)}, u32[]{:S(2)}) collective-permute-start(bf16[3,256,128]{2,1,0:T(8,128)(2,1)S(1)} %merge.1.pieces), channel_id=1, source_target_pairs={{0,12},{4,0},{8,4},{12,8},{1,13},{5,1},{9,5},{13,9},{2,14},{6,2},{... | collective-permute-start | bytes 589832 | tf_op jit(solution)/shard_map/ppermute | solution.py:380
where the time goes:
time: 63.3 us; the launch traced here: 63.1 us
  waiting for transfers between devices  30.8 us (49%)
  Pallas kernels  22.4 us (35%)
  starting transfers between devices  8.85 us (14%)
  local copies, waits for them, and re-layouts  0.86 us (1%)
    ppermute x9, waiting for transfers between devices, shifted_by(): lax.ppermute(value, 'seq', [(z, (z + shift) % size) for z in range(size)])  30.8 us
    pallas_call x4, Pallas kernels, conv(): pl.pallas_call(functools.partial(conv_kernel, shift, slots), in_specs=in_...  13.8 us
    ppermute x9, starting transfers between devices, shifted_by(): lax.ppermute(value, 'seq', [(z, (z + shift) % size) for z in range(size)])  8.85 us
    pallas_call x1, Pallas kernels, gate(): pl.pallas_call(functools.partial(gate_kernel, size, parts, fill), in_spec...  3.25 us
    pallas_call x1, Pallas kernels, lags(): pl.pallas_call(functools.partial(lags_kernel, size), grid=(group_count //...  2.49 us
    pallas_call x1, Pallas kernels, last_term(): pl.pallas_call(functools.partial(last_kernel, slots), in_specs=[SMEM_SPEC...  2.3 us
  transfers between devices with their start and end apart: 9, of which 3 were waited for; matrix products, arithmetic and copies ran while one was open for 0% of the time, Pallas kernels for 24%

commit v1 on v0

--- a/solution.py
+++ b/solution.py
@@ -15,7 +15,6 @@
 BLOCKS = LANES // GROUP_CH
 SPAN = 2 * STRETCH
 VMEM_LIMIT = 40 * 1024 * 1024
-GATE_LIMIT = 62 * 1024 * 1024
 
 SMEM_SPEC = pl.BlockSpec(memory_space=pltpu.SMEM)
 ANY_SPEC = pl.BlockSpec(memory_space=pl.ANY)
@@ -24,8 +23,8 @@
 NT = (((1,), (1,)), ((), ()))
 
 
-def params(limit=VMEM_LIMIT):
-    return pltpu.CompilerParams(vmem_limit_bytes=limit)
+def params():
+    return pltpu.CompilerParams(vmem_limit_bytes=VMEM_LIMIT)
 
 
 def lane_block(shape):
@@ -47,45 +46,31 @@
     return tiles
 
 
-def gate_kernel(size, parts, fill, sources_in, owner_in, key, value, *refs):
+def gate_kernel(size, parts, fill, sources_in, owner_in, key_in, value_in, *refs):
     sends = refs[:parts]
-    last, meta, sources, owner, rows, sems, small = refs[parts:]
+    last, meta, sources, owner, key, value, sems = refs[parts:]
     stretch_count = owner.shape[0]
     slots = key.shape[0] // STRETCH
     channels = key.shape[1]
     width = channels // parts
     me = lax.axis_index("seq")
     copies = [
-        pltpu.make_async_copy(sources_in, sources, small.at[0]),
-        pltpu.make_async_copy(owner_in, owner, small.at[1]),
+        pltpu.make_async_copy(sources_in, sources, sems.at[0]),
+        pltpu.make_async_copy(owner_in, owner, sems.at[1]),
+        pltpu.make_async_copy(key_in, key, sems.at[2]),
+        pltpu.make_async_copy(value_in, value, sems.at[3]),
     ]
     for copy in copies:
         copy.start()
 
-    def fetch(w, start):
-        span = pl.ds(start, STRETCH)
-        return (
-            pltpu.make_async_copy(key.at[span], rows.at[w, 0], sems.at[w, 0]),
-            pltpu.make_async_copy(value.at[span], rows.at[w, 1], sems.at[w, 1]),
-        )
-
-    for copy in fetch(SENT, (slots - 1) * STRETCH):
-        copy.start()
-    for copy in copies:
+    def product(start, columns):
+        rows = pl.ds(start, STRETCH)
+        rows_k = key[rows, columns].astype(jnp.float32)
+        rows_v = value[rows, columns].astype(jnp.float32)
+        return (rows_k * rows_v).astype(jnp.bfloat16).T
+
+    for copy in copies[:2]:
         copy.wait()
-    for w in range(SENT):
-        stretch = sources[w]
-        holder = owner[stretch]
-        meta[w] = holder
-
-        @pl.when(holder == me)
-        def _(w=w, stretch=stretch, holder=holder):
-            def count(k, total):
-                return total + jnp.where((owner[k] == holder) & (k < stretch), 1, 0)
-
-            slot = lax.fori_loop(0, stretch_count, count, 0)
-            for copy in fetch(w, pl.multiple_of(slot * STRETCH, STRETCH)):
-                copy.start()
 
     def target(k, slot):
         mine = owner[k] == me
@@ -104,27 +89,28 @@
     for shift in range(parts):
         meta[tail + 1 + shift] = lax.rem(me + size - shift, size) if parts > 1 else 0
 
-    def product(w, columns):
-        rows_k = rows[w, 0, :, columns].astype(jnp.float32)
-        rows_v = rows[w, 1, :, columns].astype(jnp.float32)
-        return (rows_k * rows_v).astype(jnp.bfloat16).T
-
-    for copy in fetch(SENT, 0):
+    for copy in copies[2:]:
         copy.wait()
     for start in range(0, channels, LANES):
-        last[pl.ds(start, LANES), :] = product(SENT, pl.ds(start, LANES))
+        last[pl.ds(start, LANES), :] = product((slots - 1) * STRETCH, pl.ds(start, LANES))
     for w in range(SENT):
-        mine = owner[sources[w]] == me
+        stretch = sources[w]
+        holder = owner[stretch]
+        mine = holder == me
+        meta[w] = holder
 
         @pl.when(mine)
-        def _(w=w):
-            for copy in fetch(w, 0):
-                copy.wait()
+        def _(w=w, stretch=stretch, holder=holder):
+            def count(k, total):
+                return total + jnp.where(owner[k] == holder, 1, 0)
+
+            slot = lax.fori_loop(0, stretch, count, 0)
+            first = pl.multiple_of(slot * STRETCH, STRETCH)
             for shift in range(parts):
                 base = lax.rem(me + shift, parts) * width
                 for start in range(0, width, LANES):
                     columns = pl.ds(pl.multiple_of(base + start, LANES), LANES)
-                    sends[shift][w, pl.ds(start, LANES), :] = product(w, columns)
+                    sends[shift][w, pl.ds(start, LANES), :] = product(first, columns)
 
         if fill:
 
@@ -137,6 +123,10 @@
 def gate(size, parts, fill, sources, owner, key_proj, value_proj):
     row_count, channels = key_proj.shape
     slots = row_count // STRETCH
+    operands = [
+        pltpu.with_memory_space_constraint(operand, pltpu.HBM)
+        for operand in (sources, owner, key_proj, value_proj)
+    ]
     send = jax.ShapeDtypeStruct((SENT, channels // parts, STRETCH), jnp.bfloat16)
     *sends, last, meta = pl.pallas_call(
         functools.partial(gate_kernel, size, parts, fill),
@@ -150,13 +140,13 @@
         scratch_shapes=[
             pltpu.SMEM(sources.shape, jnp.int32),
             pltpu.SMEM(owner.shape, jnp.int32),
-            pltpu.VMEM((WIN, 2, STRETCH, channels), jnp.bfloat16),
-            pltpu.SemaphoreType.DMA((WIN, 2)),
-            pltpu.SemaphoreType.DMA((2,)),
+            pltpu.VMEM(key_proj.shape, key_proj.dtype),
+            pltpu.VMEM(value_proj.shape, value_proj.dtype),
+            pltpu.SemaphoreType.DMA((4,)),
         ],
-        compiler_params=params(GATE_LIMIT),
+        compiler_params=params(),
         name="gate",
-    )(sources, owner, key_proj, value_proj)
+    )(*operands)
     return sends, last, meta
 
 
@@ -381,17 +371,29 @@
 
     filter_parts = [filters] + [shifted_by(filters, shift) for shift in range(1, size)]
     sends, last, meta = gate(size, parts, not by_parts, sources, owner, key_proj, value_proj)
+    sends, filter_parts = lax.optimization_barrier((sends, filter_parts))
     shifted = lags(size, filter_parts)
     term = last_term(slots, meta, last, shifted)
     if by_parts:
         scattered = [sends[0]] + [shifted_by(sends[shift], shift) for shift in range(1, size)]
         term, *scattered = lax.optimization_barrier((term, *scattered))
         merged = merge(size, slots, meta, scattered)
-        gathered = [merged] + [shifted_by(merged, shift) for shift in range(1, size)]
+        order = sorted(range(1, size), key=lambda shift: min(shift, size - shift))
+        gathered = [(0, merged)]
+        for shift in order[:-1]:
+            gathered.append((shift, shifted_by(merged, shift)))
+        out = conv(0, meta, merged, shifted, term, query_proj, None)
+        if len(order) > 1:
+            shift, first = gathered[1]
+            merged, first, out = lax.optimization_barrier((merged, first, out))
+            gathered[1] = (shift, first)
+        for shift in order[-1:]:
+            gathered.append((shift, shifted_by(merged, shift)))
+        gathered = gathered[1:]
     else:
-        gathered = [lax.psum(sends[0], "seq")]
-    out = None
-    for shift, pieces in enumerate(gathered):
+        gathered = [(0, lax.psum(sends[0], "seq"))]
+        out = None
+    for shift, pieces in gathered:
         out = conv(shift, meta, pieces, shifted, term, query_proj, out)
     return out
 

time: 63.3 us -> 53.6 us (0.85)
  the two profiles are of different devices: /device:TPU:20 before, /device:TPU:0 now
where the time goes in v1:
time: 53.6 us; the launch traced here: 53.4 us
  Pallas kernels  21.5 us (40%)
  starting transfers between devices  16.5 us (31%)
  waiting for transfers between devices  14.5 us (27%)
  local copies, waits for them, and re-layouts  0.84 us (2%)
    ppermute x9, starting transfers between devices, shifted_by(): lax.ppermute(value, 'seq', [(z, (z + shift) % size) for z in range(size)])  16.5 us
    ppermute x9, waiting for transfers between devices, shifted_by(): lax.ppermute(value, 'seq', [(z, (z + shift) % size) for z in range(size)])  14.5 us
    pallas_call x4, Pallas kernels, conv(): pl.pallas_call(functools.partial(conv_kernel, shift, slots), in_specs=in_...  13.8 us
    pallas_call x1, Pallas kernels, lags(): pl.pallas_call(functools.partial(lags_kernel, size), grid=(group_count //...  2.48 us
    pallas_call x1, Pallas kernels, gate(): pl.pallas_call(functools.partial(gate_kernel, size, parts, fill), in_spec...  2.31 us
    pallas_call x1, Pallas kernels, last_term(): pl.pallas_call(functools.partial(last_kernel, slots), in_specs=[SMEM_SPEC...  2.3 us
  transfers between devices with their start and end apart: 9, of which 6 were waited for; matrix products, arithmetic and copies ran while one was open for 0% of the time, Pallas kernels for 33%

profile of v1, /device:TPU:0, one launch (start us, length us, event | category | flops | bytes accessed | tf_op | source)
XLA Modules:
  0.0 53.4 jit_solution(7762260304796764475)
XLA Ops:
  0.0 3.0 %collective-permute-start = (bf16[64,512]{1,0:T(8,128)(2,1)}, bf16[64,512]{1,0:T(8,128)(2,1)S(1)}, u32[]{:S(2)}, u32[]{:S(2)}) collective-permute-start(bf16[64,512]{1,0:T(8,128)(2,1)} %refs_0_), channel_id=1, source_target_pairs={{0,4},{4,8},{8,12},{12,0},{1,5},{5,9},{9,13},{13,1},{2,6},{6,10},{... | collective-permute-start | bytes 196616 | tf_op jit(solution)/shard_map/ppermute | solution.py:370
  3.0 2.6 %collective-permute-start.1 = (bf16[64,512]{1,0:T(8,128)(2,1)}, bf16[64,512]{1,0:T(8,128)(2,1)S(1)}, u32[]{:S(2)}, u32[]{:S(2)}) collective-permute-start(bf16[64,512]{1,0:T(8,128)(2,1)} %refs_0_), channel_id=1, source_target_pairs={{0,8},{4,12},{8,0},{12,4},{1,9},{5,13},{9,1},{13,5},{2,10},{6,14},... | collective-permute-start | bytes 196616 | tf_op jit(solution)/shard_map/ppermute | solution.py:370
  5.6 1.3 %collective-permute-start.2 = (bf16[64,512]{1,0:T(8,128)(2,1)}, bf16[64,512]{1,0:T(8,128)(2,1)S(1)}, u32[]{:S(2)}, u32[]{:S(2)}) collective-permute-start(bf16[64,512]{1,0:T(8,128)(2,1)} %refs_0_), channel_id=1, source_target_pairs={{0,12},{4,0},{8,4},{12,8},{1,13},{5,1},{9,5},{13,9},{2,14},{6,2},{... | collective-permute-start | bytes 196616 | tf_op jit(solution)/shard_map/ppermute | solution.py:370
  7.0 2.3 %gate.1 = (bf16[3,256,128]{2,1,0:T(8,128)(2,1)S(1)}, bf16[3,256,128]{2,1,0:T(8,128)(2,1)S(1)}, bf16[3,256,128]{2,1,0:T(8,128)(2,1)S(1)}, bf16[3,256,128]{2,1,0:T...) custom-call(s32[4]{0:T(128)} %sources_in.1, s32[16]{0:T(128)} %owner_in.1, bf16[512,1024]{1,0:T(8,128)(2,1)} %key_in.1, ...), custom_call_target="tpu_custom_call" | custom-call | tf_op jit(solution)/shard_map/gate/pallas_call | solution.py:131
  9.3 1.0 %collective-permute-done.1.refs_2_ = bf16[64,512]{1,0:T(8,128)(2,1)S(1)} collective-permute-done((bf16[64,512]{1,0:T(8,128)(2,1)}, bf16[64,512]{1,0:T(8,128)(2,1)S(1)}, u32[]{:S(2)}, u32[]{:S(2)}) %collective-permute-start.1) | collective-permute-done | bytes 65568 | tf_op jit(solution)/shard_map/ppermute | solution.py:370
  10.3 0.2 collective-permute-done.2.refs_3_
  10.5 1.6 %collective-permute-start.3 = (bf16[3,256,128]{2,1,0:T(8,128)(2,1)S(1)}, bf16[3,256,128]{2,1,0:T(8,128)(2,1)S(1)}, u32[]{:S(2)}, u32[]{:S(2)}) collective-permute-start(bf16[3,256,128]{2,1,0:T(8,128)(2,1)S(1)} %get-tuple-element.38), channel_id=1, source_target_pairs={{0,4},{4,8},{8,12},{12,0},{1,5},{5,9},{9,13},{13,1},{2,6},{6,10},{... | collective-permute-start | bytes 589832 | tf_op jit(solution)/shard_map/ppermute | solution.py:370
  12.1 1.9 %collective-permute-start.4 = (bf16[3,256,128]{2,1,0:T(8,128)(2,1)S(1)}, bf16[3,256,128]{2,1,0:T(8,128)(2,1)S(1)}, u32[]{:S(2)}, u32[]{:S(2)}) collective-permute-start(bf16[3,256,128]{2,1,0:T(8,128)(2,1)S(1)} %get-tuple-element.39), channel_id=1, source_target_pairs={{0,8},{4,12},{8,0},{12,4},{1,9},{5,13},{9,1},{13,5},{2,10},{6,14},... | collective-permute-start | bytes 589832 | tf_op jit(solution)/shard_map/ppermute | solution.py:370
  14.1 0.4 collective-permute-start.5
  14.5 0.8 %copy-done.1 = bf16[64,512]{1,0:T(8,128)(2,1)S(1)} copy-done((bf16[64,512]{1,0:T(8,128)(2,1)S(1)}, bf16[64,512]{1,0:T(8,128)(2,1)}, u32[]{:S(2)}) %copy-start.1) | copy-done | bytes 65560
  15.3 2.5 %lags.1.shifted = bf16[64,16,2304]{2,1,0:T(8,128)(2,1)S(1)} custom-call(bf16[64,512]{1,0:T(8,128)(2,1)S(1)} %copy-done.1, bf16[64,512]{1,0:T(8,128)(2,1)S(1)} %collective-permute-done.refs_1_, bf16[64,512]{1,0:T(8,128)(2,1)S(1)} %collective-permute-done.1.refs_2_, bf16[64,512]{1,0:T(8,128)(2,1)S(1)} %collective-permute-done.2.refs_3_), custom_call_target="tpu_custom_call" | custom-call | tf_op jit(solution)/shard_map/lags/pallas_call | solution.py:226
  17.8 2.3 %last_term.1.term = f32[128,1024]{1,0:T(8,128)S(1)} custom-call(s32[24]{0:T(128)S(1)} %get-tuple-element.27.meta, bf16[1024,128]{1,0:T(8,128)(2,1)S(1)} %get-tuple-element.28.last, bf16[64,16,2304]{2,1,0:T(8,128)(2,1)S(1)} %lags.1.shifted), custom_call_target="tpu_custom_call" | custom-call | tf_op jit(solution)/shard_map/last_term/pallas_call | solution.py:282
  20.1 0.2 collective-permute-done.3.refs_1_
  20.3 7.0 %collective-permute-done.4.refs_2_ = bf16[3,256,128]{2,1,0:T(8,128)(2,1)S(1)} collective-permute-done((bf16[3,256,128]{2,1,0:T(8,128)(2,1)S(1)}, bf16[3,256,128]{2,1,0:T(8,128)(2,1)S(1)}, u32[]{:S(2)}, u32[]{:S(2)}) %collective-permute-start.4) | collective-permute-done | bytes 196640 | tf_op jit(solution)/shard_map/ppermute | solution.py:370
  27.3 0.6 %merge.1.pieces = bf16[3,256,128]{2,1,0:T(8,128)(2,1)S(1)} custom-call(s32[24]{0:T(128)S(1)} %get-tuple-element.27.meta, bf16[3,256,128]{2,1,0:T(8,128)(2,1)S(1)} %get-tuple-element.41.refs_0_, bf16[3,256,128]{2,1,0:T(8,128)(2,1)S(1)} %collective-permute-done.3.refs_1_, bf16[3,256,128]{2,1,0:T(8,128)(2,1)S(1)} %collective-permute-done.4.refs_2_, ...), custom_call_target="tpu_custom_call" | custom-call | tf_op jit(solution)/shard_map/merge/pallas_call | solution.py:166
  27.9 4.7 %collective-permute-start.6 = (bf16[3,256,128]{2,1,0:T(8,128)(2,1)S(1)}, bf16[3,256,128]{2,1,0:T(8,128)(2,1)S(1)}, u32[]{:S(2)}, u32[]{:S(2)}) collective-permute-start(bf16[3,256,128]{2,1,0:T(8,128)(2,1)S(1)} %merge.1.pieces), channel_id=1, source_target_pairs={{0,4},{4,8},{8,12},{12,0},{1,5},{5,9},{9,13},{13,1},{2,6},{6,10},{... | collective-permute-start | bytes 589832 | tf_op jit(solution)/shard_map/ppermute | solution.py:370
  32.7 0.2 collective-permute-start.8
  32.9 3.5 %conv.4.refs_0_ = bf16[512,1024]{1,0:T(8,128)(2,1)} custom-call(s32[24]{0:T(128)S(1)} %get-tuple-element.27.meta, bf16[3,256,128]{2,1,0:T(8,128)(2,1)S(1)} %merge.1.pieces, bf16[64,16,2304]{2,1,0:T(8,128)(2,1)S(1)} %lags.1.shifted, f32[128,1024]{1,0:T(8,128)S(1)} %last_term.1.term, bf16[512,1024]{1,0:T(8,128)(2,1)S(1)} %copy-done), custom_call_target="tpu_custom_call" | custom-call | tf_op jit(solution)/shard_map/conv/pallas_call | solution.py:346
  36.4 2.3 %collective-permute-done.6.pieces = bf16[3,256,128]{2,1,0:T(8,128)(2,1)S(1)} collective-permute-done((bf16[3,256,128]{2,1,0:T(8,128)(2,1)S(1)}, bf16[3,256,128]{2,1,0:T(8,128)(2,1)S(1)}, u32[]{:S(2)}, u32[]{:S(2)}) %collective-permute-start.6) | collective-permute-done | bytes 196640 | tf_op jit(solution)/shard_map/ppermute | solution.py:370
  38.6 0.6 %collective-permute-start.7 = (bf16[3,256,128]{2,1,0:T(8,128)(2,1)S(1)}, bf16[3,256,128]{2,1,0:T(8,128)(2,1)S(1)}, u32[]{:S(2)}, u32[]{:S(2)}) collective-permute-start(bf16[3,256,128]{2,1,0:T(8,128)(2,1)S(1)} %merge.1.pieces), channel_id=1, source_target_pairs={{0,8},{4,12},{8,0},{12,4},{1,9},{5,13},{9,1},{13,5},{2,10},{6,14},... | collective-permute-start | bytes 589832 | tf_op jit(solution)/shard_map/ppermute | solution.py:370
  39.2 3.4 %conv.5.refs_0_ = bf16[512,1024]{1,0:T(8,128)(2,1)} custom-call(s32[24]{0:T(128)S(1)} %get-tuple-element.27.meta, bf16[3,256,128]{2,1,0:T(8,128)(2,1)S(1)} %collective-permute-done.6.pieces, bf16[64,16,2304]{2,1,0:T(8,128)(2,1)S(1)} %lags.1.shifted, f32[128,1024]{1,0:T(8,128)S(1)} %last_term.1.term, ...), custom_call_target="tpu_custom_call", output_to_operand_aliasing={{}: (5, {})} | custom-call | tf_op jit(solution)/shard_map/conv/pallas_call | solution.py:346
  42.7 3.5 %conv.6.refs_0_ = bf16[512,1024]{1,0:T(8,128)(2,1)} custom-call(s32[24]{0:T(128)S(1)} %get-tuple-element.27.meta, bf16[3,256,128]{2,1,0:T(8,128)(2,1)S(1)} %collective-permute-done.8.pieces, bf16[64,16,2304]{2,1,0:T(8,128)(2,1)S(1)} %lags.1.shifted, f32[128,1024]{1,0:T(8,128)S(1)} %last_term.1.term, ...), custom_call_target="tpu_custom_call", output_to_operand_aliasing={{}: (5, {})} | custom-call | tf_op jit(solution)/shard_map/conv/pallas_call | solution.py:346
  46.1 3.8 %collective-permute-done.7.pieces = bf16[3,256,128]{2,1,0:T(8,128)(2,1)S(1)} collective-permute-done((bf16[3,256,128]{2,1,0:T(8,128)(2,1)S(1)}, bf16[3,256,128]{2,1,0:T(8,128)(2,1)S(1)}, u32[]{:S(2)}, u32[]{:S(2)}) %collective-permute-start.7) | collective-permute-done | bytes 196640 | tf_op jit(solution)/shard_map/ppermute | solution.py:370
  50.0 3.5 %conv.7 = bf16[512,1024]{1,0:T(8,128)(2,1)} custom-call(s32[24]{0:T(128)S(1)} %get-tuple-element.27.meta, bf16[3,256,128]{2,1,0:T(8,128)(2,1)S(1)} %collective-permute-done.7.pieces, bf16[64,16,2304]{2,1,0:T(8,128)(2,1)S(1)} %lags.1.shifted, f32[128,1024]{1,0:T(8,128)S(1)} %last_term.1.term, ...), custom_call_target="tpu_custom_call", output_to_operand_aliasing={{}: (5, {})} | custom-call | tf_op jit(solution)/shard_map/conv/pallas_call | solution.py:346
  (6 shorter events, 0.0 us)
Async XLA Ops:
  0.0 9.3 %collective-permute-start = (bf16[64,512]{1,0:T(8,128)(2,1)}, bf16[64,512]{1,0:T(8,128)(2,1)S(1)}, u32[]{:S(2)}, u32[]{:S(2)}) collective-permute-start(bf16[64,512]{1,0:T(8,128)(2,1)} %refs_0_), channel_id=1, source_target_pairs={{0,4},{4,8},{8,12},{12,0},{1,5},{5,9},{9,13},{13,1},{2,6},{6,10},{... | collective-permute-start | bytes 196616 | tf_op jit(solution)/shard_map/ppermute | solution.py:370
  3.0 7.3 %collective-permute-start.1 = (bf16[64,512]{1,0:T(8,128)(2,1)}, bf16[64,512]{1,0:T(8,128)(2,1)S(1)}, u32[]{:S(2)}, u32[]{:S(2)}) collective-permute-start(bf16[64,512]{1,0:T(8,128)(2,1)} %refs_0_), channel_id=1, source_target_pairs={{0,8},{4,12},{8,0},{12,4},{1,9},{5,13},{9,1},{13,5},{2,10},{6,14},... | collective-permute-start | bytes 196616 | tf_op jit(solution)/shard_map/ppermute | solution.py:370
  5.6 4.9 %collective-permute-start.2 = (bf16[64,512]{1,0:T(8,128)(2,1)}, bf16[64,512]{1,0:T(8,128)(2,1)S(1)}, u32[]{:S(2)}, u32[]{:S(2)}) collective-permute-start(bf16[64,512]{1,0:T(8,128)(2,1)} %refs_0_), channel_id=1, source_target_pairs={{0,12},{4,0},{8,4},{12,8},{1,13},{5,1},{9,5},{13,9},{2,14},{6,2},{... | collective-permute-start | bytes 196616 | tf_op jit(solution)/shard_map/ppermute | solution.py:370
  10.5 22.4 %copy-start = (bf16[512,1024]{1,0:T(8,128)(2,1)S(1)}, bf16[512,1024]{1,0:T(8,128)(2,1)}, u32[]{:S(2)}) copy-start(bf16[512,1024]{1,0:T(8,128)(2,1)} %query.7) | copy-start | bytes 3145732
  10.5 9.8 %collective-permute-start.3 = (bf16[3,256,128]{2,1,0:T(8,128)(2,1)S(1)}, bf16[3,256,128]{2,1,0:T(8,128)(2,1)S(1)}, u32[]{:S(2)}, u32[]{:S(2)}) collective-permute-start(bf16[3,256,128]{2,1,0:T(8,128)(2,1)S(1)} %get-tuple-element.38), channel_id=1, source_target_pairs={{0,4},{4,8},{8,12},{12,0},{1,5},{5,9},{9,13},{13,1},{2,6},{6,10},{... | collective-permute-start | bytes 589832 | tf_op jit(solution)/shard_map/ppermute | solution.py:370
  12.1 15.2 %collective-permute-start.4 = (bf16[3,256,128]{2,1,0:T(8,128)(2,1)S(1)}, bf16[3,256,128]{2,1,0:T(8,128)(2,1)S(1)}, u32[]{:S(2)}, u32[]{:S(2)}) collective-permute-start(bf16[3,256,128]{2,1,0:T(8,128)(2,1)S(1)} %get-tuple-element.39), channel_id=1, source_target_pairs={{0,8},{4,12},{8,0},{12,4},{1,9},{5,13},{9,1},{13,5},{2,10},{6,14},... | collective-permute-start | bytes 589832 | tf_op jit(solution)/shard_map/ppermute | solution.py:370
  14.1 13.2 %collective-permute-start.5 = (bf16[3,256,128]{2,1,0:T(8,128)(2,1)S(1)}, bf16[3,256,128]{2,1,0:T(8,128)(2,1)S(1)}, u32[]{:S(2)}, u32[]{:S(2)}) collective-permute-start(bf16[3,256,128]{2,1,0:T(8,128)(2,1)S(1)} %get-tuple-element.40), channel_id=1, source_target_pairs={{0,12},{4,0},{8,4},{12,8},{1,13},{5,1},{9,5},{13,9},{2,14},{6,2},{... | collective-permute-start | bytes 589832 | tf_op jit(solution)/shard_map/ppermute | solution.py:370
  14.5 0.8 %copy-start.1 = (bf16[64,512]{1,0:T(8,128)(2,1)S(1)}, bf16[64,512]{1,0:T(8,128)(2,1)}, u32[]{:S(2)}) copy-start(bf16[64,512]{1,0:T(8,128)(2,1)} %refs_0_) | copy-start | bytes 196612
  27.9 10.7 %collective-permute-start.6 = (bf16[3,256,128]{2,1,0:T(8,128)(2,1)S(1)}, bf16[3,256,128]{2,1,0:T(8,128)(2,1)S(1)}, u32[]{:S(2)}, u32[]{:S(2)}) collective-permute-start(bf16[3,256,128]{2,1,0:T(8,128)(2,1)S(1)} %merge.1.pieces), channel_id=1, source_target_pairs={{0,4},{4,8},{8,12},{12,0},{1,5},{5,9},{9,13},{13,1},{2,6},{6,10},{... | collective-permute-start | bytes 589832 | tf_op jit(solution)/shard_map/ppermute | solution.py:370
  32.7 10.0 %collective-permute-start.8 = (bf16[3,256,128]{2,1,0:T(8,128)(2,1)S(1)}, bf16[3,256,128]{2,1,0:T(8,128)(2,1)S(1)}, u32[]{:S(2)}, u32[]{:S(2)}) collective-permute-start(bf16[3,256,128]{2,1,0:T(8,128)(2,1)S(1)} %merge.1.pieces), channel_id=1, source_target_pairs={{0,12},{4,0},{8,4},{12,8},{1,13},{5,1},{9,5},{13,9},{2,14},{6,2},{... | collective-permute-start | bytes 589832 | tf_op jit(solution)/shard_map/ppermute | solution.py:370
  38.6 11.3 %collective-permute-start.7 = (bf16[3,256,128]{2,1,0:T(8,128)(2,1)S(1)}, bf16[3,256,128]{2,1,0:T(8,128)(2,1)S(1)}, u32[]{:S(2)}, u32[]{:S(2)}) collective-permute-start(bf16[3,256,128]{2,1,0:T(8,128)(2,1)S(1)} %merge.1.pieces), channel_id=1, source_target_pairs={{0,8},{4,12},{8,0},{12,4},{1,9},{5,13},{9,1},{13,5},{2,10},{6,14},... | collective-permute-start | bytes 589832 | tf_op jit(solution)/shard_map/ppermute | solution.py:370

commit v2 on v1

--- a/solution.py
+++ b/solution.py
@@ -25,6 +25,14 @@
 
 def params():
     return pltpu.CompilerParams(vmem_limit_bytes=VMEM_LIMIT)
+
+
+def partner(me, step, size):
+    return me ^ step if size & (size - 1) == 0 else lax.rem(me + step, size)
+
+
+def sender(me, step, size):
+    return me ^ step if size & (size - 1) == 0 else lax.rem(me + size - step, size)
 
 
 def lane_block(shape):
@@ -84,11 +92,6 @@
         return slot + jnp.where(mine, 1, 0)
 
     lax.fori_loop(0, stretch_count, target, 0)
-    tail = SENT + slots * WIN
-    meta[tail] = me
-    for shift in range(parts):
-        meta[tail + 1 + shift] = lax.rem(me + size - shift, size) if parts > 1 else 0
-
     for copy in copies[2:]:
         copy.wait()
     for start in range(0, channels, LANES):
@@ -106,11 +109,11 @@
 
             slot = lax.fori_loop(0, stretch, count, 0)
             first = pl.multiple_of(slot * STRETCH, STRETCH)
-            for shift in range(parts):
-                base = lax.rem(me + shift, parts) * width
+            for step in range(parts):
+                base = (partner(me, step, size) if parts > 1 else 0) * width
                 for start in range(0, width, LANES):
                     columns = pl.ds(pl.multiple_of(base + start, LANES), LANES)
-                    sends[shift][w, pl.ds(start, LANES), :] = product(first, columns)
+                    sends[step][w, pl.ds(start, LANES), :] = product(first, columns)
 
         if fill:
 
@@ -135,7 +138,7 @@
         out_shape=[send] * parts
         + [
             jax.ShapeDtypeStruct((channels, STRETCH), jnp.bfloat16),
-            jax.ShapeDtypeStruct((SENT + slots * WIN + 1 + parts,), jnp.int32),
+            jax.ShapeDtypeStruct((SENT + slots * WIN,), jnp.int32),
         ],
         scratch_shapes=[
             pltpu.SMEM(sources.shape, jnp.int32),
@@ -150,21 +153,20 @@
     return sends, last, meta
 
 
-def merge_kernel(size, slots, meta, *refs):
+def merge_kernel(size, meta, *refs):
     parts, out = refs[:-1], refs[-1]
-    me = meta[SENT + slots * WIN]
+    me = lax.axis_index("seq")
     for w in range(SENT):
-        shift = lax.rem(me + size - meta[w], size)
-        for k in range(size):
-
-            @pl.when(shift == k)
-            def _(w=w, k=k):
-                out[w] = parts[k][w]
-
-
-def merge(size, slots, meta, parts):
+        for step in range(size):
+
+            @pl.when(sender(me, step, size) == meta[w])
+            def _(w=w, step=step):
+                out[w] = parts[step][w]
+
+
+def merge(size, meta, parts):
     return pl.pallas_call(
-        functools.partial(merge_kernel, size, slots),
+        functools.partial(merge_kernel, size),
         in_specs=[SMEM_SPEC] + [VMEM_SPEC] * size,
         out_specs=VMEM_SPEC,
         out_shape=jax.ShapeDtypeStruct(parts[0].shape, parts[0].dtype),
@@ -179,16 +181,16 @@
     group_count, part = received[0].shape
     lag_count = size * part
     padded = out.shape[2]
-    step = pl.program_id(0)
-
-    @pl.when(step == 0)
+    tile_step = pl.program_id(0)
+
+    @pl.when(tile_step == 0)
     def _():
         me = lax.axis_index("seq")
         copies = [
             pltpu.make_async_copy(
-                received[shift], blocks.at[lax.rem(me + size - shift, size)], sems.at[shift]
+                received[step], blocks.at[sender(me, step, size)], sems.at[step]
             )
-            for shift in range(size)
+            for step in range(size)
         ]
         for copy in copies:
             copy.start()
@@ -209,7 +211,7 @@
     row = lax.broadcasted_iota(jnp.int32, (GROUP_CH, LANES), 0)
     column = lax.broadcasted_iota(jnp.int32, (GROUP_CH, LANES), 1)
     inside = column > row
-    tile_rows = pl.ds(pl.multiple_of(step * BLOCKS, BLOCKS), BLOCKS)
+    tile_rows = pl.ds(pl.multiple_of(tile_step * BLOCKS, BLOCKS), BLOCKS)
     before = [jnp.zeros((GROUP_CH, LANES), jnp.float32)] * BLOCKS
     for start in range(0, padded, LANES):
         tile = reverse[tile_rows, pl.ds(start, LANES)]
@@ -240,7 +242,7 @@
 
 
 def spread_rows(tile, spans, base):
-    lane = lax.broadcasted_iota(jnp.int32, tile.shape, 1)
+    lane = lax.broadcasted_iota(jnp.int16, tile.shape, 1)
     zero = jnp.zeros(tile.shape, tile.dtype)
     for i1 in range(BLOCKS):
         shift = GROUP_CH * i1
@@ -290,17 +292,33 @@
     )(meta, last, shifted)
 
 
-def conv_kernel(shift, slots, meta, pieces, shifted, term, query, *refs):
-    out, gates, result, spans, sems = refs[-5:]
+def conv_kernel(step, slots, meta_in, pieces, shifted, term, query, *refs):
+    others, (out, meta, gates, result, spans, sems) = refs[:-6], refs[-6:]
     width = pieces.shape[1]
-    row_count = query.shape[0]
-    base = pl.multiple_of(meta[SENT + slots * WIN + 1 + shift] * width, width)
-    fetch = pltpu.make_async_copy(query.at[:, pl.ds(base, width)], gates, sems.at[0])
-    fetch.start()
-    for start in range(0, width, LANES):
+    size = out.shape[1] // width
+    me = lax.axis_index("seq")
+    base = pl.multiple_of((me ^ step) * width if size > 1 else 0, width)
+    copies = [
+        pltpu.make_async_copy(meta_in, meta, sems.at[0]),
+        pltpu.make_async_copy(query.at[:, pl.ds(base, width)], gates, sems.at[1]),
+    ]
+    for copy in copies:
+        copy.start()
+    starts = range(0, width, LANES)
+
+    def spread(start):
+        for w in range(SENT):
+            tile = pieces[w, pl.ds(start, LANES), :]
+            if len(others) > 1:
+                end = (me == 0) | (me == size - 1)
+                tile = jnp.where(end, tile, others[0][w, pl.ds(start, LANES), :])
+            spread_rows(tile, spans.at[start // LANES], w * SPAN)
+
+    spread(0)
+    for copy in copies:
+        copy.wait()
+    for start in starts:
         columns = pl.ds(start, LANES)
-        for w in range(SENT):
-            spread_rows(pieces[w, columns, :], spans, w * SPAN)
         results = []
         for g in range(BLOCKS):
             group = base // GROUP_CH + (start // GROUP_CH + g)
@@ -312,10 +330,12 @@
                 axis=0,
             )
             results.append(
-                lax.dot_general(filter_rows, spans[g], NT, preferred_element_type=jnp.float32)
+                lax.dot_general(
+                    filter_rows, spans[start // LANES, g], NT, preferred_element_type=jnp.float32
+                )
             )
-        if start == 0:
-            fetch.wait()
+        if start + LANES < width:
+            spread(start + LANES)
         for slot in range(slots):
             tiles = [value[slot * GROUP_CH : (slot + 1) * GROUP_CH] for value in results]
             for m, tile in enumerate(block_transpose(tiles)):
@@ -327,33 +347,37 @@
                 result[place, columns] = (gates[place, columns].astype(jnp.float32) * tile).astype(
                     jnp.bfloat16
                 )
-    store = pltpu.make_async_copy(result, out.at[:, pl.ds(base, width)], sems.at[1])
+    store = pltpu.make_async_copy(result, out.at[:, pl.ds(base, width)], sems.at[2])
     store.start()
     store.wait()
 
 
-def conv(shift, meta, pieces, shifted, term, query_proj, before):
+def conv(step, meta, pieces, shifted, term, query_proj, before, other=None):
     row_count = query_proj.shape[0]
     slots = row_count // STRETCH
     width = pieces.shape[1]
     operands = [meta, pieces, shifted, term, query_proj]
-    in_specs = [SMEM_SPEC, VMEM_SPEC, VMEM_SPEC, VMEM_SPEC, HBM_SPEC]
+    in_specs = [ANY_SPEC, VMEM_SPEC, VMEM_SPEC, VMEM_SPEC, HBM_SPEC]
+    if other is not None:
+        operands.append(other)
+        in_specs.append(VMEM_SPEC)
     aliases = {}
     if before is not None:
         aliases = {len(operands): 0}
         operands.append(before)
         in_specs.append(HBM_SPEC)
     return pl.pallas_call(
-        functools.partial(conv_kernel, shift, slots),
+        functools.partial(conv_kernel, step, slots),
         in_specs=in_specs,
         out_specs=HBM_SPEC,
         out_shape=jax.ShapeDtypeStruct(query_proj.shape, jnp.bfloat16),
         input_output_aliases=aliases,
         scratch_shapes=[
+            pltpu.SMEM(meta.shape, jnp.int32),
             pltpu.VMEM((row_count, width), jnp.bfloat16),
             pltpu.VMEM((row_count, width), jnp.bfloat16),
-            pltpu.VMEM((BLOCKS, LANES, SENT * SPAN), jnp.bfloat16),
-            pltpu.SemaphoreType.DMA((2,)),
+            pltpu.VMEM((width // LANES, BLOCKS, LANES, SENT * SPAN), jnp.bfloat16),
+            pltpu.SemaphoreType.DMA((3,)),
         ],
         compiler_params=params(),
         name="conv",
@@ -363,39 +387,33 @@
 def shards(size, key_proj, value_proj, query_proj, filters, sources, owner):
     row_count, channels = key_proj.shape
     slots = row_count // STRETCH
-    by_parts = channels % (size * LANES) == 0
+    by_parts = size == 4 and channels % (size * LANES) == 0
     parts = size if by_parts else 1
 
-    def shifted_by(value, shift):
-        return lax.ppermute(value, "seq", [(z, (z + shift) % size) for z in range(size)])
-
-    filter_parts = [filters] + [shifted_by(filters, shift) for shift in range(1, size)]
+    def to_partner(value, step):
+        return lax.ppermute(value, "seq", [(z, z ^ step if size & (size - 1) == 0 else (z + step) % size) for z in range(size)])
+
+    filter_parts = [filters] + [to_partner(filters, step) for step in range(1, size)]
     sends, last, meta = gate(size, parts, not by_parts, sources, owner, key_proj, value_proj)
     sends, filter_parts = lax.optimization_barrier((sends, filter_parts))
     shifted = lags(size, filter_parts)
     term = last_term(slots, meta, last, shifted)
-    if by_parts:
-        scattered = [sends[0]] + [shifted_by(sends[shift], shift) for shift in range(1, size)]
-        term, *scattered = lax.optimization_barrier((term, *scattered))
-        merged = merge(size, slots, meta, scattered)
-        order = sorted(range(1, size), key=lambda shift: min(shift, size - shift))
-        gathered = [(0, merged)]
-        for shift in order[:-1]:
-            gathered.append((shift, shifted_by(merged, shift)))
-        out = conv(0, meta, merged, shifted, term, query_proj, None)
-        if len(order) > 1:
-            shift, first = gathered[1]
-            merged, first, out = lax.optimization_barrier((merged, first, out))
-            gathered[1] = (shift, first)
-        for shift in order[-1:]:
-            gathered.append((shift, shifted_by(merged, shift)))
-        gathered = gathered[1:]
-    else:
-        gathered = [(0, lax.psum(sends[0], "seq"))]
-        out = None
-    for shift, pieces in gathered:
-        out = conv(shift, meta, pieces, shifted, term, query_proj, out)
-    return out
+    if not by_parts:
+        pieces = lax.psum(sends[0], "seq")
+        return conv(0, meta, pieces, shifted, term, query_proj, None)
+
+    scattered = [sends[0]] + [to_partner(sends[step], step) for step in range(1, size)]
+    term, *scattered = lax.optimization_barrier((term, *scattered))
+    merged = merge(size, meta, scattered)
+    near = lax.ppermute(merged, "seq", [(0, 1), (1, 0), (2, 3), (3, 2)])
+    far = lax.ppermute(merged, "seq", [(0, 2), (2, 0), (1, 3), (3, 1)])
+    out = conv(0, meta, merged, shifted, term, query_proj, None)
+    merged, far, out = lax.optimization_barrier((merged, far, out))
+    onward = lax.ppermute(far, "seq", [(2, 3), (1, 0)])
+    middle = lax.ppermute(merged, "seq", [(1, 2), (2, 1)])
+    out = conv(1, meta, near, shifted, term, query_proj, out)
+    out = conv(2, meta, far, shifted, term, query_proj, out)
+    return conv(3, meta, onward, shifted, term, query_proj, out, middle)
 
 
 def solution(mesh):

time: 53.6 us -> 53.3 us (level); the launches traced: 53.4 us -> 52.4 us
  Pallas kernels: 21.5 us -> 19.1 us
  waiting for transfers between devices: 14.5 us -> 16.1 us
    pallas_call x5, Pallas kernels: 14.4 us -> 11.6 us  [the longest x4 11 us: conv(): pl.pallas_call(functools.partial(conv_kernel, step, slots), in_specs=in_s...]
    ppermute x9 -> x10, waiting for transfers between devices: 14.5 us -> 16.1 us  [the longest x6 10.4 us: to_partner(): lax.ppermute(value, 'seq', [(z, z ^ step if size & size - 1 == 0 else (z...]
    ppermute x9 -> x10, starting transfers between devices: 16.5 us -> 16.3 us  [the longest x6 10 us: to_partner(): lax.ppermute(value, 'seq', [(z, z ^ step if size & size - 1 == 0 else (z...]
  transfers between devices with their start and end apart: 9 -> 10, of which waited for: 6 -> 5; matrix products, arithmetic and copies ran while one was open for 0% -> 0% of each run, Pallas kernels for 33% -> 30%
where the time goes in v2:
time: 53.3 us; the launch traced here: 52.4 us
  Pallas kernels  19.1 us (36%)
  starting transfers between devices  16.3 us (31%)
  waiting for transfers between devices  16.1 us (30%)
  local copies, waits for them, and re-layouts  0.84 us (2%)
    pallas_call x4, Pallas kernels, conv(): pl.pallas_call(functools.partial(conv_kernel, step, slots), in_specs=in_s...  11 us
    ppermute x6, waiting for transfers between devices, to_partner(): lax.ppermute(value, 'seq', [(z, z ^ step if size & size - 1 == 0 else (z...  10.4 us
    ppermute x6, starting transfers between devices, to_partner(): lax.ppermute(value, 'seq', [(z, z ^ step if size & size - 1 == 0 else (z...  10 us
    ppermute x1, waiting for transfers between devices, shards(): far = lax.ppermute(merged, 'seq', [(0, 2), (2, 0), (1, 3), (3, 1)])  4.87 us
    ppermute x1, starting transfers between devices, shards(): far = lax.ppermute(merged, 'seq', [(0, 2), (2, 0), (1, 3), (3, 1)])  4.31 us
    pallas_call x1, Pallas kernels, gate(): pl.pallas_call(functools.partial(gate_kernel, size, parts, fill), in_spec...  2.75 us
    pallas_call x1, Pallas kernels, lags(): pl.pallas_call(functools.partial(lags_kernel, size), grid=(group_count //...  2.47 us
    pallas_call x1, Pallas kernels, last_term(): pl.pallas_call(functools.partial(last_kernel, slots), in_specs=[SMEM_SPEC...  2.28 us
  transfers between devices with their start and end apart: 10, of which 5 were waited for; matrix products, arithmetic and copies ran while one was open for 0% of the time, Pallas kernels for 30%

profile of v2, /device:TPU:0, one launch (start us, length us, event | category | flops | bytes accessed | tf_op | source)
XLA Modules:
  0.0 52.4 jit_solution(17456320564755640664)
XLA Ops:
  0.0 3.0 %collective-permute-start = (bf16[64,512]{1,0:T(8,128)(2,1)}, bf16[64,512]{1,0:T(8,128)(2,1)S(1)}, u32[]{:S(2)}, u32[]{:S(2)}) collective-permute-start(bf16[64,512]{1,0:T(8,128)(2,1)} %refs_0_), channel_id=1, source_target_pairs={{0,4},{4,0},{8,12},{12,8},{1,5},{5,1},{9,13},{13,9},{2,6},{6,2},{1... | collective-permute-start | bytes 196616 | tf_op jit(solution)/shard_map/ppermute | solution.py:394
  3.0 2.6 %collective-permute-start.1 = (bf16[64,512]{1,0:T(8,128)(2,1)}, bf16[64,512]{1,0:T(8,128)(2,1)S(1)}, u32[]{:S(2)}, u32[]{:S(2)}) collective-permute-start(bf16[64,512]{1,0:T(8,128)(2,1)} %refs_0_), channel_id=1, source_target_pairs={{0,8},{4,12},{8,0},{12,4},{1,9},{5,13},{9,1},{13,5},{2,10},{6,14},... | collective-permute-start | bytes 196616 | tf_op jit(solution)/shard_map/ppermute | solution.py:394
  5.6 2.7 %gate.1 = (bf16[3,256,128]{2,1,0:T(8,128)(2,1)S(1)}, bf16[3,256,128]{2,1,0:T(8,128)(2,1)S(1)}, bf16[3,256,128]{2,1,0:T(8,128)(2,1)S(1)}, bf16[3,256,128]{2,1,0:T...) custom-call(s32[4]{0:T(128)} %sources_in.1, s32[16]{0:T(128)} %owner_in.1, bf16[512,1024]{1,0:T(8,128)(2,1)} %key_in.1, ...), custom_call_target="tpu_custom_call" | custom-call | tf_op jit(solution)/shard_map/gate/pallas_call | solution.py:134
  8.4 0.0 collective-permute-done.refs_1_
  8.4 2.1 %collective-permute-done.1.refs_2_ = bf16[64,512]{1,0:T(8,128)(2,1)S(1)} collective-permute-done((bf16[64,512]{1,0:T(8,128)(2,1)}, bf16[64,512]{1,0:T(8,128)(2,1)S(1)}, u32[]{:S(2)}, u32[]{:S(2)}) %collective-permute-start.1) | collective-permute-done | bytes 65568 | tf_op jit(solution)/shard_map/ppermute | solution.py:394
  10.5 1.4 %collective-permute-done.2.refs_3_ = bf16[64,512]{1,0:T(8,128)(2,1)S(1)} collective-permute-done((bf16[64,512]{1,0:T(8,128)(2,1)}, bf16[64,512]{1,0:T(8,128)(2,1)S(1)}, u32[]{:S(2)}, u32[]{:S(2)}) %collective-permute-start.2) | collective-permute-done | bytes 65568 | tf_op jit(solution)/shard_map/ppermute | solution.py:394
  11.9 2.3 %collective-permute-start.4 = (bf16[3,256,128]{2,1,0:T(8,128)(2,1)S(1)}, bf16[3,256,128]{2,1,0:T(8,128)(2,1)S(1)}, u32[]{:S(2)}, u32[]{:S(2)}) collective-permute-start(bf16[3,256,128]{2,1,0:T(8,128)(2,1)S(1)} %get-tuple-element.39), channel_id=1, source_target_pairs={{0,8},{4,12},{8,0},{12,4},{1,9},{5,13},{9,1},{13,5},{2,10},{6,14},... | collective-permute-start | bytes 589832 | tf_op jit(solution)/shard_map/ppermute | solution.py:394
  14.2 2.1 %collective-permute-start.5 = (bf16[3,256,128]{2,1,0:T(8,128)(2,1)S(1)}, bf16[3,256,128]{2,1,0:T(8,128)(2,1)S(1)}, u32[]{:S(2)}, u32[]{:S(2)}) collective-permute-start(bf16[3,256,128]{2,1,0:T(8,128)(2,1)S(1)} %get-tuple-element.40), channel_id=1, source_target_pairs={{0,12},{4,8},{8,4},{12,0},{1,13},{5,9},{9,5},{13,1},{2,14},{6,10},... | collective-permute-start | bytes 589832 | tf_op jit(solution)/shard_map/ppermute | solution.py:394
  16.3 0.8 %copy-done.1 = bf16[64,512]{1,0:T(8,128)(2,1)S(1)} copy-done((bf16[64,512]{1,0:T(8,128)(2,1)S(1)}, bf16[64,512]{1,0:T(8,128)(2,1)}, u32[]{:S(2)}) %copy-start.1) | copy-done | bytes 65560
  17.1 2.5 %lags.1.shifted = bf16[64,16,2304]{2,1,0:T(8,128)(2,1)S(1)} custom-call(bf16[64,512]{1,0:T(8,128)(2,1)S(1)} %copy-done.1, bf16[64,512]{1,0:T(8,128)(2,1)S(1)} %collective-permute-done.refs_1_, bf16[64,512]{1,0:T(8,128)(2,1)S(1)} %collective-permute-done.1.refs_2_, bf16[64,512]{1,0:T(8,128)(2,1)S(1)} %collective-permute-done.2.refs_3_), custom_call_target="tpu_custom_call" | custom-call | tf_op jit(solution)/shard_map/lags/pallas_call | solution.py:228
  19.6 2.3 %last_term.1.term = f32[128,1024]{1,0:T(8,128)S(1)} custom-call(s32[19]{0:T(128)S(1)} %get-tuple-element.27.meta.meta_in, bf16[1024,128]{1,0:T(8,128)(2,1)S(1)} %get-tuple-element.28.last, bf16[64,16,2304]{2,1,0:T(8,128)(2,1)S(1)} %lags.1.shifted), custom_call_target="tpu_custom_call" | custom-call | tf_op jit(solution)/shard_map/last_term/pallas_call | solution.py:284
  21.9 0.0 collective-permute-done.3.refs_1_
  21.9 6.9 %collective-permute-done.4.refs_2_ = bf16[3,256,128]{2,1,0:T(8,128)(2,1)S(1)} collective-permute-done((bf16[3,256,128]{2,1,0:T(8,128)(2,1)S(1)}, bf16[3,256,128]{2,1,0:T(8,128)(2,1)S(1)}, u32[]{:S(2)}, u32[]{:S(2)}) %collective-permute-start.4) | collective-permute-done | bytes 196640 | tf_op jit(solution)/shard_map/ppermute | solution.py:394
  28.8 0.6 %merge.1.pieces = bf16[3,256,128]{2,1,0:T(8,128)(2,1)S(1)} custom-call(s32[19]{0:T(128)S(1)} %get-tuple-element.27.meta.meta_in, bf16[3,256,128]{2,1,0:T(8,128)(2,1)S(1)} %get-tuple-element.41.refs_0_, bf16[3,256,128]{2,1,0:T(8,128)(2,1)S(1)} %collective-permute-done.3.refs_1_, bf16[3,256,128]{2,1,0:T(8,128)(2,1)S(1)} %collective-permute-done.4.refs_2_, ...), custom_call_target="tpu_custom_call" | custom-call | tf_op jit(solution)/shard_map/merge/pallas_call | solution.py:168
  29.5 4.3 %collective-permute-start.6 = (bf16[3,256,128]{2,1,0:T(8,128)(2,1)S(1)}, bf16[3,256,128]{2,1,0:T(8,128)(2,1)S(1)}, u32[]{:S(2)}, u32[]{:S(2)}) collective-permute-start(bf16[3,256,128]{2,1,0:T(8,128)(2,1)S(1)} %merge.1.pieces), channel_id=1, source_target_pairs={{0,8},{8,0},{4,12},{12,4},{1,9},{9,1},{5,13},{13,5},{2,10},{10,2},... | collective-permute-start | bytes 589832 | tf_op jit(solution)/shard_map/ppermute | solution.py:409
  33.8 0.0 collective-permute-start.9
  33.8 2.7 %conv.4.refs_0_ = bf16[512,1024]{1,0:T(8,128)(2,1)} custom-call(s32[19]{0:T(128)S(1)} %get-tuple-element.27.meta.meta_in, bf16[3,256,128]{2,1,0:T(8,128)(2,1)S(1)} %merge.1.pieces, bf16[64,16,2304]{2,1,0:T(8,128)(2,1)S(1)} %lags.1.shifted, f32[128,1024]{1,0:T(8,128)S(1)} %last_term.1.term, bf16[512,1024]{1,0:T(8,128)(2,1)S(1)} %copy-done), custom_call_target="tpu_custom_call" | custom-call | tf_op jit(solution)/shard_map/conv/pallas_call | solution.py:369
  36.5 4.9 %collective-permute-done.6.pieces = bf16[3,256,128]{2,1,0:T(8,128)(2,1)S(1)} collective-permute-done((bf16[3,256,128]{2,1,0:T(8,128)(2,1)S(1)}, bf16[3,256,128]{2,1,0:T(8,128)(2,1)S(1)}, u32[]{:S(2)}, u32[]{:S(2)}) %collective-permute-start.6) | collective-permute-done | bytes 196640 | tf_op jit(solution)/shard_map/ppermute | solution.py:409
  41.4 1.3 %collective-permute-start.7 = (bf16[3,256,128]{2,1,0:T(8,128)(2,1)S(1)}, bf16[3,256,128]{2,1,0:T(8,128)(2,1)S(1)}, u32[]{:S(2)}, u32[]{:S(2)}) collective-permute-start(bf16[3,256,128]{2,1,0:T(8,128)(2,1)S(1)} %collective-permute-done.6.pieces), channel_id=1, source_target_pairs={{8,12},{4,0},{9,13},{5,1},{10,14},{6,2},{11,15},{7,3},{24,28},{20,... | collective-permute-start | bytes 589832 | tf_op jit(solution)/shard_map/ppermute | solution.py:412
  42.7 0.7 %collective-permute-start.8 = (bf16[3,256,128]{2,1,0:T(8,128)(2,1)S(1)}, bf16[3,256,128]{2,1,0:T(8,128)(2,1)S(1)}, u32[]{:S(2)}, u32[]{:S(2)}) collective-permute-start(bf16[3,256,128]{2,1,0:T(8,128)(2,1)S(1)} %merge.1.pieces), channel_id=1, source_target_pairs={{4,8},{8,4},{5,9},{9,5},{6,10},{10,6},{7,11},{11,7},{20,24},{24,20... | collective-permute-start | bytes 589832 | tf_op jit(solution)/shard_map/ppermute | solution.py:413
  43.4 2.7 %conv.5.refs_0_ = bf16[512,1024]{1,0:T(8,128)(2,1)} custom-call(s32[19]{0:T(128)S(1)} %get-tuple-element.27.meta.meta_in, bf16[3,256,128]{2,1,0:T(8,128)(2,1)S(1)} %collective-permute-done.9.pieces, bf16[64,16,2304]{2,1,0:T(8,128)(2,1)S(1)} %lags.1.shifted, f32[128,1024]{1,0:T(8,128)S(1)} %last_term.1.term, ...), custom_call_target="tpu_custom_call", output_to_operand_aliasing={{}: (5, {})} | custom-call | tf_op jit(solution)/shard_map/conv/pallas_call | solution.py:369
  46.1 2.7 %conv.6.refs_1_ = bf16[512,1024]{1,0:T(8,128)(2,1)} custom-call(s32[19]{0:T(128)S(1)} %get-tuple-element.27.meta.meta_in, bf16[3,256,128]{2,1,0:T(8,128)(2,1)S(1)} %collective-permute-done.6.pieces, bf16[64,16,2304]{2,1,0:T(8,128)(2,1)S(1)} %lags.1.shifted, f32[128,1024]{1,0:T(8,128)S(1)} %last_term.1.term, ...), custom_call_target="tpu_custom_call", output_to_operand_aliasing={{}: (5, {})} | custom-call | tf_op jit(solution)/shard_map/conv/pallas_call | solution.py:369
  48.9 0.8 %collective-permute-done.7.pieces = bf16[3,256,128]{2,1,0:T(8,128)(2,1)S(1)} collective-permute-done((bf16[3,256,128]{2,1,0:T(8,128)(2,1)S(1)}, bf16[3,256,128]{2,1,0:T(8,128)(2,1)S(1)}, u32[]{:S(2)}, u32[]{:S(2)}) %collective-permute-start.7) | collective-permute-done | bytes 196640 | tf_op jit(solution)/shard_map/ppermute | solution.py:412
  49.7 2.7 %conv.7 = bf16[512,1024]{1,0:T(8,128)(2,1)} custom-call(s32[19]{0:T(128)S(1)} %get-tuple-element.27.meta.meta_in, bf16[3,256,128]{2,1,0:T(8,128)(2,1)S(1)} %collective-permute-done.7.pieces, bf16[64,16,2304]{2,1,0:T(8,128)(2,1)S(1)} %lags.1.shifted, f32[128,1024]{1,0:T(8,128)S(1)} %last_term.1.term, ...), custom_call_target="tpu_custom_call", output_to_operand_aliasing={{}: (6, {})} | custom-call | tf_op jit(solution)/shard_map/conv/pallas_call | solution.py:369
  (8 shorter events, 0.0 us)
Async XLA Ops:
  0.0 8.4 %collective-permute-start = (bf16[64,512]{1,0:T(8,128)(2,1)}, bf16[64,512]{1,0:T(8,128)(2,1)S(1)}, u32[]{:S(2)}, u32[]{:S(2)}) collective-permute-start(bf16[64,512]{1,0:T(8,128)(2,1)} %refs_0_), channel_id=1, source_target_pairs={{0,4},{4,0},{8,12},{12,8},{1,5},{5,1},{9,13},{13,9},{2,6},{6,2},{1... | collective-permute-start | bytes 196616 | tf_op jit(solution)/shard_map/ppermute | solution.py:394
  3.0 7.5 %collective-permute-start.1 = (bf16[64,512]{1,0:T(8,128)(2,1)}, bf16[64,512]{1,0:T(8,128)(2,1)S(1)}, u32[]{:S(2)}, u32[]{:S(2)}) collective-permute-start(bf16[64,512]{1,0:T(8,128)(2,1)} %refs_0_), channel_id=1, source_target_pairs={{0,8},{4,12},{8,0},{12,4},{1,9},{5,13},{9,1},{13,5},{2,10},{6,14},... | collective-permute-start | bytes 196616 | tf_op jit(solution)/shard_map/ppermute | solution.py:394
  5.6 6.3 %collective-permute-start.2 = (bf16[64,512]{1,0:T(8,128)(2,1)}, bf16[64,512]{1,0:T(8,128)(2,1)S(1)}, u32[]{:S(2)}, u32[]{:S(2)}) collective-permute-start(bf16[64,512]{1,0:T(8,128)(2,1)} %refs_0_), channel_id=1, source_target_pairs={{0,12},{4,8},{8,4},{12,0},{1,13},{5,9},{9,5},{13,1},{2,14},{6,10},... | collective-permute-start | bytes 196616 | tf_op jit(solution)/shard_map/ppermute | solution.py:394
  11.9 21.9 %copy-start = (bf16[512,1024]{1,0:T(8,128)(2,1)S(1)}, bf16[512,1024]{1,0:T(8,128)(2,1)}, u32[]{:S(2)}) copy-start(bf16[512,1024]{1,0:T(8,128)(2,1)} %query.7) | copy-start | bytes 3145732
  11.9 10.0 %collective-permute-start.3 = (bf16[3,256,128]{2,1,0:T(8,128)(2,1)S(1)}, bf16[3,256,128]{2,1,0:T(8,128)(2,1)S(1)}, u32[]{:S(2)}, u32[]{:S(2)}) collective-permute-start(bf16[3,256,128]{2,1,0:T(8,128)(2,1)S(1)} %get-tuple-element.38), channel_id=1, source_target_pairs={{0,4},{4,0},{8,12},{12,8},{1,5},{5,1},{9,13},{13,9},{2,6},{6,2},{1... | collective-permute-start | bytes 589832 | tf_op jit(solution)/shard_map/ppermute | solution.py:394
  11.9 16.9 %collective-permute-start.4 = (bf16[3,256,128]{2,1,0:T(8,128)(2,1)S(1)}, bf16[3,256,128]{2,1,0:T(8,128)(2,1)S(1)}, u32[]{:S(2)}, u32[]{:S(2)}) collective-permute-start(bf16[3,256,128]{2,1,0:T(8,128)(2,1)S(1)} %get-tuple-element.39), channel_id=1, source_target_pairs={{0,8},{4,12},{8,0},{12,4},{1,9},{5,13},{9,1},{13,5},{2,10},{6,14},... | collective-permute-start | bytes 589832 | tf_op jit(solution)/shard_map/ppermute | solution.py:394
  14.2 14.6 %collective-permute-start.5 = (bf16[3,256,128]{2,1,0:T(8,128)(2,1)S(1)}, bf16[3,256,128]{2,1,0:T(8,128)(2,1)S(1)}, u32[]{:S(2)}, u32[]{:S(2)}) collective-permute-start(bf16[3,256,128]{2,1,0:T(8,128)(2,1)S(1)} %get-tuple-element.40), channel_id=1, source_target_pairs={{0,12},{4,8},{8,4},{12,0},{1,13},{5,9},{9,5},{13,1},{2,14},{6,10},... | collective-permute-start | bytes 589832 | tf_op jit(solution)/shard_map/ppermute | solution.py:394
  16.3 0.8 %copy-start.1 = (bf16[64,512]{1,0:T(8,128)(2,1)S(1)}, bf16[64,512]{1,0:T(8,128)(2,1)}, u32[]{:S(2)}) copy-start(bf16[64,512]{1,0:T(8,128)(2,1)} %refs_0_) | copy-start | bytes 196612
  29.5 11.9 %collective-permute-start.6 = (bf16[3,256,128]{2,1,0:T(8,128)(2,1)S(1)}, bf16[3,256,128]{2,1,0:T(8,128)(2,1)S(1)}, u32[]{:S(2)}, u32[]{:S(2)}) collective-permute-start(bf16[3,256,128]{2,1,0:T(8,128)(2,1)S(1)} %merge.1.pieces), channel_id=1, source_target_pairs={{0,8},{8,0},{4,12},{12,4},{1,9},{9,1},{5,13},{13,5},{2,10},{10,2},... | collective-permute-start | bytes 589832 | tf_op jit(solution)/shard_map/ppermute | solution.py:409
  33.8 9.6 %collective-permute-start.9 = (bf16[3,256,128]{2,1,0:T(8,128)(2,1)S(1)}, bf16[3,256,128]{2,1,0:T(8,128)(2,1)S(1)}, u32[]{:S(2)}, u32[]{:S(2)}) collective-permute-start(bf16[3,256,128]{2,1,0:T(8,128)(2,1)S(1)} %merge.1.pieces), channel_id=1, source_target_pairs={{0,4},{4,0},{8,12},{12,8},{1,5},{5,1},{9,13},{13,9},{2,6},{6,2},{1... | collective-permute-start | bytes 589832 | tf_op jit(solution)/shard_map/ppermute | solution.py:408
  41.4 8.3 %collective-permute-start.7 = (bf16[3,256,128]{2,1,0:T(8,128)(2,1)S(1)}, bf16[3,256,128]{2,1,0:T(8,128)(2,1)S(1)}, u32[]{:S(2)}, u32[]{:S(2)}) collective-permute-start(bf16[3,256,128]{2,1,0:T(8,128)(2,1)S(1)} %collective-permute-done.6.pieces), channel_id=1, source_target_pairs={{8,12},{4,0},{9,13},{5,1},{10,14},{6,2},{11,15},{7,3},{24,28},{20,... | collective-permute-start | bytes 589832 | tf_op jit(solution)/shard_map/ppermute | solution.py:412
  42.7 7.0 %collective-permute-start.8 = (bf16[3,256,128]{2,1,0:T(8,128)(2,1)S(1)}, bf16[3,256,128]{2,1,0:T(8,128)(2,1)S(1)}, u32[]{:S(2)}, u32[]{:S(2)}) collective-permute-start(bf16[3,256,128]{2,1,0:T(8,128)(2,1)S(1)} %merge.1.pieces), channel_id=1, source_target_pairs={{4,8},{8,4},{5,9},{9,5},{6,10},{10,6},{7,11},{11,7},{20,24},{24,20... | collective-permute-start | bytes 589832 | tf_op jit(solution)/shard_map/ppermute | solution.py:413

commit v3 on v2

--- a/solution.py
+++ b/solution.py
@@ -54,9 +54,15 @@
     return tiles
 
 
-def gate_kernel(size, parts, fill, sources_in, owner_in, key_in, value_in, *refs):
-    sends = refs[:parts]
-    last, meta, sources, owner, key, value, sems = refs[parts:]
+PLACE = SENT
+MANY = 2 * SENT
+WINDOWS = MANY + 1
+SLOTS = 2
+
+
+def gate_kernel(size, parts, sources_in, owner_in, key_in, value_in, *refs):
+    sends, extras = refs[:parts], refs[parts : 2 * parts]
+    last, meta, sources, owner, key, value, sems = refs[2 * parts :]
     stretch_count = owner.shape[0]
     slots = key.shape[0] // STRETCH
     channels = key.shape[1]
@@ -87,7 +93,7 @@
         def _():
             for w in range(WIN):
                 lag_block = jnp.maximum(k - sources[w], -1)
-                meta[SENT + slot * WIN + w] = (stretch_count - 1 - lag_block) * STRETCH
+                meta[WINDOWS + slot * WIN + w] = (stretch_count - 1 - lag_block) * STRETCH
 
         return slot + jnp.where(mine, 1, 0)
 
@@ -96,49 +102,62 @@
         copy.wait()
     for start in range(0, channels, LANES):
         last[pl.ds(start, LANES), :] = product((slots - 1) * STRETCH, pl.ds(start, LANES))
-    for w in range(SENT):
-        stretch = sources[w]
-        holder = owner[stretch]
-        mine = holder == me
+    holders = [owner[sources[w]] for w in range(SENT)]
+    many = 0
+    for w, holder in enumerate(holders):
+        place = sum([jnp.where(other == holder, 1, 0) for other in holders[:w]], 0)
         meta[w] = holder
-
-        @pl.when(mine)
-        def _(w=w, stretch=stretch, holder=holder):
+        meta[PLACE + w] = place
+        many = many + jnp.where(place >= SLOTS, 1, 0)
+
+        @pl.when(holder == me)
+        def _(w=w, holder=holder, place=place):
             def count(k, total):
                 return total + jnp.where(owner[k] == holder, 1, 0)
 
-            slot = lax.fori_loop(0, stretch, count, 0)
+            slot = lax.fori_loop(0, sources[w], count, 0)
             first = pl.multiple_of(slot * STRETCH, STRETCH)
             for step in range(parts):
                 base = (partner(me, step, size) if parts > 1 else 0) * width
-                for start in range(0, width, LANES):
-                    columns = pl.ds(pl.multiple_of(base + start, LANES), LANES)
-                    sends[step][w, pl.ds(start, LANES), :] = product(first, columns)
-
-        if fill:
-
-            @pl.when(jnp.logical_not(mine))
-            def _(w=w):
-                for send in sends:
-                    send[w] = jnp.zeros(send.shape[1:], send.dtype)
-
-
-def gate(size, parts, fill, sources, owner, key_proj, value_proj):
+
+                def fill(target, step=step, base=base):
+                    for start in range(0, width, LANES):
+                        columns = pl.ds(pl.multiple_of(base + start, LANES), LANES)
+                        target[pl.ds(start, LANES), :] = product(first, columns)
+
+                if w < SLOTS:
+                    fill(sends[step].at[place])
+                else:
+
+                    @pl.when(place < SLOTS)
+                    def _(step=step, fill=fill):
+                        fill(sends[step].at[jnp.minimum(place, SLOTS - 1)])
+
+                    @pl.when(place >= SLOTS)
+                    def _(step=step, fill=fill):
+                        fill(extras[step].at[0])
+
+    meta[MANY] = many
+
+
+def gate(size, parts, sources, owner, key_proj, value_proj):
     row_count, channels = key_proj.shape
     slots = row_count // STRETCH
     operands = [
         pltpu.with_memory_space_constraint(operand, pltpu.HBM)
         for operand in (sources, owner, key_proj, value_proj)
     ]
-    send = jax.ShapeDtypeStruct((SENT, channels // parts, STRETCH), jnp.bfloat16)
+    send = jax.ShapeDtypeStruct((SLOTS, channels // parts, STRETCH), jnp.bfloat16)
+    extra = jax.ShapeDtypeStruct((SENT - SLOTS, channels // parts, STRETCH), jnp.bfloat16)
     *sends, last, meta = pl.pallas_call(
-        functools.partial(gate_kernel, size, parts, fill),
+        functools.partial(gate_kernel, size, parts),
         in_specs=[HBM_SPEC] * 4,
-        out_specs=[VMEM_SPEC] * (parts + 1) + [SMEM_SPEC],
+        out_specs=[VMEM_SPEC] * (2 * parts + 1) + [SMEM_SPEC],
         out_shape=[send] * parts
+        + [extra] * parts
         + [
             jax.ShapeDtypeStruct((channels, STRETCH), jnp.bfloat16),
-            jax.ShapeDtypeStruct((SENT + slots * WIN,), jnp.int32),
+            jax.ShapeDtypeStruct((WINDOWS + slots * WIN,), jnp.int32),
         ],
         scratch_shapes=[
             pltpu.SMEM(sources.shape, jnp.int32),
@@ -150,29 +169,37 @@
         compiler_params=params(),
         name="gate",
     )(*operands)
-    return sends, last, meta
+    return sends[:parts], sends[parts:], last, meta
 
 
 def merge_kernel(size, meta, *refs):
-    parts, out = refs[:-1], refs[-1]
+    parts, extras, out = refs[:size], refs[size:-1], refs[-1]
     me = lax.axis_index("seq")
     for w in range(SENT):
+        place = meta[PLACE + w]
         for step in range(size):
-
-            @pl.when(sender(me, step, size) == meta[w])
-            def _(w=w, step=step):
-                out[w] = parts[step][w]
-
-
-def merge(size, meta, parts):
+            here = sender(me, step, size) == meta[w]
+
+            @pl.when(here & (place < SLOTS))
+            def _(w=w, step=step, place=place):
+                out[w] = parts[step][jnp.minimum(place, SLOTS - 1)]
+
+            if extras and w >= SLOTS:
+
+                @pl.when(here & (place >= SLOTS))
+                def _(w=w, step=step):
+                    out[w] = extras[step][0]
+
+
+def merge(size, meta, parts, extras=()):
     return pl.pallas_call(
         functools.partial(merge_kernel, size),
-        in_specs=[SMEM_SPEC] + [VMEM_SPEC] * size,
+        in_specs=[SMEM_SPEC] + [VMEM_SPEC] * (size + len(extras)),
         out_specs=VMEM_SPEC,
-        out_shape=jax.ShapeDtypeStruct(parts[0].shape, parts[0].dtype),
+        out_shape=jax.ShapeDtypeStruct((SENT,) + parts[0].shape[1:], parts[0].dtype),
         compiler_params=params(),
         name="merge",
-    )(meta, *parts)
+    )(meta, *parts, *extras)
 
 
 def lags_kernel(size, *refs):
@@ -260,7 +287,7 @@
 
 
 def window(meta, shifted, group, slot, w):
-    start = pl.multiple_of(meta[SENT + slot * WIN + w], STRETCH)
+    start = pl.multiple_of(meta[WINDOWS + slot * WIN + w], STRETCH)
     return shifted[group, :, pl.ds(start, SPAN)]
 
 
@@ -394,24 +421,36 @@
         return lax.ppermute(value, "seq", [(z, z ^ step if size & (size - 1) == 0 else (z + step) % size) for z in range(size)])
 
     filter_parts = [filters] + [to_partner(filters, step) for step in range(1, size)]
-    sends, last, meta = gate(size, parts, not by_parts, sources, owner, key_proj, value_proj)
+    sends, extras, last, meta = gate(size, parts, sources, owner, key_proj, value_proj)
     sends, filter_parts = lax.optimization_barrier((sends, filter_parts))
     shifted = lags(size, filter_parts)
     term = last_term(slots, meta, last, shifted)
     if not by_parts:
-        pieces = lax.psum(sends[0], "seq")
+        me = lax.axis_index("seq")
+        held = jnp.concatenate([sends[0], extras[0]])
+        places = meta[PLACE:MANY]
+        mine = (meta[:SENT] == me)[:, None, None]
+        pieces = lax.psum(jnp.where(mine, held[places], jnp.zeros_like(held)), "seq")
         return conv(0, meta, pieces, shifted, term, query_proj, None)
 
     scattered = [sends[0]] + [to_partner(sends[step], step) for step in range(1, size)]
     term, *scattered = lax.optimization_barrier((term, *scattered))
-    merged = merge(size, meta, scattered)
+
+    def merge_more(meta, scattered, extras):
+        more = [extras[0]] + [to_partner(extras[step], step) for step in range(1, size)]
+        return merge(size, meta, scattered, more)
+
+    def merge_plain(meta, scattered, extras):
+        return merge(size, meta, scattered)
+
+    merged = lax.cond(meta[MANY] > 0, merge_more, merge_plain, meta, scattered, extras)
+    far = lax.ppermute(merged, "seq", [(0, 2), (2, 0), (1, 3), (3, 1)])
     near = lax.ppermute(merged, "seq", [(0, 1), (1, 0), (2, 3), (3, 2)])
-    far = lax.ppermute(merged, "seq", [(0, 2), (2, 0), (1, 3), (3, 1)])
     out = conv(0, meta, merged, shifted, term, query_proj, None)
+    out = conv(1, meta, near, shifted, term, query_proj, out)
     merged, far, out = lax.optimization_barrier((merged, far, out))
     onward = lax.ppermute(far, "seq", [(2, 3), (1, 0)])
     middle = lax.ppermute(merged, "seq", [(1, 2), (2, 1)])
-    out = conv(1, meta, near, shifted, term, query_proj, out)
     out = conv(2, meta, far, shifted, term, query_proj, out)
     return conv(3, meta, onward, shifted, term, query_proj, out, middle)
 

time: 53.3 us -> 48.9 us (0.917)
  the two profiles are of different devices: /device:TPU:0 before, /device:TPU:20 now
where the time goes in v3:
time: 48.9 us; the launch traced here: 48.6 us
  Pallas kernels  18.7 us (38%)
  starting transfers between devices  15.3 us (31%)
  waiting for transfers between devices  7.98 us (16%)
  local copies, waits for them, and re-layouts  5.87 us (12%)
  between operations  0.78 us (2%)
    pallas_call x4, Pallas kernels, conv(): pl.pallas_call(functools.partial(conv_kernel, step, slots), in_specs=in_s...  11 us
    ppermute x6, starting transfers between devices, to_partner(): lax.ppermute(value, 'seq', [(z, z ^ step if size & size - 1 == 0 else (z...  6.98 us
    unnamed x8, local copies, waits for them, and re-layouts  5.29 us
    ppermute x6, waiting for transfers between devices, to_partner(): lax.ppermute(value, 'seq', [(z, z ^ step if size & size - 1 == 0 else (z...  4.67 us
    ppermute x1, starting transfers between devices, shards(): onward = lax.ppermute(far, 'seq', [(2, 3), (1, 0)])  4 us
    pallas_call x1, Pallas kernels, lags(): pl.pallas_call(functools.partial(lags_kernel, size), grid=(group_count //...  2.48 us
    ppermute x1, waiting for transfers between devices, shards(): middle = lax.ppermute(merged, 'seq', [(1, 2), (2, 1)])  2.45 us
    ppermute x1, starting transfers between devices, shards(): middle = lax.ppermute(merged, 'seq', [(1, 2), (2, 1)])  2.37 us
  transfers between devices with their start and end apart: 10, of which 5 were waited for; matrix products, arithmetic and copies ran while one was open for 1% of the time, Pallas kernels for 31%

profile of v3, /device:TPU:20, one launch (start us, length us, event | category | flops | bytes accessed | tf_op | source)
XLA Modules:
  0.0 48.6 jit_solution(4967385215785173131)
XLA Ops:
  0.0 1.6 %collective-permute-start.3 = (bf16[64,512]{1,0:T(8,128)(2,1)}, bf16[64,512]{1,0:T(8,128)(2,1)S(1)}, u32[]{:S(2)}, u32[]{:S(2)}) collective-permute-start(bf16[64,512]{1,0:T(8,128)(2,1)} %refs_0_), channel_id=1, source_target_pairs={{0,4},{4,0},{8,12},{12,8},{1,5},{5,1},{9,13},{13,9},{2,6},{6,2},{1... | collective-permute-start | bytes 196616 | tf_op jit(solution)/shard_map/ppermute | solution.py:421
  1.9 1.6 %collective-permute-start.5 = (bf16[64,512]{1,0:T(8,128)(2,1)}, bf16[64,512]{1,0:T(8,128)(2,1)S(1)}, u32[]{:S(2)}, u32[]{:S(2)}) collective-permute-start(bf16[64,512]{1,0:T(8,128)(2,1)} %refs_0_), channel_id=1, source_target_pairs={{0,12},{4,8},{8,4},{12,0},{1,13},{5,9},{9,5},{13,1},{2,14},{6,10},... | collective-permute-start | bytes 196616 | tf_op jit(solution)/shard_map/ppermute | solution.py:421
  3.5 2.3 %gate.1 = (bf16[2,256,128]{2,1,0:T(8,128)(2,1)S(1)}, bf16[2,256,128]{2,1,0:T(8,128)(2,1)S(1)}, bf16[2,256,128]{2,1,0:T(8,128)(2,1)S(1)}, bf16[2,256,128]{2,1,0:T...) custom-call(s32[4]{0:T(128)} %sources_in.1, ...), custom_call_target="tpu_custom_call" | custom-call | tf_op jit(solution)/shard_map/gate/pallas_call | solution.py:152
  5.8 1.2 %collective-permute-done.4.refs_2_ = bf16[64,512]{1,0:T(8,128)(2,1)S(1)} collective-permute-done((bf16[64,512]{1,0:T(8,128)(2,1)}, bf16[64,512]{1,0:T(8,128)(2,1)S(1)}, u32[]{:S(2)}, u32[]{:S(2)}) %collective-permute-start.4) | collective-permute-done | bytes 65568 | tf_op jit(solution)/shard_map/ppermute | solution.py:421
  7.0 2.4 %collective-permute-done.5.refs_3_ = bf16[64,512]{1,0:T(8,128)(2,1)S(1)} collective-permute-done((bf16[64,512]{1,0:T(8,128)(2,1)}, bf16[64,512]{1,0:T(8,128)(2,1)S(1)}, u32[]{:S(2)}, u32[]{:S(2)}) %collective-permute-start.5) | collective-permute-done | bytes 65568 | tf_op jit(solution)/shard_map/ppermute | solution.py:421
  9.4 0.8 %collective-permute-start.6 = (bf16[2,256,128]{2,1,0:T(8,128)(2,1)S(1)}, bf16[2,256,128]{2,1,0:T(8,128)(2,1)S(1)}, u32[]{:S(2)}, u32[]{:S(2)}) collective-permute-start(bf16[2,256,128]{2,1,0:T(8,128)(2,1)S(1)} %get-tuple-element.87), channel_id=1, source_target_pairs={{0,4},{4,0},{8,12},{12,8},{1,5},{5,1},{9,13},{13,9},{2,6},{6,2},{1... | collective-permute-start | bytes 393224 | tf_op jit(solution)/shard_map/ppermute | solution.py:421
  10.8 2.1 %collective-permute-start.8 = (bf16[2,256,128]{2,1,0:T(8,128)(2,1)S(1)}, bf16[2,256,128]{2,1,0:T(8,128)(2,1)S(1)}, u32[]{:S(2)}, u32[]{:S(2)}) collective-permute-start(bf16[2,256,128]{2,1,0:T(8,128)(2,1)S(1)} %get-tuple-element.89), channel_id=1, source_target_pairs={{0,12},{4,8},{8,4},{12,0},{1,13},{5,9},{9,5},{13,1},{2,14},{6,10},... | collective-permute-start | bytes 393224 | tf_op jit(solution)/shard_map/ppermute | solution.py:421
  14.2 0.8 %copy-done.3 = bf16[64,512]{1,0:T(8,128)(2,1)S(1)} copy-done((bf16[64,512]{1,0:T(8,128)(2,1)S(1)}, bf16[64,512]{1,0:T(8,128)(2,1)}, u32[]{:S(2)}) %copy-start.3) | copy-done | bytes 65560
  15.0 2.5 %lags.1.shifted = bf16[64,16,2304]{2,1,0:T(8,128)(2,1)S(1)} custom-call(bf16[64,512]{1,0:T(8,128)(2,1)S(1)} %copy-done.3, bf16[64,512]{1,0:T(8,128)(2,1)S(1)} %collective-permute-done.3.refs_1_, bf16[64,512]{1,0:T(8,128)(2,1)S(1)} %collective-permute-done.4.refs_2_, bf16[64,512]{1,0:T(8,128)(2,1)S(1)} %collective-permute-done.5.refs_3_), custom_call_target="tpu_custom_call" | custom-call | tf_op jit(solution)/shard_map/lags/pallas_call | solution.py:255
  17.5 2.3 %last_term.1.term = f32[128,1024]{1,0:T(8,128)S(1)} custom-call(s32[23]{0:T(128)S(1)} %get-tuple-element.76.meta.meta_in, bf16[1024,128]{1,0:T(8,128)(2,1)S(1)} %get-tuple-element.77.last, bf16[64,16,2304]{2,1,0:T(8,128)(2,1)S(1)} %lags.1.shifted), custom_call_target="tpu_custom_call" | custom-call | tf_op jit(solution)/shard_map/last_term/pallas_call | solution.py:311
  19.8 2.1 %copy-done = bf16[64,16,2304]{2,1,0:T(8,128)(2,1)} copy-done((bf16[64,16,2304]{2,1,0:T(8,128)(2,1)}, bf16[64,16,2304]{2,1,0:T(8,128)(2,1)S(1)}, u32[]{:S(2)}) %copy-start) | copy-done | bytes 4718616
  21.9 1.0 %collective-permute-done.8 = bf16[2,256,128]{2,1,0:T(8,128)(2,1)S(1)} collective-permute-done((bf16[2,256,128]{2,1,0:T(8,128)(2,1)S(1)}, bf16[2,256,128]{2,1,0:T(8,128)(2,1)S(1)}, u32[]{:S(2)}, u32[]{:S(2)}) %collective-permute-start.8) | collective-permute-done | bytes 131104 | tf_op jit(solution)/shard_map/ppermute | solution.py:421
  23.0 0.7 %conditional.1 = (bf16[3,256,128]{2,1,0:T(8,128)(2,1)S(1)}) conditional(s32[]{:T(128)} %bitcast, (s32[23]{0:T(128)S(1)}, bf16[2,256,128]{2,1,0:T(8,128)(2,1)S(1)}, bf16[2,256,128]{2,1,0:T(8,128)(2,1)S(1)}, bf16[2,256,128]{2,1,0:T(8,128)(2,1)S(1)}, bf16[2,256,128]{2,1,0:T(8,128)(2,1)S(1)}) %tuple.16, (bf16[1,256,128]{2,1,0:T(8,128)(2,1)S(1)}, ...), branch_computations={%region_0.0_spmd, %region_1.0_spmd} | conditional | bytes 786560 | solution.py:446
  23.6 0.7 %collective-permute-start.10 = (bf16[3,256,128]{2,1,0:T(8,128)(2,1)S(1)}, bf16[3,256,128]{2,1,0:T(8,128)(2,1)S(1)}, u32[]{:S(2)}, u32[]{:S(2)}) collective-permute-start(bf16[3,256,128]{2,1,0:T(8,128)(2,1)S(1)} %get-tuple-element.102.pieces), channel_id=1, source_target_pairs={{0,4},{4,0},{8,12},{12,8},{1,5},{5,1},{9,13},{13,9},{2,6},{6,2},{1... | collective-permute-start | bytes 589832 | tf_op jit(solution)/shard_map/ppermute | solution.py:448
  24.3 1.2 %collective-permute-start.9 = (bf16[3,256,128]{2,1,0:T(8,128)(2,1)S(1)}, bf16[3,256,128]{2,1,0:T(8,128)(2,1)S(1)}, u32[]{:S(2)}, u32[]{:S(2)}) collective-permute-start(bf16[3,256,128]{2,1,0:T(8,128)(2,1)S(1)} %get-tuple-element.102.pieces), channel_id=1, source_target_pairs={{0,8},{8,0},{4,12},{12,4},{1,9},{9,1},{5,13},{13,5},{2,10},{10,2},... | collective-permute-start | bytes 589832 | tf_op jit(solution)/shard_map/ppermute | solution.py:447
  25.6 2.3 %copy-done.1 = bf16[64,16,2304]{2,1,0:T(8,128)(2,1)S(1)} copy-done((bf16[64,16,2304]{2,1,0:T(8,128)(2,1)S(1)}, bf16[64,16,2304]{2,1,0:T(8,128)(2,1)}, u32[]{:S(2)}) %copy-start.1) | copy-done | bytes 4718616
  27.9 2.7 %conv.4.refs_0_ = bf16[512,1024]{1,0:T(8,128)(2,1)} custom-call(s32[23]{0:T(128)S(1)} %get-tuple-element.76.meta.meta_in, bf16[3,256,128]{2,1,0:T(8,128)(2,1)S(1)} %get-tuple-element.102.pieces, bf16[64,16,2304]{2,1,0:T(8,128)(2,1)S(1)} %copy-done.1, f32[128,1024]{1,0:T(8,128)S(1)} %last_term.1.term, bf16[512,1024]{1,0:T(8,128)(2,1)S(1)} %copy-done.2), custom_call_target="tpu_custom_call" | custom-call | tf_op jit(solution)/shard_map/conv/pallas_call | solution.py:396
  30.7 0.9 %collective-permute-done.10.pieces = bf16[3,256,128]{2,1,0:T(8,128)(2,1)S(1)} collective-permute-done((bf16[3,256,128]{2,1,0:T(8,128)(2,1)S(1)}, bf16[3,256,128]{2,1,0:T(8,128)(2,1)S(1)}, u32[]{:S(2)}, u32[]{:S(2)}) %collective-permute-start.10) | collective-permute-done | bytes 196640 | tf_op jit(solution)/shard_map/ppermute | solution.py:448
  31.5 2.7 %conv.5.refs_0_ = bf16[512,1024]{1,0:T(8,128)(2,1)} custom-call(s32[23]{0:T(128)S(1)} %get-tuple-element.76.meta.meta_in, bf16[3,256,128]{2,1,0:T(8,128)(2,1)S(1)} %collective-permute-done.10.pieces, bf16[64,16,2304]{2,1,0:T(8,128)(2,1)S(1)} %copy-done.1, f32[128,1024]{1,0:T(8,128)S(1)} %last_term.1.term, ...), custom_call_target="tpu_custom_call", output_to_operand_aliasing={{}: (5, {})} | custom-call | tf_op jit(solution)/shard_map/conv/pallas_call | solution.py:396
  34.3 4.0 %collective-permute-start.11 = (bf16[3,256,128]{2,1,0:T(8,128)(2,1)S(1)}, bf16[3,256,128]{2,1,0:T(8,128)(2,1)S(1)}, u32[]{:S(2)}, u32[]{:S(2)}) collective-permute-start(bf16[3,256,128]{2,1,0:T(8,128)(2,1)S(1)} %collective-permute-done.9.pieces), channel_id=1, source_target_pairs={{8,12},{4,0},{9,13},{5,1},{10,14},{6,2},{11,15},{7,3},{24,28},{20,... | collective-permute-start | bytes 589832 | tf_op jit(solution)/shard_map/ppermute | solution.py:452
  38.3 2.4 %collective-permute-start.12 = (bf16[3,256,128]{2,1,0:T(8,128)(2,1)S(1)}, bf16[3,256,128]{2,1,0:T(8,128)(2,1)S(1)}, u32[]{:S(2)}, u32[]{:S(2)}) collective-permute-start(bf16[3,256,128]{2,1,0:T(8,128)(2,1)S(1)} %get-tuple-element.102.pieces), channel_id=1, source_target_pairs={{4,8},{8,4},{5,9},{9,5},{6,10},{10,6},{7,11},{11,7},{20,24},{24,20... | collective-permute-start | bytes 589832 | tf_op jit(solution)/shard_map/ppermute | solution.py:453
  40.7 2.7 %conv.6.refs_1_ = bf16[512,1024]{1,0:T(8,128)(2,1)} custom-call(s32[23]{0:T(128)S(1)} %get-tuple-element.76.meta.meta_in, bf16[3,256,128]{2,1,0:T(8,128)(2,1)S(1)} %collective-permute-done.9.pieces, bf16[64,16,2304]{2,1,0:T(8,128)(2,1)S(1)} %copy-done.1, f32[128,1024]{1,0:T(8,128)S(1)} %last_term.1.term, ...), custom_call_target="tpu_custom_call", output_to_operand_aliasing={{}: (5, {})} | custom-call | tf_op jit(solution)/shard_map/conv/pallas_call | solution.py:396
  43.4 2.5 %collective-permute-done.12.refs_0_ = bf16[3,256,128]{2,1,0:T(8,128)(2,1)S(1)} collective-permute-done((bf16[3,256,128]{2,1,0:T(8,128)(2,1)S(1)}, bf16[3,256,128]{2,1,0:T(8,128)(2,1)S(1)}, u32[]{:S(2)}, u32[]{:S(2)}) %collective-permute-start.12) | collective-permute-done | bytes 196640 | tf_op jit(solution)/shard_map/ppermute | solution.py:453
  45.9 2.7 %conv.7 = bf16[512,1024]{1,0:T(8,128)(2,1)} custom-call(s32[23]{0:T(128)S(1)} %get-tuple-element.76.meta.meta_in, bf16[3,256,128]{2,1,0:T(8,128)(2,1)S(1)} %collective-permute-done.11.pieces, bf16[64,16,2304]{2,1,0:T(8,128)(2,1)S(1)} %copy-done.1, f32[128,1024]{1,0:T(8,128)S(1)} %last_term.1.term, ...), custom_call_target="tpu_custom_call", output_to_operand_aliasing={{}: (6, {})} | custom-call | tf_op jit(solution)/shard_map/conv/pallas_call | solution.py:396
  (14 shorter events, 2.2 us)
Async XLA Ops:
  0.0 5.8 %collective-permute-start.3 = (bf16[64,512]{1,0:T(8,128)(2,1)}, bf16[64,512]{1,0:T(8,128)(2,1)S(1)}, u32[]{:S(2)}, u32[]{:S(2)}) collective-permute-start(bf16[64,512]{1,0:T(8,128)(2,1)} %refs_0_), channel_id=1, source_target_pairs={{0,4},{4,0},{8,12},{12,8},{1,5},{5,1},{9,13},{13,9},{2,6},{6,2},{1... | collective-permute-start | bytes 196616 | tf_op jit(solution)/shard_map/ppermute | solution.py:421
  1.6 5.5 %collective-permute-start.4 = (bf16[64,512]{1,0:T(8,128)(2,1)}, bf16[64,512]{1,0:T(8,128)(2,1)S(1)}, u32[]{:S(2)}, u32[]{:S(2)}) collective-permute-start(bf16[64,512]{1,0:T(8,128)(2,1)} %refs_0_), channel_id=1, source_target_pairs={{0,8},{4,12},{8,0},{12,4},{1,9},{5,13},{9,1},{13,5},{2,10},{6,14},... | collective-permute-start | bytes 196616 | tf_op jit(solution)/shard_map/ppermute | solution.py:421
  1.9 7.5 %collective-permute-start.5 = (bf16[64,512]{1,0:T(8,128)(2,1)}, bf16[64,512]{1,0:T(8,128)(2,1)S(1)}, u32[]{:S(2)}, u32[]{:S(2)}) collective-permute-start(bf16[64,512]{1,0:T(8,128)(2,1)} %refs_0_), channel_id=1, source_target_pairs={{0,12},{4,8},{8,4},{12,0},{1,13},{5,9},{9,5},{13,1},{2,14},{6,10},... | collective-permute-start | bytes 196616 | tf_op jit(solution)/shard_map/ppermute | solution.py:421
  9.4 12.5 %collective-permute-start.6 = (bf16[2,256,128]{2,1,0:T(8,128)(2,1)S(1)}, bf16[2,256,128]{2,1,0:T(8,128)(2,1)S(1)}, u32[]{:S(2)}, u32[]{:S(2)}) collective-permute-start(bf16[2,256,128]{2,1,0:T(8,128)(2,1)S(1)} %get-tuple-element.87), channel_id=1, source_target_pairs={{0,4},{4,0},{8,12},{12,8},{1,5},{5,1},{9,13},{13,9},{2,6},{6,2},{1... | collective-permute-start | bytes 393224 | tf_op jit(solution)/shard_map/ppermute | solution.py:421
  10.2 11.7 %collective-permute-start.7 = (bf16[2,256,128]{2,1,0:T(8,128)(2,1)S(1)}, bf16[2,256,128]{2,1,0:T(8,128)(2,1)S(1)}, u32[]{:S(2)}, u32[]{:S(2)}) collective-permute-start(bf16[2,256,128]{2,1,0:T(8,128)(2,1)S(1)} %get-tuple-element.88), channel_id=1, source_target_pairs={{0,8},{4,12},{8,0},{12,4},{1,9},{5,13},{9,1},{13,5},{2,10},{6,14},... | collective-permute-start | bytes 393224 | tf_op jit(solution)/shard_map/ppermute | solution.py:421
  10.8 12.1 %collective-permute-start.8 = (bf16[2,256,128]{2,1,0:T(8,128)(2,1)S(1)}, bf16[2,256,128]{2,1,0:T(8,128)(2,1)S(1)}, u32[]{:S(2)}, u32[]{:S(2)}) collective-permute-start(bf16[2,256,128]{2,1,0:T(8,128)(2,1)S(1)} %get-tuple-element.89), channel_id=1, source_target_pairs={{0,12},{4,8},{8,4},{12,0},{1,13},{5,9},{9,5},{13,1},{2,14},{6,10},... | collective-permute-start | bytes 393224 | tf_op jit(solution)/shard_map/ppermute | solution.py:421
  14.2 0.8 %copy-start.3 = (bf16[64,512]{1,0:T(8,128)(2,1)S(1)}, bf16[64,512]{1,0:T(8,128)(2,1)}, u32[]{:S(2)}) copy-start(bf16[64,512]{1,0:T(8,128)(2,1)} %refs_0_) | copy-start | bytes 196612
  17.5 8.1 %copy-start.2 = (bf16[512,1024]{1,0:T(8,128)(2,1)S(1)}, bf16[512,1024]{1,0:T(8,128)(2,1)}, u32[]{:S(2)}) copy-start(bf16[512,1024]{1,0:T(8,128)(2,1)} %query.7) | copy-start | bytes 3145732
  19.8 2.1 %copy-start = (bf16[64,16,2304]{2,1,0:T(8,128)(2,1)}, bf16[64,16,2304]{2,1,0:T(8,128)(2,1)S(1)}, u32[]{:S(2)}) copy-start(bf16[64,16,2304]{2,1,0:T(8,128)(2,1)S(1)} %lags.1.shifted) | copy-start | bytes 14155780
  23.6 7.9 %collective-permute-start.10 = (bf16[3,256,128]{2,1,0:T(8,128)(2,1)S(1)}, bf16[3,256,128]{2,1,0:T(8,128)(2,1)S(1)}, u32[]{:S(2)}, u32[]{:S(2)}) collective-permute-start(bf16[3,256,128]{2,1,0:T(8,128)(2,1)S(1)} %get-tuple-element.102.pieces), channel_id=1, source_target_pairs={{0,4},{4,0},{8,12},{12,8},{1,5},{5,1},{9,13},{13,9},{2,6},{6,2},{1... | collective-permute-start | bytes 589832 | tf_op jit(solution)/shard_map/ppermute | solution.py:448
  24.3 9.9 %collective-permute-start.9 = (bf16[3,256,128]{2,1,0:T(8,128)(2,1)S(1)}, bf16[3,256,128]{2,1,0:T(8,128)(2,1)S(1)}, u32[]{:S(2)}, u32[]{:S(2)}) collective-permute-start(bf16[3,256,128]{2,1,0:T(8,128)(2,1)S(1)} %get-tuple-element.102.pieces), channel_id=1, source_target_pairs={{0,8},{8,0},{4,12},{12,4},{1,9},{9,1},{5,13},{13,5},{2,10},{10,2},... | collective-permute-start | bytes 589832 | tf_op jit(solution)/shard_map/ppermute | solution.py:447
  25.6 2.3 %copy-start.1 = (bf16[64,16,2304]{2,1,0:T(8,128)(2,1)S(1)}, bf16[64,16,2304]{2,1,0:T(8,128)(2,1)}, u32[]{:S(2)}) copy-start(bf16[64,16,2304]{2,1,0:T(8,128)(2,1)} %copy-done) | copy-start | bytes 14155780
  34.3 9.1 %collective-permute-start.11 = (bf16[3,256,128]{2,1,0:T(8,128)(2,1)S(1)}, bf16[3,256,128]{2,1,0:T(8,128)(2,1)S(1)}, u32[]{:S(2)}, u32[]{:S(2)}) collective-permute-start(bf16[3,256,128]{2,1,0:T(8,128)(2,1)S(1)} %collective-permute-done.9.pieces), channel_id=1, source_target_pairs={{8,12},{4,0},{9,13},{5,1},{10,14},{6,2},{11,15},{7,3},{24,28},{20,... | collective-permute-start | bytes 589832 | tf_op jit(solution)/shard_map/ppermute | solution.py:452
  38.3 7.6 %collective-permute-start.12 = (bf16[3,256,128]{2,1,0:T(8,128)(2,1)S(1)}, bf16[3,256,128]{2,1,0:T(8,128)(2,1)S(1)}, u32[]{:S(2)}, u32[]{:S(2)}) collective-permute-start(bf16[3,256,128]{2,1,0:T(8,128)(2,1)S(1)} %get-tuple-element.102.pieces), channel_id=1, source_target_pairs={{4,8},{8,4},{5,9},{9,5},{6,10},{10,6},{7,11},{11,7},{20,24},{24,20... | collective-permute-start | bytes 589832 | tf_op jit(solution)/shard_map/ppermute | solution.py:453

commit v4 on v3

--- a/solution.py
+++ b/solution.py
@@ -14,7 +14,7 @@
 LANES = 128
 BLOCKS = LANES // GROUP_CH
 SPAN = 2 * STRETCH
-VMEM_LIMIT = 40 * 1024 * 1024
+VMEM_LIMIT = 16 * 1024 * 1024
 
 SMEM_SPEC = pl.BlockSpec(memory_space=pltpu.SMEM)
 ANY_SPEC = pl.BlockSpec(memory_space=pl.ANY)
@@ -60,9 +60,8 @@
 SLOTS = 2
 
 
-def gate_kernel(size, parts, sources_in, owner_in, key_in, value_in, *refs):
-    sends, extras = refs[:parts], refs[parts : 2 * parts]
-    last, meta, sources, owner, key, value, sems = refs[2 * parts :]
+def gate_kernel(size, parts, sources_in, owner_in, key_in, value_in, filters_in, *refs):
+    send, extra, last, meta, sources, owner, key, value, filters, sems = refs
     stretch_count = owner.shape[0]
     slots = key.shape[0] // STRETCH
     channels = key.shape[1]
@@ -73,6 +72,7 @@
         pltpu.make_async_copy(owner_in, owner, sems.at[1]),
         pltpu.make_async_copy(key_in, key, sems.at[2]),
         pltpu.make_async_copy(value_in, value, sems.at[3]),
+        pltpu.make_async_copy(filters_in, filters, sems.at[4]),
     ]
     for copy in copies:
         copy.start()
@@ -118,44 +118,50 @@
             slot = lax.fori_loop(0, sources[w], count, 0)
             first = pl.multiple_of(slot * STRETCH, STRETCH)
             for step in range(parts):
-                base = (partner(me, step, size) if parts > 1 else 0) * width
-
-                def fill(target, step=step, base=base):
+                part = partner(me, step, size) if parts > 1 else 0
+                base = part * width
+
+                def fill(target, offset, base=base):
                     for start in range(0, width, LANES):
                         columns = pl.ds(pl.multiple_of(base + start, LANES), LANES)
-                        target[pl.ds(start, LANES), :] = product(first, columns)
+                        target[pl.ds(offset + start, LANES), :] = product(first, columns)
 
                 if w < SLOTS:
-                    fill(sends[step].at[place])
+                    fill(send.at[part], pl.multiple_of(place * width, LANES))
                 else:
 
                     @pl.when(place < SLOTS)
-                    def _(step=step, fill=fill):
-                        fill(sends[step].at[jnp.minimum(place, SLOTS - 1)])
+                    def _(part=part, fill=fill):
+                        fill(send.at[part], pl.multiple_of(place * width, LANES))
 
                     @pl.when(place >= SLOTS)
                     def _(step=step, fill=fill):
-                        fill(extras[step].at[0])
+                        fill(extra.at[step], 0)
 
     meta[MANY] = many
-
-
-def gate(size, parts, sources, owner, key_proj, value_proj):
+    group_count = filters.shape[0]
+    for tile in range(filters.shape[1] // LANES):
+        rows = pl.ds(SLOTS * width + tile * group_count, group_count)
+        for part in range(parts):
+            send[part, rows, :] = filters[:, pl.ds(tile * LANES, LANES)]
+
+
+def gate(size, parts, sources, owner, key_proj, value_proj, filters):
     row_count, channels = key_proj.shape
     slots = row_count // STRETCH
+    width = channels // parts
     operands = [
         pltpu.with_memory_space_constraint(operand, pltpu.HBM)
-        for operand in (sources, owner, key_proj, value_proj)
+        for operand in (sources, owner, key_proj, value_proj, filters)
     ]
-    send = jax.ShapeDtypeStruct((SLOTS, channels // parts, STRETCH), jnp.bfloat16)
-    extra = jax.ShapeDtypeStruct((SENT - SLOTS, channels // parts, STRETCH), jnp.bfloat16)
-    *sends, last, meta = pl.pallas_call(
+    rows = SLOTS * width + filters.size // LANES
+    return pl.pallas_call(
         functools.partial(gate_kernel, size, parts),
-        in_specs=[HBM_SPEC] * 4,
-        out_specs=[VMEM_SPEC] * (2 * parts + 1) + [SMEM_SPEC],
-        out_shape=[send] * parts
-        + [extra] * parts
-        + [
+        in_specs=[HBM_SPEC] * 5,
+        out_specs=[VMEM_SPEC] * 3 + [SMEM_SPEC],
+        out_shape=[
+            jax.ShapeDtypeStruct((parts, rows, LANES), jnp.bfloat16),
+            jax.ShapeDtypeStruct((parts, width, LANES), jnp.bfloat16),
             jax.ShapeDtypeStruct((channels, STRETCH), jnp.bfloat16),
             jax.ShapeDtypeStruct((WINDOWS + slots * WIN,), jnp.int32),
         ],
@@ -164,71 +170,54 @@
             pltpu.SMEM(owner.shape, jnp.int32),
             pltpu.VMEM(key_proj.shape, key_proj.dtype),
             pltpu.VMEM(value_proj.shape, value_proj.dtype),
-            pltpu.SemaphoreType.DMA((4,)),
+            pltpu.VMEM(filters.shape, filters.dtype),
+            pltpu.SemaphoreType.DMA((5,)),
         ],
         compiler_params=params(),
         name="gate",
     )(*operands)
-    return sends[:parts], sends[parts:], last, meta
-
-
-def merge_kernel(size, meta, *refs):
-    parts, extras, out = refs[:size], refs[size:-1], refs[-1]
+
+
+def merge_kernel(size, width, meta, received, *refs):
+    extras, out = refs[:-1], refs[-1]
     me = lax.axis_index("seq")
     for w in range(SENT):
         place = meta[PLACE + w]
-        for step in range(size):
-            here = sender(me, step, size) == meta[w]
-
-            @pl.when(here & (place < SLOTS))
-            def _(w=w, step=step, place=place):
-                out[w] = parts[step][jnp.minimum(place, SLOTS - 1)]
-
-            if extras and w >= SLOTS:
-
-                @pl.when(here & (place >= SLOTS))
-                def _(w=w, step=step):
-                    out[w] = extras[step][0]
-
-
-def merge(size, meta, parts, extras=()):
+        rows = pl.ds(pl.multiple_of(jnp.minimum(place, SLOTS - 1) * width, LANES), width)
+        out[w] = received[meta[w], rows, :]
+    for w in range(SLOTS, SENT):
+        for step, extra in enumerate(extras):
+
+            @pl.when((sender(me, step, size) == meta[w]) & (meta[PLACE + w] >= SLOTS))
+            def _(w=w, extra=extra):
+                out[w] = extra[...]
+
+
+def merge(size, width, meta, received, extras=()):
     return pl.pallas_call(
-        functools.partial(merge_kernel, size),
-        in_specs=[SMEM_SPEC] + [VMEM_SPEC] * (size + len(extras)),
+        functools.partial(merge_kernel, size, width),
+        in_specs=[SMEM_SPEC] + [VMEM_SPEC] * (1 + len(extras)),
         out_specs=VMEM_SPEC,
-        out_shape=jax.ShapeDtypeStruct((SENT,) + parts[0].shape[1:], parts[0].dtype),
+        out_shape=jax.ShapeDtypeStruct((SENT, width, LANES), received.dtype),
         compiler_params=params(),
         name="merge",
-    )(meta, *parts, *extras)
-
-
-def lags_kernel(size, *refs):
-    received = refs[:size]
-    out, blocks, reverse, sems = refs[size:]
-    group_count, part = received[0].shape
-    lag_count = size * part
-    padded = out.shape[2]
+    )(meta, received, *extras)
+
+
+def lags_kernel(first, blocks, out, reverse):
+    group_count, padded = reverse.shape
+    tiles = (blocks.shape[1] - first) // group_count
+    lag_count = blocks.shape[0] * tiles * LANES
     tile_step = pl.program_id(0)
 
     @pl.when(tile_step == 0)
     def _():
-        me = lax.axis_index("seq")
-        copies = [
-            pltpu.make_async_copy(
-                received[step], blocks.at[sender(me, step, size)], sems.at[step]
-            )
-            for step in range(size)
-        ]
-        for copy in copies:
-            copy.start()
-        for copy in copies:
-            copy.wait()
         row = lax.broadcasted_iota(jnp.int32, (LANES, LANES), 0)
         column = lax.broadcasted_iota(jnp.int32, (LANES, LANES), 1)
         flip = jnp.where(row + column == LANES - 1, 1.0, 0.0).astype(jnp.bfloat16)
-        for start in range(0, lag_count, LANES):
-            piece = blocks[start // part, :, pl.ds(start % part, LANES)]
-            reverse[:, pl.ds(lag_count - LANES - start, LANES)] = jnp.dot(
+        for tile in range(lag_count // LANES):
+            piece = blocks[tile // tiles, pl.ds(first + tile % tiles * group_count, group_count), :]
+            reverse[:, pl.ds(lag_count - LANES * (tile + 1), LANES)] = jnp.dot(
                 piece, flip, preferred_element_type=jnp.float32
             )
         reverse[:, pl.ds(lag_count, padded - lag_count)] = jnp.zeros(
@@ -249,23 +238,19 @@
             before[g] = rolled
 
 
-def lags(size, received):
-    group_count, part = received[0].shape
-    padded = size * part + SPAN
+def lags(blocks, first, group_count):
+    size, rows, _ = blocks.shape
+    padded = size * (rows - first) // group_count * LANES + SPAN
     return pl.pallas_call(
-        functools.partial(lags_kernel, size),
+        functools.partial(lags_kernel, first),
         grid=(group_count // BLOCKS,),
-        in_specs=[ANY_SPEC] * size,
+        in_specs=[VMEM_SPEC],
         out_specs=pl.BlockSpec((BLOCKS, GROUP_CH, padded), lambda i: (i, 0, 0)),
         out_shape=jax.ShapeDtypeStruct((group_count, GROUP_CH, padded), jnp.bfloat16),
-        scratch_shapes=[
-            pltpu.VMEM((size, group_count, part), jnp.bfloat16),
-            pltpu.VMEM((group_count, padded), jnp.float32),
-            pltpu.SemaphoreType.DMA((size,)),
-        ],
+        scratch_shapes=[pltpu.VMEM((group_count, padded), jnp.float32)],
         compiler_params=params(),
         name="lags",
-    )(*received)
+    )(blocks)
 
 
 def spread_rows(tile, spans, base):
@@ -320,11 +305,11 @@
 
 
 def conv_kernel(step, slots, meta_in, pieces, shifted, term, query, *refs):
-    others, (out, meta, gates, result, spans, sems) = refs[:-6], refs[-6:]
+    out, meta, gates, result, spans, sems = refs[-6:]
     width = pieces.shape[1]
     size = out.shape[1] // width
     me = lax.axis_index("seq")
-    base = pl.multiple_of((me ^ step) * width if size > 1 else 0, width)
+    base = pl.multiple_of(lax.rem(me + size - step, size) * width, width)
     copies = [
         pltpu.make_async_copy(meta_in, meta, sems.at[0]),
         pltpu.make_async_copy(query.at[:, pl.ds(base, width)], gates, sems.at[1]),
@@ -336,9 +321,6 @@
     def spread(start):
         for w in range(SENT):
             tile = pieces[w, pl.ds(start, LANES), :]
-            if len(others) > 1:
-                end = (me == 0) | (me == size - 1)
-                tile = jnp.where(end, tile, others[0][w, pl.ds(start, LANES), :])
             spread_rows(tile, spans.at[start // LANES], w * SPAN)
 
     spread(0)
@@ -379,15 +361,12 @@
     store.wait()
 
 
-def conv(step, meta, pieces, shifted, term, query_proj, before, other=None):
+def conv(step, meta, pieces, shifted, term, query_proj, before):
     row_count = query_proj.shape[0]
     slots = row_count // STRETCH
     width = pieces.shape[1]
     operands = [meta, pieces, shifted, term, query_proj]
     in_specs = [ANY_SPEC, VMEM_SPEC, VMEM_SPEC, VMEM_SPEC, HBM_SPEC]
-    if other is not None:
-        operands.append(other)
-        in_specs.append(VMEM_SPEC)
     aliases = {}
     if before is not None:
         aliases = {len(operands): 0}
@@ -417,42 +396,41 @@
     by_parts = size == 4 and channels % (size * LANES) == 0
     parts = size if by_parts else 1
 
-    def to_partner(value, step):
-        return lax.ppermute(value, "seq", [(z, z ^ step if size & (size - 1) == 0 else (z + step) % size) for z in range(size)])
-
-    filter_parts = [filters] + [to_partner(filters, step) for step in range(1, size)]
-    sends, extras, last, meta = gate(size, parts, sources, owner, key_proj, value_proj)
-    sends, filter_parts = lax.optimization_barrier((sends, filter_parts))
-    shifted = lags(size, filter_parts)
+    width = channels // parts
+    send, extra, last, meta = gate(size, parts, sources, owner, key_proj, value_proj, filters)
+    first = SLOTS * width
+    group_count = filters.shape[0]
+    if not by_parts:
+        shifted = lags(lax.all_gather(send[0, first:], "seq"), 0, group_count)
+        term = last_term(slots, meta, last, shifted)
+        held = jnp.concatenate([send[0, :first].reshape(SLOTS, width, LANES), extra])
+        mine = (meta[:SENT] == lax.axis_index("seq"))[:, None, None]
+        pieces = lax.psum(jnp.where(mine, held[meta[PLACE:MANY]], jnp.zeros_like(held)), "seq")
+        return conv(0, meta, pieces, shifted, term, query_proj, None)
+
+    received = lax.all_to_all(send, "seq", 0, 0, tiled=True)
+
+    def merge_more(meta, received, extra):
+        more = [extra[0]] + [
+            lax.ppermute(extra[step], "seq", [(z, z ^ step) for z in range(size)])
+            for step in range(1, size)
+        ]
+        return merge(size, width, meta, received, more)
+
+    def merge_plain(meta, received, extra):
+        return merge(size, width, meta, received)
+
+    merged = lax.cond(meta[MANY] > 0, merge_more, merge_plain, meta, received, extra)
+    gathered = [(0, merged)]
+    for step in (1, 3, 2):
+        moved = lax.ppermute(merged, "seq", [(z, (z + step) % size) for z in range(size)])
+        gathered.append((step, moved))
+    shifted = lags(received, first, group_count)
     term = last_term(slots, meta, last, shifted)
-    if not by_parts:
-        me = lax.axis_index("seq")
-        held = jnp.concatenate([sends[0], extras[0]])
-        places = meta[PLACE:MANY]
-        mine = (meta[:SENT] == me)[:, None, None]
-        pieces = lax.psum(jnp.where(mine, held[places], jnp.zeros_like(held)), "seq")
-        return conv(0, meta, pieces, shifted, term, query_proj, None)
-
-    scattered = [sends[0]] + [to_partner(sends[step], step) for step in range(1, size)]
-    term, *scattered = lax.optimization_barrier((term, *scattered))
-
-    def merge_more(meta, scattered, extras):
-        more = [extras[0]] + [to_partner(extras[step], step) for step in range(1, size)]
-        return merge(size, meta, scattered, more)
-
-    def merge_plain(meta, scattered, extras):
-        return merge(size, meta, scattered)
-
-    merged = lax.cond(meta[MANY] > 0, merge_more, merge_plain, meta, scattered, extras)
-    far = lax.ppermute(merged, "seq", [(0, 2), (2, 0), (1, 3), (3, 1)])
-    near = lax.ppermute(merged, "seq", [(0, 1), (1, 0), (2, 3), (3, 2)])
-    out = conv(0, meta, merged, shifted, term, query_proj, None)
-    out = conv(1, meta, near, shifted, term, query_proj, out)
-    merged, far, out = lax.optimization_barrier((merged, far, out))
-    onward = lax.ppermute(far, "seq", [(2, 3), (1, 0)])
-    middle = lax.ppermute(merged, "seq", [(1, 2), (2, 1)])
-    out = conv(2, meta, far, shifted, term, query_proj, out)
-    return conv(3, meta, onward, shifted, term, query_proj, out, middle)
+    out = None
+    for step, pieces in gathered:
+        out = conv(step, meta, pieces, shifted, term, query_proj, out)
+    return out
 
 
 def solution(mesh):

time: 48.9 us -> 51.1 us (1.045)
  the two profiles are of different devices: /device:TPU:20 before, /device:TPU:0 now
where the time goes in v4:
time: 51.1 us; the launch traced here: 50.7 us
  waiting for transfers between devices  20.6 us (40%)
  Pallas kernels  19.2 us (38%)
  starting transfers between devices  9.56 us (19%)
  between operations  0.66 us (1%)
  local copies, waits for them, and re-layouts  0.59 us (1%)
    all_to_all x1, waiting for transfers between devices, shards(): received = lax.all_to_all(send, 'seq', 0, 0, tiled=True)  19 us
    pallas_call x4, Pallas kernels, conv(): pl.pallas_call(functools.partial(conv_kernel, step, slots), in_specs=in_s...  11 us
    all_to_all x1, starting transfers between devices, shards(): received = lax.all_to_all(send, 'seq', 0, 0, tiled=True)  5.69 us
    ppermute x3, starting transfers between devices, shards(): lax.ppermute(merged, 'seq', [(z, (z + step) % size) for z in range(size)])  3.87 us
    pallas_call x1, Pallas kernels, gate(): pl.pallas_call(functools.partial(gate_kernel, size, parts), in_specs=[HBM...  3.28 us
    pallas_call x1, Pallas kernels, last_term(): pl.pallas_call(functools.partial(last_kernel, slots), in_specs=[SMEM_SPEC...  2.28 us
    pallas_call x1, Pallas kernels, lags(): pl.pallas_call(functools.partial(lags_kernel, first), grid=(group_count /...  2.14 us
    ppermute x3, waiting for transfers between devices, shards(): lax.ppermute(merged, 'seq', [(z, (z + step) % size) for z in range(size)])  1.66 us
  transfers between devices with their start and end apart: 4, of which 2 were waited for; matrix products, arithmetic and copies ran while one was open for 1% of the time, Pallas kernels for 25%

profile of v4, /device:TPU:0, one launch (start us, length us, event | category | flops | bytes accessed | tf_op | source)
XLA Modules:
  0.0 50.7 jit_solution(17806082067790712558)
XLA Ops:
  0.0 3.3 %gate.1 = (bf16[4,768,128]{2,1,0:T(8,128)(2,1)}, bf16[4,256,128]{2,1,0:T(8,128)(2,1)S(1)}, bf16[1024,128]{1,0:T(8,128)(2,1)S(1)}, s32[23]{0:T(128)S(1)}) custom-call(s32[4]{0:T(128)} %sources_in.1, s32[16]{0:T(128)} %owner_in.1, bf16[512,1024]{1,0:T(8,128)(2,1)} %key_in.1, bf16[512,1024]{1,0:T(8,128)(2,1)} %value_in.1, bf16[64,512]{1,0:T(8,128)(2,1)} %filters_in.1), custom_call_target="tpu_custom_call" | custom-call | tf_op jit(solution)/shard_map/gate/pallas_call | solution.py:158
  3.3 5.7 %all-to-all-start = ((bf16[4,768,128]{2,1,0:T(8,128)(2,1)}), bf16[4,768,128]{2,1,0:T(8,128)(2,1)S(1)}, u32[]{:S(2)}, u32[]{:S(2)}) async-start(bf16[4,768,128]{2,1,0:T(8,128)(2,1)} %get-tuple-element.28), calls=%async_computation | async-start | bytes 1572864 | tf_op jit(solution)/shard_map/all_to_all | solution.py:411
  9.0 0.6 %slice.15 = s32[1]{0:T(128)} slice(s32[23]{0:T(128)S(1)} %get-tuple-element.27.meta.meta_in), slice={[6:7]} | slice | bytes 8 | tf_op jit(solution)/shard_map/slice | solution.py:423
  10.1 19.0 %all-to-all-done.blocks = bf16[4,768,128]{2,1,0:T(8,128)(2,1)S(1)} async-done(((bf16[4,768,128]{2,1,0:T(8,128)(2,1)}), bf16[4,768,128]{2,1,0:T(8,128)(2,1)S(1)}, u32[]{:S(2)}, u32[]{:S(2)}) %all-to-all-start) | async-done | bytes 786464 | tf_op jit(solution)/shard_map/all_to_all | solution.py:411
  29.1 0.6 %conditional.1 = (bf16[3,256,128]{2,1,0:T(8,128)(2,1)S(1)}) conditional(s32[]{:T(128)} %bitcast.4, (s32[23]{0:T(128)S(1)}, bf16[4,768,128]{2,1,0:T(8,128)(2,1)S(1)}) %tuple.11, (bf16[4,256,128]{2,1,0:T(8,128)(2,1)S(1)}, s32[23]{0:T(128)S(1)}, bf16[4,768,128]{2,1,0:T(8,128)(2,1)S(1)}) %tuple.12), branch_computations={%region_0.0_spmd, %region_1.0_spmd} | conditional | bytes 1310848 | solution.py:423
  29.1 0.6 %merge.2 = bf16[3,256,128]{2,1,0:T(8,128)(2,1)S(1)} custom-call(s32[23]{0:T(128)S(1)} %get-tuple-element.18.meta, bf16[4,768,128]{2,1,0:T(8,128)(2,1)S(1)} %get-tuple-element.19.received), custom_call_target="tpu_custom_call" | custom-call | tf_op jit(solution)/shard_map/cond/branch_0_fun/merge/pallas_call | solution.py:197
  29.7 0.0 copy-start
  29.7 0.1 collective-permute-start.5
  29.7 3.8 %collective-permute-start.4 = (bf16[3,256,128]{2,1,0:T(8,128)(2,1)S(1)}, bf16[3,256,128]{2,1,0:T(8,128)(2,1)S(1)}, u32[]{:S(2)}, u32[]{:S(2)}) collective-permute-start(bf16[3,256,128]{2,1,0:T(8,128)(2,1)S(1)} %get-tuple-element.35.pieces), channel_id=1, source_target_pairs={{0,12},{4,0},{8,4},{12,8},{1,13},{5,1},{9,5},{13,9},{2,14},{6,2},{... | collective-permute-start | bytes 589832 | tf_op jit(solution)/shard_map/ppermute | solution.py:426
  33.6 0.0 collective-permute-start.3
  33.6 2.1 %lags.1.shifted = bf16[64,16,2304]{2,1,0:T(8,128)(2,1)S(1)} custom-call(bf16[4,768,128]{2,1,0:T(8,128)(2,1)S(1)} %all-to-all-done.blocks), custom_call_target="tpu_custom_call" | custom-call | tf_op jit(solution)/shard_map/lags/pallas_call | solution.py:244
  35.7 2.3 %last_term.1.term = f32[128,1024]{1,0:T(8,128)S(1)} custom-call(s32[23]{0:T(128)S(1)} %get-tuple-element.27.meta.meta_in, bf16[1024,128]{1,0:T(8,128)(2,1)S(1)} %get-tuple-element.30.last, bf16[64,16,2304]{2,1,0:T(8,128)(2,1)S(1)} %lags.1.shifted), custom_call_target="tpu_custom_call" | custom-call | tf_op jit(solution)/shard_map/last_term/pallas_call | solution.py:296
  38.0 0.0 copy-done
  38.0 2.7 %conv.4.refs_0_ = bf16[512,1024]{1,0:T(8,128)(2,1)} custom-call(s32[23]{0:T(128)S(1)} %get-tuple-element.27.meta.meta_in, bf16[3,256,128]{2,1,0:T(8,128)(2,1)S(1)} %get-tuple-element.35.pieces, bf16[64,16,2304]{2,1,0:T(8,128)(2,1)S(1)} %lags.1.shifted, f32[128,1024]{1,0:T(8,128)S(1)} %last_term.1.term, bf16[512,1024]{1,0:T(8,128)(2,1)S(1)} %copy-done), custom_call_target="tpu_custom_call" | custom-call | tf_op jit(solution)/shard_map/conv/pallas_call | solution.py:375
  40.7 0.0 collective-permute-done.5.pieces
  40.8 2.7 %conv.5.refs_0_ = bf16[512,1024]{1,0:T(8,128)(2,1)} custom-call(s32[23]{0:T(128)S(1)} %get-tuple-element.27.meta.meta_in, bf16[3,256,128]{2,1,0:T(8,128)(2,1)S(1)} %collective-permute-done.5.pieces, bf16[64,16,2304]{2,1,0:T(8,128)(2,1)S(1)} %lags.1.shifted, f32[128,1024]{1,0:T(8,128)S(1)} %last_term.1.term, ...), custom_call_target="tpu_custom_call", output_to_operand_aliasing={{}: (5, {})} | custom-call | tf_op jit(solution)/shard_map/conv/pallas_call | solution.py:375
  43.5 0.0 collective-permute-done.4.pieces
  43.5 2.7 %conv.6.refs_0_ = bf16[512,1024]{1,0:T(8,128)(2,1)} custom-call(s32[23]{0:T(128)S(1)} %get-tuple-element.27.meta.meta_in, bf16[3,256,128]{2,1,0:T(8,128)(2,1)S(1)} %collective-permute-done.4.pieces, bf16[64,16,2304]{2,1,0:T(8,128)(2,1)S(1)} %lags.1.shifted, f32[128,1024]{1,0:T(8,128)S(1)} %last_term.1.term, ...), custom_call_target="tpu_custom_call", output_to_operand_aliasing={{}: (5, {})} | custom-call | tf_op jit(solution)/shard_map/conv/pallas_call | solution.py:375
  46.3 1.7 %collective-permute-done.3.pieces = bf16[3,256,128]{2,1,0:T(8,128)(2,1)S(1)} collective-permute-done((bf16[3,256,128]{2,1,0:T(8,128)(2,1)S(1)}, bf16[3,256,128]{2,1,0:T(8,128)(2,1)S(1)}, u32[]{:S(2)}, u32[]{:S(2)}) %collective-permute-start.3) | collective-permute-done | bytes 196640 | tf_op jit(solution)/shard_map/ppermute | solution.py:426
  47.9 2.7 %conv.7 = bf16[512,1024]{1,0:T(8,128)(2,1)} custom-call(s32[23]{0:T(128)S(1)} %get-tuple-element.27.meta.meta_in, bf16[3,256,128]{2,1,0:T(8,128)(2,1)S(1)} %collective-permute-done.3.pieces, bf16[64,16,2304]{2,1,0:T(8,128)(2,1)S(1)} %lags.1.shifted, f32[128,1024]{1,0:T(8,128)S(1)} %last_term.1.term, ...), custom_call_target="tpu_custom_call", output_to_operand_aliasing={{}: (5, {})} | custom-call | tf_op jit(solution)/shard_map/conv/pallas_call | solution.py:375
Async XLA Ops:
  3.3 25.8 %all-to-all-start = ((bf16[4,768,128]{2,1,0:T(8,128)(2,1)}), bf16[4,768,128]{2,1,0:T(8,128)(2,1)S(1)}, u32[]{:S(2)}, u32[]{:S(2)}) async-start(bf16[4,768,128]{2,1,0:T(8,128)(2,1)} %get-tuple-element.28), calls=%async_computation | async-start | bytes 1572864 | tf_op jit(solution)/shard_map/all_to_all | solution.py:411
  29.7 8.3 %copy-start = (bf16[512,1024]{1,0:T(8,128)(2,1)S(1)}, bf16[512,1024]{1,0:T(8,128)(2,1)}, u32[]{:S(2)}) copy-start(bf16[512,1024]{1,0:T(8,128)(2,1)} %query.7) | copy-start | bytes 3145732
  29.7 11.1 %collective-permute-start.5 = (bf16[3,256,128]{2,1,0:T(8,128)(2,1)S(1)}, bf16[3,256,128]{2,1,0:T(8,128)(2,1)S(1)}, u32[]{:S(2)}, u32[]{:S(2)}) collective-permute-start(bf16[3,256,128]{2,1,0:T(8,128)(2,1)S(1)} %get-tuple-element.35.pieces), channel_id=1, source_target_pairs={{0,4},{4,8},{8,12},{12,0},{1,5},{5,9},{9,13},{13,1},{2,6},{6,10},{... | collective-permute-start | bytes 589832 | tf_op jit(solution)/shard_map/ppermute | solution.py:426
  29.7 13.8 %collective-permute-start.4 = (bf16[3,256,128]{2,1,0:T(8,128)(2,1)S(1)}, bf16[3,256,128]{2,1,0:T(8,128)(2,1)S(1)}, u32[]{:S(2)}, u32[]{:S(2)}) collective-permute-start(bf16[3,256,128]{2,1,0:T(8,128)(2,1)S(1)} %get-tuple-element.35.pieces), channel_id=1, source_target_pairs={{0,12},{4,0},{8,4},{12,8},{1,13},{5,1},{9,5},{13,9},{2,14},{6,2},{... | collective-permute-start | bytes 589832 | tf_op jit(solution)/shard_map/ppermute | solution.py:426
  33.6 14.4 %collective-permute-start.3 = (bf16[3,256,128]{2,1,0:T(8,128)(2,1)S(1)}, bf16[3,256,128]{2,1,0:T(8,128)(2,1)S(1)}, u32[]{:S(2)}, u32[]{:S(2)}) collective-permute-start(bf16[3,256,128]{2,1,0:T(8,128)(2,1)S(1)} %get-tuple-element.35.pieces), channel_id=1, source_target_pairs={{0,8},{4,12},{8,0},{12,4},{1,9},{5,13},{9,1},{13,5},{2,10},{6,14},... | collective-permute-start | bytes 589832 | tf_op jit(solution)/shard_map/ppermute | solution.py:426

commit v5 on v4

--- a/solution.py
+++ b/solution.py
@@ -35,25 +35,6 @@
     return me ^ step if size & (size - 1) == 0 else lax.rem(me + size - step, size)
 
 
-def lane_block(shape):
-    return lax.broadcasted_iota(jnp.int32, shape, 1) // GROUP_CH
-
-
-def block_transpose(tiles):
-    block = lane_block(tiles[0].shape)
-    tiles = list(tiles)
-    for distance in (4, 2, 1):
-        low = (block & distance) == 0
-        for first in range(BLOCKS):
-            if first & distance:
-                continue
-            a, b = tiles[first], tiles[first + distance]
-            shift = GROUP_CH * distance
-            tiles[first] = jnp.where(low, a, pltpu.roll(b, shift, 1))
-            tiles[first + distance] = jnp.where(low, pltpu.roll(a, LANES - shift, 1), b)
-    return tiles
-
-
 PLACE = SENT
 MANY = 2 * SENT
 WINDOWS = MANY + 1
@@ -61,7 +42,8 @@
 
 
 def gate_kernel(size, parts, sources_in, owner_in, key_in, value_in, filters_in, *refs):
-    send, extra, last, meta, sources, owner, key, value, filters, sems = refs
+    sends = refs[:parts]
+    extra, last, meta, sources, owner, key, value, filters, sems = refs[parts:]
     stretch_count = owner.shape[0]
     slots = key.shape[0] // STRETCH
     channels = key.shape[1]
@@ -127,12 +109,12 @@
                         target[pl.ds(offset + start, LANES), :] = product(first, columns)
 
                 if w < SLOTS:
-                    fill(send.at[part], pl.multiple_of(place * width, LANES))
+                    fill(sends[step], pl.multiple_of(place * width, LANES))
                 else:
 
                     @pl.when(place < SLOTS)
-                    def _(part=part, fill=fill):
-                        fill(send.at[part], pl.multiple_of(place * width, LANES))
+                    def _(step=step, fill=fill):
+                        fill(sends[step], pl.multiple_of(place * width, LANES))
 
                     @pl.when(place >= SLOTS)
                     def _(step=step, fill=fill):
@@ -142,8 +124,8 @@
     group_count = filters.shape[0]
     for tile in range(filters.shape[1] // LANES):
         rows = pl.ds(SLOTS * width + tile * group_count, group_count)
-        for part in range(parts):
-            send[part, rows, :] = filters[:, pl.ds(tile * LANES, LANES)]
+        for send in sends:
+            send[rows, :] = filters[:, pl.ds(tile * LANES, LANES)]
 
 
 def gate(size, parts, sources, owner, key_proj, value_proj, filters):
@@ -155,12 +137,12 @@
         for operand in (sources, owner, key_proj, value_proj, filters)
     ]
     rows = SLOTS * width + filters.size // LANES
-    return pl.pallas_call(
+    *sends, extra, last, meta = pl.pallas_call(
         functools.partial(gate_kernel, size, parts),
         in_specs=[HBM_SPEC] * 5,
-        out_specs=[VMEM_SPEC] * 3 + [SMEM_SPEC],
-        out_shape=[
-            jax.ShapeDtypeStruct((parts, rows, LANES), jnp.bfloat16),
+        out_specs=[VMEM_SPEC] * (parts + 2) + [SMEM_SPEC],
+        out_shape=[jax.ShapeDtypeStruct((rows, LANES), jnp.bfloat16)] * parts
+        + [
             jax.ShapeDtypeStruct((parts, width, LANES), jnp.bfloat16),
             jax.ShapeDtypeStruct((channels, STRETCH), jnp.bfloat16),
             jax.ShapeDtypeStruct((WINDOWS + slots * WIN,), jnp.int32),
@@ -176,15 +158,21 @@
         compiler_params=params(),
         name="gate",
     )(*operands)
-
-
-def merge_kernel(size, width, meta, received, *refs):
-    extras, out = refs[:-1], refs[-1]
+    return sends, extra, last, meta
+
+
+def merge_kernel(size, width, meta, *refs):
+    received, extras, out = refs[:size], refs[size:-1], refs[-1]
     me = lax.axis_index("seq")
     for w in range(SENT):
         place = meta[PLACE + w]
         rows = pl.ds(pl.multiple_of(jnp.minimum(place, SLOTS - 1) * width, LANES), width)
-        out[w] = received[meta[w], rows, :]
+        for step in range(size):
+
+            @pl.when(sender(me, step, size) == meta[w])
+            def _(w=w, step=step, rows=rows):
+                out[w] = received[step][rows, :]
+
     for w in range(SLOTS, SENT):
         for step, extra in enumerate(extras):
 
@@ -196,30 +184,36 @@
 def merge(size, width, meta, received, extras=()):
     return pl.pallas_call(
         functools.partial(merge_kernel, size, width),
-        in_specs=[SMEM_SPEC] + [VMEM_SPEC] * (1 + len(extras)),
+        in_specs=[SMEM_SPEC] + [VMEM_SPEC] * (size + len(extras)),
         out_specs=VMEM_SPEC,
-        out_shape=jax.ShapeDtypeStruct((SENT, width, LANES), received.dtype),
+        out_shape=jax.ShapeDtypeStruct((SENT, width, LANES), received[0].dtype),
         compiler_params=params(),
         name="merge",
-    )(meta, received, *extras)
-
-
-def lags_kernel(first, blocks, out, reverse):
+    )(meta, *received, *extras)
+
+
+def lags_kernel(first, *refs):
+    received, (out, reverse) = refs[:-2], refs[-2:]
+    size = len(received)
     group_count, padded = reverse.shape
-    tiles = (blocks.shape[1] - first) // group_count
-    lag_count = blocks.shape[0] * tiles * LANES
+    tiles = (received[0].shape[0] - first) // group_count
+    lag_count = size * tiles * LANES
     tile_step = pl.program_id(0)
 
     @pl.when(tile_step == 0)
     def _():
+        me = lax.axis_index("seq")
         row = lax.broadcasted_iota(jnp.int32, (LANES, LANES), 0)
         column = lax.broadcasted_iota(jnp.int32, (LANES, LANES), 1)
         flip = jnp.where(row + column == LANES - 1, 1.0, 0.0).astype(jnp.bfloat16)
-        for tile in range(lag_count // LANES):
-            piece = blocks[tile // tiles, pl.ds(first + tile % tiles * group_count, group_count), :]
-            reverse[:, pl.ds(lag_count - LANES * (tile + 1), LANES)] = jnp.dot(
-                piece, flip, preferred_element_type=jnp.float32
-            )
+        for step in range(size):
+            shard = sender(me, step, size)
+            for tile in range(tiles):
+                piece = received[step][pl.ds(first + tile * group_count, group_count), :]
+                start = lag_count - LANES * (shard * tiles + tile + 1)
+                reverse[:, pl.ds(pl.multiple_of(start, LANES), LANES)] = jnp.dot(
+                    piece, flip, preferred_element_type=jnp.float32
+                )
         reverse[:, pl.ds(lag_count, padded - lag_count)] = jnp.zeros(
             (group_count, padded - lag_count), jnp.float32
         )
@@ -238,19 +232,19 @@
             before[g] = rolled
 
 
-def lags(blocks, first, group_count):
-    size, rows, _ = blocks.shape
-    padded = size * (rows - first) // group_count * LANES + SPAN
+def lags(received, first, group_count):
+    size = len(received)
+    padded = size * (received[0].shape[0] - first) // group_count * LANES + SPAN
     return pl.pallas_call(
         functools.partial(lags_kernel, first),
         grid=(group_count // BLOCKS,),
-        in_specs=[VMEM_SPEC],
+        in_specs=[VMEM_SPEC] * size,
         out_specs=pl.BlockSpec((BLOCKS, GROUP_CH, padded), lambda i: (i, 0, 0)),
         out_shape=jax.ShapeDtypeStruct((group_count, GROUP_CH, padded), jnp.bfloat16),
         scratch_shapes=[pltpu.VMEM((group_count, padded), jnp.float32)],
         compiler_params=params(),
         name="lags",
-    )(blocks)
+    )(*received)
 
 
 def spread_rows(tile, spans, base):
@@ -276,20 +270,25 @@
     return shifted[group, :, pl.ds(start, SPAN)]
 
 
+def rows_of(results, block):
+    part = slice(block * GROUP_CH, (block + 1) * GROUP_CH)
+    return jnp.concatenate([result[part] for result in results], axis=0).T
+
+
 def last_kernel(slots, meta, last, shifted, out, spans):
     for start in range(0, last.shape[0], LANES):
         spread_rows(last[pl.ds(start, LANES), :], spans, 0)
         results = [
             lax.dot_general(
+                spans[g],
                 window(meta, shifted, start // GROUP_CH + g, slots - 1, SENT),
-                spans[g],
                 NT,
                 preferred_element_type=jnp.float32,
             )
             for g in range(BLOCKS)
         ]
-        for m, tile in enumerate(block_transpose(results)):
-            out[pl.ds(m * GROUP_CH, GROUP_CH), pl.ds(start, LANES)] = tile
+        for m in range(BLOCKS):
+            out[pl.ds(m * GROUP_CH, GROUP_CH), pl.ds(start, LANES)] = rows_of(results, m)
 
 
 def last_term(slots, meta, last, shifted):
@@ -340,15 +339,16 @@
             )
             results.append(
                 lax.dot_general(
-                    filter_rows, spans[start // LANES, g], NT, preferred_element_type=jnp.float32
+                    spans[start // LANES, g], filter_rows, NT, preferred_element_type=jnp.float32
                 )
             )
         if start + LANES < width:
             spread(start + LANES)
-        for slot in range(slots):
-            tiles = [value[slot * GROUP_CH : (slot + 1) * GROUP_CH] for value in results]
-            for m, tile in enumerate(block_transpose(tiles)):
+        for m in range(BLOCKS):
+            rows = rows_of(results, m)
+            for slot in range(slots):
                 place = pl.ds(slot * STRETCH + m * GROUP_CH, GROUP_CH)
+                tile = rows[slot * GROUP_CH : (slot + 1) * GROUP_CH]
                 if slot == slots - 1:
                     tile = tile + term[
                         pl.ds(m * GROUP_CH, GROUP_CH), pl.ds(pl.multiple_of(base + start, LANES), LANES)
@@ -397,38 +397,46 @@
     parts = size if by_parts else 1
 
     width = channels // parts
-    send, extra, last, meta = gate(size, parts, sources, owner, key_proj, value_proj, filters)
+    sends, extra, last, meta = gate(
+        size, parts, sources, owner, key_proj, value_proj, filters
+    )
     first = SLOTS * width
     group_count = filters.shape[0]
     if not by_parts:
-        shifted = lags(lax.all_gather(send[0, first:], "seq"), 0, group_count)
+        blocks = lax.all_gather(sends[0][first:], "seq")
+        steps = sender(lax.axis_index("seq"), jnp.arange(size, dtype=jnp.int32), size)
+        blocks = jnp.take(blocks, steps, axis=0)
+        shifted = lags([blocks[step] for step in range(size)], 0, group_count)
         term = last_term(slots, meta, last, shifted)
-        held = jnp.concatenate([send[0, :first].reshape(SLOTS, width, LANES), extra])
+        held = jnp.concatenate([sends[0][:first].reshape(SLOTS, width, LANES), extra])
         mine = (meta[:SENT] == lax.axis_index("seq"))[:, None, None]
         pieces = lax.psum(jnp.where(mine, held[meta[PLACE:MANY]], jnp.zeros_like(held)), "seq")
         return conv(0, meta, pieces, shifted, term, query_proj, None)
 
-    received = lax.all_to_all(send, "seq", 0, 0, tiled=True)
+    def exchange(value, step):
+        return lax.ppermute(value, "seq", [(z, z ^ step) for z in range(size)])
+
+    received = [sends[0]] + [exchange(sends[step], step) for step in range(1, size)]
 
     def merge_more(meta, received, extra):
-        more = [extra[0]] + [
-            lax.ppermute(extra[step], "seq", [(z, z ^ step) for z in range(size)])
-            for step in range(1, size)
-        ]
+        more = [extra[0]] + [exchange(extra[step], step) for step in range(1, size)]
         return merge(size, width, meta, received, more)
 
     def merge_plain(meta, received, extra):
         return merge(size, width, meta, received)
 
     merged = lax.cond(meta[MANY] > 0, merge_more, merge_plain, meta, received, extra)
-    gathered = [(0, merged)]
-    for step in (1, 3, 2):
-        moved = lax.ppermute(merged, "seq", [(z, (z + step) % size) for z in range(size)])
-        gathered.append((step, moved))
+
+    def shift(value, step):
+        return lax.ppermute(value, "seq", [(z, (z + step) % size) for z in range(size)])
+
+    up, down = shift(merged, 1), shift(merged, size - 1)
     shifted = lags(received, first, group_count)
+    far_part, shifted = lax.optimization_barrier((merged, shifted))
+    far = shift(far_part, 2)
     term = last_term(slots, meta, last, shifted)
     out = None
-    for step, pieces in gathered:
+    for step, pieces in ((0, merged), (1, up), (size - 1, down), (2, far)):
         out = conv(step, meta, pieces, shifted, term, query_proj, out)
     return out
 

time: 51.1 us -> 47.7 us (0.933)
  the two profiles are of different devices: /device:TPU:0 before, /device:TPU:20 now
where the time goes in v5:
time: 47.7 us; the launch traced here: 47.5 us
  waiting for transfers between devices  21.2 us (44%)
  Pallas kernels  17.3 us (36%)
  starting transfers between devices  7.62 us (16%)
  between operations  0.74 us (2%)
  local copies, waits for them, and re-layouts  0.59 us (1%)
    ppermute x3, waiting for transfers between devices, exchange(): return lax.ppermute(value, 'seq', [(z, z ^ step) for z in range(size)])  16.5 us
    pallas_call x4, Pallas kernels, conv(): pl.pallas_call(functools.partial(conv_kernel, step, slots), in_specs=in_s...  9.65 us
    ppermute x3, waiting for transfers between devices, shift(): lax.ppermute(value, 'seq', [(z, (z + step) % size) for z in range(size)])  4.69 us
    ppermute x3, starting transfers between devices, shift(): lax.ppermute(value, 'seq', [(z, (z + step) % size) for z in range(size)])  4.06 us
    ppermute x3, starting transfers between devices, exchange(): return lax.ppermute(value, 'seq', [(z, z ^ step) for z in range(size)])  3.55 us
    pallas_call x1, Pallas kernels, last_term(): pl.pallas_call(functools.partial(last_kernel, slots), in_specs=[SMEM_SPEC...  2.5 us
    pallas_call x1, Pallas kernels, gate(): pl.pallas_call(functools.partial(gate_kernel, size, parts), in_specs=[HBM...  2.33 us
    pallas_call x1, Pallas kernels, lags(): pl.pallas_call(functools.partial(lags_kernel, first), grid=(group_count /...  2.15 us
  transfers between devices with their start and end apart: 6, of which 4 were waited for; matrix products, arithmetic and copies ran while one was open for 1% of the time, Pallas kernels for 25%

profile of v5, /device:TPU:20, one launch (start us, length us, event | category | flops | bytes accessed | tf_op | source)
XLA Modules:
  0.0 47.5 jit_solution(8535108897456724066)
XLA Ops:
  0.0 2.3 %gate.1 = (bf16[768,128]{1,0:T(8,128)(2,1)S(1)}, bf16[768,128]{1,0:T(8,128)(2,1)S(1)}, bf16[768,128]{1,0:T(8,128)(2,1)S(1)}, bf16[768,128]{1,0:T(8,128)(2,1)S(1)...) custom-call(s32[4]{0:T(128)} %sources_in.1, s32[16]{0:T(128)} %owner_in.1, ...), custom_call_target="tpu_custom_call" | custom-call | tf_op jit(solution)/shard_map/gate/pallas_call | solution.py:140
  2.3 1.8 %collective-permute-start.3 = (bf16[768,128]{1,0:T(8,128)(2,1)S(1)}, bf16[768,128]{1,0:T(8,128)(2,1)S(1)}, u32[]{:S(2)}, u32[]{:S(2)}) collective-permute-start(bf16[768,128]{1,0:T(8,128)(2,1)S(1)} %get-tuple-element.52), channel_id=1, source_target_pairs={{0,4},{4,0},{8,12},{12,8},{1,5},{5,1},{9,13},{13,9},{2,6},{6,2},{1... | collective-permute-start | bytes 589832 | tf_op jit(solution)/shard_map/ppermute | solution.py:417
  4.2 0.8 %collective-permute-start.4 = (bf16[768,128]{1,0:T(8,128)(2,1)S(1)}, bf16[768,128]{1,0:T(8,128)(2,1)S(1)}, u32[]{:S(2)}, u32[]{:S(2)}) collective-permute-start(bf16[768,128]{1,0:T(8,128)(2,1)S(1)} %get-tuple-element.53), channel_id=1, source_target_pairs={{0,8},{4,12},{8,0},{12,4},{1,9},{5,13},{9,1},{13,5},{2,10},{6,14},... | collective-permute-start | bytes 589832 | tf_op jit(solution)/shard_map/ppermute | solution.py:417
  5.0 0.9 %collective-permute-start.5 = (bf16[768,128]{1,0:T(8,128)(2,1)S(1)}, bf16[768,128]{1,0:T(8,128)(2,1)S(1)}, u32[]{:S(2)}, u32[]{:S(2)}) collective-permute-start(bf16[768,128]{1,0:T(8,128)(2,1)S(1)} %get-tuple-element.54), channel_id=1, source_target_pairs={{0,12},{4,8},{8,4},{12,0},{1,13},{5,9},{9,5},{13,1},{2,14},{6,10},... | collective-permute-start | bytes 589832 | tf_op jit(solution)/shard_map/ppermute | solution.py:417
  5.9 0.6 %slice.15 = s32[1]{0:T(128)} slice(s32[23]{0:T(128)S(1)} %get-tuple-element.50.meta.meta_in), slice={[6:7]} | slice | bytes 8 | tf_op jit(solution)/shard_map/slice | solution.py:428
  7.1 4.4 %collective-permute-done.3.refs_1_ = bf16[768,128]{1,0:T(8,128)(2,1)S(1)} collective-permute-done((bf16[768,128]{1,0:T(8,128)(2,1)S(1)}, bf16[768,128]{1,0:T(8,128)(2,1)S(1)}, u32[]{:S(2)}, u32[]{:S(2)}) %collective-permute-start.3) | collective-permute-done | bytes 196640 | tf_op jit(solution)/shard_map/ppermute | solution.py:417
  11.6 7.2 %collective-permute-done.4.refs_2_ = bf16[768,128]{1,0:T(8,128)(2,1)S(1)} collective-permute-done((bf16[768,128]{1,0:T(8,128)(2,1)S(1)}, bf16[768,128]{1,0:T(8,128)(2,1)S(1)}, u32[]{:S(2)}, u32[]{:S(2)}) %collective-permute-start.4) | collective-permute-done | bytes 196640 | tf_op jit(solution)/shard_map/ppermute | solution.py:417
  18.8 4.9 %collective-permute-done.5.refs_3_ = bf16[768,128]{1,0:T(8,128)(2,1)S(1)} collective-permute-done((bf16[768,128]{1,0:T(8,128)(2,1)S(1)}, bf16[768,128]{1,0:T(8,128)(2,1)S(1)}, u32[]{:S(2)}, u32[]{:S(2)}) %collective-permute-start.5) | collective-permute-done | bytes 196640 | tf_op jit(solution)/shard_map/ppermute | solution.py:417
  23.7 0.7 %conditional.1 = (bf16[3,256,128]{2,1,0:T(8,128)(2,1)S(1)}) conditional(s32[]{:T(128)} %bitcast.4, (s32[23]{0:T(128)S(1)}, bf16[768,128]{1,0:T(8,128)(2,1)S(1)}, bf16[768,128]{1,0:T(8,128)(2,1)S(1)}, bf16[768,128]{1,0:T(8,128)(2,1)S(1)}, bf16[768,128]{1,0:T(8,128)(2,1)S(1)}) %tuple.12, (bf16[4,256,128]{2,1,0:T(8,128)(2,1)S(1)}, s32[23]{0:T(128)S(1)}, ...), branch_computations={%region_0.0_spmd, %region_1.0_spmd} | conditional | bytes 1310848 | solution.py:428
  23.7 0.7 %merge.2 = bf16[3,256,128]{2,1,0:T(8,128)(2,1)S(1)} custom-call(s32[23]{0:T(128)S(1)} %get-tuple-element.30.meta, bf16[768,128]{1,0:T(8,128)(2,1)S(1)} %get-tuple-element.31.refs_0_, bf16[768,128]{1,0:T(8,128)(2,1)S(1)} %get-tuple-element.32.refs_1_, bf16[768,128]{1,0:T(8,128)(2,1)S(1)} %get-tuple-element.33.refs_2_, ...), custom_call_target="tpu_custom_call" | custom-call | tf_op jit(solution)/shard_map/cond/branch_0_fun/merge/pallas_call | solution.py:185
  24.3 0.0 copy-start
  24.4 0.1 collective-permute-start.8
  24.4 2.5 %collective-permute-start.7 = (bf16[3,256,128]{2,1,0:T(8,128)(2,1)S(1)}, bf16[3,256,128]{2,1,0:T(8,128)(2,1)S(1)}, u32[]{:S(2)}, u32[]{:S(2)}) collective-permute-start(bf16[3,256,128]{2,1,0:T(8,128)(2,1)S(1)} %get-tuple-element.63.pieces), channel_id=1, source_target_pairs={{0,12},{4,0},{8,4},{12,8},{1,13},{5,1},{9,5},{13,9},{2,14},{6,2},{... | collective-permute-start | bytes 589832 | tf_op jit(solution)/shard_map/ppermute | solution.py:431
  27.0 2.1 %lags.1.shifted = bf16[64,16,2304]{2,1,0:T(8,128)(2,1)S(1)} custom-call(bf16[768,128]{1,0:T(8,128)(2,1)S(1)} %get-tuple-element.51.refs_0_, bf16[768,128]{1,0:T(8,128)(2,1)S(1)} %collective-permute-done.3.refs_1_, bf16[768,128]{1,0:T(8,128)(2,1)S(1)} %collective-permute-done.4.refs_2_, bf16[768,128]{1,0:T(8,128)(2,1)S(1)} %collective-permute-done.5.refs_3_), custom_call_target="tpu_custom_call" | custom-call | tf_op jit(solution)/shard_map/lags/pallas_call | solution.py:238
  29.1 1.5 %collective-permute-start.6 = (bf16[3,256,128]{2,1,0:T(8,128)(2,1)S(1)}, bf16[3,256,128]{2,1,0:T(8,128)(2,1)S(1)}, u32[]{:S(2)}, u32[]{:S(2)}) collective-permute-start(bf16[3,256,128]{2,1,0:T(8,128)(2,1)S(1)} %get-tuple-element.63.pieces), channel_id=1, source_target_pairs={{0,8},{4,12},{8,0},{12,4},{1,9},{5,13},{9,1},{13,5},{2,10},{6,14},... | collective-permute-start | bytes 589832 | tf_op jit(solution)/shard_map/ppermute | solution.py:431
  30.6 2.5 %last_term.1.term = f32[128,1024]{1,0:T(8,128)S(1)} custom-call(s32[23]{0:T(128)S(1)} %get-tuple-element.50.meta.meta_in, bf16[1024,128]{1,0:T(8,128)(2,1)S(1)} %get-tuple-element.58.last, bf16[64,16,2304]{2,1,0:T(8,128)(2,1)S(1)} %lags.1.shifted), custom_call_target="tpu_custom_call" | custom-call | tf_op jit(solution)/shard_map/last_term/pallas_call | solution.py:295
  33.1 0.0 copy-done
  33.1 2.4 %conv.4.refs_0_ = bf16[512,1024]{1,0:T(8,128)(2,1)} custom-call(s32[23]{0:T(128)S(1)} %get-tuple-element.50.meta.meta_in, bf16[3,256,128]{2,1,0:T(8,128)(2,1)S(1)} %get-tuple-element.63.pieces, bf16[64,16,2304]{2,1,0:T(8,128)(2,1)S(1)} %lags.1.shifted, f32[128,1024]{1,0:T(8,128)S(1)} %last_term.1.term, bf16[512,1024]{1,0:T(8,128)(2,1)S(1)} %copy-done), custom_call_target="tpu_custom_call" | custom-call | tf_op jit(solution)/shard_map/conv/pallas_call | solution.py:375
  35.5 4.7 %collective-permute-done.8.pieces = bf16[3,256,128]{2,1,0:T(8,128)(2,1)S(1)} collective-permute-done((bf16[3,256,128]{2,1,0:T(8,128)(2,1)S(1)}, bf16[3,256,128]{2,1,0:T(8,128)(2,1)S(1)}, u32[]{:S(2)}, u32[]{:S(2)}) %collective-permute-start.8) | collective-permute-done | bytes 196640 | tf_op jit(solution)/shard_map/ppermute | solution.py:431
  40.2 2.4 %conv.5.refs_0_ = bf16[512,1024]{1,0:T(8,128)(2,1)} custom-call(s32[23]{0:T(128)S(1)} %get-tuple-element.50.meta.meta_in, bf16[3,256,128]{2,1,0:T(8,128)(2,1)S(1)} %collective-permute-done.8.pieces, bf16[64,16,2304]{2,1,0:T(8,128)(2,1)S(1)} %lags.1.shifted, f32[128,1024]{1,0:T(8,128)S(1)} %last_term.1.term, ...), custom_call_target="tpu_custom_call", output_to_operand_aliasing={{}: (5, {})} | custom-call | tf_op jit(solution)/shard_map/conv/pallas_call | solution.py:375
  42.6 0.0 collective-permute-done.7.pieces
  42.6 2.4 %conv.6.refs_0_ = bf16[512,1024]{1,0:T(8,128)(2,1)} custom-call(s32[23]{0:T(128)S(1)} %get-tuple-element.50.meta.meta_in, bf16[3,256,128]{2,1,0:T(8,128)(2,1)S(1)} %collective-permute-done.7.pieces, bf16[64,16,2304]{2,1,0:T(8,128)(2,1)S(1)} %lags.1.shifted, f32[128,1024]{1,0:T(8,128)S(1)} %last_term.1.term, ...), custom_call_target="tpu_custom_call", output_to_operand_aliasing={{}: (5, {})} | custom-call | tf_op jit(solution)/shard_map/conv/pallas_call | solution.py:375
  45.1 0.0 collective-permute-done.6.pieces
  45.1 2.4 %conv.7 = bf16[512,1024]{1,0:T(8,128)(2,1)} custom-call(s32[23]{0:T(128)S(1)} %get-tuple-element.50.meta.meta_in, bf16[3,256,128]{2,1,0:T(8,128)(2,1)S(1)} %collective-permute-done.6.pieces, bf16[64,16,2304]{2,1,0:T(8,128)(2,1)S(1)} %lags.1.shifted, f32[128,1024]{1,0:T(8,128)S(1)} %last_term.1.term, ...), custom_call_target="tpu_custom_call", output_to_operand_aliasing={{}: (5, {})} | custom-call | tf_op jit(solution)/shard_map/conv/pallas_call | solution.py:375
Async XLA Ops:
  2.3 9.2 %collective-permute-start.3 = (bf16[768,128]{1,0:T(8,128)(2,1)S(1)}, bf16[768,128]{1,0:T(8,128)(2,1)S(1)}, u32[]{:S(2)}, u32[]{:S(2)}) collective-permute-start(bf16[768,128]{1,0:T(8,128)(2,1)S(1)} %get-tuple-element.52), channel_id=1, source_target_pairs={{0,4},{4,0},{8,12},{12,8},{1,5},{5,1},{9,13},{13,9},{2,6},{6,2},{1... | collective-permute-start | bytes 589832 | tf_op jit(solution)/shard_map/ppermute | solution.py:417
  4.2 14.6 %collective-permute-start.4 = (bf16[768,128]{1,0:T(8,128)(2,1)S(1)}, bf16[768,128]{1,0:T(8,128)(2,1)S(1)}, u32[]{:S(2)}, u32[]{:S(2)}) collective-permute-start(bf16[768,128]{1,0:T(8,128)(2,1)S(1)} %get-tuple-element.53), channel_id=1, source_target_pairs={{0,8},{4,12},{8,0},{12,4},{1,9},{5,13},{9,1},{13,5},{2,10},{6,14},... | collective-permute-start | bytes 589832 | tf_op jit(solution)/shard_map/ppermute | solution.py:417
  5.0 18.7 %collective-permute-start.5 = (bf16[768,128]{1,0:T(8,128)(2,1)S(1)}, bf16[768,128]{1,0:T(8,128)(2,1)S(1)}, u32[]{:S(2)}, u32[]{:S(2)}) collective-permute-start(bf16[768,128]{1,0:T(8,128)(2,1)S(1)} %get-tuple-element.54), channel_id=1, source_target_pairs={{0,12},{4,8},{8,4},{12,0},{1,13},{5,9},{9,5},{13,1},{2,14},{6,10},... | collective-permute-start | bytes 589832 | tf_op jit(solution)/shard_map/ppermute | solution.py:417
  24.3 8.7 %copy-start = (bf16[512,1024]{1,0:T(8,128)(2,1)S(1)}, bf16[512,1024]{1,0:T(8,128)(2,1)}, u32[]{:S(2)}) copy-start(bf16[512,1024]{1,0:T(8,128)(2,1)} %query.7) | copy-start | bytes 3145732
  24.4 15.9 %collective-permute-start.8 = (bf16[3,256,128]{2,1,0:T(8,128)(2,1)S(1)}, bf16[3,256,128]{2,1,0:T(8,128)(2,1)S(1)}, u32[]{:S(2)}, u32[]{:S(2)}) collective-permute-start(bf16[3,256,128]{2,1,0:T(8,128)(2,1)S(1)} %get-tuple-element.63.pieces), channel_id=1, source_target_pairs={{0,4},{4,8},{8,12},{12,0},{1,5},{5,9},{9,13},{13,1},{2,6},{6,10},{... | collective-permute-start | bytes 589832 | tf_op jit(solution)/shard_map/ppermute | solution.py:431
  24.4 18.2 %collective-permute-start.7 = (bf16[3,256,128]{2,1,0:T(8,128)(2,1)S(1)}, bf16[3,256,128]{2,1,0:T(8,128)(2,1)S(1)}, u32[]{:S(2)}, u32[]{:S(2)}) collective-permute-start(bf16[3,256,128]{2,1,0:T(8,128)(2,1)S(1)} %get-tuple-element.63.pieces), channel_id=1, source_target_pairs={{0,12},{4,0},{8,4},{12,8},{1,13},{5,1},{9,5},{13,9},{2,14},{6,2},{... | collective-permute-start | bytes 589832 | tf_op jit(solution)/shard_map/ppermute | solution.py:431
  29.1 15.9 %collective-permute-start.6 = (bf16[3,256,128]{2,1,0:T(8,128)(2,1)S(1)}, bf16[3,256,128]{2,1,0:T(8,128)(2,1)S(1)}, u32[]{:S(2)}, u32[]{:S(2)}) collective-permute-start(bf16[3,256,128]{2,1,0:T(8,128)(2,1)S(1)} %get-tuple-element.63.pieces), channel_id=1, source_target_pairs={{0,8},{4,12},{8,0},{12,4},{1,9},{5,13},{9,1},{13,5},{2,10},{6,14},... | collective-permute-start | bytes 589832 | tf_op jit(solution)/shard_map/ppermute | solution.py:431

commit v6 on v5

--- a/solution.py
+++ b/solution.py
@@ -27,12 +27,16 @@
     return pltpu.CompilerParams(vmem_limit_bytes=VMEM_LIMIT)
 
 
+def steps_of(size):
+    return sorted(range(size), key=lambda step: (min(step, size - step), step))
+
+
 def partner(me, step, size):
-    return me ^ step if size & (size - 1) == 0 else lax.rem(me + step, size)
+    return lax.rem(me + step, size)
 
 
 def sender(me, step, size):
-    return me ^ step if size & (size - 1) == 0 else lax.rem(me + size - step, size)
+    return lax.rem(me + size - step, size)
 
 
 PLACE = SENT
@@ -41,11 +45,17 @@
 SLOTS = 2
 
 
+def product(key, value, start, columns):
+    rows = pl.ds(start, STRETCH)
+    rows_k = key[rows, columns].astype(jnp.float32)
+    rows_v = value[rows, columns].astype(jnp.float32)
+    return (rows_k * rows_v).astype(jnp.bfloat16).T
+
+
 def gate_kernel(size, parts, sources_in, owner_in, key_in, value_in, filters_in, *refs):
     sends = refs[:parts]
-    extra, last, meta, sources, owner, key, value, filters, sems = refs[parts:]
+    extra, meta, sources, owner, key, value, filters, sems = refs[parts:]
     stretch_count = owner.shape[0]
-    slots = key.shape[0] // STRETCH
     channels = key.shape[1]
     width = channels // parts
     me = lax.axis_index("seq")
@@ -59,12 +69,6 @@
     for copy in copies:
         copy.start()
 
-    def product(start, columns):
-        rows = pl.ds(start, STRETCH)
-        rows_k = key[rows, columns].astype(jnp.float32)
-        rows_v = value[rows, columns].astype(jnp.float32)
-        return (rows_k * rows_v).astype(jnp.bfloat16).T
-
     for copy in copies[:2]:
         copy.wait()
 
@@ -82,8 +86,6 @@
     lax.fori_loop(0, stretch_count, target, 0)
     for copy in copies[2:]:
         copy.wait()
-    for start in range(0, channels, LANES):
-        last[pl.ds(start, LANES), :] = product((slots - 1) * STRETCH, pl.ds(start, LANES))
     holders = [owner[sources[w]] for w in range(SENT)]
     many = 0
     for w, holder in enumerate(holders):
@@ -106,7 +108,7 @@
                 def fill(target, offset, base=base):
                     for start in range(0, width, LANES):
                         columns = pl.ds(pl.multiple_of(base + start, LANES), LANES)
-                        target[pl.ds(offset + start, LANES), :] = product(first, columns)
+                        target[pl.ds(offset + start, LANES), :] = product(key, value, first, columns)
 
                 if w < SLOTS:
                     fill(sends[step], pl.multiple_of(place * width, LANES))
@@ -137,14 +139,13 @@
         for operand in (sources, owner, key_proj, value_proj, filters)
     ]
     rows = SLOTS * width + filters.size // LANES
-    *sends, extra, last, meta = pl.pallas_call(
+    *sends, extra, meta = pl.pallas_call(
         functools.partial(gate_kernel, size, parts),
         in_specs=[HBM_SPEC] * 5,
-        out_specs=[VMEM_SPEC] * (parts + 2) + [SMEM_SPEC],
+        out_specs=[VMEM_SPEC] * (parts + 1) + [SMEM_SPEC],
         out_shape=[jax.ShapeDtypeStruct((rows, LANES), jnp.bfloat16)] * parts
         + [
             jax.ShapeDtypeStruct((parts, width, LANES), jnp.bfloat16),
-            jax.ShapeDtypeStruct((channels, STRETCH), jnp.bfloat16),
             jax.ShapeDtypeStruct((WINDOWS + slots * WIN,), jnp.int32),
         ],
         scratch_shapes=[
@@ -158,7 +159,7 @@
         compiler_params=params(),
         name="gate",
     )(*operands)
-    return sends, extra, last, meta
+    return sends, extra, meta
 
 
 def merge_kernel(size, width, meta, *refs):
@@ -167,11 +168,11 @@
     for w in range(SENT):
         place = meta[PLACE + w]
         rows = pl.ds(pl.multiple_of(jnp.minimum(place, SLOTS - 1) * width, LANES), width)
-        for step in range(size):
+        for block, step in zip(received, steps_of(size)):
 
             @pl.when(sender(me, step, size) == meta[w])
-            def _(w=w, step=step, rows=rows):
-                out[w] = received[step][rows, :]
+            def _(w=w, block=block, rows=rows):
+                out[w] = block[rows, :]
 
     for w in range(SLOTS, SENT):
         for step, extra in enumerate(extras):
@@ -206,10 +207,10 @@
         row = lax.broadcasted_iota(jnp.int32, (LANES, LANES), 0)
         column = lax.broadcasted_iota(jnp.int32, (LANES, LANES), 1)
         flip = jnp.where(row + column == LANES - 1, 1.0, 0.0).astype(jnp.bfloat16)
-        for step in range(size):
+        for block, step in zip(received, steps_of(size)):
             shard = sender(me, step, size)
             for tile in range(tiles):
-                piece = received[step][pl.ds(first + tile * group_count, group_count), :]
+                piece = block[pl.ds(first + tile * group_count, group_count), :]
                 start = lag_count - LANES * (shard * tiles + tile + 1)
                 reverse[:, pl.ds(pl.multiple_of(start, LANES), LANES)] = jnp.dot(
                     piece, flip, preferred_element_type=jnp.float32
@@ -270,6 +271,26 @@
     return shifted[group, :, pl.ds(start, SPAN)]
 
 
+def last_rows_kernel(key, value, out):
+    for start in range(0, out.shape[0], LANES):
+        out[pl.ds(start, LANES), :] = product(key, value, 0, pl.ds(start, LANES))
+
+
+def last_rows(key_proj, value_proj):
+    row_count, channels = key_proj.shape
+    block = pl.BlockSpec((STRETCH, channels), lambda i: (row_count // STRETCH - 1, 0))
+    operands = [pltpu.with_memory_space_constraint(x, pltpu.HBM) for x in (key_proj, value_proj)]
+    return pl.pallas_call(
+        last_rows_kernel,
+        grid=(1,),
+        in_specs=[block, block],
+        out_specs=pl.BlockSpec((channels, STRETCH), lambda i: (0, 0)),
+        out_shape=jax.ShapeDtypeStruct((channels, STRETCH), jnp.bfloat16),
+        compiler_params=params(),
+        name="last_rows",
+    )(*operands)
+
+
 def rows_of(results, block):
     part = slice(block * GROUP_CH, (block + 1) * GROUP_CH)
     return jnp.concatenate([result[part] for result in results], axis=0).T
@@ -304,17 +325,13 @@
 
 
 def conv_kernel(step, slots, meta_in, pieces, shifted, term, query, *refs):
-    out, meta, gates, result, spans, sems = refs[-6:]
+    out, meta, result, spans, sems = refs[-5:]
     width = pieces.shape[1]
     size = out.shape[1] // width
     me = lax.axis_index("seq")
     base = pl.multiple_of(lax.rem(me + size - step, size) * width, width)
-    copies = [
-        pltpu.make_async_copy(meta_in, meta, sems.at[0]),
-        pltpu.make_async_copy(query.at[:, pl.ds(base, width)], gates, sems.at[1]),
-    ]
-    for copy in copies:
-        copy.start()
+    scalars = pltpu.make_async_copy(meta_in, meta, sems.at[0])
+    scalars.start()
     starts = range(0, width, LANES)
 
     def spread(start):
@@ -323,8 +340,8 @@
             spread_rows(tile, spans.at[start // LANES], w * SPAN)
 
     spread(0)
-    for copy in copies:
-        copy.wait()
+    scalars.wait()
+    stores = []
     for start in starts:
         columns = pl.ds(start, LANES)
         results = []
@@ -353,12 +370,17 @@
                     tile = tile + term[
                         pl.ds(m * GROUP_CH, GROUP_CH), pl.ds(pl.multiple_of(base + start, LANES), LANES)
                     ]
-                result[place, columns] = (gates[place, columns].astype(jnp.float32) * tile).astype(
-                    jnp.bfloat16
-                )
-    store = pltpu.make_async_copy(result, out.at[:, pl.ds(base, width)], sems.at[2])
-    store.start()
-    store.wait()
+                gates = query[place, pl.ds(pl.multiple_of(base + start, LANES), LANES)]
+                result[place, columns] = (gates.astype(jnp.float32) * tile).astype(jnp.bfloat16)
+        store = pltpu.make_async_copy(
+            result.at[:, columns],
+            out.at[:, pl.ds(pl.multiple_of(base + start, LANES), LANES)],
+            sems.at[1 + start // LANES],
+        )
+        store.start()
+        stores.append(store)
+    for store in stores:
+        store.wait()
 
 
 def conv(step, meta, pieces, shifted, term, query_proj, before):
@@ -366,7 +388,7 @@
     slots = row_count // STRETCH
     width = pieces.shape[1]
     operands = [meta, pieces, shifted, term, query_proj]
-    in_specs = [ANY_SPEC, VMEM_SPEC, VMEM_SPEC, VMEM_SPEC, HBM_SPEC]
+    in_specs = [ANY_SPEC] + [VMEM_SPEC] * 4
     aliases = {}
     if before is not None:
         aliases = {len(operands): 0}
@@ -381,9 +403,8 @@
         scratch_shapes=[
             pltpu.SMEM(meta.shape, jnp.int32),
             pltpu.VMEM((row_count, width), jnp.bfloat16),
-            pltpu.VMEM((row_count, width), jnp.bfloat16),
             pltpu.VMEM((width // LANES, BLOCKS, LANES, SENT * SPAN), jnp.bfloat16),
-            pltpu.SemaphoreType.DMA((3,)),
+            pltpu.SemaphoreType.DMA((1 + width // LANES,)),
         ],
         compiler_params=params(),
         name="conv",
@@ -397,38 +418,36 @@
     parts = size if by_parts else 1
 
     width = channels // parts
-    sends, extra, last, meta = gate(
-        size, parts, sources, owner, key_proj, value_proj, filters
-    )
+    sends, extra, meta = gate(size, parts, sources, owner, key_proj, value_proj, filters)
+    last = last_rows(key_proj, value_proj)
     first = SLOTS * width
     group_count = filters.shape[0]
     if not by_parts:
         blocks = lax.all_gather(sends[0][first:], "seq")
         steps = sender(lax.axis_index("seq"), jnp.arange(size, dtype=jnp.int32), size)
         blocks = jnp.take(blocks, steps, axis=0)
-        shifted = lags([blocks[step] for step in range(size)], 0, group_count)
+        shifted = lags([blocks[step] for step in steps_of(size)], 0, group_count)
         term = last_term(slots, meta, last, shifted)
         held = jnp.concatenate([sends[0][:first].reshape(SLOTS, width, LANES), extra])
         mine = (meta[:SENT] == lax.axis_index("seq"))[:, None, None]
         pieces = lax.psum(jnp.where(mine, held[meta[PLACE:MANY]], jnp.zeros_like(held)), "seq")
         return conv(0, meta, pieces, shifted, term, query_proj, None)
 
-    def exchange(value, step):
-        return lax.ppermute(value, "seq", [(z, z ^ step) for z in range(size)])
-
-    received = [sends[0]] + [exchange(sends[step], step) for step in range(1, size)]
+    def shift(value, step):
+        return lax.ppermute(value, "seq", [(z, (z + step) % size) for z in range(size)])
+
+    up, down, far = (shift(sends[step], step) for step in (1, size - 1, 2))
+    last, up = lax.optimization_barrier((last, up))
+    received = [sends[0], up, down, far]
 
     def merge_more(meta, received, extra):
-        more = [extra[0]] + [exchange(extra[step], step) for step in range(1, size)]
+        more = [extra[0]] + [shift(extra[step], step) for step in range(1, size)]
         return merge(size, width, meta, received, more)
 
     def merge_plain(meta, received, extra):
         return merge(size, width, meta, received)
 
     merged = lax.cond(meta[MANY] > 0, merge_more, merge_plain, meta, received, extra)
-
-    def shift(value, step):
-        return lax.ppermute(value, "seq", [(z, (z + step) % size) for z in range(size)])
 
     up, down = shift(merged, 1), shift(merged, size - 1)
     shifted = lags(received, first, group_count)

time: 47.7 us -> 47.2 us (0.990)
  the two profiles are of different devices: /device:TPU:20 before, /device:TPU:0 now
where the time goes in v6:
time: 47.2 us; the launch traced here: 47.1 us
  Pallas kernels  18.5 us (39%)
  waiting for transfers between devices  17.4 us (37%)
  starting transfers between devices  9.86 us (21%)
  between operations  0.74 us (2%)
  local copies, waits for them, and re-layouts  0.59 us (1%)
    ppermute x6, waiting for transfers between devices, shift(): lax.ppermute(value, 'seq', [(z, (z + step) % size) for z in range(size)])  17.4 us
    ppermute x6, starting transfers between devices, shift(): lax.ppermute(value, 'seq', [(z, (z + step) % size) for z in range(size)])  9.86 us
    pallas_call x4, Pallas kernels, conv(): pl.pallas_call(functools.partial(conv_kernel, step, slots), in_specs=in_s...  9.59 us
    pallas_call x1, Pallas kernels, last_term(): pl.pallas_call(functools.partial(last_kernel, slots), in_specs=[SMEM_SPEC...  2.51 us
    pallas_call x1, Pallas kernels, gate(): pl.pallas_call(functools.partial(gate_kernel, size, parts), in_specs=[HBM...  2.39 us
    pallas_call x1, Pallas kernels, lags(): pl.pallas_call(functools.partial(lags_kernel, first), grid=(group_count /...  2.15 us
    pallas_call x1, Pallas kernels, last_rows(): pl.pallas_call(last_rows_kernel, grid=(1,), in_specs=[block, block], out_...  1.16 us
  transfers between devices with their start and end apart: 6, of which 5 were waited for; matrix products, arithmetic and copies ran while one was open for 1% of the time, Pallas kernels for 28%

profile of v6, /device:TPU:0, one launch (start us, length us, event | category | flops | bytes accessed | tf_op | source)
XLA Modules:
  0.0 47.1 jit_solution(11804833771037335131)
XLA Ops:
  0.0 2.4 %gate.1 = (bf16[768,128]{1,0:T(8,128)(2,1)S(1)}, bf16[768,128]{1,0:T(8,128)(2,1)S(1)}, bf16[768,128]{1,0:T(8,128)(2,1)S(1)}, bf16[768,128]{1,0:T(8,128)(2,1)S(1)...) custom-call(s32[4]{0:T(128)} %sources_in.1, s32[16]{0:T(128)} %owner_in.1, bf16[512,1024]{1,0:T(8,128)(2,1)} %key.1, ...), custom_call_target="tpu_custom_call" | custom-call | tf_op jit(solution)/shard_map/gate/pallas_call | solution.py:142
  2.4 3.1 %collective-permute-start.3 = (bf16[768,128]{1,0:T(8,128)(2,1)S(1)}, bf16[768,128]{1,0:T(8,128)(2,1)S(1)}, u32[]{:S(2)}, u32[]{:S(2)}) collective-permute-start(bf16[768,128]{1,0:T(8,128)(2,1)S(1)} %get-tuple-element.53), channel_id=1, source_target_pairs={{0,4},{4,8},{8,12},{12,0},{1,5},{5,9},{9,13},{13,1},{2,6},{6,10},{... | collective-permute-start | bytes 589832 | tf_op jit(solution)/shard_map/ppermute | solution.py:437
  5.5 2.3 %collective-permute-start.4 = (bf16[768,128]{1,0:T(8,128)(2,1)S(1)}, bf16[768,128]{1,0:T(8,128)(2,1)S(1)}, u32[]{:S(2)}, u32[]{:S(2)}) collective-permute-start(bf16[768,128]{1,0:T(8,128)(2,1)S(1)} %get-tuple-element.55), channel_id=1, source_target_pairs={{0,12},{4,0},{8,4},{12,8},{1,13},{5,1},{9,5},{13,9},{2,14},{6,2},{... | collective-permute-start | bytes 589832 | tf_op jit(solution)/shard_map/ppermute | solution.py:437
  7.7 0.6 %collective-permute-start.5 = (bf16[768,128]{1,0:T(8,128)(2,1)S(1)}, bf16[768,128]{1,0:T(8,128)(2,1)S(1)}, u32[]{:S(2)}, u32[]{:S(2)}) collective-permute-start(bf16[768,128]{1,0:T(8,128)(2,1)S(1)} %get-tuple-element.56), channel_id=1, source_target_pairs={{0,8},{4,12},{8,0},{12,4},{1,9},{5,13},{9,1},{13,5},{2,10},{6,14},... | collective-permute-start | bytes 589832 | tf_op jit(solution)/shard_map/ppermute | solution.py:437
  8.3 1.2 %last_rows.1.last = bf16[1024,128]{1,0:T(8,128)(2,1)S(1)} custom-call(bf16[512,1024]{1,0:T(8,128)(2,1)} %key.1, bf16[512,1024]{1,0:T(8,128)(2,1)} %value.1), custom_call_target="tpu_custom_call" | custom-call | tf_op jit(solution)/shard_map/last_rows/pallas_call | solution.py:283
  9.5 0.6 %slice.15 = s32[1]{0:T(128)} slice(s32[23]{0:T(128)S(1)} %get-tuple-element.51.meta.meta_in), slice={[6:7]} | slice | bytes 8 | tf_op jit(solution)/shard_map/slice | solution.py:450
  10.7 2.7 %collective-permute-done.3.refs_1_ = bf16[768,128]{1,0:T(8,128)(2,1)S(1)} collective-permute-done((bf16[768,128]{1,0:T(8,128)(2,1)S(1)}, bf16[768,128]{1,0:T(8,128)(2,1)S(1)}, u32[]{:S(2)}, u32[]{:S(2)}) %collective-permute-start.3) | collective-permute-done | bytes 196640 | tf_op jit(solution)/shard_map/ppermute | solution.py:437
  13.5 2.6 %collective-permute-done.4.refs_2_ = bf16[768,128]{1,0:T(8,128)(2,1)S(1)} collective-permute-done((bf16[768,128]{1,0:T(8,128)(2,1)S(1)}, bf16[768,128]{1,0:T(8,128)(2,1)S(1)}, u32[]{:S(2)}, u32[]{:S(2)}) %collective-permute-start.4) | collective-permute-done | bytes 196640 | tf_op jit(solution)/shard_map/ppermute | solution.py:437
  16.0 9.2 %collective-permute-done.5.refs_3_ = bf16[768,128]{1,0:T(8,128)(2,1)S(1)} collective-permute-done((bf16[768,128]{1,0:T(8,128)(2,1)S(1)}, bf16[768,128]{1,0:T(8,128)(2,1)S(1)}, u32[]{:S(2)}, u32[]{:S(2)}) %collective-permute-start.5) | collective-permute-done | bytes 196640 | tf_op jit(solution)/shard_map/ppermute | solution.py:437
  25.2 0.7 %conditional.1 = (bf16[3,256,128]{2,1,0:T(8,128)(2,1)S(1)}) conditional(s32[]{:T(128)} %bitcast.4, (s32[23]{0:T(128)S(1)}, bf16[768,128]{1,0:T(8,128)(2,1)S(1)}, bf16[768,128]{1,0:T(8,128)(2,1)S(1)}, bf16[768,128]{1,0:T(8,128)(2,1)S(1)}, bf16[768,128]{1,0:T(8,128)(2,1)S(1)}) %tuple.14, (bf16[4,256,128]{2,1,0:T(8,128)(2,1)S(1)}, s32[23]{0:T(128)S(1)}, ...), branch_computations={%region_0.0_spmd, %region_1.0_spmd} | conditional | bytes 1310848 | solution.py:450
  25.2 0.7 %merge.2 = bf16[3,256,128]{2,1,0:T(8,128)(2,1)S(1)} custom-call(s32[23]{0:T(128)S(1)} %get-tuple-element.30.meta, bf16[768,128]{1,0:T(8,128)(2,1)S(1)} %get-tuple-element.31.refs_0_, bf16[768,128]{1,0:T(8,128)(2,1)S(1)} %get-tuple-element.32.refs_1_, bf16[768,128]{1,0:T(8,128)(2,1)S(1)} %get-tuple-element.33.refs_2_, ...), custom_call_target="tpu_custom_call" | custom-call | tf_op jit(solution)/shard_map/cond/branch_0_fun/merge/pallas_call | solution.py:186
  25.9 0.0 copy-start
  25.9 0.1 collective-permute-start.8
  26.0 3.8 %collective-permute-start.7 = (bf16[3,256,128]{2,1,0:T(8,128)(2,1)S(1)}, bf16[3,256,128]{2,1,0:T(8,128)(2,1)S(1)}, u32[]{:S(2)}, u32[]{:S(2)}) collective-permute-start(bf16[3,256,128]{2,1,0:T(8,128)(2,1)S(1)} %get-tuple-element.65.pieces), channel_id=1, source_target_pairs={{0,12},{4,0},{8,4},{12,8},{1,13},{5,1},{9,5},{13,9},{2,14},{6,2},{... | collective-permute-start | bytes 589832 | tf_op jit(solution)/shard_map/ppermute | solution.py:437
  29.8 2.2 %lags.1.shifted = bf16[64,16,2304]{2,1,0:T(8,128)(2,1)S(1)} custom-call(bf16[768,128]{1,0:T(8,128)(2,1)S(1)} %get-tuple-element.52.refs_0_, bf16[768,128]{1,0:T(8,128)(2,1)S(1)} %collective-permute-done.3.refs_1_, bf16[768,128]{1,0:T(8,128)(2,1)S(1)} %collective-permute-done.4.refs_2_, bf16[768,128]{1,0:T(8,128)(2,1)S(1)} %collective-permute-done.5.refs_3_), custom_call_target="tpu_custom_call" | custom-call | tf_op jit(solution)/shard_map/lags/pallas_call | solution.py:239
  31.9 0.1 collective-permute-start.6
  32.0 2.5 %last_term.1.term = f32[128,1024]{1,0:T(8,128)S(1)} custom-call(s32[23]{0:T(128)S(1)} %get-tuple-element.51.meta.meta_in, bf16[1024,128]{1,0:T(8,128)(2,1)S(1)} %last_rows.1.last, bf16[64,16,2304]{2,1,0:T(8,128)(2,1)S(1)} %lags.1.shifted), custom_call_target="tpu_custom_call" | custom-call | tf_op jit(solution)/shard_map/last_term/pallas_call | solution.py:316
  34.5 2.4 %conv.4.refs_0_ = bf16[512,1024]{1,0:T(8,128)(2,1)} custom-call(s32[23]{0:T(128)S(1)} %get-tuple-element.51.meta.meta_in, bf16[3,256,128]{2,1,0:T(8,128)(2,1)S(1)} %get-tuple-element.65.pieces, bf16[64,16,2304]{2,1,0:T(8,128)(2,1)S(1)} %lags.1.shifted, f32[128,1024]{1,0:T(8,128)S(1)} %last_term.1.term, bf16[512,1024]{1,0:T(8,128)(2,1)S(1)} %copy-done), custom_call_target="tpu_custom_call" | custom-call | tf_op jit(solution)/shard_map/conv/pallas_call | solution.py:397
  37.0 0.0 collective-permute-done.8.pieces
  37.0 2.4 %conv.5.refs_0_ = bf16[512,1024]{1,0:T(8,128)(2,1)} custom-call(s32[23]{0:T(128)S(1)} %get-tuple-element.51.meta.meta_in, bf16[3,256,128]{2,1,0:T(8,128)(2,1)S(1)} %collective-permute-done.8.pieces, bf16[64,16,2304]{2,1,0:T(8,128)(2,1)S(1)} %lags.1.shifted, f32[128,1024]{1,0:T(8,128)S(1)} %last_term.1.term, ...), custom_call_target="tpu_custom_call", output_to_operand_aliasing={{}: (5, {})} | custom-call | tf_op jit(solution)/shard_map/conv/pallas_call | solution.py:397
  39.4 0.1 collective-permute-done.7.pieces
  39.5 2.4 %conv.6.refs_0_ = bf16[512,1024]{1,0:T(8,128)(2,1)} custom-call(s32[23]{0:T(128)S(1)} %get-tuple-element.51.meta.meta_in, bf16[3,256,128]{2,1,0:T(8,128)(2,1)S(1)} %collective-permute-done.7.pieces, bf16[64,16,2304]{2,1,0:T(8,128)(2,1)S(1)} %lags.1.shifted, f32[128,1024]{1,0:T(8,128)S(1)} %last_term.1.term, ...), custom_call_target="tpu_custom_call", output_to_operand_aliasing={{}: (5, {})} | custom-call | tf_op jit(solution)/shard_map/conv/pallas_call | solution.py:397
  41.9 2.8 %collective-permute-done.6.pieces = bf16[3,256,128]{2,1,0:T(8,128)(2,1)S(1)} collective-permute-done((bf16[3,256,128]{2,1,0:T(8,128)(2,1)S(1)}, bf16[3,256,128]{2,1,0:T(8,128)(2,1)S(1)}, u32[]{:S(2)}, u32[]{:S(2)}) %collective-permute-start.6) | collective-permute-done | bytes 196640 | tf_op jit(solution)/shard_map/ppermute | solution.py:437
  44.7 2.4 %conv.7 = bf16[512,1024]{1,0:T(8,128)(2,1)} custom-call(s32[23]{0:T(128)S(1)} %get-tuple-element.51.meta.meta_in, bf16[3,256,128]{2,1,0:T(8,128)(2,1)S(1)} %collective-permute-done.6.pieces, bf16[64,16,2304]{2,1,0:T(8,128)(2,1)S(1)} %lags.1.shifted, f32[128,1024]{1,0:T(8,128)S(1)} %last_term.1.term, ...), custom_call_target="tpu_custom_call", output_to_operand_aliasing={{}: (5, {})} | custom-call | tf_op jit(solution)/shard_map/conv/pallas_call | solution.py:397
  (1 shorter events, 0.0 us)
Async XLA Ops:
  2.4 11.1 %collective-permute-start.3 = (bf16[768,128]{1,0:T(8,128)(2,1)S(1)}, bf16[768,128]{1,0:T(8,128)(2,1)S(1)}, u32[]{:S(2)}, u32[]{:S(2)}) collective-permute-start(bf16[768,128]{1,0:T(8,128)(2,1)S(1)} %get-tuple-element.53), channel_id=1, source_target_pairs={{0,4},{4,8},{8,12},{12,0},{1,5},{5,9},{9,13},{13,1},{2,6},{6,10},{... | collective-permute-start | bytes 589832 | tf_op jit(solution)/shard_map/ppermute | solution.py:437
  5.5 10.6 %collective-permute-start.4 = (bf16[768,128]{1,0:T(8,128)(2,1)S(1)}, bf16[768,128]{1,0:T(8,128)(2,1)S(1)}, u32[]{:S(2)}, u32[]{:S(2)}) collective-permute-start(bf16[768,128]{1,0:T(8,128)(2,1)S(1)} %get-tuple-element.55), channel_id=1, source_target_pairs={{0,12},{4,0},{8,4},{12,8},{1,13},{5,1},{9,5},{13,9},{2,14},{6,2},{... | collective-permute-start | bytes 589832 | tf_op jit(solution)/shard_map/ppermute | solution.py:437
  7.7 17.5 %collective-permute-start.5 = (bf16[768,128]{1,0:T(8,128)(2,1)S(1)}, bf16[768,128]{1,0:T(8,128)(2,1)S(1)}, u32[]{:S(2)}, u32[]{:S(2)}) collective-permute-start(bf16[768,128]{1,0:T(8,128)(2,1)S(1)} %get-tuple-element.56), channel_id=1, source_target_pairs={{0,8},{4,12},{8,0},{12,4},{1,9},{5,13},{9,1},{13,5},{2,10},{6,14},... | collective-permute-start | bytes 589832 | tf_op jit(solution)/shard_map/ppermute | solution.py:437
  25.9 8.6 %copy-start = (bf16[512,1024]{1,0:T(8,128)(2,1)S(1)}, bf16[512,1024]{1,0:T(8,128)(2,1)}, u32[]{:S(2)}) copy-start(bf16[512,1024]{1,0:T(8,128)(2,1)} %query.7) | copy-start | bytes 3145732
  25.9 11.0 %collective-permute-start.8 = (bf16[3,256,128]{2,1,0:T(8,128)(2,1)S(1)}, bf16[3,256,128]{2,1,0:T(8,128)(2,1)S(1)}, u32[]{:S(2)}, u32[]{:S(2)}) collective-permute-start(bf16[3,256,128]{2,1,0:T(8,128)(2,1)S(1)} %get-tuple-element.65.pieces), channel_id=1, source_target_pairs={{0,4},{4,8},{8,12},{12,0},{1,5},{5,9},{9,13},{13,1},{2,6},{6,10},{... | collective-permute-start | bytes 589832 | tf_op jit(solution)/shard_map/ppermute | solution.py:437
  26.0 13.5 %collective-permute-start.7 = (bf16[3,256,128]{2,1,0:T(8,128)(2,1)S(1)}, bf16[3,256,128]{2,1,0:T(8,128)(2,1)S(1)}, u32[]{:S(2)}, u32[]{:S(2)}) collective-permute-start(bf16[3,256,128]{2,1,0:T(8,128)(2,1)S(1)} %get-tuple-element.65.pieces), channel_id=1, source_target_pairs={{0,12},{4,0},{8,4},{12,8},{1,13},{5,1},{9,5},{13,9},{2,14},{6,2},{... | collective-permute-start | bytes 589832 | tf_op jit(solution)/shard_map/ppermute | solution.py:437
  31.9 12.7 %collective-permute-start.6 = (bf16[3,256,128]{2,1,0:T(8,128)(2,1)S(1)}, bf16[3,256,128]{2,1,0:T(8,128)(2,1)S(1)}, u32[]{:S(2)}, u32[]{:S(2)}) collective-permute-start(bf16[3,256,128]{2,1,0:T(8,128)(2,1)S(1)} %get-tuple-element.65.pieces), channel_id=1, source_target_pairs={{0,8},{4,12},{8,0},{12,4},{1,9},{5,13},{9,1},{13,5},{2,10},{6,14},... | collective-permute-start | bytes 589832 | tf_op jit(solution)/shard_map/ppermute | solution.py:437

commit v7 on v6

--- a/solution.py
+++ b/solution.py
@@ -52,7 +52,7 @@
     return (rows_k * rows_v).astype(jnp.bfloat16).T
 
 
-def gate_kernel(size, parts, sources_in, owner_in, key_in, value_in, filters_in, *refs):
+def gate_kernel(size, parts, shares, sources_in, owner_in, key_in, value_in, filters_in, *refs):
     sends = refs[:parts]
     extra, meta, sources, owner, key, value, filters, sems = refs[parts:]
     stretch_count = owner.shape[0]
@@ -123,14 +123,17 @@
                         fill(extra.at[step], 0)
 
     meta[MANY] = many
-    group_count = filters.shape[0]
+    share = filters.shape[0] // shares
+    groups = pl.ds(0, share)
+    if shares > 1:
+        groups = pl.ds(pl.multiple_of(lax.axis_index("rep") * share, share), share)
     for tile in range(filters.shape[1] // LANES):
-        rows = pl.ds(SLOTS * width + tile * group_count, group_count)
+        piece = filters[groups, pl.ds(tile * LANES, LANES)]
         for send in sends:
-            send[rows, :] = filters[:, pl.ds(tile * LANES, LANES)]
-
-
-def gate(size, parts, sources, owner, key_proj, value_proj, filters):
+            send[pl.ds(SLOTS * width + tile * share, share), :] = piece
+
+
+def gate(size, parts, shares, sources, owner, key_proj, value_proj, filters):
     row_count, channels = key_proj.shape
     slots = row_count // STRETCH
     width = channels // parts
@@ -138,9 +141,9 @@
         pltpu.with_memory_space_constraint(operand, pltpu.HBM)
         for operand in (sources, owner, key_proj, value_proj, filters)
     ]
-    rows = SLOTS * width + filters.size // LANES
+    rows = SLOTS * width + filters.size // (shares * LANES)
     *sends, extra, meta = pl.pallas_call(
-        functools.partial(gate_kernel, size, parts),
+        functools.partial(gate_kernel, size, parts, shares),
         in_specs=[HBM_SPEC] * 5,
         out_specs=[VMEM_SPEC] * (parts + 1) + [SMEM_SPEC],
         out_shape=[jax.ShapeDtypeStruct((rows, LANES), jnp.bfloat16)] * parts
@@ -163,8 +166,15 @@
 
 
 def merge_kernel(size, width, meta, *refs):
-    received, extras, out = refs[:size], refs[size:-1], refs[-1]
+    received, extras = refs[:size], refs[size:-4]
+    out, low, high, filters = refs[-4:]
     me = lax.axis_index("seq")
+
+    def write(w, piece):
+        out[w] = piece
+        low[w] = piece[: width // 2]
+        high[w] = piece[width // 2 :]
+
     for w in range(SENT):
         place = meta[PLACE + w]
         rows = pl.ds(pl.multiple_of(jnp.minimum(place, SLOTS - 1) * width, LANES), width)
@@ -172,47 +182,60 @@
 
             @pl.when(sender(me, step, size) == meta[w])
             def _(w=w, block=block, rows=rows):
-                out[w] = block[rows, :]
+                write(w, block[rows, :])
 
     for w in range(SLOTS, SENT):
         for step, extra in enumerate(extras):
 
             @pl.when((sender(me, step, size) == meta[w]) & (meta[PLACE + w] >= SLOTS))
             def _(w=w, extra=extra):
-                out[w] = extra[...]
+                write(w, extra[...])
+
+    for block, step in zip(received, steps_of(size)):
+        filters[sender(me, step, size)] = block[pl.ds(SLOTS * width, filters.shape[1]), :]
 
 
 def merge(size, width, meta, received, extras=()):
     return pl.pallas_call(
         functools.partial(merge_kernel, size, width),
         in_specs=[SMEM_SPEC] + [VMEM_SPEC] * (size + len(extras)),
-        out_specs=VMEM_SPEC,
-        out_shape=jax.ShapeDtypeStruct((SENT, width, LANES), received[0].dtype),
+        out_specs=[VMEM_SPEC] * 4,
+        out_shape=[
+            jax.ShapeDtypeStruct(shape, received[0].dtype)
+            for shape in (
+                (SENT, width, LANES),
+                (SENT, width // 2, LANES),
+                (SENT, width // 2, LANES),
+                (size, received[0].shape[0] - SLOTS * width, LANES),
+            )
+        ],
         compiler_params=params(),
         name="merge",
     )(meta, *received, *extras)
 
 
-def lags_kernel(first, *refs):
-    received, (out, reverse) = refs[:-2], refs[-2:]
-    size = len(received)
+def lags_kernel(*refs):
+    shares, (out, reverse) = refs[:-2], refs[-2:]
+    size = shares[0].shape[0]
     group_count, padded = reverse.shape
-    tiles = (received[0].shape[0] - first) // group_count
+    share = group_count // len(shares)
+    tiles = shares[0].shape[1] // share
     lag_count = size * tiles * LANES
     tile_step = pl.program_id(0)
 
     @pl.when(tile_step == 0)
     def _():
-        me = lax.axis_index("seq")
         row = lax.broadcasted_iota(jnp.int32, (LANES, LANES), 0)
         column = lax.broadcasted_iota(jnp.int32, (LANES, LANES), 1)
         flip = jnp.where(row + column == LANES - 1, 1.0, 0.0).astype(jnp.bfloat16)
-        for block, step in zip(received, steps_of(size)):
-            shard = sender(me, step, size)
-            for tile in range(tiles):
-                piece = block[pl.ds(first + tile * group_count, group_count), :]
-                start = lag_count - LANES * (shard * tiles + tile + 1)
-                reverse[:, pl.ds(pl.multiple_of(start, LANES), LANES)] = jnp.dot(
+        for index, blocks in enumerate(shares):
+            groups = pl.ds(0, share)
+            if len(shares) > 1:
+                place = lax.axis_index("rep") if index == 0 else 1 - lax.axis_index("rep")
+                groups = pl.ds(pl.multiple_of(place * share, share), share)
+            for tile in range(size * tiles):
+                piece = blocks[tile // tiles, pl.ds(tile % tiles * share, share), :]
+                reverse[groups, pl.ds(lag_count - LANES * (tile + 1), LANES)] = jnp.dot(
                     piece, flip, preferred_element_type=jnp.float32
                 )
         reverse[:, pl.ds(lag_count, padded - lag_count)] = jnp.zeros(
@@ -233,19 +256,18 @@
             before[g] = rolled
 
 
-def lags(received, first, group_count):
-    size = len(received)
-    padded = size * (received[0].shape[0] - first) // group_count * LANES + SPAN
+def lags(shares, group_count):
+    padded = sum(blocks.size for blocks in shares) // group_count + SPAN
     return pl.pallas_call(
-        functools.partial(lags_kernel, first),
+        lags_kernel,
         grid=(group_count // BLOCKS,),
-        in_specs=[VMEM_SPEC] * size,
+        in_specs=[VMEM_SPEC] * len(shares),
         out_specs=pl.BlockSpec((BLOCKS, GROUP_CH, padded), lambda i: (i, 0, 0)),
         out_shape=jax.ShapeDtypeStruct((group_count, GROUP_CH, padded), jnp.bfloat16),
         scratch_shapes=[pltpu.VMEM((group_count, padded), jnp.float32)],
         compiler_params=params(),
         name="lags",
-    )(*received)
+    )(*shares)
 
 
 def spread_rows(tile, spans, base):
@@ -324,12 +346,12 @@
     )(meta, last, shifted)
 
 
-def conv_kernel(step, slots, meta_in, pieces, shifted, term, query, *refs):
+def conv_kernel(step, slots, part, offset, meta_in, pieces, shifted, term, query, *refs):
     out, meta, result, spans, sems = refs[-5:]
     width = pieces.shape[1]
-    size = out.shape[1] // width
+    size = out.shape[1] // part
     me = lax.axis_index("seq")
-    base = pl.multiple_of(lax.rem(me + size - step, size) * width, width)
+    base = pl.multiple_of(lax.rem(me + size - step, size) * part + offset, width)
     scalars = pltpu.make_async_copy(meta_in, meta, sems.at[0])
     scalars.start()
     starts = range(0, width, LANES)
@@ -383,7 +405,7 @@
         store.wait()
 
 
-def conv(step, meta, pieces, shifted, term, query_proj, before):
+def conv(step, meta, pieces, shifted, term, query_proj, before, part=None, offset=0):
     row_count = query_proj.shape[0]
     slots = row_count // STRETCH
     width = pieces.shape[1]
@@ -395,7 +417,7 @@
         operands.append(before)
         in_specs.append(HBM_SPEC)
     return pl.pallas_call(
-        functools.partial(conv_kernel, step, slots),
+        functools.partial(conv_kernel, step, slots, part or width, offset),
         in_specs=in_specs,
         out_specs=HBM_SPEC,
         out_shape=jax.ShapeDtypeStruct(query_proj.shape, jnp.bfloat16),
@@ -411,22 +433,20 @@
     )(*operands)
 
 
-def shards(size, key_proj, value_proj, query_proj, filters, sources, owner):
+def shards(size, reps, key_proj, value_proj, query_proj, filters, sources, owner):
     row_count, channels = key_proj.shape
     slots = row_count // STRETCH
-    by_parts = size == 4 and channels % (size * LANES) == 0
+    by_parts = (size, reps) == (4, 2) and channels % (2 * size * LANES) == 0
+    shares = reps if by_parts else 1
     parts = size if by_parts else 1
 
     width = channels // parts
-    sends, extra, meta = gate(size, parts, sources, owner, key_proj, value_proj, filters)
+    sends, extra, meta = gate(size, parts, shares, sources, owner, key_proj, value_proj, filters)
     last = last_rows(key_proj, value_proj)
     first = SLOTS * width
     group_count = filters.shape[0]
     if not by_parts:
-        blocks = lax.all_gather(sends[0][first:], "seq")
-        steps = sender(lax.axis_index("seq"), jnp.arange(size, dtype=jnp.int32), size)
-        blocks = jnp.take(blocks, steps, axis=0)
-        shifted = lags([blocks[step] for step in steps_of(size)], 0, group_count)
+        shifted = lags([lax.all_gather(sends[0][first:], "seq")], group_count)
         term = last_term(slots, meta, last, shifted)
         held = jnp.concatenate([sends[0][:first].reshape(SLOTS, width, LANES), extra])
         mine = (meta[:SENT] == lax.axis_index("seq"))[:, None, None]
@@ -447,22 +467,29 @@
     def merge_plain(meta, received, extra):
         return merge(size, width, meta, received)
 
-    merged = lax.cond(meta[MANY] > 0, merge_more, merge_plain, meta, received, extra)
-
-    up, down = shift(merged, 1), shift(merged, size - 1)
-    shifted = lags(received, first, group_count)
-    far_part, shifted = lax.optimization_barrier((merged, shifted))
-    far = shift(far_part, 2)
+    merged, low, high, share = lax.cond(
+        meta[MANY] > 0, merge_more, merge_plain, meta, received, extra
+    )
+    up = shift(merged, 1)
+    other = lax.ppermute(share, "rep", [(0, 1), (1, 0)])
+    down = shift(merged, size - 1)
+    shifted = lags([share, other], group_count)
+    low, high, shifted = lax.optimization_barrier((low, high, shifted))
+    far = [shift(half, 2) for half in (low, high)]
     term = last_term(slots, meta, last, shifted)
     out = None
-    for step, pieces in ((0, merged), (1, up), (size - 1, down), (2, far)):
+    for step, pieces in ((0, merged), (1, up), (size - 1, down)):
         out = conv(step, meta, pieces, shifted, term, query_proj, out)
+    for index, pieces in enumerate(far):
+        out = conv(
+            2, meta, pieces, shifted, term, query_proj, out, width, index * (width // len(far))
+        )
     return out
 
 
 def solution(mesh):
     return jax.shard_map(
-        functools.partial(shards, mesh.shape["seq"]),
+        functools.partial(shards, mesh.shape["seq"], mesh.shape["rep"]),
         mesh=mesh,
         in_specs=(
             P(("rep", "seq"), "ch"),

time: 47.2 us -> 47.5 us (level)
  waiting for transfers between devices: 17.4 us -> 10.9 us
  starting transfers between devices: 9.86 us -> 15.1 us
  Pallas kernels: 18.5 us -> 19.9 us
    ppermute x6 -> x7, waiting for transfers between devices: 17.4 us -> 10.9 us  [shift(): lax.ppermute(value, 'seq', [(z, (z + step) % size) for z in range(size)])]
    ppermute x6 -> x7, starting transfers between devices: 9.86 us -> 13.3 us  [shift(): lax.ppermute(value, 'seq', [(z, (z + step) % size) for z in range(size)])]
    ppermute x0 -> x1, starting transfers between devices: none -> 1.78 us  [shards(): other = lax.ppermute(share, 'rep', [(0, 1), (1, 0)])]
    pallas_call x6 -> x7, Pallas kernels: 14.1 us -> 15.5 us  [the longest x5 11.1 us: conv(): pl.pallas_call(functools.partial(conv_kernel, step, slots, part or width,...]
  transfers between devices with their start and end apart: 6 -> 8, of which waited for: 5 -> 3; matrix products, arithmetic and copies ran while one was open for 1% -> 1% of each run, Pallas kernels for 28% -> 32%
where the time goes in v7:
time: 47.5 us; the launch traced here: 47.3 us
  Pallas kernels  19.9 us (42%)
  starting transfers between devices  15.1 us (32%)
  waiting for transfers between devices  10.9 us (23%)
  between operations  0.76 us (2%)
  local copies, waits for them, and re-layouts  0.59 us (1%)
    ppermute x7, starting transfers between devices, shift(): lax.ppermute(value, 'seq', [(z, (z + step) % size) for z in range(size)])  13.3 us
    pallas_call x5, Pallas kernels, conv(): pl.pallas_call(functools.partial(conv_kernel, step, slots, part or width,...  11.1 us
    ppermute x7, waiting for transfers between devices, shift(): lax.ppermute(value, 'seq', [(z, (z + step) % size) for z in range(size)])  10.9 us
    pallas_call x1, Pallas kernels, last_term(): pl.pallas_call(functools.partial(last_kernel, slots), in_specs=[SMEM_SPEC...  2.51 us
    pallas_call x1, Pallas kernels, lags(): pl.pallas_call(lags_kernel, grid=(group_count // BLOCKS,), in_specs=[VMEM...  2.26 us
    pallas_call x1, Pallas kernels, gate(): pl.pallas_call(functools.partial(gate_kernel, size, parts, shares), in_sp...  2.18 us
    ppermute x1, starting transfers between devices, shards(): other = lax.ppermute(share, 'rep', [(0, 1), (1, 0)])  1.78 us
    pallas_call x1, Pallas kernels, last_rows(): pl.pallas_call(last_rows_kernel, grid=(1,), in_specs=[block, block], out_...  1.16 us
  transfers between devices with their start and end apart: 8, of which 3 were waited for; matrix products, arithmetic and copies ran while one was open for 1% of the time, Pallas kernels for 32%

profile of v7, /device:TPU:0, one launch (start us, length us, event | category | flops | bytes accessed | tf_op | source)
XLA Modules:
  0.0 47.3 jit_solution(14869996537010710222)
XLA Ops:
  0.0 2.2 %gate.1 = (bf16[640,128]{1,0:T(8,128)(2,1)S(1)}, bf16[640,128]{1,0:T(8,128)(2,1)S(1)}, bf16[640,128]{1,0:T(8,128)(2,1)S(1)}, bf16[640,128]{1,0:T(8,128)(2,1)S(1)...) custom-call(s32[4]{0:T(128)} %sources_in.1, s32[16]{0:T(128)} %owner_in.1, bf16[512,1024]{1,0:T(8,128)(2,1)} %key.1, ...), custom_call_target="tpu_custom_call" | custom-call | tf_op jit(solution)/shard_map/gate/pallas_call | solution.py:145
  2.2 3.5 %collective-permute-start.3 = (bf16[640,128]{1,0:T(8,128)(2,1)S(1)}, bf16[640,128]{1,0:T(8,128)(2,1)S(1)}, u32[]{:S(2)}, u32[]{:S(2)}) collective-permute-start(bf16[640,128]{1,0:T(8,128)(2,1)S(1)} %get-tuple-element.55), channel_id=1, source_target_pairs={{0,4},{4,8},{8,12},{12,0},{1,5},{5,9},{9,13},{13,1},{2,6},{6,10},{... | collective-permute-start | bytes 491528 | tf_op jit(solution)/shard_map/ppermute | solution.py:457
  5.6 1.7 %collective-permute-start.4 = (bf16[640,128]{1,0:T(8,128)(2,1)S(1)}, bf16[640,128]{1,0:T(8,128)(2,1)S(1)}, u32[]{:S(2)}, u32[]{:S(2)}) collective-permute-start(bf16[640,128]{1,0:T(8,128)(2,1)S(1)} %get-tuple-element.57), channel_id=1, source_target_pairs={{0,12},{4,0},{8,4},{12,8},{1,13},{5,1},{9,5},{13,9},{2,14},{6,2},{... | collective-permute-start | bytes 491528 | tf_op jit(solution)/shard_map/ppermute | solution.py:457
  7.4 1.4 %collective-permute-start.5 = (bf16[640,128]{1,0:T(8,128)(2,1)S(1)}, bf16[640,128]{1,0:T(8,128)(2,1)S(1)}, u32[]{:S(2)}, u32[]{:S(2)}) collective-permute-start(bf16[640,128]{1,0:T(8,128)(2,1)S(1)} %get-tuple-element.58), channel_id=1, source_target_pairs={{0,8},{4,12},{8,0},{12,4},{1,9},{5,13},{9,1},{13,5},{2,10},{6,14},... | collective-permute-start | bytes 491528 | tf_op jit(solution)/shard_map/ppermute | solution.py:457
  8.7 1.2 %last_rows.1.last = bf16[1024,128]{1,0:T(8,128)(2,1)S(1)} custom-call(bf16[512,1024]{1,0:T(8,128)(2,1)} %key.1, bf16[512,1024]{1,0:T(8,128)(2,1)} %value.1), custom_call_target="tpu_custom_call" | custom-call | tf_op jit(solution)/shard_map/last_rows/pallas_call | solution.py:305
  9.9 0.6 %slice.15 = s32[1]{0:T(128)} slice(s32[23]{0:T(128)S(1)} %get-tuple-element.53.meta.meta_in), slice={[6:7]} | slice | bytes 8 | tf_op jit(solution)/shard_map/slice | solution.py:471
  11.1 1.3 %collective-permute-done.3 = bf16[640,128]{1,0:T(8,128)(2,1)S(1)} collective-permute-done((bf16[640,128]{1,0:T(8,128)(2,1)S(1)}, bf16[640,128]{1,0:T(8,128)(2,1)S(1)}, u32[]{:S(2)}, u32[]{:S(2)}) %collective-permute-start.3) | collective-permute-done | bytes 163872 | tf_op jit(solution)/shard_map/ppermute | solution.py:457
  12.4 2.4 %collective-permute-done.4 = bf16[640,128]{1,0:T(8,128)(2,1)S(1)} collective-permute-done((bf16[640,128]{1,0:T(8,128)(2,1)S(1)}, bf16[640,128]{1,0:T(8,128)(2,1)S(1)}, u32[]{:S(2)}, u32[]{:S(2)}) %collective-permute-start.4) | collective-permute-done | bytes 163872 | tf_op jit(solution)/shard_map/ppermute | solution.py:457
  14.8 7.2 %collective-permute-done.5 = bf16[640,128]{1,0:T(8,128)(2,1)S(1)} collective-permute-done((bf16[640,128]{1,0:T(8,128)(2,1)S(1)}, bf16[640,128]{1,0:T(8,128)(2,1)S(1)}, u32[]{:S(2)}, u32[]{:S(2)}) %collective-permute-start.5) | collective-permute-done | bytes 163872 | tf_op jit(solution)/shard_map/ppermute | solution.py:457
  22.0 0.7 %conditional.1 = ((bf16[3,256,128]{2,1,0:T(8,128)(2,1)S(1)}, bf16[3,128,128]{2,1,0:T(8,128)(2,1)S(1)}, bf16[3,128,128]{2,1,0:T(8,128)(2,1)S(1)}, bf16[4,128,128]{2,1,0:T(8,128)(2,1)S(1)})) conditional(s32[]{:T(128)} %bitcast.4, (s32[23]{0:T(128)S(1)}, bf16[640,128]{1,0:T(8,128)(2,1)S(1)}, bf16[640,128]{1,0:T(8,128)(2,1)S(1)}, ...), branch_computations={%region_0.0_spmd, %region_1.0_spmd} | conditional | bytes 1310848 | solution.py:470
  22.0 0.7 %merge.2 = (bf16[3,256,128]{2,1,0:T(8,128)(2,1)S(1)}, bf16[3,128,128]{2,1,0:T(8,128)(2,1)S(1)}, bf16[3,128,128]{2,1,0:T(8,128)(2,1)S(1)}, bf16[4,128,128]{2,1,0:T(8,128)(2,1)S(1)}) custom-call(s32[23]{0:T(128)S(1)} %get-tuple-element.27.meta, bf16[640,128]{1,0:T(8,128)(2,1)S(1)} %get-tuple-element.28.refs_0_, ...), custom_call_target="tpu_custom_call" | custom-call | tf_op jit(solution)/shard_map/cond/branch_0_fun/merge/pallas_call | solution.py:199
  22.7 1.8 %collective-permute-start.6 = (bf16[4,128,128]{2,1,0:T(8,128)(2,1)S(1)}, bf16[4,128,128]{2,1,0:T(8,128)(2,1)S(1)}, u32[]{:S(2)}, u32[]{:S(2)}) collective-permute-start(bf16[4,128,128]{2,1,0:T(8,128)(2,1)S(1)} %get-tuple-element.62.refs_0_), channel_id=1, source_target_pairs={{0,16},{16,0},{1,17},{17,1},{2,18},{18,2},{3,19},{19,3},{4,20},{20... | collective-permute-start | bytes 393224 | tf_op jit(solution)/shard_map/ppermute | solution.py:474
  24.5 0.0 collective-permute-start.10
  24.5 3.8 %collective-permute-start.9 = (bf16[3,256,128]{2,1,0:T(8,128)(2,1)S(1)}, bf16[3,256,128]{2,1,0:T(8,128)(2,1)S(1)}, u32[]{:S(2)}, u32[]{:S(2)}) collective-permute-start(bf16[3,256,128]{2,1,0:T(8,128)(2,1)S(1)} %get-tuple-element.67.pieces), channel_id=1, source_target_pairs={{0,12},{4,0},{8,4},{12,8},{1,13},{5,1},{9,5},{13,9},{2,14},{6,2},{... | collective-permute-start | bytes 589832 | tf_op jit(solution)/shard_map/ppermute | solution.py:457
  28.3 0.0 collective-permute-done.6.refs_1_
  28.4 2.3 %lags.1.shifted = bf16[64,16,2304]{2,1,0:T(8,128)(2,1)S(1)} custom-call(bf16[4,128,128]{2,1,0:T(8,128)(2,1)S(1)} %get-tuple-element.62.refs_0_, bf16[4,128,128]{2,1,0:T(8,128)(2,1)S(1)} %collective-permute-done.6.refs_1_), custom_call_target="tpu_custom_call" | custom-call | tf_op jit(solution)/shard_map/lags/pallas_call | solution.py:261
  30.6 0.1 collective-permute-start.8
  30.7 2.9 %collective-permute-start.7 = (bf16[3,128,128]{2,1,0:T(8,128)(2,1)S(1)}, bf16[3,128,128]{2,1,0:T(8,128)(2,1)S(1)}, u32[]{:S(2)}, u32[]{:S(2)}) collective-permute-start(bf16[3,128,128]{2,1,0:T(8,128)(2,1)S(1)} %get-tuple-element.63), channel_id=1, source_target_pairs={{0,8},{4,12},{8,0},{12,4},{1,9},{5,13},{9,1},{13,5},{2,10},{6,14},... | collective-permute-start | bytes 294920 | tf_op jit(solution)/shard_map/ppermute | solution.py:457
  33.6 2.5 %last_term.1.term = f32[128,1024]{1,0:T(8,128)S(1)} custom-call(s32[23]{0:T(128)S(1)} %get-tuple-element.53.meta.meta_in, bf16[1024,128]{1,0:T(8,128)(2,1)S(1)} %last_rows.1.last, bf16[64,16,2304]{2,1,0:T(8,128)(2,1)S(1)} %lags.1.shifted), custom_call_target="tpu_custom_call" | custom-call | tf_op jit(solution)/shard_map/last_term/pallas_call | solution.py:338
  36.1 2.4 %conv.5.refs_0_ = bf16[512,1024]{1,0:T(8,128)(2,1)} custom-call(s32[23]{0:T(128)S(1)} %get-tuple-element.53.meta.meta_in, bf16[3,256,128]{2,1,0:T(8,128)(2,1)S(1)} %get-tuple-element.67.pieces, bf16[64,16,2304]{2,1,0:T(8,128)(2,1)S(1)} %lags.1.shifted, f32[128,1024]{1,0:T(8,128)S(1)} %last_term.1.term, bf16[512,1024]{1,0:T(8,128)(2,1)S(1)} %copy-done), custom_call_target="tpu_custom_call" | custom-call | tf_op jit(solution)/shard_map/conv/pallas_call | solution.py:419
  38.5 2.4 %conv.6.refs_0_ = bf16[512,1024]{1,0:T(8,128)(2,1)} custom-call(s32[23]{0:T(128)S(1)} %get-tuple-element.53.meta.meta_in, bf16[3,256,128]{2,1,0:T(8,128)(2,1)S(1)} %collective-permute-done.10.pieces, bf16[64,16,2304]{2,1,0:T(8,128)(2,1)S(1)} %lags.1.shifted, f32[128,1024]{1,0:T(8,128)S(1)} %last_term.1.term, ...), custom_call_target="tpu_custom_call", output_to_operand_aliasing={{}: (5, {})} | custom-call | tf_op jit(solution)/shard_map/conv/pallas_call | solution.py:419
  41.0 2.4 %conv.7.refs_0_ = bf16[512,1024]{1,0:T(8,128)(2,1)} custom-call(s32[23]{0:T(128)S(1)} %get-tuple-element.53.meta.meta_in, bf16[3,256,128]{2,1,0:T(8,128)(2,1)S(1)} %collective-permute-done.9.pieces, bf16[64,16,2304]{2,1,0:T(8,128)(2,1)S(1)} %lags.1.shifted, f32[128,1024]{1,0:T(8,128)S(1)} %last_term.1.term, ...), custom_call_target="tpu_custom_call", output_to_operand_aliasing={{}: (5, {})} | custom-call | tf_op jit(solution)/shard_map/conv/pallas_call | solution.py:419
  43.4 1.9 %conv.8.refs_0_ = bf16[512,1024]{1,0:T(8,128)(2,1)} custom-call(s32[23]{0:T(128)S(1)} %get-tuple-element.53.meta.meta_in, bf16[3,128,128]{2,1,0:T(8,128)(2,1)S(1)} %collective-permute-done.8.pieces, bf16[64,16,2304]{2,1,0:T(8,128)(2,1)S(1)} %lags.1.shifted, f32[128,1024]{1,0:T(8,128)S(1)} %last_term.1.term, ...), custom_call_target="tpu_custom_call", output_to_operand_aliasing={{}: (5, {})} | custom-call | tf_op jit(solution)/shard_map/conv/pallas_call | solution.py:419
  45.3 1.9 %conv.9 = bf16[512,1024]{1,0:T(8,128)(2,1)} custom-call(s32[23]{0:T(128)S(1)} %get-tuple-element.53.meta.meta_in, bf16[3,128,128]{2,1,0:T(8,128)(2,1)S(1)} %collective-permute-done.7.pieces, bf16[64,16,2304]{2,1,0:T(8,128)(2,1)S(1)} %lags.1.shifted, f32[128,1024]{1,0:T(8,128)S(1)} %last_term.1.term, ...), custom_call_target="tpu_custom_call", output_to_operand_aliasing={{}: (5, {})} | custom-call | tf_op jit(solution)/shard_map/conv/pallas_call | solution.py:419
  (6 shorter events, 0.0 us)
Async XLA Ops:
  2.2 10.2 %collective-permute-start.3 = (bf16[640,128]{1,0:T(8,128)(2,1)S(1)}, bf16[640,128]{1,0:T(8,128)(2,1)S(1)}, u32[]{:S(2)}, u32[]{:S(2)}) collective-permute-start(bf16[640,128]{1,0:T(8,128)(2,1)S(1)} %get-tuple-element.55), channel_id=1, source_target_pairs={{0,4},{4,8},{8,12},{12,0},{1,5},{5,9},{9,13},{13,1},{2,6},{6,10},{... | collective-permute-start | bytes 491528 | tf_op jit(solution)/shard_map/ppermute | solution.py:457
  5.6 9.2 %collective-permute-start.4 = (bf16[640,128]{1,0:T(8,128)(2,1)S(1)}, bf16[640,128]{1,0:T(8,128)(2,1)S(1)}, u32[]{:S(2)}, u32[]{:S(2)}) collective-permute-start(bf16[640,128]{1,0:T(8,128)(2,1)S(1)} %get-tuple-element.57), channel_id=1, source_target_pairs={{0,12},{4,0},{8,4},{12,8},{1,13},{5,1},{9,5},{13,9},{2,14},{6,2},{... | collective-permute-start | bytes 491528 | tf_op jit(solution)/shard_map/ppermute | solution.py:457
  7.4 14.7 %collective-permute-start.5 = (bf16[640,128]{1,0:T(8,128)(2,1)S(1)}, bf16[640,128]{1,0:T(8,128)(2,1)S(1)}, u32[]{:S(2)}, u32[]{:S(2)}) collective-permute-start(bf16[640,128]{1,0:T(8,128)(2,1)S(1)} %get-tuple-element.58), channel_id=1, source_target_pairs={{0,8},{4,12},{8,0},{12,4},{1,9},{5,13},{9,1},{13,5},{2,10},{6,14},... | collective-permute-start | bytes 491528 | tf_op jit(solution)/shard_map/ppermute | solution.py:457
  22.7 5.6 %collective-permute-start.6 = (bf16[4,128,128]{2,1,0:T(8,128)(2,1)S(1)}, bf16[4,128,128]{2,1,0:T(8,128)(2,1)S(1)}, u32[]{:S(2)}, u32[]{:S(2)}) collective-permute-start(bf16[4,128,128]{2,1,0:T(8,128)(2,1)S(1)} %get-tuple-element.62.refs_0_), channel_id=1, source_target_pairs={{0,16},{16,0},{1,17},{17,1},{2,18},{18,2},{3,19},{19,3},{4,20},{20... | collective-permute-start | bytes 393224 | tf_op jit(solution)/shard_map/ppermute | solution.py:474
  24.5 11.6 %copy-start = (bf16[512,1024]{1,0:T(8,128)(2,1)S(1)}, bf16[512,1024]{1,0:T(8,128)(2,1)}, u32[]{:S(2)}) copy-start(bf16[512,1024]{1,0:T(8,128)(2,1)} %query.9) | copy-start | bytes 3145732
  24.5 14.0 %collective-permute-start.10 = (bf16[3,256,128]{2,1,0:T(8,128)(2,1)S(1)}, bf16[3,256,128]{2,1,0:T(8,128)(2,1)S(1)}, u32[]{:S(2)}, u32[]{:S(2)}) collective-permute-start(bf16[3,256,128]{2,1,0:T(8,128)(2,1)S(1)} %get-tuple-element.67.pieces), channel_id=1, source_target_pairs={{0,4},{4,8},{8,12},{12,0},{1,5},{5,9},{9,13},{13,1},{2,6},{6,10},{... | collective-permute-start | bytes 589832 | tf_op jit(solution)/shard_map/ppermute | solution.py:457
  24.5 16.4 %collective-permute-start.9 = (bf16[3,256,128]{2,1,0:T(8,128)(2,1)S(1)}, bf16[3,256,128]{2,1,0:T(8,128)(2,1)S(1)}, u32[]{:S(2)}, u32[]{:S(2)}) collective-permute-start(bf16[3,256,128]{2,1,0:T(8,128)(2,1)S(1)} %get-tuple-element.67.pieces), channel_id=1, source_target_pairs={{0,12},{4,0},{8,4},{12,8},{1,13},{5,1},{9,5},{13,9},{2,14},{6,2},{... | collective-permute-start | bytes 589832 | tf_op jit(solution)/shard_map/ppermute | solution.py:457
  30.6 12.8 %collective-permute-start.8 = (bf16[3,128,128]{2,1,0:T(8,128)(2,1)S(1)}, bf16[3,128,128]{2,1,0:T(8,128)(2,1)S(1)}, u32[]{:S(2)}, u32[]{:S(2)}) collective-permute-start(bf16[3,128,128]{2,1,0:T(8,128)(2,1)S(1)} %get-tuple-element.66), channel_id=1, source_target_pairs={{0,8},{4,12},{8,0},{12,4},{1,9},{5,13},{9,1},{13,5},{2,10},{6,14},... | collective-permute-start | bytes 294920 | tf_op jit(solution)/shard_map/ppermute | solution.py:457
  30.7 14.6 %collective-permute-start.7 = (bf16[3,128,128]{2,1,0:T(8,128)(2,1)S(1)}, bf16[3,128,128]{2,1,0:T(8,128)(2,1)S(1)}, u32[]{:S(2)}, u32[]{:S(2)}) collective-permute-start(bf16[3,128,128]{2,1,0:T(8,128)(2,1)S(1)} %get-tuple-element.63), channel_id=1, source_target_pairs={{0,8},{4,12},{8,0},{12,4},{1,9},{5,13},{9,1},{13,5},{2,10},{6,14},... | collective-permute-start | bytes 294920 | tf_op jit(solution)/shard_map/ppermute | solution.py:457

commit v8 on v6

v8 whole, which is shorter than its diff:
```python
import functools

import jax
import jax.numpy as jnp
from jax import lax
from jax.experimental import pallas as pl
from jax.experimental.pallas import tpu as pltpu
from jax.sharding import PartitionSpec as P

GROUP_CH = 16
STRETCH = 128
WIN = 4
SENT = WIN - 1
LANES = 128
BLOCKS = LANES // GROUP_CH
SPAN = 2 * STRETCH
VMEM_LIMIT = 16 * 1024 * 1024

SMEM_SPEC = pl.BlockSpec(memory_space=pltpu.SMEM)
ANY_SPEC = pl.BlockSpec(memory_space=pl.ANY)
HBM_SPEC = pl.BlockSpec(memory_space=pltpu.HBM)
VMEM_SPEC = pl.BlockSpec(memory_space=pltpu.VMEM)
NT = (((1,), (1,)), ((), ()))


def params():
    return pltpu.CompilerParams(vmem_limit_bytes=VMEM_LIMIT)


def steps_of(size):
    return sorted(range(size), key=lambda step: (min(step, size - step), step))


def partner(me, step, size):
    return lax.rem(me + step, size)


def sender(me, step, size):
    return lax.rem(me + size - step, size)


PLACE = SENT
MANY = 2 * SENT
WINDOWS = MANY + 1
SLOTS = 2


def product(key, value, start, columns):
    rows = pl.ds(start, STRETCH)
    rows_k = key[rows, columns].astype(jnp.float32)
    rows_v = value[rows, columns].astype(jnp.float32)
    return (rows_k * rows_v).astype(jnp.bfloat16).T


def gate_kernel(size, parts, sources_in, owner_in, key_in, value_in, filters_in, *refs):
    sends = refs[:parts]
    extra, meta, sources, owner, key, value, filters, sems = refs[parts:]
    stretch_count = owner.shape[0]
    channels = key.shape[1]
    width = channels // parts
    me = lax.axis_index("seq")
    copies = [
        pltpu.make_async_copy(sources_in, sources, sems.at[0]),
        pltpu.make_async_copy(owner_in, owner, sems.at[1]),
        pltpu.make_async_copy(key_in, key, sems.at[2]),
        pltpu.make_async_copy(value_in, value, sems.at[3]),
        pltpu.make_async_copy(filters_in, filters, sems.at[4]),
    ]
    for copy in copies:
        copy.start()

    for copy in copies[:2]:
        copy.wait()

    def target(k, slot):
        mine = owner[k] == me

        @pl.when(mine)
        def _():
            for w in range(WIN):
                lag_block = jnp.maximum(k - sources[w], -1)
                meta[WINDOWS + slot * WIN + w] = (stretch_count - 1 - lag_block) * STRETCH

        return slot + jnp.where(mine, 1, 0)

    lax.fori_loop(0, stretch_count, target, 0)
    for copy in copies[2:]:
        copy.wait()
    holders = [owner[sources[w]] for w in range(SENT)]
    many = 0
    for w, holder in enumerate(holders):
        place = sum([jnp.where(other == holder, 1, 0) for other in holders[:w]], 0)
        meta[w] = holder
        meta[PLACE + w] = place
        many = many + jnp.where(place >= SLOTS, 1, 0)

        @pl.when(holder == me)
        def _(w=w, holder=holder, place=place):
            def count(k, total):
                return total + jnp.where(owner[k] == holder, 1, 0)

            slot = lax.fori_loop(0, sources[w], count, 0)
            first = pl.multiple_of(slot * STRETCH, STRETCH)
            for step in range(parts):
                part = partner(me, step, size) if parts > 1 else 0
                base = part * width

                def fill(target, offset, base=base):
                    for start in range(0, width, LANES):
                        columns = pl.ds(pl.multiple_of(base + start, LANES), LANES)
                        target[pl.ds(offset + start, LANES), :] = product(key, value, first, columns)

                if w < SLOTS:
                    fill(sends[step], pl.multiple_of(place * width, LANES))
                else:

                    @pl.when(place < SLOTS)
                    def _(step=step, fill=fill):
                        fill(sends[step], pl.multiple_of(place * width, LANES))

                    @pl.when(place >= SLOTS)
                    def _(step=step, fill=fill):
                        fill(extra.at[step], 0)

    meta[MANY] = many
    group_count = filters.shape[0]
    for send in sends:
        rows = (send.shape[0] - SLOTS * width) * LANES // filters.shape[1]
        groups = pl.ds(0, rows)
        if 0 < rows < group_count:
            groups = pl.ds(pl.multiple_of(lax.axis_index("rep") * rows, rows), rows)
        for tile in range(filters.shape[1] // LANES if rows else 0):
            send[pl.ds(SLOTS * width + tile * rows, rows), :] = filters[
                groups, pl.ds(tile * LANES, LANES)
            ]


def gate(size, filter_rows, sources, owner, key_proj, value_proj, filters):
    row_count, channels = key_proj.shape
    slots = row_count // STRETCH
    parts = len(filter_rows)
    width = channels // parts
    operands = [
        pltpu.with_memory_space_constraint(operand, pltpu.HBM)
        for operand in (sources, owner, key_proj, value_proj, filters)
    ]
    *sends, extra, meta = pl.pallas_call(
        functools.partial(gate_kernel, size, parts),
        in_specs=[HBM_SPEC] * 5,
        out_specs=[VMEM_SPEC] * (parts + 1) + [SMEM_SPEC],
        out_shape=[
            jax.ShapeDtypeStruct((SLOTS * width + rows, LANES), jnp.bfloat16) for rows in filter_rows
        ]
        + [
            jax.ShapeDtypeStruct((parts, width, LANES), jnp.bfloat16),
            jax.ShapeDtypeStruct((WINDOWS + slots * WIN,), jnp.int32),
        ],
        scratch_shapes=[
            pltpu.SMEM(sources.shape, jnp.int32),
            pltpu.SMEM(owner.shape, jnp.int32),
            pltpu.VMEM(key_proj.shape, key_proj.dtype),
            pltpu.VMEM(value_proj.shape, value_proj.dtype),
            pltpu.VMEM(filters.shape, filters.dtype),
            pltpu.SemaphoreType.DMA((5,)),
        ],
        compiler_params=params(),
        name="gate",
    )(*operands)
    return sends, extra, meta


def merge_kernel(size, width, meta, *refs):
    received, extras, out = refs[:size], refs[size:-1], refs[-1]
    me = lax.axis_index("seq")

    for w in range(SENT):
        place = meta[PLACE + w]
        rows = pl.ds(pl.multiple_of(jnp.minimum(place, SLOTS - 1) * width, LANES), width)
        for block, step in zip(received, steps_of(size)):

            @pl.when(sender(me, step, size) == meta[w])
            def _(w=w, block=block, rows=rows):
                out[w] = block[rows, :]

    for w in range(SLOTS, SENT):
        for step, extra in enumerate(extras):

            @pl.when((sender(me, step, size) == meta[w]) & (meta[PLACE + w] >= SLOTS))
            def _(w=w, extra=extra):
                out[w] = extra[...]


def merge(size, width, meta, received, extras=()):
    return pl.pallas_call(
        functools.partial(merge_kernel, size, width),
        in_specs=[SMEM_SPEC] + [VMEM_SPEC] * (size + len(extras)),
        out_specs=VMEM_SPEC,
        out_shape=jax.ShapeDtypeStruct((SENT, width, LANES), received[0].dtype),
        compiler_params=params(),
        name="merge",
    )(meta, *received, *extras)


def pick_kernel(first, *refs):
    received, out = refs[:-1], refs[-1]
    for index, block in enumerate(received):
        out[index] = block[pl.ds(first, out.shape[1]), :]


def pick(first, received):
    rows = received[0].shape[0] - first
    return pl.pallas_call(
        functools.partial(pick_kernel, first),
        in_specs=[VMEM_SPEC] * len(received),
        out_specs=VMEM_SPEC,
        out_shape=jax.ShapeDtypeStruct((len(received), rows, LANES), received[0].dtype),
        compiler_params=params(),
        name="pick",
    )(*received)


def lag_tiles(size, first, filters):
    if len(filters) == 1:
        blocks = filters[0]
        group_count = blocks.shape[1] // first
        for shard in range(size):
            for tile in range(first):
                rows = pl.ds(tile * group_count, group_count)
                yield pl.ds(0, group_count), shard * first + tile, blocks[shard, rows, :]
        return
    own, far, mine, other = filters
    me, rep = lax.axis_index("seq"), lax.axis_index("rep")
    group_count = own.shape[0]
    tiles = own.shape[1] // LANES
    half = group_count // 2
    for tile in range(tiles):
        whole = pl.ds(0, group_count)
        yield whole, me * tiles + tile, own[:, pl.ds(tile * LANES, LANES)]
        rows = pl.ds(first + tile * group_count, group_count)
        yield whole, sender(me, 2, size) * tiles + tile, far[rows, :]
        for index, step in enumerate((1, size - 1)):
            number = sender(me, step, size) * tiles + tile
            for place, halves in ((rep, mine), (1 - rep, other)):
                groups = pl.ds(pl.multiple_of(place * half, half), half)
                yield groups, number, halves[index, pl.ds(tile * half, half), :]


def build_shifted(size, first, filters, reverse, shifted):
    group_count, padded = reverse.shape
    lag_count = padded - SPAN
    row = lax.broadcasted_iota(jnp.int32, (LANES, LANES), 0)
    column = lax.broadcasted_iota(jnp.int32, (LANES, LANES), 1)
    flip = jnp.where(row + column == LANES - 1, 1.0, 0.0).astype(jnp.bfloat16)
    for groups, number, values in lag_tiles(size, first, filters):
        start = lag_count - LANES - number * LANES
        if not isinstance(start, int):
            start = pl.multiple_of(start, LANES)
        reverse[groups, pl.ds(start, LANES)] = jnp.dot(
            values, flip, preferred_element_type=jnp.float32
        )
    reverse[:, pl.ds(lag_count, SPAN)] = jnp.zeros((group_count, SPAN), jnp.float32)
    inside = (
        lax.broadcasted_iota(jnp.int32, (GROUP_CH, LANES), 1)
        > lax.broadcasted_iota(jnp.int32, (GROUP_CH, LANES), 0)
    )

    @pl.loop(0, group_count // BLOCKS)
    def _(block):
        tile_rows = pl.ds(pl.multiple_of(block * BLOCKS, BLOCKS), BLOCKS)
        before = [jnp.zeros((GROUP_CH, LANES), jnp.float32)] * BLOCKS
        for start in range(0, padded, LANES):
            tile = reverse[tile_rows, pl.ds(start, LANES)]
            for g in range(BLOCKS):
                spread = jnp.broadcast_to(tile[g : g + 1, :], (GROUP_CH, LANES))
                rolled = pltpu.roll(spread, 1, 1, stride=1, stride_axis=0)
                shifted[block * BLOCKS + g, :, pl.ds(start, LANES)] = jnp.where(
                    inside, rolled, before[g]
                ).astype(jnp.bfloat16)
                before[g] = rolled


def spread_rows(tile, spans, base):
    lane = lax.broadcasted_iota(jnp.int16, tile.shape, 1)
    zero = jnp.zeros(tile.shape, tile.dtype)
    for i1 in range(BLOCKS):
        shift = GROUP_CH * i1
        if i1 == 0:
            low, high = zero, tile
        else:
            moved = pltpu.roll(tile, LANES - shift, 1)
            early = lane < LANES - shift
            low, high = jnp.where(early, zero, moved), jnp.where(early, moved, zero)
        rows = pl.ds(shift, GROUP_CH)
        for g in range(BLOCKS):
            part = slice(g * GROUP_CH, (g + 1) * GROUP_CH)
            spans[g, rows, pl.ds(base, LANES)] = low[part]
            spans[g, rows, pl.ds(base + LANES, LANES)] = high[part]


def window(meta, shifted, group, slot, w):
    start = pl.multiple_of(meta[WINDOWS + slot * WIN + w], STRETCH)
    return shifted[group, :, pl.ds(start, SPAN)]


def filter_rows(meta, shifted, group, slots):
    return jnp.concatenate(
        [
            jnp.concatenate([window(meta, shifted, group, slot, w) for w in range(SENT)], axis=1)
            for slot in range(slots)
        ],
        axis=0,
    )


def rows_of(results, block):
    part = slice(block * GROUP_CH, (block + 1) * GROUP_CH)
    return jnp.concatenate([result[part] for result in results], axis=0).T


def last_rows_kernel(key, value, out):
    for start in range(0, out.shape[0], LANES):
        out[pl.ds(start, LANES), :] = product(key, value, 0, pl.ds(start, LANES))


def last_rows(key_proj, value_proj):
    row_count, channels = key_proj.shape
    block = pl.BlockSpec((STRETCH, channels), lambda i: (row_count // STRETCH - 1, 0))
    operands = [pltpu.with_memory_space_constraint(x, pltpu.HBM) for x in (key_proj, value_proj)]
    return pl.pallas_call(
        last_rows_kernel,
        grid=(1,),
        in_specs=[block, block],
        out_specs=pl.BlockSpec((channels, STRETCH), lambda i: (0, 0)),
        out_shape=jax.ShapeDtypeStruct((channels, STRETCH), jnp.bfloat16),
        compiler_params=params(),
        name="last_rows",
    )(*operands)


def last_term(slots, meta, last, shifted, term, spans):
    for start in range(0, last.shape[0], LANES):
        held = spans.at[start // LANES % 2]
        spread_rows(last[pl.ds(start, LANES), :], held, 0)
        results = [
            lax.dot_general(
                held[g],
                window(meta, shifted, start // GROUP_CH + g, slots - 1, SENT),
                NT,
                preferred_element_type=jnp.float32,
            )
            for g in range(BLOCKS)
        ]
        for m in range(BLOCKS):
            term[pl.ds(m * GROUP_CH, GROUP_CH), pl.ds(start, LANES)] = rows_of(results, m)


def spread_part(pieces, start, spans):
    for w in range(SENT):
        spread_rows(pieces[w, pl.ds(start, LANES), :], spans, w * SPAN)


def conv_part(filter_rows_of, base, start, term, query, out, result, spans, sem):
    slots = query.shape[0] // STRETCH
    columns = pl.ds(pl.multiple_of(base + start, LANES), LANES)
    results = [
        lax.dot_general(
            spans[g],
            filter_rows_of(start // GROUP_CH + g),
            NT,
            preferred_element_type=jnp.float32,
        )
        for g in range(BLOCKS)
    ]
    for m in range(BLOCKS):
        rows = rows_of(results, m)
        for slot in range(slots):
            place = pl.ds(slot * STRETCH + m * GROUP_CH, GROUP_CH)
            tile = rows[slot * GROUP_CH : (slot + 1) * GROUP_CH]
            if slot == slots - 1:
                tile = tile + term[pl.ds(m * GROUP_CH, GROUP_CH), columns]
            gates = query[place, columns].astype(jnp.float32)
            result[place, :] = (gates * tile).astype(jnp.bfloat16)
    store = pltpu.make_async_copy(result, out.at[:, columns], sem)
    store.start()
    return store


def part_base(step, size, width):
    me = lax.axis_index("seq")
    return pl.multiple_of(sender(me, step, size) * width, width)


def scratch(count, row_count):
    return [
        pltpu.VMEM((count, row_count, LANES), jnp.bfloat16),
        pltpu.VMEM((count, BLOCKS, LANES, SENT * SPAN), jnp.bfloat16),
        pltpu.SemaphoreType.DMA((count + 1,)),
    ]


def open_kernel(size, first, meta_in, last, pieces, query, *refs):
    filters = refs[:-9]
    shifted, term, out, reverse, meta, last_spans, result, spans, sems = refs[-9:]
    slots = query.shape[0] // STRETCH
    width = pieces.shape[1]
    scalars = pltpu.make_async_copy(meta_in, meta, sems.at[width // LANES])
    scalars.start()
    build_shifted(size, first, filters, reverse, shifted)
    scalars.wait()
    last_term(slots, meta, last, shifted, term, last_spans)
    base = part_base(0, out.shape[1] // width, width)
    stores = []
    for index, start in enumerate(range(0, width, LANES)):
        spread_part(pieces, start, spans.at[index])
        stores.append(
            conv_part(
                lambda group: filter_rows(meta, shifted, base // GROUP_CH + group, slots),
                base,
                start,
                term,
                query,
                out,
                result.at[index],
                spans.at[index],
                sems.at[index],
            )
        )
    for store in stores:
        store.wait()


def open_conv(size, first, meta, last, pieces, query_proj, group_count, lag_count, filters):
    row_count, channels = query_proj.shape
    padded = lag_count + SPAN
    return pl.pallas_call(
        functools.partial(open_kernel, size, first),
        in_specs=[ANY_SPEC] + [VMEM_SPEC] * (3 + len(filters)),
        out_specs=[VMEM_SPEC, VMEM_SPEC, HBM_SPEC],
        out_shape=[
            jax.ShapeDtypeStruct((group_count, GROUP_CH, padded), jnp.bfloat16),
            jax.ShapeDtypeStruct((STRETCH, channels), jnp.float32),
            jax.ShapeDtypeStruct((row_count, channels), jnp.bfloat16),
        ],
        scratch_shapes=[
            pltpu.VMEM((group_count, padded), jnp.float32),
            pltpu.SMEM(meta.shape, jnp.int32),
            pltpu.VMEM((2, BLOCKS, LANES, SPAN), jnp.bfloat16),
            *scratch(pieces.shape[1] // LANES, row_count),
        ],
        compiler_params=params(),
        name="open_conv",
    )(meta, last, pieces, query_proj, *filters)


def near_kernel(size, steps, next_step, meta_in, shifted, term, query, before, *refs):
    parts = refs[: len(steps)]
    out, ready, meta, result, spans, sems = refs[len(steps) :]
    slots = query.shape[0] // STRETCH
    width = parts[0].shape[1]
    places = [(index, start) for index in range(len(steps)) for start in range(0, width, LANES)]
    scalars = pltpu.make_async_copy(meta_in, meta, sems.at[len(places)])
    scalars.start()
    for number, (index, start) in enumerate(places[: len(places) // 2]):
        spread_part(parts[index], start, spans.at[number])
    scalars.wait()
    stores = []
    for number, (index, start) in enumerate(places):
        if number >= len(places) // 2:
            spread_part(parts[index], start, spans.at[number])
        base = part_base(steps[index], size, width)
        stores.append(
            conv_part(
                lambda group, base=base: filter_rows(meta, shifted, base // GROUP_CH + group, slots),
                base,
                start,
                term,
                query,
                out,
                result.at[number],
                spans.at[number],
                sems.at[number],
            )
        )
    base = part_base(next_step, size, width)
    for group in range(width // GROUP_CH):
        ready[group] = filter_rows(meta, shifted, base // GROUP_CH + group, slots)
    for store in stores:
        store.wait()


def near_conv(size, steps, next_step, meta, parts, shifted, term, query_proj, before):
    row_count, channels = query_proj.shape
    width = channels // size
    slots = row_count // STRETCH
    return pl.pallas_call(
        functools.partial(near_kernel, size, steps, next_step),
        in_specs=[ANY_SPEC] + [VMEM_SPEC] * 3 + [HBM_SPEC] + [VMEM_SPEC] * len(parts),
        out_specs=[HBM_SPEC, VMEM_SPEC],
        out_shape=[
            jax.ShapeDtypeStruct((row_count, channels), jnp.bfloat16),
            jax.ShapeDtypeStruct((width // GROUP_CH, slots * GROUP_CH, SENT * SPAN), jnp.bfloat16),
        ],
        input_output_aliases={4: 0},
        scratch_shapes=[
            pltpu.SMEM(meta.shape, jnp.int32),
            *scratch(len(parts) * width // LANES, row_count),
        ],
        compiler_params=params(),
        name="near_conv",
    )(meta, shifted, term, query_proj, before, *parts)


def far_kernel(size, step, pieces, ready, term, query, before, out, result, spans, sems):
    width = pieces.shape[1]
    base = part_base(step, size, width)
    stores = []
    for index, start in enumerate(range(0, width, LANES)):
        spread_part(pieces, start, spans.at[index])
        stores.append(
            conv_part(
                lambda group: ready[group],
                base,
                start,
                term,
                query,
                out,
                result.at[index],
                spans.at[index],
                sems.at[index],
            )
        )
    for store in stores:
        store.wait()


def far_conv(size, step, pieces, ready, term, query_proj, before):
    row_count, channels = query_proj.shape
    return pl.pallas_call(
        functools.partial(far_kernel, size, step),
        in_specs=[VMEM_SPEC] * 4 + [HBM_SPEC],
        out_specs=HBM_SPEC,
        out_shape=jax.ShapeDtypeStruct((row_count, channels), jnp.bfloat16),
        input_output_aliases={4: 0},
        scratch_shapes=scratch(pieces.shape[1] // LANES, row_count),
        compiler_params=params(),
        name="far_conv",
    )(pieces, ready, term, query_proj, before)


def shards(size, reps, key_proj, value_proj, query_proj, filters, sources, owner):
    row_count, channels = key_proj.shape
    group_count, part = filters.shape
    lag_count = size * part
    tiles = part // LANES
    by_parts = (size, reps) == (4, 2) and channels % (size * LANES) == 0
    half = group_count // 2 * tiles
    filter_rows = [0, half, 2 * half, half] if by_parts else [2 * half]
    parts = len(filter_rows)
    width = channels // parts
    sends, extra, meta = gate(size, filter_rows, sources, owner, key_proj, value_proj, filters)
    last = last_rows(key_proj, value_proj)
    first = SLOTS * width
    if not by_parts:
        blocks = lax.all_gather(sends[0][first:], "seq")
        held = jnp.concatenate([sends[0][:first].reshape(SLOTS, width, LANES), extra])
        mine = (meta[:SENT] == lax.axis_index("seq"))[:, None, None]
        pieces = lax.psum(jnp.where(mine, held[meta[PLACE:MANY]], jnp.zeros_like(held)), "seq")
        return open_conv(
            size, tiles, meta, last, pieces, query_proj, group_count, lag_count, [blocks]
        )[2]

    def shift(value, step):
        return lax.ppermute(value, "seq", [(z, (z + step) % size) for z in range(size)])

    up, down, far = (shift(sends[step], step) for step in (1, size - 1, 2))
    mine = pick(first, [up, down])
    other = lax.ppermute(mine, "rep", [(0, 1), (1, 0)])
    last, other, far = lax.optimization_barrier((last, other, far))
    received = [sends[0], up, down, far]

    def merge_more(meta, received, extra):
        more = [extra[0]] + [shift(extra[step], step) for step in range(1, size)]
        return merge(size, width, meta, received, more)

    def merge_plain(meta, received, extra):
        return merge(size, width, meta, received)

    merged = lax.cond(meta[MANY] > 0, merge_more, merge_plain, meta, received, extra)
    up, down, far_part = shift(merged, 1), shift(merged, size - 1), shift(merged, 2)
    shifted, term, out = open_conv(
        size,
        first,
        meta,
        last,
        merged,
        query_proj,
        group_count,
        lag_count,
        [filters, far, mine, other],
    )
    out, ready = near_conv(
        size, (1, size - 1), 2, meta, [up, down], shifted, term, query_proj, out
    )
    return far_conv(size, 2, far_part, ready, term, query_proj, out)


def solution(mesh):
    return jax.shard_map(
        functools.partial(shards, mesh.shape["seq"], mesh.shape["rep"]),
        mesh=mesh,
        in_specs=(
            P(("rep", "seq"), "ch"),
            P(("rep", "seq"), "ch"),
            P(("rep", "seq"), "ch"),
            P("ch", "seq"),
            P("rep"),
            P("rep"),
        ),
        out_specs=P(("rep", "seq"), "ch"),
        check_vma=False,
    )
```

time: 47.2 us -> 45 us (0.953)
  Pallas kernels: 18.5 us -> 15.1 us
  starting transfers between devices: 9.86 us -> 12.5 us
  waiting for transfers between devices: 17.4 us -> 16.2 us
    pallas_call x6 -> x4, Pallas kernels: 14.2 us -> 10.8 us  [the longest x1 5.51 us: open_conv(): pl.pallas_call(functools.partial(open_kernel, size, first), in_specs=[ANY...]
    ppermute x6, starting transfers between devices: 9.86 us -> 11.3 us  [shift(): lax.ppermute(value, 'seq', [(z, (z + step) % size) for z in range(size)])]
    ppermute x0 -> x1, starting transfers between devices: none -> 1.23 us  [shards(): other = lax.ppermute(mine, 'rep', [(0, 1), (1, 0)])]
    ppermute x6, waiting for transfers between devices: 17.4 us -> 16.2 us  [shift(): lax.ppermute(value, 'seq', [(z, (z + step) % size) for z in range(size)])]
  transfers between devices with their start and end apart: 6 -> 7, of which waited for: 5 -> 6; matrix products, arithmetic and copies ran while one was open for 1% -> 1% of each run, Pallas kernels for 28% -> 22%
where the time goes in v8:
time: 45 us; the launch traced here: 45.1 us
  waiting for transfers between devices  16.2 us (36%)
  Pallas kernels  15.1 us (34%)
  starting transfers between devices  12.5 us (28%)
  between operations  0.7 us (2%)
  local copies, waits for them, and re-layouts  0.59 us (1%)
    ppermute x6, waiting for transfers between devices, shift(): lax.ppermute(value, 'seq', [(z, (z + step) % size) for z in range(size)])  16.2 us
    ppermute x6, starting transfers between devices, shift(): lax.ppermute(value, 'seq', [(z, (z + step) % size) for z in range(size)])  11.3 us
    pallas_call x1, Pallas kernels, open_conv(): pl.pallas_call(functools.partial(open_kernel, size, first), in_specs=[ANY...  5.51 us
    pallas_call x1, Pallas kernels, near_conv(): pl.pallas_call(functools.partial(near_kernel, size, steps, next_step), in...  3.37 us
    pallas_call x1, Pallas kernels, gate(): pl.pallas_call(functools.partial(gate_kernel, size, parts), in_specs=[HBM...  2.49 us
    pallas_call x1, Pallas kernels, far_conv(): pl.pallas_call(functools.partial(far_kernel, size, step), in_specs=[VMEM_...  1.89 us
    ppermute x1, starting transfers between devices, shards(): other = lax.ppermute(mine, 'rep', [(0, 1), (1, 0)])  1.23 us
    pallas_call x1, Pallas kernels, last_rows(): pl.pallas_call(last_rows_kernel, grid=(1,), in_specs=[block, block], out_...  1.16 us
  transfers between devices with their start and end apart: 7, of which 6 were waited for; matrix products, arithmetic and copies ran while one was open for 1% of the time, Pallas kernels for 22%

profile of v8, /device:TPU:0, one launch (start us, length us, event | category | flops | bytes accessed | tf_op | source)
XLA Modules:
  0.0 45.1 jit_solution(9881264574135942737)
XLA Ops:
  0.0 2.5 %gate.1 = (bf16[512,128]{1,0:T(8,128)(2,1)S(1)}, bf16[640,128]{1,0:T(8,128)(2,1)S(1)}, bf16[768,128]{1,0:T(8,128)(2,1)S(1)}, bf16[640,128]{1,0:T(8,128)(2,1)S(1)...) custom-call(s32[4]{0:T(128)} %sources_in.1, s32[16]{0:T(128)} %owner_in.1, bf16[512,1024]{1,0:T(8,128)(2,1)} %key.1, ...), custom_call_target="tpu_custom_call" | custom-call | tf_op jit(solution)/shard_map/gate/pallas_call | solution.py:147
  2.5 2.9 %collective-permute-start.3 = (bf16[640,128]{1,0:T(8,128)(2,1)S(1)}, bf16[640,128]{1,0:T(8,128)(2,1)S(1)}, u32[]{:S(2)}, u32[]{:S(2)}) collective-permute-start(bf16[640,128]{1,0:T(8,128)(2,1)S(1)} %get-tuple-element.57), channel_id=1, source_target_pairs={{0,4},{4,8},{8,12},{12,0},{1,5},{5,9},{9,13},{13,1},{2,6},{6,10},{... | collective-permute-start | bytes 491528 | tf_op jit(solution)/shard_map/ppermute | solution.py:573
  5.4 2.1 %collective-permute-start.4 = (bf16[640,128]{1,0:T(8,128)(2,1)S(1)}, bf16[640,128]{1,0:T(8,128)(2,1)S(1)}, u32[]{:S(2)}, u32[]{:S(2)}) collective-permute-start(bf16[640,128]{1,0:T(8,128)(2,1)S(1)} %get-tuple-element.58), channel_id=1, source_target_pairs={{0,12},{4,0},{8,4},{12,8},{1,13},{5,1},{9,5},{13,9},{2,14},{6,2},{... | collective-permute-start | bytes 491528 | tf_op jit(solution)/shard_map/ppermute | solution.py:573
  7.5 1.6 %collective-permute-start.6 = (bf16[768,128]{1,0:T(8,128)(2,1)S(1)}, bf16[768,128]{1,0:T(8,128)(2,1)S(1)}, u32[]{:S(2)}, u32[]{:S(2)}) collective-permute-start(bf16[768,128]{1,0:T(8,128)(2,1)S(1)} %get-tuple-element.59), channel_id=1, source_target_pairs={{0,8},{4,12},{8,0},{12,4},{1,9},{5,13},{9,1},{13,5},{2,10},{6,14},... | collective-permute-start | bytes 589832 | tf_op jit(solution)/shard_map/ppermute | solution.py:573
  9.1 3.4 %collective-permute-done.3.refs_0_ = bf16[640,128]{1,0:T(8,128)(2,1)S(1)} collective-permute-done((bf16[640,128]{1,0:T(8,128)(2,1)S(1)}, bf16[640,128]{1,0:T(8,128)(2,1)S(1)}, u32[]{:S(2)}, u32[]{:S(2)}) %collective-permute-start.3) | collective-permute-done | bytes 163872 | tf_op jit(solution)/shard_map/ppermute | solution.py:573
  12.5 2.5 %collective-permute-done.4.refs_1_ = bf16[640,128]{1,0:T(8,128)(2,1)S(1)} collective-permute-done((bf16[640,128]{1,0:T(8,128)(2,1)S(1)}, bf16[640,128]{1,0:T(8,128)(2,1)S(1)}, u32[]{:S(2)}, u32[]{:S(2)}) %collective-permute-start.4) | collective-permute-done | bytes 163872 | tf_op jit(solution)/shard_map/ppermute | solution.py:573
  15.0 1.2 %collective-permute-start.5 = (bf16[2,128,128]{2,1,0:T(8,128)(2,1)S(1)}, bf16[2,128,128]{2,1,0:T(8,128)(2,1)S(1)}, u32[]{:S(2)}, u32[]{:S(2)}) collective-permute-start(bf16[2,128,128]{2,1,0:T(8,128)(2,1)S(1)} %pick.1.refs_2_), channel_id=1, source_target_pairs={{0,16},{16,0},{1,17},{17,1},{2,18},{18,2},{3,19},{19,3},{4,20},{20... | collective-permute-start | bytes 196616 | tf_op jit(solution)/shard_map/ppermute | solution.py:577
  16.3 1.2 %last_rows.1.last = bf16[1024,128]{1,0:T(8,128)(2,1)S(1)} custom-call(bf16[512,1024]{1,0:T(8,128)(2,1)} %key.1, bf16[512,1024]{1,0:T(8,128)(2,1)} %value.1), custom_call_target="tpu_custom_call" | custom-call | tf_op jit(solution)/shard_map/last_rows/pallas_call | solution.py:329
  17.4 0.6 %slice.15 = s32[1]{0:T(128)} slice(s32[23]{0:T(128)S(1)} %get-tuple-element.55.meta_in), slice={[6:7]} | slice | bytes 8 | tf_op jit(solution)/shard_map/slice | solution.py:588
  18.7 4.9 %collective-permute-done.6.refs_1_ = bf16[768,128]{1,0:T(8,128)(2,1)S(1)} collective-permute-done((bf16[768,128]{1,0:T(8,128)(2,1)S(1)}, bf16[768,128]{1,0:T(8,128)(2,1)S(1)}, u32[]{:S(2)}, u32[]{:S(2)}) %collective-permute-start.6) | collective-permute-done | bytes 196640 | tf_op jit(solution)/shard_map/ppermute | solution.py:573
  23.6 0.0 collective-permute-done.5.refs_3_
  23.6 0.7 %conditional.1 = (bf16[3,256,128]{2,1,0:T(8,128)(2,1)S(1)}) conditional(s32[]{:T(128)} %bitcast.4, (s32[23]{0:T(128)S(1)}, bf16[512,128]{1,0:T(8,128)(2,1)S(1)}, bf16[640,128]{1,0:T(8,128)(2,1)S(1)}, bf16[640,128]{1,0:T(8,128)(2,1)S(1)}, bf16[768,128]{1,0:T(8,128)(2,1)S(1)}) %tuple.13, (bf16[4,256,128]{2,1,0:T(8,128)(2,1)S(1)}, s32[23]{0:T(128)S(1)}, ...), branch_computations={%region_0.0_spmd, %region_1.0_spmd} | conditional | bytes 1310848 | solution.py:588
  23.6 0.7 %merge.2 = bf16[3,256,128]{2,1,0:T(8,128)(2,1)S(1)} custom-call(s32[23]{0:T(128)S(1)} %get-tuple-element.30.meta, bf16[512,128]{1,0:T(8,128)(2,1)S(1)} %get-tuple-element.31.refs_0_, bf16[640,128]{1,0:T(8,128)(2,1)S(1)} %get-tuple-element.32.refs_1_, bf16[640,128]{1,0:T(8,128)(2,1)S(1)} %get-tuple-element.33.refs_2_, ...), custom_call_target="tpu_custom_call" | custom-call | tf_op jit(solution)/shard_map/cond/branch_0_fun/merge/pallas_call | solution.py:194
  24.3 2.3 %collective-permute-start.9 = (bf16[3,256,128]{2,1,0:T(8,128)(2,1)S(1)}, bf16[3,256,128]{2,1,0:T(8,128)(2,1)S(1)}, u32[]{:S(2)}, u32[]{:S(2)}) collective-permute-start(bf16[3,256,128]{2,1,0:T(8,128)(2,1)S(1)} %get-tuple-element.73.pieces), channel_id=1, source_target_pairs={{0,12},{4,0},{8,4},{12,8},{1,13},{5,1},{9,5},{13,9},{2,14},{6,2},{... | collective-permute-start | bytes 589832 | tf_op jit(solution)/shard_map/ppermute | solution.py:573
  26.5 0.0 collective-permute-start.8
  26.6 2.4 %collective-permute-start.7 = (bf16[3,256,128]{2,1,0:T(8,128)(2,1)S(1)}, bf16[3,256,128]{2,1,0:T(8,128)(2,1)S(1)}, u32[]{:S(2)}, u32[]{:S(2)}) collective-permute-start(bf16[3,256,128]{2,1,0:T(8,128)(2,1)S(1)} %get-tuple-element.73.pieces), channel_id=1, source_target_pairs={{0,8},{4,12},{8,0},{12,4},{1,9},{5,13},{9,1},{13,5},{2,10},{6,14},... | collective-permute-start | bytes 589832 | tf_op jit(solution)/shard_map/ppermute | solution.py:573
  29.0 0.0 copy-done.1
  29.0 0.0 copy-done
  29.0 5.5 %open_conv.1 = (bf16[64,16,2304]{2,1,0:T(8,128)(2,1)S(1)}, f32[128,1024]{1,0:T(8,128)S(1)}, bf16[512,1024]{1,0:T(8,128)(2,1)}) custom-call(s32[23]{0:T(128)S(1)} %get-tuple-element.55.meta_in, bf16[1024,128]{1,0:T(8,128)(2,1)S(1)} %last_rows.1.last, bf16[3,256,128]{2,1,0:T(8,128)(2,1)S(1)} %get-tuple-element.73.pieces, bf16[512,1024]{1,0:T(8,128)(2,1)S(1)} %copy-done, ...), custom_call_target="tpu_custom_call" | custom-call | tf_op jit(solution)/shard_map/open_conv/pallas_call | solution.py:435
  34.5 0.3 collective-permute-done.9.refs_1_
  34.8 3.2 %collective-permute-done.8.refs_0_ = bf16[3,256,128]{2,1,0:T(8,128)(2,1)S(1)} collective-permute-done((bf16[3,256,128]{2,1,0:T(8,128)(2,1)S(1)}, bf16[3,256,128]{2,1,0:T(8,128)(2,1)S(1)}, u32[]{:S(2)}, u32[]{:S(2)}) %collective-permute-start.8) | collective-permute-done | bytes 196640 | tf_op jit(solution)/shard_map/ppermute | solution.py:573
  38.1 3.4 %near_conv.1 = (bf16[512,1024]{1,0:T(8,128)(2,1)}, bf16[16,64,768]{2,1,0:T(8,128)(2,1)S(1)}) custom-call(s32[23]{0:T(128)S(1)} %get-tuple-element.55.meta_in, bf16[64,16,2304]{2,1,0:T(8,128)(2,1)S(1)} %get-tuple-element.64.shifted, f32[128,1024]{1,0:T(8,128)S(1)} %get-tuple-element.65.term, ...), custom_call_target="tpu_custom_call", output_to_operand_aliasing={{0}: (4, {})} | custom-call | tf_op jit(solution)/shard_map/near_conv/pallas_call | solution.py:495
  41.4 1.8 %collective-permute-done.7.pieces = bf16[3,256,128]{2,1,0:T(8,128)(2,1)S(1)} collective-permute-done((bf16[3,256,128]{2,1,0:T(8,128)(2,1)S(1)}, bf16[3,256,128]{2,1,0:T(8,128)(2,1)S(1)}, u32[]{:S(2)}, u32[]{:S(2)}) %collective-permute-start.7) | collective-permute-done | bytes 196640 | tf_op jit(solution)/shard_map/ppermute | solution.py:573
  43.2 1.9 %far_conv.1 = bf16[512,1024]{1,0:T(8,128)(2,1)} custom-call(bf16[3,256,128]{2,1,0:T(8,128)(2,1)S(1)} %collective-permute-done.7.pieces, bf16[16,64,768]{2,1,0:T(8,128)(2,1)S(1)} %get-tuple-element.67.ready, f32[128,1024]{1,0:T(8,128)S(1)} %get-tuple-element.65.term, bf16[512,1024]{1,0:T(8,128)(2,1)S(1)} %copy-done, ...), custom_call_target="tpu_custom_call", output_to_operand_aliasing={{}: (4, {})} | custom-call | tf_op jit(solution)/shard_map/far_conv/pallas_call | solution.py:538
  (3 shorter events, 0.0 us)
Async XLA Ops:
  0.0 29.0 %copy-start.1 = (bf16[64,512]{1,0:T(8,128)(2,1)S(1)}, bf16[64,512]{1,0:T(8,128)(2,1)}, u32[]{:S(2)}) copy-start(bf16[64,512]{1,0:T(8,128)(2,1)} %refs_0_.1) | copy-start | bytes 196612
  0.0 29.0 %copy-start = (bf16[512,1024]{1,0:T(8,128)(2,1)S(1)}, bf16[512,1024]{1,0:T(8,128)(2,1)}, u32[]{:S(2)}) copy-start(bf16[512,1024]{1,0:T(8,128)(2,1)} %query.5) | copy-start | bytes 3145732
  2.5 10.0 %collective-permute-start.3 = (bf16[640,128]{1,0:T(8,128)(2,1)S(1)}, bf16[640,128]{1,0:T(8,128)(2,1)S(1)}, u32[]{:S(2)}, u32[]{:S(2)}) collective-permute-start(bf16[640,128]{1,0:T(8,128)(2,1)S(1)} %get-tuple-element.57), channel_id=1, source_target_pairs={{0,4},{4,8},{8,12},{12,0},{1,5},{5,9},{9,13},{13,1},{2,6},{6,10},{... | collective-permute-start | bytes 491528 | tf_op jit(solution)/shard_map/ppermute | solution.py:573
  5.4 9.7 %collective-permute-start.4 = (bf16[640,128]{1,0:T(8,128)(2,1)S(1)}, bf16[640,128]{1,0:T(8,128)(2,1)S(1)}, u32[]{:S(2)}, u32[]{:S(2)}) collective-permute-start(bf16[640,128]{1,0:T(8,128)(2,1)S(1)} %get-tuple-element.58), channel_id=1, source_target_pairs={{0,12},{4,0},{8,4},{12,8},{1,13},{5,1},{9,5},{13,9},{2,14},{6,2},{... | collective-permute-start | bytes 491528 | tf_op jit(solution)/shard_map/ppermute | solution.py:573
  7.5 16.1 %collective-permute-start.6 = (bf16[768,128]{1,0:T(8,128)(2,1)S(1)}, bf16[768,128]{1,0:T(8,128)(2,1)S(1)}, u32[]{:S(2)}, u32[]{:S(2)}) collective-permute-start(bf16[768,128]{1,0:T(8,128)(2,1)S(1)} %get-tuple-element.59), channel_id=1, source_target_pairs={{0,8},{4,12},{8,0},{12,4},{1,9},{5,13},{9,1},{13,5},{2,10},{6,14},... | collective-permute-start | bytes 589832 | tf_op jit(solution)/shard_map/ppermute | solution.py:573
  15.0 8.5 %collective-permute-start.5 = (bf16[2,128,128]{2,1,0:T(8,128)(2,1)S(1)}, bf16[2,128,128]{2,1,0:T(8,128)(2,1)S(1)}, u32[]{:S(2)}, u32[]{:S(2)}) collective-permute-start(bf16[2,128,128]{2,1,0:T(8,128)(2,1)S(1)} %pick.1.refs_2_), channel_id=1, source_target_pairs={{0,16},{16,0},{1,17},{17,1},{2,18},{18,2},{3,19},{19,3},{4,20},{20... | collective-permute-start | bytes 196616 | tf_op jit(solution)/shard_map/ppermute | solution.py:577
  24.3 10.6 %collective-permute-start.9 = (bf16[3,256,128]{2,1,0:T(8,128)(2,1)S(1)}, bf16[3,256,128]{2,1,0:T(8,128)(2,1)S(1)}, u32[]{:S(2)}, u32[]{:S(2)}) collective-permute-start(bf16[3,256,128]{2,1,0:T(8,128)(2,1)S(1)} %get-tuple-element.73.pieces), channel_id=1, source_target_pairs={{0,12},{4,0},{8,4},{12,8},{1,13},{5,1},{9,5},{13,9},{2,14},{6,2},{... | collective-permute-start | bytes 589832 | tf_op jit(solution)/shard_map/ppermute | solution.py:573
  26.5 11.5 %collective-permute-start.8 = (bf16[3,256,128]{2,1,0:T(8,128)(2,1)S(1)}, bf16[3,256,128]{2,1,0:T(8,128)(2,1)S(1)}, u32[]{:S(2)}, u32[]{:S(2)}) collective-permute-start(bf16[3,256,128]{2,1,0:T(8,128)(2,1)S(1)} %get-tuple-element.73.pieces), channel_id=1, source_target_pairs={{0,4},{4,8},{8,12},{12,0},{1,5},{5,9},{9,13},{13,1},{2,6},{6,10},{... | collective-permute-start | bytes 589832 | tf_op jit(solution)/shard_map/ppermute | solution.py:573
  26.6 16.7 %collective-permute-start.7 = (bf16[3,256,128]{2,1,0:T(8,128)(2,1)S(1)}, bf16[3,256,128]{2,1,0:T(8,128)(2,1)S(1)}, u32[]{:S(2)}, u32[]{:S(2)}) collective-permute-start(bf16[3,256,128]{2,1,0:T(8,128)(2,1)S(1)} %get-tuple-element.73.pieces), channel_id=1, source_target_pairs={{0,8},{4,12},{8,0},{12,4},{1,9},{5,13},{9,1},{13,5},{2,10},{6,14},... | collective-permute-start | bytes 589832 | tf_op jit(solution)/shard_map/ppermute | solution.py:573

commit v9 on v8

--- a/solution.py
+++ b/solution.py
@@ -236,8 +236,7 @@
     for tile in range(tiles):
         whole = pl.ds(0, group_count)
         yield whole, me * tiles + tile, own[:, pl.ds(tile * LANES, LANES)]
-        rows = pl.ds(first + tile * group_count, group_count)
-        yield whole, sender(me, 2, size) * tiles + tile, far[rows, :]
+        yield whole, sender(me, 2, size) * tiles + tile, far[:, pl.ds(tile * LANES, LANES)]
         for index, step in enumerate((1, size - 1)):
             number = sender(me, step, size) * tiles + tile
             for place, halves in ((rep, mine), (1 - rep, other)):
@@ -554,7 +553,7 @@
     tiles = part // LANES
     by_parts = (size, reps) == (4, 2) and channels % (size * LANES) == 0
     half = group_count // 2 * tiles
-    filter_rows = [0, half, 2 * half, half] if by_parts else [2 * half]
+    filter_rows = [0, half, 0, half] if by_parts else [2 * half]
     parts = len(filter_rows)
     width = channels // parts
     sends, extra, meta = gate(size, filter_rows, sources, owner, key_proj, value_proj, filters)
@@ -572,6 +571,8 @@
     def shift(value, step):
         return lax.ppermute(value, "seq", [(z, (z + step) % size) for z in range(size)])
 
+    far_filters = shift(filters, 2)
+    sends, far_filters = lax.optimization_barrier((sends, far_filters))
     up, down, far = (shift(sends[step], step) for step in (1, size - 1, 2))
     mine = pick(first, [up, down])
     other = lax.ppermute(mine, "rep", [(0, 1), (1, 0)])
@@ -596,7 +597,7 @@
         query_proj,
         group_count,
         lag_count,
-        [filters, far, mine, other],
+        [filters, far_filters, mine, other],
     )
     out, ready = near_conv(
         size, (1, size - 1), 2, meta, [up, down], shifted, term, query_proj, out

time: 45 us -> 46.7 us (1.038)
  waiting for transfers between devices: 16.2 us -> 16.8 us
  starting transfers between devices: 12.5 us -> 13.1 us
    ppermute x6 -> x7, waiting for transfers between devices: 16.2 us -> 16.8 us  [shift(): lax.ppermute(value, 'seq', [(z, (z + step) % size) for z in range(size)])]
    ppermute x6 -> x7, starting transfers between devices: 11.3 us -> 11.6 us  [shift(): lax.ppermute(value, 'seq', [(z, (z + step) % size) for z in range(size)])]
  transfers between devices with their start and end apart: 7 -> 8, of which waited for: 6 -> 6; matrix products, arithmetic and copies ran while one was open for 1% -> 1% of each run, Pallas kernels for 22% -> 28%
where the time goes in v9:
time: 46.7 us; the launch traced here: 46.5 us
  waiting for transfers between devices  16.8 us (36%)
  Pallas kernels  15.4 us (33%)
  starting transfers between devices  13.1 us (28%)
  between operations  0.7 us (1%)
  local copies, waits for them, and re-layouts  0.59 us (1%)
    ppermute x7, waiting for transfers between devices, shift(): lax.ppermute(value, 'seq', [(z, (z + step) % size) for z in range(size)])  16.8 us
    ppermute x7, starting transfers between devices, shift(): lax.ppermute(value, 'seq', [(z, (z + step) % size) for z in range(size)])  11.6 us
    pallas_call x1, Pallas kernels, open_conv(): pl.pallas_call(functools.partial(open_kernel, size, first), in_specs=[ANY...  5.5 us
    pallas_call x1, Pallas kernels, near_conv(): pl.pallas_call(functools.partial(near_kernel, size, steps, next_step), in...  3.36 us
    pallas_call x1, Pallas kernels, gate(): pl.pallas_call(functools.partial(gate_kernel, size, parts), in_specs=[HBM...  2.8 us
    pallas_call x1, Pallas kernels, far_conv(): pl.pallas_call(functools.partial(far_kernel, size, step), in_specs=[VMEM_...  1.89 us
    ppermute x1, starting transfers between devices, shards(): other = lax.ppermute(mine, 'rep', [(0, 1), (1, 0)])  1.52 us
    pallas_call x1, Pallas kernels, last_rows(): pl.pallas_call(last_rows_kernel, grid=(1,), in_specs=[block, block], out_...  1.16 us
  transfers between devices with their start and end apart: 8, of which 6 were waited for; matrix products, arithmetic and copies ran while one was open for 1% of the time, Pallas kernels for 28%

profile of v9, /device:TPU:0, one launch (start us, length us, event | category | flops | bytes accessed | tf_op | source)
XLA Modules:
  0.0 46.5 jit_solution(5070180304152162942)
XLA Ops:
  0.0 4.0 %collective-permute-start.3 = (bf16[64,512]{1,0:T(8,128)(2,1)}, bf16[64,512]{1,0:T(8,128)(2,1)S(1)}, u32[]{:S(2)}, u32[]{:S(2)}) collective-permute-start(bf16[64,512]{1,0:T(8,128)(2,1)} %refs_0_.1), channel_id=1, source_target_pairs={{0,8},{4,12},{8,0},{12,4},{1,9},{5,13},{9,1},{13,5},{2,10},{6,14},... | collective-permute-start | bytes 196616 | tf_op jit(solution)/shard_map/ppermute | solution.py:572
  4.0 2.8 %gate.1 = (bf16[512,128]{1,0:T(8,128)(2,1)S(1)}, bf16[640,128]{1,0:T(8,128)(2,1)S(1)}, bf16[512,128]{1,0:T(8,128)(2,1)S(1)}, bf16[640,128]{1,0:T(8,128)(2,1)S(1)...) custom-call(s32[4]{0:T(128)} %sources_in.1, s32[16]{0:T(128)} %owner_in.1, bf16[512,1024]{1,0:T(8,128)(2,1)} %key.1, ...), custom_call_target="tpu_custom_call" | custom-call | tf_op jit(solution)/shard_map/gate/pallas_call | solution.py:147
  6.9 1.1 %collective-permute-done.3.refs_1_ = bf16[64,512]{1,0:T(8,128)(2,1)S(1)} collective-permute-done((bf16[64,512]{1,0:T(8,128)(2,1)}, bf16[64,512]{1,0:T(8,128)(2,1)S(1)}, u32[]{:S(2)}, u32[]{:S(2)}) %collective-permute-start.3) | collective-permute-done | bytes 65568 | tf_op jit(solution)/shard_map/ppermute | solution.py:572
  8.0 0.6 %collective-permute-start.4 = (bf16[640,128]{1,0:T(8,128)(2,1)S(1)}, bf16[640,128]{1,0:T(8,128)(2,1)S(1)}, u32[]{:S(2)}, u32[]{:S(2)}) collective-permute-start(bf16[640,128]{1,0:T(8,128)(2,1)S(1)} %get-tuple-element.66), channel_id=1, source_target_pairs={{0,4},{4,8},{8,12},{12,0},{1,5},{5,9},{9,13},{13,1},{2,6},{6,10},{... | collective-permute-start | bytes 491528 | tf_op jit(solution)/shard_map/ppermute | solution.py:572
  8.6 3.2 %collective-permute-start.5 = (bf16[640,128]{1,0:T(8,128)(2,1)S(1)}, bf16[640,128]{1,0:T(8,128)(2,1)S(1)}, u32[]{:S(2)}, u32[]{:S(2)}) collective-permute-start(bf16[640,128]{1,0:T(8,128)(2,1)S(1)} %get-tuple-element.67), channel_id=1, source_target_pairs={{0,12},{4,0},{8,4},{12,8},{1,13},{5,1},{9,5},{13,9},{2,14},{6,2},{... | collective-permute-start | bytes 491528 | tf_op jit(solution)/shard_map/ppermute | solution.py:572
  11.8 0.1 collective-permute-start.7
  11.9 5.1 %collective-permute-done.4.refs_0_ = bf16[640,128]{1,0:T(8,128)(2,1)S(1)} collective-permute-done((bf16[640,128]{1,0:T(8,128)(2,1)S(1)}, bf16[640,128]{1,0:T(8,128)(2,1)S(1)}, u32[]{:S(2)}, u32[]{:S(2)}) %collective-permute-start.4) | collective-permute-done | bytes 163872 | tf_op jit(solution)/shard_map/ppermute | solution.py:572
  16.9 0.5 %collective-permute-done.5.refs_1_ = bf16[640,128]{1,0:T(8,128)(2,1)S(1)} collective-permute-done((bf16[640,128]{1,0:T(8,128)(2,1)S(1)}, bf16[640,128]{1,0:T(8,128)(2,1)S(1)}, u32[]{:S(2)}, u32[]{:S(2)}) %collective-permute-start.5) | collective-permute-done | bytes 163872 | tf_op jit(solution)/shard_map/ppermute | solution.py:572
  17.4 1.5 %collective-permute-start.6 = (bf16[2,128,128]{2,1,0:T(8,128)(2,1)S(1)}, bf16[2,128,128]{2,1,0:T(8,128)(2,1)S(1)}, u32[]{:S(2)}, u32[]{:S(2)}) collective-permute-start(bf16[2,128,128]{2,1,0:T(8,128)(2,1)S(1)} %pick.1.refs_2_), channel_id=1, source_target_pairs={{0,16},{16,0},{1,17},{17,1},{2,18},{18,2},{3,19},{19,3},{4,20},{20... | collective-permute-start | bytes 196616 | tf_op jit(solution)/shard_map/ppermute | solution.py:578
  19.0 1.2 %last_rows.1.last = bf16[1024,128]{1,0:T(8,128)(2,1)S(1)} custom-call(bf16[512,1024]{1,0:T(8,128)(2,1)} %key.1, bf16[512,1024]{1,0:T(8,128)(2,1)} %value.1), custom_call_target="tpu_custom_call" | custom-call | tf_op jit(solution)/shard_map/last_rows/pallas_call | solution.py:328
  20.1 0.6 %slice.15 = s32[1]{0:T(128)} slice(s32[23]{0:T(128)S(1)} %get-tuple-element.60.meta_in), slice={[6:7]} | slice | bytes 8 | tf_op jit(solution)/shard_map/slice | solution.py:589
  21.4 3.1 %collective-permute-done.7 = bf16[512,128]{1,0:T(8,128)(2,1)S(1)} collective-permute-done((bf16[512,128]{1,0:T(8,128)(2,1)S(1)}, bf16[512,128]{1,0:T(8,128)(2,1)S(1)}, u32[]{:S(2)}, u32[]{:S(2)}) %collective-permute-start.7) | collective-permute-done | bytes 131104 | tf_op jit(solution)/shard_map/ppermute | solution.py:572
  24.4 0.0 collective-permute-done.6.refs_3_
  24.4 0.7 %conditional.1 = (bf16[3,256,128]{2,1,0:T(8,128)(2,1)S(1)}) conditional(s32[]{:T(128)} %bitcast.4, (s32[23]{0:T(128)S(1)}, bf16[512,128]{1,0:T(8,128)(2,1)S(1)}, bf16[640,128]{1,0:T(8,128)(2,1)S(1)}, bf16[640,128]{1,0:T(8,128)(2,1)S(1)}, bf16[512,128]{1,0:T(8,128)(2,1)S(1)}) %tuple.15, (bf16[4,256,128]{2,1,0:T(8,128)(2,1)S(1)}, s32[23]{0:T(128)S(1)}, ...), branch_computations={%region_0.0_spmd, %region_1.0_spmd} | conditional | bytes 1310848 | solution.py:589
  24.4 0.7 %merge.2 = bf16[3,256,128]{2,1,0:T(8,128)(2,1)S(1)} custom-call(s32[23]{0:T(128)S(1)} %get-tuple-element.30.meta, bf16[512,128]{1,0:T(8,128)(2,1)S(1)} %get-tuple-element.31.refs_0_, bf16[640,128]{1,0:T(8,128)(2,1)S(1)} %get-tuple-element.32.refs_1_, bf16[640,128]{1,0:T(8,128)(2,1)S(1)} %get-tuple-element.33.refs_2_, ...), custom_call_target="tpu_custom_call" | custom-call | tf_op jit(solution)/shard_map/cond/branch_0_fun/merge/pallas_call | solution.py:194
  25.1 1.0 %collective-permute-start.10 = (bf16[3,256,128]{2,1,0:T(8,128)(2,1)S(1)}, bf16[3,256,128]{2,1,0:T(8,128)(2,1)S(1)}, u32[]{:S(2)}, u32[]{:S(2)}) collective-permute-start(bf16[3,256,128]{2,1,0:T(8,128)(2,1)S(1)} %get-tuple-element.83.pieces), channel_id=1, source_target_pairs={{0,12},{4,0},{8,4},{12,8},{1,13},{5,1},{9,5},{13,9},{2,14},{6,2},{... | collective-permute-start | bytes 589832 | tf_op jit(solution)/shard_map/ppermute | solution.py:572
  26.1 1.3 %collective-permute-start.9 = (bf16[3,256,128]{2,1,0:T(8,128)(2,1)S(1)}, bf16[3,256,128]{2,1,0:T(8,128)(2,1)S(1)}, u32[]{:S(2)}, u32[]{:S(2)}) collective-permute-start(bf16[3,256,128]{2,1,0:T(8,128)(2,1)S(1)} %get-tuple-element.83.pieces), channel_id=1, source_target_pairs={{0,4},{4,8},{8,12},{12,0},{1,5},{5,9},{9,13},{13,1},{2,6},{6,10},{... | collective-permute-start | bytes 589832 | tf_op jit(solution)/shard_map/ppermute | solution.py:572
  27.4 1.4 %collective-permute-start.8 = (bf16[3,256,128]{2,1,0:T(8,128)(2,1)S(1)}, bf16[3,256,128]{2,1,0:T(8,128)(2,1)S(1)}, u32[]{:S(2)}, u32[]{:S(2)}) collective-permute-start(bf16[3,256,128]{2,1,0:T(8,128)(2,1)S(1)} %get-tuple-element.83.pieces), channel_id=1, source_target_pairs={{0,8},{4,12},{8,0},{12,4},{1,9},{5,13},{9,1},{13,5},{2,10},{6,14},... | collective-permute-start | bytes 589832 | tf_op jit(solution)/shard_map/ppermute | solution.py:572
  28.8 5.5 %open_conv.1 = (bf16[64,16,2304]{2,1,0:T(8,128)(2,1)S(1)}, f32[128,1024]{1,0:T(8,128)S(1)}, bf16[512,1024]{1,0:T(8,128)(2,1)}) custom-call(s32[23]{0:T(128)S(1)} %get-tuple-element.60.meta_in, bf16[1024,128]{1,0:T(8,128)(2,1)S(1)} %last_rows.1.last, bf16[3,256,128]{2,1,0:T(8,128)(2,1)S(1)} %get-tuple-element.83.pieces, bf16[512,1024]{1,0:T(8,128)(2,1)S(1)} %copy-done, ...), custom_call_target="tpu_custom_call" | custom-call | tf_op jit(solution)/shard_map/open_conv/pallas_call | solution.py:434
  34.3 2.6 %collective-permute-done.10.refs_1_ = bf16[3,256,128]{2,1,0:T(8,128)(2,1)S(1)} collective-permute-done((bf16[3,256,128]{2,1,0:T(8,128)(2,1)S(1)}, bf16[3,256,128]{2,1,0:T(8,128)(2,1)S(1)}, u32[]{:S(2)}, u32[]{:S(2)}) %collective-permute-start.10) | collective-permute-done | bytes 196640 | tf_op jit(solution)/shard_map/ppermute | solution.py:572
  36.8 0.0 collective-permute-done.9.refs_0_
  36.8 3.4 %near_conv.1 = (bf16[512,1024]{1,0:T(8,128)(2,1)}, bf16[16,64,768]{2,1,0:T(8,128)(2,1)S(1)}) custom-call(s32[23]{0:T(128)S(1)} %get-tuple-element.60.meta_in, bf16[64,16,2304]{2,1,0:T(8,128)(2,1)S(1)} %get-tuple-element.74.shifted, f32[128,1024]{1,0:T(8,128)S(1)} %get-tuple-element.75.term, ...), custom_call_target="tpu_custom_call", output_to_operand_aliasing={{0}: (4, {})} | custom-call | tf_op jit(solution)/shard_map/near_conv/pallas_call | solution.py:494
  40.2 4.4 %collective-permute-done.8.pieces = bf16[3,256,128]{2,1,0:T(8,128)(2,1)S(1)} collective-permute-done((bf16[3,256,128]{2,1,0:T(8,128)(2,1)S(1)}, bf16[3,256,128]{2,1,0:T(8,128)(2,1)S(1)}, u32[]{:S(2)}, u32[]{:S(2)}) %collective-permute-start.8) | collective-permute-done | bytes 196640 | tf_op jit(solution)/shard_map/ppermute | solution.py:572
  44.6 1.9 %far_conv.1 = bf16[512,1024]{1,0:T(8,128)(2,1)} custom-call(bf16[3,256,128]{2,1,0:T(8,128)(2,1)S(1)} %collective-permute-done.8.pieces, bf16[16,64,768]{2,1,0:T(8,128)(2,1)S(1)} %get-tuple-element.77.ready, f32[128,1024]{1,0:T(8,128)S(1)} %get-tuple-element.75.term, bf16[512,1024]{1,0:T(8,128)(2,1)S(1)} %copy-done, ...), custom_call_target="tpu_custom_call", output_to_operand_aliasing={{}: (4, {})} | custom-call | tf_op jit(solution)/shard_map/far_conv/pallas_call | solution.py:537
  (5 shorter events, 0.0 us)
Async XLA Ops:
  0.0 28.8 %copy-start.1 = (bf16[64,512]{1,0:T(8,128)(2,1)S(1)}, bf16[64,512]{1,0:T(8,128)(2,1)}, u32[]{:S(2)}) copy-start(bf16[64,512]{1,0:T(8,128)(2,1)} %refs_0_.1) | copy-start | bytes 196612
  0.0 28.8 %copy-start = (bf16[512,1024]{1,0:T(8,128)(2,1)S(1)}, bf16[512,1024]{1,0:T(8,128)(2,1)}, u32[]{:S(2)}) copy-start(bf16[512,1024]{1,0:T(8,128)(2,1)} %query.5) | copy-start | bytes 3145732
  0.0 8.0 %collective-permute-start.3 = (bf16[64,512]{1,0:T(8,128)(2,1)}, bf16[64,512]{1,0:T(8,128)(2,1)S(1)}, u32[]{:S(2)}, u32[]{:S(2)}) collective-permute-start(bf16[64,512]{1,0:T(8,128)(2,1)} %refs_0_.1), channel_id=1, source_target_pairs={{0,8},{4,12},{8,0},{12,4},{1,9},{5,13},{9,1},{13,5},{2,10},{6,14},... | collective-permute-start | bytes 196616 | tf_op jit(solution)/shard_map/ppermute | solution.py:572
  8.0 9.0 %collective-permute-start.4 = (bf16[640,128]{1,0:T(8,128)(2,1)S(1)}, bf16[640,128]{1,0:T(8,128)(2,1)S(1)}, u32[]{:S(2)}, u32[]{:S(2)}) collective-permute-start(bf16[640,128]{1,0:T(8,128)(2,1)S(1)} %get-tuple-element.66), channel_id=1, source_target_pairs={{0,4},{4,8},{8,12},{12,0},{1,5},{5,9},{9,13},{13,1},{2,6},{6,10},{... | collective-permute-start | bytes 491528 | tf_op jit(solution)/shard_map/ppermute | solution.py:572
  8.6 8.9 %collective-permute-start.5 = (bf16[640,128]{1,0:T(8,128)(2,1)S(1)}, bf16[640,128]{1,0:T(8,128)(2,1)S(1)}, u32[]{:S(2)}, u32[]{:S(2)}) collective-permute-start(bf16[640,128]{1,0:T(8,128)(2,1)S(1)} %get-tuple-element.67), channel_id=1, source_target_pairs={{0,12},{4,0},{8,4},{12,8},{1,13},{5,1},{9,5},{13,9},{2,14},{6,2},{... | collective-permute-start | bytes 491528 | tf_op jit(solution)/shard_map/ppermute | solution.py:572
  11.8 12.7 %collective-permute-start.7 = (bf16[512,128]{1,0:T(8,128)(2,1)S(1)}, bf16[512,128]{1,0:T(8,128)(2,1)S(1)}, u32[]{:S(2)}, u32[]{:S(2)}) collective-permute-start(bf16[512,128]{1,0:T(8,128)(2,1)S(1)} %get-tuple-element.68), channel_id=1, source_target_pairs={{0,8},{4,12},{8,0},{12,4},{1,9},{5,13},{9,1},{13,5},{2,10},{6,14},... | collective-permute-start | bytes 393224 | tf_op jit(solution)/shard_map/ppermute | solution.py:572
  17.4 7.0 %collective-permute-start.6 = (bf16[2,128,128]{2,1,0:T(8,128)(2,1)S(1)}, bf16[2,128,128]{2,1,0:T(8,128)(2,1)S(1)}, u32[]{:S(2)}, u32[]{:S(2)}) collective-permute-start(bf16[2,128,128]{2,1,0:T(8,128)(2,1)S(1)} %pick.1.refs_2_), channel_id=1, source_target_pairs={{0,16},{16,0},{1,17},{17,1},{2,18},{18,2},{3,19},{19,3},{4,20},{20... | collective-permute-start | bytes 196616 | tf_op jit(solution)/shard_map/ppermute | solution.py:578
  25.1 11.7 %collective-permute-start.10 = (bf16[3,256,128]{2,1,0:T(8,128)(2,1)S(1)}, bf16[3,256,128]{2,1,0:T(8,128)(2,1)S(1)}, u32[]{:S(2)}, u32[]{:S(2)}) collective-permute-start(bf16[3,256,128]{2,1,0:T(8,128)(2,1)S(1)} %get-tuple-element.83.pieces), channel_id=1, source_target_pairs={{0,12},{4,0},{8,4},{12,8},{1,13},{5,1},{9,5},{13,9},{2,14},{6,2},{... | collective-permute-start | bytes 589832 | tf_op jit(solution)/shard_map/ppermute | solution.py:572
  26.1 10.8 %collective-permute-start.9 = (bf16[3,256,128]{2,1,0:T(8,128)(2,1)S(1)}, bf16[3,256,128]{2,1,0:T(8,128)(2,1)S(1)}, u32[]{:S(2)}, u32[]{:S(2)}) collective-permute-start(bf16[3,256,128]{2,1,0:T(8,128)(2,1)S(1)} %get-tuple-element.83.pieces), channel_id=1, source_target_pairs={{0,4},{4,8},{8,12},{12,0},{1,5},{5,9},{9,13},{13,1},{2,6},{6,10},{... | collective-permute-start | bytes 589832 | tf_op jit(solution)/shard_map/ppermute | solution.py:572
  27.4 17.3 %collective-permute-start.8 = (bf16[3,256,128]{2,1,0:T(8,128)(2,1)S(1)}, bf16[3,256,128]{2,1,0:T(8,128)(2,1)S(1)}, u32[]{:S(2)}, u32[]{:S(2)}) collective-permute-start(bf16[3,256,128]{2,1,0:T(8,128)(2,1)S(1)} %get-tuple-element.83.pieces), channel_id=1, source_target_pairs={{0,8},{4,12},{8,0},{12,4},{1,9},{5,13},{9,1},{13,5},{2,10},{6,14},... | collective-permute-start | bytes 589832 | tf_op jit(solution)/shard_map/ppermute | solution.py:572

commit v10 on v8

--- a/solution.py
+++ b/solution.py
@@ -387,7 +387,7 @@
 
 def part_base(step, size, width):
     me = lax.axis_index("seq")
-    return pl.multiple_of(sender(me, step, size) * width, width)
+    return pl.multiple_of((me ^ step if size > 1 else 0) * width, width)
 
 
 def scratch(count, row_count):
@@ -586,7 +586,8 @@
         return merge(size, width, meta, received)
 
     merged = lax.cond(meta[MANY] > 0, merge_more, merge_plain, meta, received, extra)
-    up, down, far_part = shift(merged, 1), shift(merged, size - 1), shift(merged, 2)
+    far_part = lax.ppermute(merged, "seq", [(0, 2), (2, 0), (1, 3), (3, 1)])
+    near_part = lax.ppermute(merged, "seq", [(0, 1), (1, 0), (2, 3), (3, 2)])
     shifted, term, out = open_conv(
         size,
         first,
@@ -598,10 +599,12 @@
         lag_count,
         [filters, far, mine, other],
     )
+    far_part, out = lax.optimization_barrier((far_part, out))
+    last_part = lax.ppermute(far_part, "seq", [(0, 1), (1, 0), (2, 3), (3, 2)])
     out, ready = near_conv(
-        size, (1, size - 1), 2, meta, [up, down], shifted, term, query_proj, out
+        size, (1, 2), 3, meta, [near_part, far_part], shifted, term, query_proj, out
     )
-    return far_conv(size, 2, far_part, ready, term, query_proj, out)
+    return far_conv(size, 3, last_part, ready, term, query_proj, out)
 
 
 def solution(mesh):

time: 45 us -> 43.4 us (0.964)
  starting transfers between devices: 12.5 us -> 10.8 us
    ppermute x6 -> x3, waiting for transfers between devices: 16.2 us -> 10.7 us  [shift(): lax.ppermute(value, 'seq', [(z, (z + step) % size) for z in range(size)])]
    ppermute x0 -> x3, waiting for transfers between devices: none -> 5.34 us  [the longest x1 2.33 us: shards(): last_part = lax.ppermute(far_part, 'seq', [(0, 1), (1, 0), (2, 3), (3, 2)])]
    ppermute x6 -> x3, starting transfers between devices: 11.3 us -> 6.55 us  [shift(): lax.ppermute(value, 'seq', [(z, (z + step) % size) for z in range(size)])]
    ppermute x0 -> x3, starting transfers between devices: none -> 2.84 us  [the longest x1 2.65 us: shards(): far_part = lax.ppermute(merged, 'seq', [(0, 2), (2, 0), (1, 3), (3, 1)])]
  transfers between devices with their start and end apart: 7 -> 7, of which waited for: 6 -> 6; matrix products, arithmetic and copies ran while one was open for 1% -> 1% of each run, Pallas kernels for 22% -> 23%
where the time goes in v10:
time: 43.4 us; the launch traced here: 43.3 us
  waiting for transfers between devices  16 us (37%)
  Pallas kernels  15.1 us (35%)
  starting transfers between devices  10.8 us (25%)
  between operations  0.7 us (2%)
  local copies, waits for them, and re-layouts  0.59 us (1%)
    ppermute x3, waiting for transfers between devices, shift(): lax.ppermute(value, 'seq', [(z, (z + step) % size) for z in range(size)])  10.7 us
    ppermute x3, starting transfers between devices, shift(): lax.ppermute(value, 'seq', [(z, (z + step) % size) for z in range(size)])  6.55 us
    pallas_call x1, Pallas kernels, open_conv(): pl.pallas_call(functools.partial(open_kernel, size, first), in_specs=[ANY...  5.51 us
    pallas_call x1, Pallas kernels, near_conv(): pl.pallas_call(functools.partial(near_kernel, size, steps, next_step), in...  3.4 us
    ppermute x1, starting transfers between devices, shards(): far_part = lax.ppermute(merged, 'seq', [(0, 2), (2, 0), (1, 3), (3, 1)])  2.65 us
    pallas_call x1, Pallas kernels, gate(): pl.pallas_call(functools.partial(gate_kernel, size, parts), in_specs=[HBM...  2.49 us
    ppermute x1, waiting for transfers between devices, shards(): last_part = lax.ppermute(far_part, 'seq', [(0, 1), (1, 0), (2, 3), (3, 2)])  2.33 us
    ppermute x1, waiting for transfers between devices, shards(): far_part = lax.ppermute(merged, 'seq', [(0, 2), (2, 0), (1, 3), (3, 1)])  2.22 us
  transfers between devices with their start and end apart: 7, of which 6 were waited for; matrix products, arithmetic and copies ran while one was open for 1% of the time, Pallas kernels for 23%

profile of v10, /device:TPU:0, one launch (start us, length us, event | category | flops | bytes accessed | tf_op | source)
XLA Modules:
  0.0 43.3 jit_solution(15413696308596473186)
XLA Ops:
  0.0 2.5 %gate.1 = (bf16[512,128]{1,0:T(8,128)(2,1)S(1)}, bf16[640,128]{1,0:T(8,128)(2,1)S(1)}, bf16[768,128]{1,0:T(8,128)(2,1)S(1)}, bf16[640,128]{1,0:T(8,128)(2,1)S(1)...) custom-call(s32[4]{0:T(128)} %sources_in.1, s32[16]{0:T(128)} %owner_in.1, bf16[512,1024]{1,0:T(8,128)(2,1)} %key.1, ...), custom_call_target="tpu_custom_call" | custom-call | tf_op jit(solution)/shard_map/gate/pallas_call | solution.py:147
  2.5 2.9 %collective-permute-start.3 = (bf16[640,128]{1,0:T(8,128)(2,1)S(1)}, bf16[640,128]{1,0:T(8,128)(2,1)S(1)}, u32[]{:S(2)}, u32[]{:S(2)}) collective-permute-start(bf16[640,128]{1,0:T(8,128)(2,1)S(1)} %get-tuple-element.59), channel_id=1, source_target_pairs={{0,4},{4,8},{8,12},{12,0},{1,5},{5,9},{9,13},{13,1},{2,6},{6,10},{... | collective-permute-start | bytes 491528 | tf_op jit(solution)/shard_map/ppermute | solution.py:573
  5.4 2.1 %collective-permute-start.4 = (bf16[640,128]{1,0:T(8,128)(2,1)S(1)}, bf16[640,128]{1,0:T(8,128)(2,1)S(1)}, u32[]{:S(2)}, u32[]{:S(2)}) collective-permute-start(bf16[640,128]{1,0:T(8,128)(2,1)S(1)} %get-tuple-element.60), channel_id=1, source_target_pairs={{0,12},{4,0},{8,4},{12,8},{1,13},{5,1},{9,5},{13,9},{2,14},{6,2},{... | collective-permute-start | bytes 491528 | tf_op jit(solution)/shard_map/ppermute | solution.py:573
  7.5 1.6 %collective-permute-start.6 = (bf16[768,128]{1,0:T(8,128)(2,1)S(1)}, bf16[768,128]{1,0:T(8,128)(2,1)S(1)}, u32[]{:S(2)}, u32[]{:S(2)}) collective-permute-start(bf16[768,128]{1,0:T(8,128)(2,1)S(1)} %get-tuple-element.61), channel_id=1, source_target_pairs={{0,8},{4,12},{8,0},{12,4},{1,9},{5,13},{9,1},{13,5},{2,10},{6,14},... | collective-permute-start | bytes 589832 | tf_op jit(solution)/shard_map/ppermute | solution.py:573
  9.1 3.4 %collective-permute-done.3.refs_0_ = bf16[640,128]{1,0:T(8,128)(2,1)S(1)} collective-permute-done((bf16[640,128]{1,0:T(8,128)(2,1)S(1)}, bf16[640,128]{1,0:T(8,128)(2,1)S(1)}, u32[]{:S(2)}, u32[]{:S(2)}) %collective-permute-start.3) | collective-permute-done | bytes 163872 | tf_op jit(solution)/shard_map/ppermute | solution.py:573
  12.5 2.5 %collective-permute-done.4.refs_1_ = bf16[640,128]{1,0:T(8,128)(2,1)S(1)} collective-permute-done((bf16[640,128]{1,0:T(8,128)(2,1)S(1)}, bf16[640,128]{1,0:T(8,128)(2,1)S(1)}, u32[]{:S(2)}, u32[]{:S(2)}) %collective-permute-start.4) | collective-permute-done | bytes 163872 | tf_op jit(solution)/shard_map/ppermute | solution.py:573
  15.0 1.4 %collective-permute-start.5 = (bf16[2,128,128]{2,1,0:T(8,128)(2,1)S(1)}, bf16[2,128,128]{2,1,0:T(8,128)(2,1)S(1)}, u32[]{:S(2)}, u32[]{:S(2)}) collective-permute-start(bf16[2,128,128]{2,1,0:T(8,128)(2,1)S(1)} %pick.1.refs_2_), channel_id=1, source_target_pairs={{0,16},{16,0},{1,17},{17,1},{2,18},{18,2},{3,19},{19,3},{4,20},{20... | collective-permute-start | bytes 196616 | tf_op jit(solution)/shard_map/ppermute | solution.py:577
  16.5 1.2 %last_rows.1.last = bf16[1024,128]{1,0:T(8,128)(2,1)S(1)} custom-call(bf16[512,1024]{1,0:T(8,128)(2,1)} %key.1, bf16[512,1024]{1,0:T(8,128)(2,1)} %value.1), custom_call_target="tpu_custom_call" | custom-call | tf_op jit(solution)/shard_map/last_rows/pallas_call | solution.py:329
  17.6 0.6 %slice.15 = s32[1]{0:T(128)} slice(s32[23]{0:T(128)S(1)} %get-tuple-element.57.meta_in), slice={[6:7]} | slice | bytes 8 | tf_op jit(solution)/shard_map/slice | solution.py:588
  18.8 4.7 %collective-permute-done.6.refs_1_ = bf16[768,128]{1,0:T(8,128)(2,1)S(1)} collective-permute-done((bf16[768,128]{1,0:T(8,128)(2,1)S(1)}, bf16[768,128]{1,0:T(8,128)(2,1)S(1)}, u32[]{:S(2)}, u32[]{:S(2)}) %collective-permute-start.6) | collective-permute-done | bytes 196640 | tf_op jit(solution)/shard_map/ppermute | solution.py:573
  23.6 0.0 collective-permute-done.5.refs_3_
  23.6 0.7 %conditional.1 = (bf16[3,256,128]{2,1,0:T(8,128)(2,1)S(1)}) conditional(s32[]{:T(128)} %bitcast.4, (s32[23]{0:T(128)S(1)}, bf16[512,128]{1,0:T(8,128)(2,1)S(1)}, bf16[640,128]{1,0:T(8,128)(2,1)S(1)}, bf16[640,128]{1,0:T(8,128)(2,1)S(1)}, bf16[768,128]{1,0:T(8,128)(2,1)S(1)}) %tuple.14, (bf16[4,256,128]{2,1,0:T(8,128)(2,1)S(1)}, s32[23]{0:T(128)S(1)}, ...), branch_computations={%region_0.0_spmd, %region_1.0_spmd} | conditional | bytes 1310848 | solution.py:588
  23.6 0.7 %merge.2 = bf16[3,256,128]{2,1,0:T(8,128)(2,1)S(1)} custom-call(s32[23]{0:T(128)S(1)} %get-tuple-element.30.meta, bf16[512,128]{1,0:T(8,128)(2,1)S(1)} %get-tuple-element.31.refs_0_, bf16[640,128]{1,0:T(8,128)(2,1)S(1)} %get-tuple-element.32.refs_1_, bf16[640,128]{1,0:T(8,128)(2,1)S(1)} %get-tuple-element.33.refs_2_, ...), custom_call_target="tpu_custom_call" | custom-call | tf_op jit(solution)/shard_map/cond/branch_0_fun/merge/pallas_call | solution.py:194
  24.3 2.7 %collective-permute-start.7 = (bf16[3,256,128]{2,1,0:T(8,128)(2,1)S(1)}, bf16[3,256,128]{2,1,0:T(8,128)(2,1)S(1)}, u32[]{:S(2)}, u32[]{:S(2)}) collective-permute-start(bf16[3,256,128]{2,1,0:T(8,128)(2,1)S(1)} %get-tuple-element.77.pieces), channel_id=1, source_target_pairs={{0,8},{8,0},{4,12},{12,4},{1,9},{9,1},{5,13},{13,5},{2,10},{10,2},... | collective-permute-start | bytes 589832 | tf_op jit(solution)/shard_map/ppermute | solution.py:589
  26.9 0.2 collective-permute-start.9
  27.1 0.0 copy-done.1
  27.1 0.0 copy-done
  27.1 5.5 %open_conv.1 = (bf16[64,16,2304]{2,1,0:T(8,128)(2,1)S(1)}, f32[128,1024]{1,0:T(8,128)S(1)}, bf16[512,1024]{1,0:T(8,128)(2,1)}) custom-call(s32[23]{0:T(128)S(1)} %get-tuple-element.57.meta_in, bf16[1024,128]{1,0:T(8,128)(2,1)S(1)} %last_rows.1.last, bf16[3,256,128]{2,1,0:T(8,128)(2,1)S(1)} %get-tuple-element.77.pieces, bf16[512,1024]{1,0:T(8,128)(2,1)S(1)} %copy-done, ...), custom_call_target="tpu_custom_call" | custom-call | tf_op jit(solution)/shard_map/open_conv/pallas_call | solution.py:435
  32.6 2.2 %collective-permute-done.7.refs_1_ = bf16[3,256,128]{2,1,0:T(8,128)(2,1)S(1)} collective-permute-done((bf16[3,256,128]{2,1,0:T(8,128)(2,1)S(1)}, bf16[3,256,128]{2,1,0:T(8,128)(2,1)S(1)}, u32[]{:S(2)}, u32[]{:S(2)}) %collective-permute-start.7) | collective-permute-done | bytes 196640 | tf_op jit(solution)/shard_map/ppermute | solution.py:589
  34.8 0.0 collective-permute-start.8
  34.8 0.8 %collective-permute-done.9.refs_0_ = bf16[3,256,128]{2,1,0:T(8,128)(2,1)S(1)} collective-permute-done((bf16[3,256,128]{2,1,0:T(8,128)(2,1)S(1)}, bf16[3,256,128]{2,1,0:T(8,128)(2,1)S(1)}, u32[]{:S(2)}, u32[]{:S(2)}) %collective-permute-start.9) | collective-permute-done | bytes 196640 | tf_op jit(solution)/shard_map/ppermute | solution.py:590
  35.6 3.4 %near_conv.1 = (bf16[512,1024]{1,0:T(8,128)(2,1)}, bf16[16,64,768]{2,1,0:T(8,128)(2,1)S(1)}) custom-call(s32[23]{0:T(128)S(1)} %get-tuple-element.57.meta_in, bf16[64,16,2304]{2,1,0:T(8,128)(2,1)S(1)} %get-tuple-element.68.shifted, f32[128,1024]{1,0:T(8,128)S(1)} %get-tuple-element.69.term, ...), custom_call_target="tpu_custom_call", output_to_operand_aliasing={{0}: (4, {})} | custom-call | tf_op jit(solution)/shard_map/near_conv/pallas_call | solution.py:495
  39.1 2.3 %collective-permute-done.8.pieces = bf16[3,256,128]{2,1,0:T(8,128)(2,1)S(1)} collective-permute-done((bf16[3,256,128]{2,1,0:T(8,128)(2,1)S(1)}, bf16[3,256,128]{2,1,0:T(8,128)(2,1)S(1)}, u32[]{:S(2)}, u32[]{:S(2)}) %collective-permute-start.8) | collective-permute-done | bytes 196640 | tf_op jit(solution)/shard_map/ppermute | solution.py:603
  41.4 1.9 %far_conv.1 = bf16[512,1024]{1,0:T(8,128)(2,1)} custom-call(bf16[3,256,128]{2,1,0:T(8,128)(2,1)S(1)} %collective-permute-done.8.pieces, bf16[16,64,768]{2,1,0:T(8,128)(2,1)S(1)} %get-tuple-element.71.ready, f32[128,1024]{1,0:T(8,128)S(1)} %get-tuple-element.69.term, bf16[512,1024]{1,0:T(8,128)(2,1)S(1)} %copy-done, ...), custom_call_target="tpu_custom_call", output_to_operand_aliasing={{}: (4, {})} | custom-call | tf_op jit(solution)/shard_map/far_conv/pallas_call | solution.py:538
  (3 shorter events, 0.0 us)
Async XLA Ops:
  0.0 27.1 %copy-start.1 = (bf16[64,512]{1,0:T(8,128)(2,1)S(1)}, bf16[64,512]{1,0:T(8,128)(2,1)}, u32[]{:S(2)}) copy-start(bf16[64,512]{1,0:T(8,128)(2,1)} %refs_0_.1) | copy-start | bytes 196612
  0.0 27.1 %copy-start = (bf16[512,1024]{1,0:T(8,128)(2,1)S(1)}, bf16[512,1024]{1,0:T(8,128)(2,1)}, u32[]{:S(2)}) copy-start(bf16[512,1024]{1,0:T(8,128)(2,1)} %query.5) | copy-start | bytes 3145732
  2.5 10.0 %collective-permute-start.3 = (bf16[640,128]{1,0:T(8,128)(2,1)S(1)}, bf16[640,128]{1,0:T(8,128)(2,1)S(1)}, u32[]{:S(2)}, u32[]{:S(2)}) collective-permute-start(bf16[640,128]{1,0:T(8,128)(2,1)S(1)} %get-tuple-element.59), channel_id=1, source_target_pairs={{0,4},{4,8},{8,12},{12,0},{1,5},{5,9},{9,13},{13,1},{2,6},{6,10},{... | collective-permute-start | bytes 491528 | tf_op jit(solution)/shard_map/ppermute | solution.py:573
  5.4 9.6 %collective-permute-start.4 = (bf16[640,128]{1,0:T(8,128)(2,1)S(1)}, bf16[640,128]{1,0:T(8,128)(2,1)S(1)}, u32[]{:S(2)}, u32[]{:S(2)}) collective-permute-start(bf16[640,128]{1,0:T(8,128)(2,1)S(1)} %get-tuple-element.60), channel_id=1, source_target_pairs={{0,12},{4,0},{8,4},{12,8},{1,13},{5,1},{9,5},{13,9},{2,14},{6,2},{... | collective-permute-start | bytes 491528 | tf_op jit(solution)/shard_map/ppermute | solution.py:573
  7.5 16.1 %collective-permute-start.6 = (bf16[768,128]{1,0:T(8,128)(2,1)S(1)}, bf16[768,128]{1,0:T(8,128)(2,1)S(1)}, u32[]{:S(2)}, u32[]{:S(2)}) collective-permute-start(bf16[768,128]{1,0:T(8,128)(2,1)S(1)} %get-tuple-element.61), channel_id=1, source_target_pairs={{0,8},{4,12},{8,0},{12,4},{1,9},{5,13},{9,1},{13,5},{2,10},{6,14},... | collective-permute-start | bytes 589832 | tf_op jit(solution)/shard_map/ppermute | solution.py:573
  15.0 8.6 %collective-permute-start.5 = (bf16[2,128,128]{2,1,0:T(8,128)(2,1)S(1)}, bf16[2,128,128]{2,1,0:T(8,128)(2,1)S(1)}, u32[]{:S(2)}, u32[]{:S(2)}) collective-permute-start(bf16[2,128,128]{2,1,0:T(8,128)(2,1)S(1)} %pick.1.refs_2_), channel_id=1, source_target_pairs={{0,16},{16,0},{1,17},{17,1},{2,18},{18,2},{3,19},{19,3},{4,20},{20... | collective-permute-start | bytes 196616 | tf_op jit(solution)/shard_map/ppermute | solution.py:577
  24.3 10.6 %collective-permute-start.7 = (bf16[3,256,128]{2,1,0:T(8,128)(2,1)S(1)}, bf16[3,256,128]{2,1,0:T(8,128)(2,1)S(1)}, u32[]{:S(2)}, u32[]{:S(2)}) collective-permute-start(bf16[3,256,128]{2,1,0:T(8,128)(2,1)S(1)} %get-tuple-element.77.pieces), channel_id=1, source_target_pairs={{0,8},{8,0},{4,12},{12,4},{1,9},{9,1},{5,13},{13,5},{2,10},{10,2},... | collective-permute-start | bytes 589832 | tf_op jit(solution)/shard_map/ppermute | solution.py:589
  26.9 8.7 %collective-permute-start.9 = (bf16[3,256,128]{2,1,0:T(8,128)(2,1)S(1)}, bf16[3,256,128]{2,1,0:T(8,128)(2,1)S(1)}, u32[]{:S(2)}, u32[]{:S(2)}) collective-permute-start(bf16[3,256,128]{2,1,0:T(8,128)(2,1)S(1)} %get-tuple-element.77.pieces), channel_id=1, source_target_pairs={{0,4},{4,0},{8,12},{12,8},{1,5},{5,1},{9,13},{13,9},{2,6},{6,2},{1... | collective-permute-start | bytes 589832 | tf_op jit(solution)/shard_map/ppermute | solution.py:590
  34.8 6.5 %collective-permute-start.8 = (bf16[3,256,128]{2,1,0:T(8,128)(2,1)S(1)}, bf16[3,256,128]{2,1,0:T(8,128)(2,1)S(1)}, u32[]{:S(2)}, u32[]{:S(2)}) collective-permute-start(bf16[3,256,128]{2,1,0:T(8,128)(2,1)S(1)} %collective-permute-done.7.refs_1_), channel_id=1, source_target_pairs={{0,4},{4,0},{8,12},{12,8},{1,5},{5,1},{9,13},{13,9},{2,6},{6,2},{1... | collective-permute-start | bytes 589832 | tf_op jit(solution)/shard_map/ppermute | solution.py:603

commit v11 on v10

--- a/solution.py
+++ b/solution.py
@@ -27,16 +27,7 @@
     return pltpu.CompilerParams(vmem_limit_bytes=VMEM_LIMIT)
 
 
-def steps_of(size):
-    return sorted(range(size), key=lambda step: (min(step, size - step), step))
-
-
-def partner(me, step, size):
-    return lax.rem(me + step, size)
-
-
-def sender(me, step, size):
-    return lax.rem(me + size - step, size)
+STEPS = (0, 2, 1, 3)
 
 
 PLACE = SENT
@@ -52,7 +43,7 @@
     return (rows_k * rows_v).astype(jnp.bfloat16).T
 
 
-def gate_kernel(size, parts, sources_in, owner_in, key_in, value_in, filters_in, *refs):
+def gate_kernel(parts, sources_in, owner_in, key_in, value_in, filters_in, *refs):
     sends = refs[:parts]
     extra, meta, sources, owner, key, value, filters, sems = refs[parts:]
     stretch_count = owner.shape[0]
@@ -102,7 +93,7 @@
             slot = lax.fori_loop(0, sources[w], count, 0)
             first = pl.multiple_of(slot * STRETCH, STRETCH)
             for step in range(parts):
-                part = partner(me, step, size) if parts > 1 else 0
+                part = me ^ step if parts > 1 else 0
                 base = part * width
 
                 def fill(target, offset, base=base):
@@ -124,18 +115,14 @@
 
     meta[MANY] = many
     group_count = filters.shape[0]
-    for send in sends:
-        rows = (send.shape[0] - SLOTS * width) * LANES // filters.shape[1]
-        groups = pl.ds(0, rows)
-        if 0 < rows < group_count:
-            groups = pl.ds(pl.multiple_of(lax.axis_index("rep") * rows, rows), rows)
-        for tile in range(filters.shape[1] // LANES if rows else 0):
-            send[pl.ds(SLOTS * width + tile * rows, rows), :] = filters[
-                groups, pl.ds(tile * LANES, LANES)
-            ]
-
-
-def gate(size, filter_rows, sources, owner, key_proj, value_proj, filters):
+    for tile in range(filters.shape[1] // LANES):
+        piece = filters[:, pl.ds(tile * LANES, LANES)]
+        for send in sends:
+            if send.shape[0] > SLOTS * width:
+                send[pl.ds(SLOTS * width + tile * group_count, group_count), :] = piece
+
+
+def gate(filter_rows, sources, owner, key_proj, value_proj, filters):
     row_count, channels = key_proj.shape
     slots = row_count // STRETCH
     parts = len(filter_rows)
@@ -145,7 +132,7 @@
         for operand in (sources, owner, key_proj, value_proj, filters)
     ]
     *sends, extra, meta = pl.pallas_call(
-        functools.partial(gate_kernel, size, parts),
+        functools.partial(gate_kernel, parts),
         in_specs=[HBM_SPEC] * 5,
         out_specs=[VMEM_SPEC] * (parts + 1) + [SMEM_SPEC],
         out_shape=[
@@ -169,31 +156,31 @@
     return sends, extra, meta
 
 
-def merge_kernel(size, width, meta, *refs):
-    received, extras, out = refs[:size], refs[size:-1], refs[-1]
+def merge_kernel(width, meta, *refs):
+    received, extras, out = refs[: len(STEPS)], refs[len(STEPS) : -1], refs[-1]
     me = lax.axis_index("seq")
 
     for w in range(SENT):
         place = meta[PLACE + w]
         rows = pl.ds(pl.multiple_of(jnp.minimum(place, SLOTS - 1) * width, LANES), width)
-        for block, step in zip(received, steps_of(size)):
-
-            @pl.when(sender(me, step, size) == meta[w])
+        for block, step in zip(received, STEPS):
+
+            @pl.when(me ^ step == meta[w])
             def _(w=w, block=block, rows=rows):
                 out[w] = block[rows, :]
 
     for w in range(SLOTS, SENT):
-        for step, extra in enumerate(extras):
-
-            @pl.when((sender(me, step, size) == meta[w]) & (meta[PLACE + w] >= SLOTS))
+        for extra, step in zip(extras, STEPS):
+
+            @pl.when((me ^ step == meta[w]) & (meta[PLACE + w] >= SLOTS))
             def _(w=w, extra=extra):
                 out[w] = extra[...]
 
 
-def merge(size, width, meta, received, extras=()):
-    return pl.pallas_call(
-        functools.partial(merge_kernel, size, width),
-        in_specs=[SMEM_SPEC] + [VMEM_SPEC] * (size + len(extras)),
+def merge(width, meta, received, extras=()):
+    return pl.pallas_call(
+        functools.partial(merge_kernel, width),
+        in_specs=[SMEM_SPEC] + [VMEM_SPEC] * (len(received) + len(extras)),
         out_specs=VMEM_SPEC,
         out_shape=jax.ShapeDtypeStruct((SENT, width, LANES), received[0].dtype),
         compiler_params=params(),
@@ -201,22 +188,19 @@
     )(meta, *received, *extras)
 
 
-def pick_kernel(first, *refs):
-    received, out = refs[:-1], refs[-1]
-    for index, block in enumerate(received):
-        out[index] = block[pl.ds(first, out.shape[1]), :]
+def pick_kernel(first, received, out):
+    out[...] = received[pl.ds(first, out.shape[0]), :]
 
 
 def pick(first, received):
-    rows = received[0].shape[0] - first
     return pl.pallas_call(
         functools.partial(pick_kernel, first),
-        in_specs=[VMEM_SPEC] * len(received),
+        in_specs=[VMEM_SPEC],
         out_specs=VMEM_SPEC,
-        out_shape=jax.ShapeDtypeStruct((len(received), rows, LANES), received[0].dtype),
+        out_shape=jax.ShapeDtypeStruct((received.shape[0] - first, LANES), received.dtype),
         compiler_params=params(),
         name="pick",
-    )(*received)
+    )(received)
 
 
 def lag_tiles(size, first, filters):
@@ -226,23 +210,17 @@
         for shard in range(size):
             for tile in range(first):
                 rows = pl.ds(tile * group_count, group_count)
-                yield pl.ds(0, group_count), shard * first + tile, blocks[shard, rows, :]
+                yield shard * first + tile, blocks[shard, rows, :]
         return
-    own, far, mine, other = filters
-    me, rep = lax.axis_index("seq"), lax.axis_index("rep")
+    own, far, near, cross = filters
+    me = lax.axis_index("seq")
     group_count = own.shape[0]
     tiles = own.shape[1] // LANES
-    half = group_count // 2
     for tile in range(tiles):
-        whole = pl.ds(0, group_count)
-        yield whole, me * tiles + tile, own[:, pl.ds(tile * LANES, LANES)]
-        rows = pl.ds(first + tile * group_count, group_count)
-        yield whole, sender(me, 2, size) * tiles + tile, far[rows, :]
-        for index, step in enumerate((1, size - 1)):
-            number = sender(me, step, size) * tiles + tile
-            for place, halves in ((rep, mine), (1 - rep, other)):
-                groups = pl.ds(pl.multiple_of(place * half, half), half)
-                yield groups, number, halves[index, pl.ds(tile * half, half), :]
+        yield me * tiles + tile, own[:, pl.ds(tile * LANES, LANES)]
+        for block, start, step in ((far, first, 2), (near, first, 1), (cross, 0, 3)):
+            rows = pl.ds(start + tile * group_count, group_count)
+            yield (me ^ step) * tiles + tile, block[rows, :]
 
 
 def build_shifted(size, first, filters, reverse, shifted):
@@ -251,11 +229,11 @@
     row = lax.broadcasted_iota(jnp.int32, (LANES, LANES), 0)
     column = lax.broadcasted_iota(jnp.int32, (LANES, LANES), 1)
     flip = jnp.where(row + column == LANES - 1, 1.0, 0.0).astype(jnp.bfloat16)
-    for groups, number, values in lag_tiles(size, first, filters):
+    for number, values in lag_tiles(size, first, filters):
         start = lag_count - LANES - number * LANES
         if not isinstance(start, int):
             start = pl.multiple_of(start, LANES)
-        reverse[groups, pl.ds(start, LANES)] = jnp.dot(
+        reverse[:, pl.ds(start, LANES)] = jnp.dot(
             values, flip, preferred_element_type=jnp.float32
         )
     reverse[:, pl.ds(lag_count, SPAN)] = jnp.zeros((group_count, SPAN), jnp.float32)
@@ -547,17 +525,425 @@
     )(pieces, ready, term, query_proj, before)
 
 
-def shards(size, reps, key_proj, value_proj, query_proj, filters, sources, owner):
+def shards(size, key_proj, value_proj, query_proj, filters, sources, owner):
     row_count, channels = key_proj.shape
     group_count, part = filters.shape
     lag_count = size * part
     tiles = part // LANES
-    by_parts = (size, reps) == (4, 2) and channels % (size * LANES) == 0
-    half = group_count // 2 * tiles
-    filter_rows = [0, half, 2 * half, half] if by_parts else [2 * half]
+    by_parts = size == 4 and channels % (size * LANES) == 0
+    block = group_count * tiles
+    filter_rows = [0, block, block, 0] if by_parts else [block]
     parts = len(filter_rows)
     width = channels // parts
-    sends, extra, meta = gate(size, filter_rows, sources, owner, key_proj, value_proj, filters)
+    operands = [
+        pltpu.with_memory_space_constraint(operand, pltpu.HBM)
+        for operand in (sources, owner, key_proj, value_proj, filters)
+    ]
+    *sends, extra, meta = pl.pallas_call(
+        functools.partial(gate_kernel, parts),
+        in_specs=[HBM_SPEC] * 5,
+        out_specs=[VMEM_SPEC] * (parts + 1) + [SMEM_SPEC],
+        out_shape=[
+            jax.ShapeDtypeStruct((SLOTS * width + rows, LANES), jnp.bfloat16) for rows in filter_rows
+        ]
+        + [
+            jax.ShapeDtypeStruct((parts, width, LANES), jnp.bfloat16),
+            jax.ShapeDtypeStruct((WINDOWS + slots * WIN,), jnp.int32),
+        ],
+        scratch_shapes=[
+            pltpu.SMEM(sources.shape, jnp.int32),
+            pltpu.SMEM(owner.shape, jnp.int32),
+            pltpu.VMEM(key_proj.shape, key_proj.dtype),
+            pltpu.VMEM(value_proj.shape, value_proj.dtype),
+            pltpu.VMEM(filters.shape, filters.dtype),
+            pltpu.SemaphoreType.DMA((5,)),
+        ],
+        compiler_params=params(),
+        name="gate",
+    )(*operands)
+    return sends, extra, meta
+
+
+def merge_kernel(width, meta, *refs):
+    received, extras, out = refs[: len(STEPS)], refs[len(STEPS) : -1], refs[-1]
+    me = lax.axis_index("seq")
+
+    for w in range(SENT):
+        place = meta[PLACE + w]
+        rows = pl.ds(pl.multiple_of(jnp.minimum(place, SLOTS - 1) * width, LANES), width)
+        for block, step in zip(received, STEPS):
+
+            @pl.when(me ^ step == meta[w])
+            def _(w=w, block=block, rows=rows):
+                out[w] = block[rows, :]
+
+    for w in range(SLOTS, SENT):
+        for extra, step in zip(extras, STEPS):
+
+            @pl.when((me ^ step == meta[w]) & (meta[PLACE + w] >= SLOTS))
+            def _(w=w, extra=extra):
+                out[w] = extra[...]
+
+
+def merge(width, meta, received, extras=()):
+    return pl.pallas_call(
+        functools.partial(merge_kernel, width),
+        in_specs=[SMEM_SPEC] + [VMEM_SPEC] * (len(received) + len(extras)),
+        out_specs=VMEM_SPEC,
+        out_shape=jax.ShapeDtypeStruct((SENT, width, LANES), received[0].dtype),
+        compiler_params=params(),
+        name="merge",
+    )(meta, *received, *extras)
+
+
+def pick_kernel(first, received, out):
+    out[...] = received[pl.ds(first, out.shape[0]), :]
+
+
+def pick(first, received):
+    return pl.pallas_call(
+        functools.partial(pick_kernel, first),
+        in_specs=[VMEM_SPEC],
+        out_specs=VMEM_SPEC,
+        out_shape=jax.ShapeDtypeStruct((received.shape[0] - first, LANES), received.dtype),
+        compiler_params=params(),
+        name="pick",
+    )(received)
+
+
+def lag_tiles(size, first, filters):
+    if len(filters) == 1:
+        blocks = filters[0]
+        group_count = blocks.shape[1] // first
+        for shard in range(size):
+            for tile in range(first):
+                rows = pl.ds(tile * group_count, group_count)
+                yield shard * first + tile, blocks[shard, rows, :]
+        return
+    own, far, near, cross = filters
+    me = lax.axis_index("seq")
+    group_count = own.shape[0]
+    tiles = own.shape[1] // LANES
+    for tile in range(tiles):
+        yield me * tiles + tile, own[:, pl.ds(tile * LANES, LANES)]
+        for block, start, step in ((far, first, 2), (near, first, 1), (cross, 0, 3)):
+            rows = pl.ds(start + tile * group_count, group_count)
+            yield (me ^ step) * tiles + tile, block[rows, :]
+
+
+def build_shifted(size, first, filters, reverse, shifted):
+    group_count, padded = reverse.shape
+    lag_count = padded - SPAN
+    row = lax.broadcasted_iota(jnp.int32, (LANES, LANES), 0)
+    column = lax.broadcasted_iota(jnp.int32, (LANES, LANES), 1)
+    flip = jnp.where(row + column == LANES - 1, 1.0, 0.0).astype(jnp.bfloat16)
+    for number, values in lag_tiles(size, first, filters):
+        start = lag_count - LANES - number * LANES
+        if not isinstance(start, int):
+            start = pl.multiple_of(start, LANES)
+        reverse[:, pl.ds(start, LANES)] = jnp.dot(
+            values, flip, preferred_element_type=jnp.float32
+        )
+    reverse[:, pl.ds(lag_count, SPAN)] = jnp.zeros((group_count, SPAN), jnp.float32)
+    inside = (
+        lax.broadcasted_iota(jnp.int32, (GROUP_CH, LANES), 1)
+        > lax.broadcasted_iota(jnp.int32, (GROUP_CH, LANES), 0)
+    )
+
+    @pl.loop(0, group_count // BLOCKS)
+    def _(block):
+        tile_rows = pl.ds(pl.multiple_of(block * BLOCKS, BLOCKS), BLOCKS)
+        before = [jnp.zeros((GROUP_CH, LANES), jnp.float32)] * BLOCKS
+        for start in range(0, padded, LANES):
+            tile = reverse[tile_rows, pl.ds(start, LANES)]
+            for g in range(BLOCKS):
+                spread = jnp.broadcast_to(tile[g : g + 1, :], (GROUP_CH, LANES))
+                rolled = pltpu.roll(spread, 1, 1, stride=1, stride_axis=0)
+                shifted[block * BLOCKS + g, :, pl.ds(start, LANES)] = jnp.where(
+                    inside, rolled, before[g]
+                ).astype(jnp.bfloat16)
+                before[g] = rolled
+
+
+def spread_rows(tile, spans, base):
+    lane = lax.broadcasted_iota(jnp.int16, tile.shape, 1)
+    zero = jnp.zeros(tile.shape, tile.dtype)
+    for i1 in range(BLOCKS):
+        shift = GROUP_CH * i1
+        if i1 == 0:
+            low, high = zero, tile
+        else:
+            moved = pltpu.roll(tile, LANES - shift, 1)
+            early = lane < LANES - shift
+            low, high = jnp.where(early, zero, moved), jnp.where(early, moved, zero)
+        rows = pl.ds(shift, GROUP_CH)
+        for g in range(BLOCKS):
+            part = slice(g * GROUP_CH, (g + 1) * GROUP_CH)
+            spans[g, rows, pl.ds(base, LANES)] = low[part]
+            spans[g, rows, pl.ds(base + LANES, LANES)] = high[part]
+
+
+def window(meta, shifted, group, slot, w):
+    start = pl.multiple_of(meta[WINDOWS + slot * WIN + w], STRETCH)
+    return shifted[group, :, pl.ds(start, SPAN)]
+
+
+def filter_rows(meta, shifted, group, slots):
+    return jnp.concatenate(
+        [
+            jnp.concatenate([window(meta, shifted, group, slot, w) for w in range(SENT)], axis=1)
+            for slot in range(slots)
+        ],
+        axis=0,
+    )
+
+
+def rows_of(results, block):
+    part = slice(block * GROUP_CH, (block + 1) * GROUP_CH)
+    return jnp.concatenate([result[part] for result in results], axis=0).T
+
+
+def last_rows_kernel(key, value, out):
+    for start in range(0, out.shape[0], LANES):
+        out[pl.ds(start, LANES), :] = product(key, value, 0, pl.ds(start, LANES))
+
+
+def last_rows(key_proj, value_proj):
+    row_count, channels = key_proj.shape
+    block = pl.BlockSpec((STRETCH, channels), lambda i: (row_count // STRETCH - 1, 0))
+    operands = [pltpu.with_memory_space_constraint(x, pltpu.HBM) for x in (key_proj, value_proj)]
+    return pl.pallas_call(
+        last_rows_kernel,
+        grid=(1,),
+        in_specs=[block, block],
+        out_specs=pl.BlockSpec((channels, STRETCH), lambda i: (0, 0)),
+        out_shape=jax.ShapeDtypeStruct((channels, STRETCH), jnp.bfloat16),
+        compiler_params=params(),
+        name="last_rows",
+    )(*operands)
+
+
+def last_term(slots, meta, last, shifted, term, spans):
+    for start in range(0, last.shape[0], LANES):
+        held = spans.at[start // LANES % 2]
+        spread_rows(last[pl.ds(start, LANES), :], held, 0)
+        results = [
+            lax.dot_general(
+                held[g],
+                window(meta, shifted, start // GROUP_CH + g, slots - 1, SENT),
+                NT,
+                preferred_element_type=jnp.float32,
+            )
+            for g in range(BLOCKS)
+        ]
+        for m in range(BLOCKS):
+            term[pl.ds(m * GROUP_CH, GROUP_CH), pl.ds(start, LANES)] = rows_of(results, m)
+
+
+def spread_part(pieces, start, spans):
+    for w in range(SENT):
+        spread_rows(pieces[w, pl.ds(start, LANES), :], spans, w * SPAN)
+
+
+def conv_part(filter_rows_of, base, start, term, query, out, result, spans, sem):
+    slots = query.shape[0] // STRETCH
+    columns = pl.ds(pl.multiple_of(base + start, LANES), LANES)
+    results = [
+        lax.dot_general(
+            spans[g],
+            filter_rows_of(start // GROUP_CH + g),
+            NT,
+            preferred_element_type=jnp.float32,
+        )
+        for g in range(BLOCKS)
+    ]
+    for m in range(BLOCKS):
+        rows = rows_of(results, m)
+        for slot in range(slots):
+            place = pl.ds(slot * STRETCH + m * GROUP_CH, GROUP_CH)
+            tile = rows[slot * GROUP_CH : (slot + 1) * GROUP_CH]
+            if slot == slots - 1:
+                tile = tile + term[pl.ds(m * GROUP_CH, GROUP_CH), columns]
+            gates = query[place, columns].astype(jnp.float32)
+            result[place, :] = (gates * tile).astype(jnp.bfloat16)
+    store = pltpu.make_async_copy(result, out.at[:, columns], sem)
+    store.start()
+    return store
+
+
+def part_base(step, size, width):
+    me = lax.axis_index("seq")
+    return pl.multiple_of((me ^ step if size > 1 else 0) * width, width)
+
+
+def scratch(count, row_count):
+    return [
+        pltpu.VMEM((count, row_count, LANES), jnp.bfloat16),
+        pltpu.VMEM((count, BLOCKS, LANES, SENT * SPAN), jnp.bfloat16),
+        pltpu.SemaphoreType.DMA((count + 1,)),
+    ]
+
+
+def open_kernel(size, first, meta_in, last, pieces, query, *refs):
+    filters = refs[:-9]
+    shifted, term, out, reverse, meta, last_spans, result, spans, sems = refs[-9:]
+    slots = query.shape[0] // STRETCH
+    width = pieces.shape[1]
+    scalars = pltpu.make_async_copy(meta_in, meta, sems.at[width // LANES])
+    scalars.start()
+    build_shifted(size, first, filters, reverse, shifted)
+    scalars.wait()
+    last_term(slots, meta, last, shifted, term, last_spans)
+    base = part_base(0, out.shape[1] // width, width)
+    stores = []
+    for index, start in enumerate(range(0, width, LANES)):
+        spread_part(pieces, start, spans.at[index])
+        stores.append(
+            conv_part(
+                lambda group: filter_rows(meta, shifted, base // GROUP_CH + group, slots),
+                base,
+                start,
+                term,
+                query,
+                out,
+                result.at[index],
+                spans.at[index],
+                sems.at[index],
+            )
+        )
+    for store in stores:
+        store.wait()
+
+
+def open_conv(size, first, meta, last, pieces, query_proj, group_count, lag_count, filters):
+    row_count, channels = query_proj.shape
+    padded = lag_count + SPAN
+    return pl.pallas_call(
+        functools.partial(open_kernel, size, first),
+        in_specs=[ANY_SPEC] + [VMEM_SPEC] * (3 + len(filters)),
+        out_specs=[VMEM_SPEC, VMEM_SPEC, HBM_SPEC],
+        out_shape=[
+            jax.ShapeDtypeStruct((group_count, GROUP_CH, padded), jnp.bfloat16),
+            jax.ShapeDtypeStruct((STRETCH, channels), jnp.float32),
+            jax.ShapeDtypeStruct((row_count, channels), jnp.bfloat16),
+        ],
+        scratch_shapes=[
+            pltpu.VMEM((group_count, padded), jnp.float32),
+            pltpu.SMEM(meta.shape, jnp.int32),
+            pltpu.VMEM((2, BLOCKS, LANES, SPAN), jnp.bfloat16),
+            *scratch(pieces.shape[1] // LANES, row_count),
+        ],
+        compiler_params=params(),
+        name="open_conv",
+    )(meta, last, pieces, query_proj, *filters)
+
+
+def near_kernel(size, steps, next_step, meta_in, shifted, term, query, before, *refs):
+    parts = refs[: len(steps)]
+    out, ready, meta, result, spans, sems = refs[len(steps) :]
+    slots = query.shape[0] // STRETCH
+    width = parts[0].shape[1]
+    places = [(index, start) for index in range(len(steps)) for start in range(0, width, LANES)]
+    scalars = pltpu.make_async_copy(meta_in, meta, sems.at[len(places)])
+    scalars.start()
+    for number, (index, start) in enumerate(places[: len(places) // 2]):
+        spread_part(parts[index], start, spans.at[number])
+    scalars.wait()
+    stores = []
+    for number, (index, start) in enumerate(places):
+        if number >= len(places) // 2:
+            spread_part(parts[index], start, spans.at[number])
+        base = part_base(steps[index], size, width)
+        stores.append(
+            conv_part(
+                lambda group, base=base: filter_rows(meta, shifted, base // GROUP_CH + group, slots),
+                base,
+                start,
+                term,
+                query,
+                out,
+                result.at[number],
+                spans.at[number],
+                sems.at[number],
+            )
+        )
+    base = part_base(next_step, size, width)
+    for group in range(width // GROUP_CH):
+        ready[group] = filter_rows(meta, shifted, base // GROUP_CH + group, slots)
+    for store in stores:
+        store.wait()
+
+
+def near_conv(size, steps, next_step, meta, parts, shifted, term, query_proj, before):
+    row_count, channels = query_proj.shape
+    width = channels // size
+    slots = row_count // STRETCH
+    return pl.pallas_call(
+        functools.partial(near_kernel, size, steps, next_step),
+        in_specs=[ANY_SPEC] + [VMEM_SPEC] * 3 + [HBM_SPEC] + [VMEM_SPEC] * len(parts),
+        out_specs=[HBM_SPEC, VMEM_SPEC],
+        out_shape=[
+            jax.ShapeDtypeStruct((row_count, channels), jnp.bfloat16),
+            jax.ShapeDtypeStruct((width // GROUP_CH, slots * GROUP_CH, SENT * SPAN), jnp.bfloat16),
+        ],
+        input_output_aliases={4: 0},
+        scratch_shapes=[
+            pltpu.SMEM(meta.shape, jnp.int32),
+            *scratch(len(parts) * width // LANES, row_count),
+        ],
+        compiler_params=params(),
+        name="near_conv",
+    )(meta, shifted, term, query_proj, before, *parts)
+
+
+def far_kernel(size, step, pieces, ready, term, query, before, out, result, spans, sems):
+    width = pieces.shape[1]
+    base = part_base(step, size, width)
+    stores = []
+    for index, start in enumerate(range(0, width, LANES)):
+        spread_part(pieces, start, spans.at[index])
+        stores.append(
+            conv_part(
+                lambda group: ready[group],
+                base,
+                start,
+                term,
+                query,
+                out,
+                result.at[index],
+                spans.at[index],
+                sems.at[index],
+            )
+        )
+    for store in stores:
+        store.wait()
+
+
+def far_conv(size, step, pieces, ready, term, query_proj, before):
+    row_count, channels = query_proj.shape
+    return pl.pallas_call(
+        functools.partial(far_kernel, size, step),
+        in_specs=[VMEM_SPEC] * 4 + [HBM_SPEC],
+        out_specs=HBM_SPEC,
+        out_shape=jax.ShapeDtypeStruct((row_count, channels), jnp.bfloat16),
+        input_output_aliases={4: 0},
+        scratch_shapes=scratch(pieces.shape[1] // LANES, row_count),
+        compiler_params=params(),
+        name="far_conv",
+    )(pieces, ready, term, query_proj, before)
+
+
+def shards(size, key_proj, value_proj, query_proj, filters, sources, owner):
+    row_count, channels = key_proj.shape
+    group_count, part = filters.shape
+    lag_count = size * part
+    tiles = part // LANES
+    by_parts = size == 4 and channels % (size * LANES) == 0
+    block = group_count * tiles
+    filter_rows = [0, block, block, 0] if by_parts else [block]
+    parts = len(filter_rows)
+    width = channels // parts
+    sends, extra, meta = gate(filter_rows, sources, owner, key_proj, value_proj, filters)
     last = last_rows(key_proj, value_proj)
     first = SLOTS * width
     if not by_parts:
@@ -569,25 +955,23 @@
             size, tiles, meta, last, pieces, query_proj, group_count, lag_count, [blocks]
         )[2]
 
-    def shift(value, step):
-        return lax.ppermute(value, "seq", [(z, (z + step) % size) for z in range(size)])
-
-    up, down, far = (shift(sends[step], step) for step in (1, size - 1, 2))
-    mine = pick(first, [up, down])
-    other = lax.ppermute(mine, "rep", [(0, 1), (1, 0)])
-    last, other, far = lax.optimization_barrier((last, other, far))
-    received = [sends[0], up, down, far]
+    def exchange(value, step):
+        return lax.ppermute(value, "seq", [(z, z ^ step) for z in range(size)])
+
+    far, near, cross = (exchange(sends[step], step) for step in STEPS[1:])
+    cross_filters = exchange(pick(first, far), 1)
+    last, cross_filters, cross = lax.optimization_barrier((last, cross_filters, cross))
+    received = [sends[0], far, near, cross]
 
     def merge_more(meta, received, extra):
-        more = [extra[0]] + [shift(extra[step], step) for step in range(1, size)]
-        return merge(size, width, meta, received, more)
+        more = [extra[0]] + [exchange(extra[step], step) for step in STEPS[1:]]
+        return merge(width, meta, received, more)
 
     def merge_plain(meta, received, extra):
-        return merge(size, width, meta, received)
+        return merge(width, meta, received)
 
     merged = lax.cond(meta[MANY] > 0, merge_more, merge_plain, meta, received, extra)
-    far_part = lax.ppermute(merged, "seq", [(0, 2), (2, 0), (1, 3), (3, 1)])
-    near_part = lax.ppermute(merged, "seq", [(0, 1), (1, 0), (2, 3), (3, 2)])
+    far_part, near_part = exchange(merged, 2), exchange(merged, 1)
     shifted, term, out = open_conv(
         size,
         first,
@@ -597,10 +981,10 @@
         query_proj,
         group_count,
         lag_count,
-        [filters, far, mine, other],
+        [filters, far, near, cross_filters],
     )
     far_part, out = lax.optimization_barrier((far_part, out))
-    last_part = lax.ppermute(far_part, "seq", [(0, 1), (1, 0), (2, 3), (3, 2)])
+    last_part = exchange(far_part, 1)
     out, ready = near_conv(
         size, (1, 2), 3, meta, [near_part, far_part], shifted, term, query_proj, out
     )
@@ -609,7 +993,7 @@
 
 def solution(mesh):
     return jax.shard_map(
-        functools.partial(shards, mesh.shape["seq"], mesh.shape["rep"]),
+        functools.partial(shards, mesh.shape["seq"]),
         mesh=mesh,
         in_specs=(
             P(("rep", "seq"), "ch"),

time: 43.4 us -> 42.6 us (0.982)
  transfers between devices with their start and end apart: 7 -> 7, of which waited for: 6 -> 6; matrix products, arithmetic and copies ran while one was open for 1% -> 1% of each run, Pallas kernels for 23% -> 24%
where the time goes in v11:
time: 42.6 us; the launch traced here: 42.4 us
  waiting for transfers between devices  15.8 us (37%)
  Pallas kernels  14.8 us (35%)
  starting transfers between devices  10.5 us (25%)
  between operations  0.7 us (2%)
  local copies, waits for them, and re-layouts  0.59 us (1%)
    ppermute x7, waiting for transfers between devices, exchange(): return lax.ppermute(value, 'seq', [(z, z ^ step) for z in range(size)])  15.8 us
    ppermute x7, starting transfers between devices, exchange(): return lax.ppermute(value, 'seq', [(z, z ^ step) for z in range(size)])  10.5 us
    pallas_call x1, Pallas kernels, open_conv(): pl.pallas_call(functools.partial(open_kernel, size, first), in_specs=[ANY...  5.45 us
    pallas_call x1, Pallas kernels, near_conv(): pl.pallas_call(functools.partial(near_kernel, size, steps, next_step), in...  3.41 us
    pallas_call x1, Pallas kernels, gate(): pl.pallas_call(functools.partial(gate_kernel, parts), in_specs=[HBM_SPEC]...  2.29 us
    pallas_call x1, Pallas kernels, far_conv(): pl.pallas_call(functools.partial(far_kernel, size, step), in_specs=[VMEM_...  1.89 us
    pallas_call x1, Pallas kernels, last_rows(): pl.pallas_call(last_rows_kernel, grid=(1,), in_specs=[block, block], out_...  1.16 us
  transfers between devices with their start and end apart: 7, of which 6 were waited for; matrix products, arithmetic and copies ran while one was open for 1% of the time, Pallas kernels for 24%

profile of v11, /device:TPU:0, one launch (start us, length us, event | category | flops | bytes accessed | tf_op | source)
XLA Modules:
  0.0 42.4 jit_solution(17879872450958480750)
XLA Ops:
  0.0 2.3 %gate.1 = (bf16[512,128]{1,0:T(8,128)(2,1)S(1)}, bf16[768,128]{1,0:T(8,128)(2,1)S(1)}, bf16[768,128]{1,0:T(8,128)(2,1)S(1)}, bf16[512,128]{1,0:T(8,128)(2,1)S(1)...) custom-call(s32[4]{0:T(128)} %sources_in.1, s32[16]{0:T(128)} %owner_in.1, bf16[512,1024]{1,0:T(8,128)(2,1)} %key.1, ...), custom_call_target="tpu_custom_call" | custom-call | tf_op jit(solution)/shard_map/gate/pallas_call | solution.py:134
  2.3 4.3 %collective-permute-start.3 = (bf16[768,128]{1,0:T(8,128)(2,1)S(1)}, bf16[768,128]{1,0:T(8,128)(2,1)S(1)}, u32[]{:S(2)}, u32[]{:S(2)}) collective-permute-start(bf16[768,128]{1,0:T(8,128)(2,1)S(1)} %get-tuple-element.59), channel_id=1, source_target_pairs={{0,8},{4,12},{8,0},{12,4},{1,9},{5,13},{9,1},{13,5},{2,10},{6,14},... | collective-permute-start | bytes 589832 | tf_op jit(solution)/shard_map/ppermute | solution.py:959
  6.6 1.4 %collective-permute-start.4 = (bf16[768,128]{1,0:T(8,128)(2,1)S(1)}, bf16[768,128]{1,0:T(8,128)(2,1)S(1)}, u32[]{:S(2)}, u32[]{:S(2)}) collective-permute-start(bf16[768,128]{1,0:T(8,128)(2,1)S(1)} %get-tuple-element.60), channel_id=1, source_target_pairs={{0,4},{4,0},{8,12},{12,8},{1,5},{5,1},{9,13},{13,9},{2,6},{6,2},{1... | collective-permute-start | bytes 589832 | tf_op jit(solution)/shard_map/ppermute | solution.py:959
  8.0 0.4 collective-permute-start.6
  8.4 8.6 %collective-permute-done.3.received.refs_1_ = bf16[768,128]{1,0:T(8,128)(2,1)S(1)} collective-permute-done((bf16[768,128]{1,0:T(8,128)(2,1)S(1)}, bf16[768,128]{1,0:T(8,128)(2,1)S(1)}, u32[]{:S(2)}, u32[]{:S(2)}) %collective-permute-start.3) | collective-permute-done | bytes 196640 | tf_op jit(solution)/shard_map/ppermute | solution.py:959
  16.9 0.2 collective-permute-start.5
  17.2 1.2 %last_rows.1.last = bf16[1024,128]{1,0:T(8,128)(2,1)S(1)} custom-call(bf16[512,1024]{1,0:T(8,128)(2,1)} %key.1, bf16[512,1024]{1,0:T(8,128)(2,1)} %value.1), custom_call_target="tpu_custom_call" | custom-call | tf_op jit(solution)/shard_map/last_rows/pallas_call | solution.py:715
  18.4 0.6 %slice.15 = s32[1]{0:T(128)} slice(s32[23]{0:T(128)S(1)} %get-tuple-element.57.meta_in), slice={[6:7]} | slice | bytes 8 | tf_op jit(solution)/shard_map/slice | solution.py:973
  19.6 0.6 %collective-permute-done.6 = bf16[512,128]{1,0:T(8,128)(2,1)S(1)} collective-permute-done((bf16[512,128]{1,0:T(8,128)(2,1)S(1)}, bf16[512,128]{1,0:T(8,128)(2,1)S(1)}, u32[]{:S(2)}, u32[]{:S(2)}) %collective-permute-start.6) | collective-permute-done | bytes 131104 | tf_op jit(solution)/shard_map/ppermute | solution.py:959
  20.2 1.0 %collective-permute-done.5.refs_3_ = bf16[256,128]{1,0:T(8,128)(2,1)S(1)} collective-permute-done((bf16[256,128]{1,0:T(8,128)(2,1)S(1)}, bf16[256,128]{1,0:T(8,128)(2,1)S(1)}, u32[]{:S(2)}, u32[]{:S(2)}) %collective-permute-start.5) | collective-permute-done | bytes 65568 | tf_op jit(solution)/shard_map/ppermute | solution.py:959
  21.2 0.0 collective-permute-done.4.refs_2_
  21.2 0.7 %conditional.1 = (bf16[3,256,128]{2,1,0:T(8,128)(2,1)S(1)}) conditional(s32[]{:T(128)} %bitcast.4, (s32[23]{0:T(128)S(1)}, bf16[512,128]{1,0:T(8,128)(2,1)S(1)}, bf16[768,128]{1,0:T(8,128)(2,1)S(1)}, bf16[768,128]{1,0:T(8,128)(2,1)S(1)}, bf16[512,128]{1,0:T(8,128)(2,1)S(1)}) %tuple.14, (bf16[4,256,128]{2,1,0:T(8,128)(2,1)S(1)}, s32[23]{0:T(128)S(1)}, ...), branch_computations={%region_0.0_spmd, %region_1.0_spmd} | conditional | bytes 1310848 | solution.py:973
  21.2 0.7 %merge.2 = bf16[3,256,128]{2,1,0:T(8,128)(2,1)S(1)} custom-call(s32[23]{0:T(128)S(1)} %get-tuple-element.30.meta, bf16[512,128]{1,0:T(8,128)(2,1)S(1)} %get-tuple-element.31.refs_0_, bf16[768,128]{1,0:T(8,128)(2,1)S(1)} %get-tuple-element.32.refs_1_, bf16[768,128]{1,0:T(8,128)(2,1)S(1)} %get-tuple-element.33.refs_2_, ...), custom_call_target="tpu_custom_call" | custom-call | tf_op jit(solution)/shard_map/cond/branch_0_fun/merge/pallas_call | solution.py:589
  21.9 2.7 %collective-permute-start.7 = (bf16[3,256,128]{2,1,0:T(8,128)(2,1)S(1)}, bf16[3,256,128]{2,1,0:T(8,128)(2,1)S(1)}, u32[]{:S(2)}, u32[]{:S(2)}) collective-permute-start(bf16[3,256,128]{2,1,0:T(8,128)(2,1)S(1)} %get-tuple-element.77.pieces), channel_id=1, source_target_pairs={{0,8},{4,12},{8,0},{12,4},{1,9},{5,13},{9,1},{13,5},{2,10},{6,14},... | collective-permute-start | bytes 589832 | tf_op jit(solution)/shard_map/ppermute | solution.py:959
  24.6 1.4 %collective-permute-start.9 = (bf16[3,256,128]{2,1,0:T(8,128)(2,1)S(1)}, bf16[3,256,128]{2,1,0:T(8,128)(2,1)S(1)}, u32[]{:S(2)}, u32[]{:S(2)}) collective-permute-start(bf16[3,256,128]{2,1,0:T(8,128)(2,1)S(1)} %get-tuple-element.77.pieces), channel_id=1, source_target_pairs={{0,4},{4,0},{8,12},{12,8},{1,5},{5,1},{9,13},{13,9},{2,6},{6,2},{1... | collective-permute-start | bytes 589832 | tf_op jit(solution)/shard_map/ppermute | solution.py:959
  26.0 0.0 copy-done.1
  26.0 0.0 copy-done
  26.0 5.5 %open_conv.1 = (bf16[64,16,2304]{2,1,0:T(8,128)(2,1)S(1)}, f32[128,1024]{1,0:T(8,128)S(1)}, bf16[512,1024]{1,0:T(8,128)(2,1)}) custom-call(s32[23]{0:T(128)S(1)} %get-tuple-element.57.meta_in, bf16[1024,128]{1,0:T(8,128)(2,1)S(1)} %last_rows.1.last, bf16[3,256,128]{2,1,0:T(8,128)(2,1)S(1)} %get-tuple-element.77.pieces, bf16[512,1024]{1,0:T(8,128)(2,1)S(1)} %copy-done, ...), custom_call_target="tpu_custom_call" | custom-call | tf_op jit(solution)/shard_map/open_conv/pallas_call | solution.py:821
  31.5 2.5 %collective-permute-done.7.refs_1_ = bf16[3,256,128]{2,1,0:T(8,128)(2,1)S(1)} collective-permute-done((bf16[3,256,128]{2,1,0:T(8,128)(2,1)S(1)}, bf16[3,256,128]{2,1,0:T(8,128)(2,1)S(1)}, u32[]{:S(2)}, u32[]{:S(2)}) %collective-permute-start.7) | collective-permute-done | bytes 196640 | tf_op jit(solution)/shard_map/ppermute | solution.py:959
  34.0 0.0 collective-permute-start.8
  34.0 1.1 %collective-permute-done.9.refs_0_ = bf16[3,256,128]{2,1,0:T(8,128)(2,1)S(1)} collective-permute-done((bf16[3,256,128]{2,1,0:T(8,128)(2,1)S(1)}, bf16[3,256,128]{2,1,0:T(8,128)(2,1)S(1)}, u32[]{:S(2)}, u32[]{:S(2)}) %collective-permute-start.9) | collective-permute-done | bytes 196640 | tf_op jit(solution)/shard_map/ppermute | solution.py:959
  35.0 3.4 %near_conv.1 = (bf16[512,1024]{1,0:T(8,128)(2,1)}, bf16[16,64,768]{2,1,0:T(8,128)(2,1)S(1)}) custom-call(s32[23]{0:T(128)S(1)} %get-tuple-element.57.meta_in, bf16[64,16,2304]{2,1,0:T(8,128)(2,1)S(1)} %get-tuple-element.68.shifted, f32[128,1024]{1,0:T(8,128)S(1)} %get-tuple-element.69.term, ...), custom_call_target="tpu_custom_call", output_to_operand_aliasing={{0}: (4, {})} | custom-call | tf_op jit(solution)/shard_map/near_conv/pallas_call | solution.py:881
  38.5 2.1 %collective-permute-done.8.pieces = bf16[3,256,128]{2,1,0:T(8,128)(2,1)S(1)} collective-permute-done((bf16[3,256,128]{2,1,0:T(8,128)(2,1)S(1)}, bf16[3,256,128]{2,1,0:T(8,128)(2,1)S(1)}, u32[]{:S(2)}, u32[]{:S(2)}) %collective-permute-start.8) | collective-permute-done | bytes 196640 | tf_op jit(solution)/shard_map/ppermute | solution.py:959
  40.6 1.9 %far_conv.1 = bf16[512,1024]{1,0:T(8,128)(2,1)} custom-call(bf16[3,256,128]{2,1,0:T(8,128)(2,1)S(1)} %collective-permute-done.8.pieces, bf16[16,64,768]{2,1,0:T(8,128)(2,1)S(1)} %get-tuple-element.71.ready, f32[128,1024]{1,0:T(8,128)S(1)} %get-tuple-element.69.term, bf16[512,1024]{1,0:T(8,128)(2,1)S(1)} %copy-done, ...), custom_call_target="tpu_custom_call", output_to_operand_aliasing={{}: (4, {})} | custom-call | tf_op jit(solution)/shard_map/far_conv/pallas_call | solution.py:924
  (3 shorter events, 0.0 us)
Async XLA Ops:
  0.0 26.0 %copy-start.1 = (bf16[64,512]{1,0:T(8,128)(2,1)S(1)}, bf16[64,512]{1,0:T(8,128)(2,1)}, u32[]{:S(2)}) copy-start(bf16[64,512]{1,0:T(8,128)(2,1)} %refs_0_.1) | copy-start | bytes 196612
  0.0 26.0 %copy-start = (bf16[512,1024]{1,0:T(8,128)(2,1)S(1)}, bf16[512,1024]{1,0:T(8,128)(2,1)}, u32[]{:S(2)}) copy-start(bf16[512,1024]{1,0:T(8,128)(2,1)} %query.5) | copy-start | bytes 3145732
  2.3 14.6 %collective-permute-start.3 = (bf16[768,128]{1,0:T(8,128)(2,1)S(1)}, bf16[768,128]{1,0:T(8,128)(2,1)S(1)}, u32[]{:S(2)}, u32[]{:S(2)}) collective-permute-start(bf16[768,128]{1,0:T(8,128)(2,1)S(1)} %get-tuple-element.59), channel_id=1, source_target_pairs={{0,8},{4,12},{8,0},{12,4},{1,9},{5,13},{9,1},{13,5},{2,10},{6,14},... | collective-permute-start | bytes 589832 | tf_op jit(solution)/shard_map/ppermute | solution.py:959
  6.6 14.6 %collective-permute-start.4 = (bf16[768,128]{1,0:T(8,128)(2,1)S(1)}, bf16[768,128]{1,0:T(8,128)(2,1)S(1)}, u32[]{:S(2)}, u32[]{:S(2)}) collective-permute-start(bf16[768,128]{1,0:T(8,128)(2,1)S(1)} %get-tuple-element.60), channel_id=1, source_target_pairs={{0,4},{4,0},{8,12},{12,8},{1,5},{5,1},{9,13},{13,9},{2,6},{6,2},{1... | collective-permute-start | bytes 589832 | tf_op jit(solution)/shard_map/ppermute | solution.py:959
  8.0 12.2 %collective-permute-start.6 = (bf16[512,128]{1,0:T(8,128)(2,1)S(1)}, bf16[512,128]{1,0:T(8,128)(2,1)S(1)}, u32[]{:S(2)}, u32[]{:S(2)}) collective-permute-start(bf16[512,128]{1,0:T(8,128)(2,1)S(1)} %get-tuple-element.61), channel_id=1, source_target_pairs={{0,12},{4,8},{8,4},{12,0},{1,13},{5,9},{9,5},{13,1},{2,14},{6,10},... | collective-permute-start | bytes 393224 | tf_op jit(solution)/shard_map/ppermute | solution.py:959
  16.9 4.3 %collective-permute-start.5 = (bf16[256,128]{1,0:T(8,128)(2,1)S(1)}, bf16[256,128]{1,0:T(8,128)(2,1)S(1)}, u32[]{:S(2)}, u32[]{:S(2)}) collective-permute-start(bf16[256,128]{1,0:T(8,128)(2,1)S(1)} %pick.1), channel_id=1, source_target_pairs={{0,4},{4,0},{8,12},{12,8},{1,5},{5,1},{9,13},{13,9},{2,6},{6,2},{1... | collective-permute-start | bytes 196616 | tf_op jit(solution)/shard_map/ppermute | solution.py:959
  21.9 12.1 %collective-permute-start.7 = (bf16[3,256,128]{2,1,0:T(8,128)(2,1)S(1)}, bf16[3,256,128]{2,1,0:T(8,128)(2,1)S(1)}, u32[]{:S(2)}, u32[]{:S(2)}) collective-permute-start(bf16[3,256,128]{2,1,0:T(8,128)(2,1)S(1)} %get-tuple-element.77.pieces), channel_id=1, source_target_pairs={{0,8},{4,12},{8,0},{12,4},{1,9},{5,13},{9,1},{13,5},{2,10},{6,14},... | collective-permute-start | bytes 589832 | tf_op jit(solution)/shard_map/ppermute | solution.py:959
  24.6 10.4 %collective-permute-start.9 = (bf16[3,256,128]{2,1,0:T(8,128)(2,1)S(1)}, bf16[3,256,128]{2,1,0:T(8,128)(2,1)S(1)}, u32[]{:S(2)}, u32[]{:S(2)}) collective-permute-start(bf16[3,256,128]{2,1,0:T(8,128)(2,1)S(1)} %get-tuple-element.77.pieces), channel_id=1, source_target_pairs={{0,4},{4,0},{8,12},{12,8},{1,5},{5,1},{9,13},{13,9},{2,6},{6,2},{1... | collective-permute-start | bytes 589832 | tf_op jit(solution)/shard_map/ppermute | solution.py:959
  34.0 6.6 %collective-permute-start.8 = (bf16[3,256,128]{2,1,0:T(8,128)(2,1)S(1)}, bf16[3,256,128]{2,1,0:T(8,128)(2,1)S(1)}, u32[]{:S(2)}, u32[]{:S(2)}) collective-permute-start(bf16[3,256,128]{2,1,0:T(8,128)(2,1)S(1)} %collective-permute-done.7.refs_1_), channel_id=1, source_target_pairs={{0,4},{4,0},{8,12},{12,8},{1,5},{5,1},{9,13},{13,9},{2,6},{6,2},{1... | collective-permute-start | bytes 589832 | tf_op jit(solution)/shard_map/ppermute | solution.py:959

commit v12 on v11

--- a/solution.py
+++ b/solution.py
@@ -53,13 +53,15 @@
     copies = [
         pltpu.make_async_copy(sources_in, sources, sems.at[0]),
         pltpu.make_async_copy(owner_in, owner, sems.at[1]),
-        pltpu.make_async_copy(key_in, key, sems.at[2]),
-        pltpu.make_async_copy(value_in, value, sems.at[3]),
-        pltpu.make_async_copy(filters_in, filters, sems.at[4]),
+        pltpu.make_async_copy(filters_in, filters, sems.at[2]),
     ]
+    for start in range(0, key.shape[0], STRETCH):
+        rows = pl.ds(start, STRETCH)
+        for number, (held, array) in enumerate(((key_in, key), (value_in, value))):
+            sem = sems.at[3 + start // STRETCH * 2 + number]
+            copies.append(pltpu.make_async_copy(held.at[rows], array.at[rows], sem))
     for copy in copies:
         copy.start()
-
     for copy in copies[:2]:
         copy.wait()
 
@@ -75,7 +77,14 @@
         return slot + jnp.where(mine, 1, 0)
 
     lax.fori_loop(0, stretch_count, target, 0)
-    for copy in copies[2:]:
+    copies[2].wait()
+    group_count = filters.shape[0]
+    for tile in range(filters.shape[1] // LANES):
+        piece = filters[:, pl.ds(tile * LANES, LANES)]
+        for send in sends:
+            if send.shape[0] > SLOTS * width:
+                send[pl.ds(SLOTS * width + tile * group_count, group_count), :] = piece
+    for copy in copies[3:]:
         copy.wait()
     holders = [owner[sources[w]] for w in range(SENT)]
     many = 0
@@ -114,12 +123,6 @@
                         fill(extra.at[step], 0)
 
     meta[MANY] = many
-    group_count = filters.shape[0]
-    for tile in range(filters.shape[1] // LANES):
-        piece = filters[:, pl.ds(tile * LANES, LANES)]
-        for send in sends:
-            if send.shape[0] > SLOTS * width:
-                send[pl.ds(SLOTS * width + tile * group_count, group_count), :] = piece
 
 
 def gate(filter_rows, sources, owner, key_proj, value_proj, filters):
@@ -148,7 +151,7 @@
             pltpu.VMEM(key_proj.shape, key_proj.dtype),
             pltpu.VMEM(value_proj.shape, value_proj.dtype),
             pltpu.VMEM(filters.shape, filters.dtype),
-            pltpu.SemaphoreType.DMA((5,)),
+            pltpu.SemaphoreType.DMA((3 + 2 * slots,)),
         ],
         compiler_params=params(),
         name="gate",
@@ -358,9 +361,13 @@
                 tile = tile + term[pl.ds(m * GROUP_CH, GROUP_CH), columns]
             gates = query[place, columns].astype(jnp.float32)
             result[place, :] = (gates * tile).astype(jnp.bfloat16)
-    store = pltpu.make_async_copy(result, out.at[:, columns], sem)
-    store.start()
-    return store
+    stores = []
+    for slot in range(slots):
+        place = pl.ds(slot * STRETCH, STRETCH)
+        store = pltpu.make_async_copy(result.at[place], out.at[place, columns], sem.at[slot])
+        store.start()
+        stores.append(store)
+    return stores
 
 
 def part_base(step, size, width):
@@ -372,7 +379,7 @@
     return [
         pltpu.VMEM((count, row_count, LANES), jnp.bfloat16),
         pltpu.VMEM((count, BLOCKS, LANES, SENT * SPAN), jnp.bfloat16),
-        pltpu.SemaphoreType.DMA((count + 1,)),
+        pltpu.SemaphoreType.DMA((count + 1, row_count // STRETCH)),
     ]
 
 
@@ -381,7 +388,7 @@
     shifted, term, out, reverse, meta, last_spans, result, spans, sems = refs[-9:]
     slots = query.shape[0] // STRETCH
     width = pieces.shape[1]
-    scalars = pltpu.make_async_copy(meta_in, meta, sems.at[width // LANES])
+    scalars = pltpu.make_async_copy(meta_in, meta, sems.at[width // LANES, 0])
     scalars.start()
     build_shifted(size, first, filters, reverse, shifted)
     scalars.wait()
@@ -390,7 +397,7 @@
     stores = []
     for index, start in enumerate(range(0, width, LANES)):
         spread_part(pieces, start, spans.at[index])
-        stores.append(
+        stores.extend(
             conv_part(
                 lambda group: filter_rows(meta, shifted, base // GROUP_CH + group, slots),
                 base,
@@ -436,7 +443,7 @@
     slots = query.shape[0] // STRETCH
     width = parts[0].shape[1]
     places = [(index, start) for index in range(len(steps)) for start in range(0, width, LANES)]
-    scalars = pltpu.make_async_copy(meta_in, meta, sems.at[len(places)])
+    scalars = pltpu.make_async_copy(meta_in, meta, sems.at[len(places), 0])
     scalars.start()
     for number, (index, start) in enumerate(places[: len(places) // 2]):
         spread_part(parts[index], start, spans.at[number])
@@ -446,7 +453,7 @@
         if number >= len(places) // 2:
             spread_part(parts[index], start, spans.at[number])
         base = part_base(steps[index], size, width)
-        stores.append(
+        stores.extend(
             conv_part(
                 lambda group, base=base: filter_rows(meta, shifted, base // GROUP_CH + group, slots),
                 base,
@@ -494,7 +501,7 @@
     stores = []
     for index, start in enumerate(range(0, width, LANES)):
         spread_part(pieces, start, spans.at[index])
-        stores.append(
+        stores.extend(
             conv_part(
                 lambda group: ready[group],
                 base,
@@ -556,7 +563,7 @@
             pltpu.VMEM(key_proj.shape, key_proj.dtype),
             pltpu.VMEM(value_proj.shape, value_proj.dtype),
             pltpu.VMEM(filters.shape, filters.dtype),
-            pltpu.SemaphoreType.DMA((5,)),
+            pltpu.SemaphoreType.DMA((3 + 2 * slots,)),
         ],
         compiler_params=params(),
         name="gate",
@@ -766,9 +773,13 @@
                 tile = tile + term[pl.ds(m * GROUP_CH, GROUP_CH), columns]
             gates = query[place, columns].astype(jnp.float32)
             result[place, :] = (gates * tile).astype(jnp.bfloat16)
-    store = pltpu.make_async_copy(result, out.at[:, columns], sem)
-    store.start()
-    return store
+    stores = []
+    for slot in range(slots):
+        place = pl.ds(slot * STRETCH, STRETCH)
+        store = pltpu.make_async_copy(result.at[place], out.at[place, columns], sem.at[slot])
+        store.start()
+        stores.append(store)
+    return stores
 
 
 def part_base(step, size, width):
@@ -780,7 +791,7 @@
     return [
         pltpu.VMEM((count, row_count, LANES), jnp.bfloat16),
         pltpu.VMEM((count, BLOCKS, LANES, SENT * SPAN), jnp.bfloat16),
-        pltpu.SemaphoreType.DMA((count + 1,)),
+        pltpu.SemaphoreType.DMA((count + 1, row_count // STRETCH)),
     ]
 
 
@@ -789,7 +800,7 @@
     shifted, term, out, reverse, meta, last_spans, result, spans, sems = refs[-9:]
     slots = query.shape[0] // STRETCH
     width = pieces.shape[1]
-    scalars = pltpu.make_async_copy(meta_in, meta, sems.at[width // LANES])
+    scalars = pltpu.make_async_copy(meta_in, meta, sems.at[width // LANES, 0])
     scalars.start()
     build_shifted(size, first, filters, reverse, shifted)
     scalars.wait()
@@ -798,7 +809,7 @@
     stores = []
     for index, start in enumerate(range(0, width, LANES)):
         spread_part(pieces, start, spans.at[index])
-        stores.append(
+        stores.extend(
             conv_part(
                 lambda group: filter_rows(meta, shifted, base // GROUP_CH + group, slots),
                 base,
@@ -844,7 +855,7 @@
     slots = query.shape[0] // STRETCH
     width = parts[0].shape[1]
     places = [(index, start) for index in range(len(steps)) for start in range(0, width, LANES)]
-    scalars = pltpu.make_async_copy(meta_in, meta, sems.at[len(places)])
+    scalars = pltpu.make_async_copy(meta_in, meta, sems.at[len(places), 0])
     scalars.start()
     for number, (index, start) in enumerate(places[: len(places) // 2]):
         spread_part(parts[index], start, spans.at[number])
@@ -854,7 +865,7 @@
         if number >= len(places) // 2:
             spread_part(parts[index], start, spans.at[number])
         base = part_base(steps[index], size, width)
-        stores.append(
+        stores.extend(
             conv_part(
                 lambda group, base=base: filter_rows(meta, shifted, base // GROUP_CH + group, slots),
                 base,
@@ -902,7 +913,7 @@
     stores = []
     for index, start in enumerate(range(0, width, LANES)):
         spread_part(pieces, start, spans.at[index])
-        stores.append(
+        stores.extend(
             conv_part(
                 lambda group: ready[group],
                 base,

time: 42.6 us -> 42.8 us (level)
  starting transfers between devices: 10.5 us -> 9.85 us
  waiting for transfers between devices: 15.8 us -> 16.4 us
    ppermute x7, starting transfers between devices: 10.5 us -> 9.85 us  [exchange(): return lax.ppermute(value, 'seq', [(z, z ^ step) for z in range(size)])]
    ppermute x7, waiting for transfers between devices: 15.8 us -> 16.4 us  [exchange(): return lax.ppermute(value, 'seq', [(z, z ^ step) for z in range(size)])]
where the time goes in v12:
time: 42.8 us; the launch traced here: 42.7 us
  waiting for transfers between devices  16.4 us (38%)
  Pallas kernels  15.2 us (36%)
  starting transfers between devices  9.85 us (23%)
  between operations  0.7 us (2%)
  local copies, waits for them, and re-layouts  0.59 us (1%)
    ppermute x7, waiting for transfers between devices, exchange(): return lax.ppermute(value, 'seq', [(z, z ^ step) for z in range(size)])  16.4 us
    ppermute x7, starting transfers between devices, exchange(): return lax.ppermute(value, 'seq', [(z, z ^ step) for z in range(size)])  9.85 us
    pallas_call x1, Pallas kernels, open_conv(): pl.pallas_call(functools.partial(open_kernel, size, first), in_specs=[ANY...  5.54 us
    pallas_call x1, Pallas kernels, near_conv(): pl.pallas_call(functools.partial(near_kernel, size, steps, next_step), in...  3.55 us
    pallas_call x1, Pallas kernels, gate(): pl.pallas_call(functools.partial(gate_kernel, parts), in_specs=[HBM_SPEC]...  2.31 us
    pallas_call x1, Pallas kernels, far_conv(): pl.pallas_call(functools.partial(far_kernel, size, step), in_specs=[VMEM_...  1.96 us
    pallas_call x1, Pallas kernels, last_rows(): pl.pallas_call(last_rows_kernel, grid=(1,), in_specs=[block, block], out_...  1.16 us
  transfers between devices with their start and end apart: 7, of which 6 were waited for; matrix products, arithmetic and copies ran while one was open for 1% of the time, Pallas kernels for 24%

profile of v12, /device:TPU:0, one launch (start us, length us, event | category | flops | bytes accessed | tf_op | source)
XLA Modules:
  0.0 42.7 jit_solution(9944190279059182130)
XLA Ops:
  0.0 2.3 %gate.1 = (bf16[512,128]{1,0:T(8,128)(2,1)S(1)}, bf16[768,128]{1,0:T(8,128)(2,1)S(1)}, bf16[768,128]{1,0:T(8,128)(2,1)S(1)}, bf16[512,128]{1,0:T(8,128)(2,1)S(1)...) custom-call(s32[4]{0:T(128)} %sources_in.1, s32[16]{0:T(128)} %owner_in.1, bf16[512,1024]{1,0:T(8,128)(2,1)} %key.1, ...), custom_call_target="tpu_custom_call" | custom-call | tf_op jit(solution)/shard_map/gate/pallas_call | solution.py:137
  2.3 4.3 %collective-permute-start.3 = (bf16[768,128]{1,0:T(8,128)(2,1)S(1)}, bf16[768,128]{1,0:T(8,128)(2,1)S(1)}, u32[]{:S(2)}, u32[]{:S(2)}) collective-permute-start(bf16[768,128]{1,0:T(8,128)(2,1)S(1)} %get-tuple-element.59), channel_id=1, source_target_pairs={{0,8},{4,12},{8,0},{12,4},{1,9},{5,13},{9,1},{13,5},{2,10},{6,14},... | collective-permute-start | bytes 589832 | tf_op jit(solution)/shard_map/ppermute | solution.py:970
  6.6 1.6 %collective-permute-start.4 = (bf16[768,128]{1,0:T(8,128)(2,1)S(1)}, bf16[768,128]{1,0:T(8,128)(2,1)S(1)}, u32[]{:S(2)}, u32[]{:S(2)}) collective-permute-start(bf16[768,128]{1,0:T(8,128)(2,1)S(1)} %get-tuple-element.60), channel_id=1, source_target_pairs={{0,4},{4,0},{8,12},{12,8},{1,5},{5,1},{9,13},{13,9},{2,6},{6,2},{1... | collective-permute-start | bytes 589832 | tf_op jit(solution)/shard_map/ppermute | solution.py:970
  8.2 0.0 collective-permute-start.6
  8.2 9.1 %collective-permute-done.3.received.refs_1_ = bf16[768,128]{1,0:T(8,128)(2,1)S(1)} collective-permute-done((bf16[768,128]{1,0:T(8,128)(2,1)S(1)}, bf16[768,128]{1,0:T(8,128)(2,1)S(1)}, u32[]{:S(2)}, u32[]{:S(2)}) %collective-permute-start.3) | collective-permute-done | bytes 196640 | tf_op jit(solution)/shard_map/ppermute | solution.py:970
  17.3 0.1 collective-permute-start.5
  17.4 1.2 %last_rows.1.last = bf16[1024,128]{1,0:T(8,128)(2,1)S(1)} custom-call(bf16[512,1024]{1,0:T(8,128)(2,1)} %key.1, bf16[512,1024]{1,0:T(8,128)(2,1)} %value.1), custom_call_target="tpu_custom_call" | custom-call | tf_op jit(solution)/shard_map/last_rows/pallas_call | solution.py:722
  18.6 0.6 %slice.15 = s32[1]{0:T(128)} slice(s32[23]{0:T(128)S(1)} %get-tuple-element.57.meta_in), slice={[6:7]} | slice | bytes 8 | tf_op jit(solution)/shard_map/slice | solution.py:984
  19.8 0.2 collective-permute-done.6
  20.0 1.6 %collective-permute-done.5.refs_3_ = bf16[256,128]{1,0:T(8,128)(2,1)S(1)} collective-permute-done((bf16[256,128]{1,0:T(8,128)(2,1)S(1)}, bf16[256,128]{1,0:T(8,128)(2,1)S(1)}, u32[]{:S(2)}, u32[]{:S(2)}) %collective-permute-start.5) | collective-permute-done | bytes 65568 | tf_op jit(solution)/shard_map/ppermute | solution.py:970
  21.6 0.0 collective-permute-done.4.refs_2_
  21.6 0.7 %conditional.1 = (bf16[3,256,128]{2,1,0:T(8,128)(2,1)S(1)}) conditional(s32[]{:T(128)} %bitcast.4, (s32[23]{0:T(128)S(1)}, bf16[512,128]{1,0:T(8,128)(2,1)S(1)}, bf16[768,128]{1,0:T(8,128)(2,1)S(1)}, bf16[768,128]{1,0:T(8,128)(2,1)S(1)}, bf16[512,128]{1,0:T(8,128)(2,1)S(1)}) %tuple.14, (bf16[4,256,128]{2,1,0:T(8,128)(2,1)S(1)}, s32[23]{0:T(128)S(1)}, ...), branch_computations={%region_0.0_spmd, %region_1.0_spmd} | conditional | bytes 1310848 | solution.py:984
  21.6 0.7 %merge.2 = bf16[3,256,128]{2,1,0:T(8,128)(2,1)S(1)} custom-call(s32[23]{0:T(128)S(1)} %get-tuple-element.30.meta, bf16[512,128]{1,0:T(8,128)(2,1)S(1)} %get-tuple-element.31.refs_0_, bf16[768,128]{1,0:T(8,128)(2,1)S(1)} %get-tuple-element.32.refs_1_, bf16[768,128]{1,0:T(8,128)(2,1)S(1)} %get-tuple-element.33.refs_2_, ...), custom_call_target="tpu_custom_call" | custom-call | tf_op jit(solution)/shard_map/cond/branch_0_fun/merge/pallas_call | solution.py:596
  22.2 2.5 %collective-permute-start.7 = (bf16[3,256,128]{2,1,0:T(8,128)(2,1)S(1)}, bf16[3,256,128]{2,1,0:T(8,128)(2,1)S(1)}, u32[]{:S(2)}, u32[]{:S(2)}) collective-permute-start(bf16[3,256,128]{2,1,0:T(8,128)(2,1)S(1)} %get-tuple-element.77.pieces), channel_id=1, source_target_pairs={{0,8},{4,12},{8,0},{12,4},{1,9},{5,13},{9,1},{13,5},{2,10},{6,14},... | collective-permute-start | bytes 589832 | tf_op jit(solution)/shard_map/ppermute | solution.py:970
  24.7 1.4 %collective-permute-start.9 = (bf16[3,256,128]{2,1,0:T(8,128)(2,1)S(1)}, bf16[3,256,128]{2,1,0:T(8,128)(2,1)S(1)}, u32[]{:S(2)}, u32[]{:S(2)}) collective-permute-start(bf16[3,256,128]{2,1,0:T(8,128)(2,1)S(1)} %get-tuple-element.77.pieces), channel_id=1, source_target_pairs={{0,4},{4,0},{8,12},{12,8},{1,5},{5,1},{9,13},{13,9},{2,6},{6,2},{1... | collective-permute-start | bytes 589832 | tf_op jit(solution)/shard_map/ppermute | solution.py:970
  26.1 0.0 copy-done.1
  26.1 0.0 copy-done
  26.1 5.5 %open_conv.1 = (bf16[64,16,2304]{2,1,0:T(8,128)(2,1)S(1)}, f32[128,1024]{1,0:T(8,128)S(1)}, bf16[512,1024]{1,0:T(8,128)(2,1)}) custom-call(s32[23]{0:T(128)S(1)} %get-tuple-element.57.meta_in, bf16[1024,128]{1,0:T(8,128)(2,1)S(1)} %last_rows.1.last, bf16[3,256,128]{2,1,0:T(8,128)(2,1)S(1)} %get-tuple-element.77.pieces, bf16[512,1024]{1,0:T(8,128)(2,1)S(1)} %copy-done, ...), custom_call_target="tpu_custom_call" | custom-call | tf_op jit(solution)/shard_map/open_conv/pallas_call | solution.py:832
  31.7 2.5 %collective-permute-done.7.refs_1_ = bf16[3,256,128]{2,1,0:T(8,128)(2,1)S(1)} collective-permute-done((bf16[3,256,128]{2,1,0:T(8,128)(2,1)S(1)}, bf16[3,256,128]{2,1,0:T(8,128)(2,1)S(1)}, u32[]{:S(2)}, u32[]{:S(2)}) %collective-permute-start.7) | collective-permute-done | bytes 196640 | tf_op jit(solution)/shard_map/ppermute | solution.py:970
  34.1 0.0 collective-permute-start.8
  34.1 1.1 %collective-permute-done.9.refs_0_ = bf16[3,256,128]{2,1,0:T(8,128)(2,1)S(1)} collective-permute-done((bf16[3,256,128]{2,1,0:T(8,128)(2,1)S(1)}, bf16[3,256,128]{2,1,0:T(8,128)(2,1)S(1)}, u32[]{:S(2)}, u32[]{:S(2)}) %collective-permute-start.9) | collective-permute-done | bytes 196640 | tf_op jit(solution)/shard_map/ppermute | solution.py:970
  35.2 3.5 %near_conv.1 = (bf16[512,1024]{1,0:T(8,128)(2,1)}, bf16[16,64,768]{2,1,0:T(8,128)(2,1)S(1)}) custom-call(s32[23]{0:T(128)S(1)} %get-tuple-element.57.meta_in, bf16[64,16,2304]{2,1,0:T(8,128)(2,1)S(1)} %get-tuple-element.68.shifted, f32[128,1024]{1,0:T(8,128)S(1)} %get-tuple-element.69.term, ...), custom_call_target="tpu_custom_call", output_to_operand_aliasing={{0}: (4, {})} | custom-call | tf_op jit(solution)/shard_map/near_conv/pallas_call | solution.py:892
  38.8 1.9 %collective-permute-done.8.pieces = bf16[3,256,128]{2,1,0:T(8,128)(2,1)S(1)} collective-permute-done((bf16[3,256,128]{2,1,0:T(8,128)(2,1)S(1)}, bf16[3,256,128]{2,1,0:T(8,128)(2,1)S(1)}, u32[]{:S(2)}, u32[]{:S(2)}) %collective-permute-start.8) | collective-permute-done | bytes 196640 | tf_op jit(solution)/shard_map/ppermute | solution.py:970
  40.7 2.0 %far_conv.1 = bf16[512,1024]{1,0:T(8,128)(2,1)} custom-call(bf16[3,256,128]{2,1,0:T(8,128)(2,1)S(1)} %collective-permute-done.8.pieces, bf16[16,64,768]{2,1,0:T(8,128)(2,1)S(1)} %get-tuple-element.71.ready, f32[128,1024]{1,0:T(8,128)S(1)} %get-tuple-element.69.term, bf16[512,1024]{1,0:T(8,128)(2,1)S(1)} %copy-done, ...), custom_call_target="tpu_custom_call", output_to_operand_aliasing={{}: (4, {})} | custom-call | tf_op jit(solution)/shard_map/far_conv/pallas_call | solution.py:935
  (3 shorter events, 0.0 us)
Async XLA Ops:
  0.0 26.1 %copy-start.1 = (bf16[64,512]{1,0:T(8,128)(2,1)S(1)}, bf16[64,512]{1,0:T(8,128)(2,1)}, u32[]{:S(2)}) copy-start(bf16[64,512]{1,0:T(8,128)(2,1)} %refs_0_.1) | copy-start | bytes 196612
  0.0 26.1 %copy-start = (bf16[512,1024]{1,0:T(8,128)(2,1)S(1)}, bf16[512,1024]{1,0:T(8,128)(2,1)}, u32[]{:S(2)}) copy-start(bf16[512,1024]{1,0:T(8,128)(2,1)} %query.5) | copy-start | bytes 3145732
  2.3 15.0 %collective-permute-start.3 = (bf16[768,128]{1,0:T(8,128)(2,1)S(1)}, bf16[768,128]{1,0:T(8,128)(2,1)S(1)}, u32[]{:S(2)}, u32[]{:S(2)}) collective-permute-start(bf16[768,128]{1,0:T(8,128)(2,1)S(1)} %get-tuple-element.59), channel_id=1, source_target_pairs={{0,8},{4,12},{8,0},{12,4},{1,9},{5,13},{9,1},{13,5},{2,10},{6,14},... | collective-permute-start | bytes 589832 | tf_op jit(solution)/shard_map/ppermute | solution.py:970
  6.6 15.0 %collective-permute-start.4 = (bf16[768,128]{1,0:T(8,128)(2,1)S(1)}, bf16[768,128]{1,0:T(8,128)(2,1)S(1)}, u32[]{:S(2)}, u32[]{:S(2)}) collective-permute-start(bf16[768,128]{1,0:T(8,128)(2,1)S(1)} %get-tuple-element.60), channel_id=1, source_target_pairs={{0,4},{4,0},{8,12},{12,8},{1,5},{5,1},{9,13},{13,9},{2,6},{6,2},{1... | collective-permute-start | bytes 589832 | tf_op jit(solution)/shard_map/ppermute | solution.py:970
  8.2 11.8 %collective-permute-start.6 = (bf16[512,128]{1,0:T(8,128)(2,1)S(1)}, bf16[512,128]{1,0:T(8,128)(2,1)S(1)}, u32[]{:S(2)}, u32[]{:S(2)}) collective-permute-start(bf16[512,128]{1,0:T(8,128)(2,1)S(1)} %get-tuple-element.61), channel_id=1, source_target_pairs={{0,12},{4,8},{8,4},{12,0},{1,13},{5,9},{9,5},{13,1},{2,14},{6,10},... | collective-permute-start | bytes 393224 | tf_op jit(solution)/shard_map/ppermute | solution.py:970
  17.3 4.3 %collective-permute-start.5 = (bf16[256,128]{1,0:T(8,128)(2,1)S(1)}, bf16[256,128]{1,0:T(8,128)(2,1)S(1)}, u32[]{:S(2)}, u32[]{:S(2)}) collective-permute-start(bf16[256,128]{1,0:T(8,128)(2,1)S(1)} %pick.1), channel_id=1, source_target_pairs={{0,4},{4,0},{8,12},{12,8},{1,5},{5,1},{9,13},{13,9},{2,6},{6,2},{1... | collective-permute-start | bytes 196616 | tf_op jit(solution)/shard_map/ppermute | solution.py:970
  22.2 11.9 %collective-permute-start.7 = (bf16[3,256,128]{2,1,0:T(8,128)(2,1)S(1)}, bf16[3,256,128]{2,1,0:T(8,128)(2,1)S(1)}, u32[]{:S(2)}, u32[]{:S(2)}) collective-permute-start(bf16[3,256,128]{2,1,0:T(8,128)(2,1)S(1)} %get-tuple-element.77.pieces), channel_id=1, source_target_pairs={{0,8},{4,12},{8,0},{12,4},{1,9},{5,13},{9,1},{13,5},{2,10},{6,14},... | collective-permute-start | bytes 589832 | tf_op jit(solution)/shard_map/ppermute | solution.py:970
  24.7 10.5 %collective-permute-start.9 = (bf16[3,256,128]{2,1,0:T(8,128)(2,1)S(1)}, bf16[3,256,128]{2,1,0:T(8,128)(2,1)S(1)}, u32[]{:S(2)}, u32[]{:S(2)}) collective-permute-start(bf16[3,256,128]{2,1,0:T(8,128)(2,1)S(1)} %get-tuple-element.77.pieces), channel_id=1, source_target_pairs={{0,4},{4,0},{8,12},{12,8},{1,5},{5,1},{9,13},{13,9},{2,6},{6,2},{1... | collective-permute-start | bytes 589832 | tf_op jit(solution)/shard_map/ppermute | solution.py:970
  34.1 6.6 %collective-permute-start.8 = (bf16[3,256,128]{2,1,0:T(8,128)(2,1)S(1)}, bf16[3,256,128]{2,1,0:T(8,128)(2,1)S(1)}, u32[]{:S(2)}, u32[]{:S(2)}) collective-permute-start(bf16[3,256,128]{2,1,0:T(8,128)(2,1)S(1)} %collective-permute-done.7.refs_1_), channel_id=1, source_target_pairs={{0,4},{4,0},{8,12},{12,8},{1,5},{5,1},{9,13},{13,9},{2,6},{6,2},{1... | collective-permute-start | bytes 589832 | tf_op jit(solution)/shard_map/ppermute | solution.py:970

commit v13 on v11

--- a/solution.py
+++ b/solution.py
@@ -960,17 +960,18 @@
 
     far, near, cross = (exchange(sends[step], step) for step in STEPS[1:])
     cross_filters = exchange(pick(first, far), 1)
-    last, cross_filters, cross = lax.optimization_barrier((last, cross_filters, cross))
-    received = [sends[0], far, near, cross]
-
-    def merge_more(meta, received, extra):
-        more = [extra[0]] + [exchange(extra[step], step) for step in STEPS[1:]]
-        return merge(width, meta, received, more)
-
-    def merge_plain(meta, received, extra):
-        return merge(width, meta, received)
-
-    merged = lax.cond(meta[MANY] > 0, merge_more, merge_plain, meta, received, extra)
+
+    def more(extra):
+        return [extra[0]] + [exchange(extra[step], step) for step in STEPS[1:]]
+
+    def none(extra):
+        return [extra[step] for step in STEPS]
+
+    extras = lax.cond(meta[MANY] > 0, more, none, extra)
+    last, cross_filters, extras, cross = lax.optimization_barrier(
+        (last, cross_filters, extras, cross)
+    )
+    merged = merge(width, meta, [sends[0], far, near, cross], extras)
     far_part, near_part = exchange(merged, 2), exchange(merged, 1)
     shifted, term, out = open_conv(
         size,

time: 42.6 us -> 44.3 us (1.040)
  waiting for transfers between devices: 15.8 us -> 17.5 us
  starting transfers between devices: 10.5 us -> 9.38 us
  local copies, waits for them, and re-layouts: 0.59 us -> 1.28 us
  Pallas kernels: 14.8 us -> 15.3 us
    ppermute x7, waiting for transfers between devices: 15.8 us -> 17.5 us  [exchange(): return lax.ppermute(value, 'seq', [(z, z ^ step) for z in range(size)])]
    ppermute x7, starting transfers between devices: 10.5 us -> 9.38 us  [exchange(): return lax.ppermute(value, 'seq', [(z, z ^ step) for z in range(size)])]
    squeeze x0 -> x2, local copies, waits for them, and re-layouts: none -> 0.69 us  [none(): return [extra[step] for step in STEPS]]
  transfers between devices with their start and end apart: 7 -> 7, of which waited for: 6 -> 5; matrix products, arithmetic and copies ran while one was open for 1% -> 3% of each run, Pallas kernels for 24% -> 23%
where the time goes in v13:
time: 44.3 us; the launch traced here: 44.1 us
  waiting for transfers between devices  17.5 us (40%)
  Pallas kernels  15.3 us (35%)
  starting transfers between devices  9.38 us (21%)
  local copies, waits for them, and re-layouts  1.28 us (3%)
  between operations  0.71 us (2%)
    ppermute x7, waiting for transfers between devices, exchange(): return lax.ppermute(value, 'seq', [(z, z ^ step) for z in range(size)])  17.5 us
    ppermute x7, starting transfers between devices, exchange(): return lax.ppermute(value, 'seq', [(z, z ^ step) for z in range(size)])  9.38 us
    pallas_call x1, Pallas kernels, open_conv(): pl.pallas_call(functools.partial(open_kernel, size, first), in_specs=[ANY...  5.47 us
    pallas_call x1, Pallas kernels, near_conv(): pl.pallas_call(functools.partial(near_kernel, size, steps, next_step), in...  3.4 us
    pallas_call x1, Pallas kernels, gate(): pl.pallas_call(functools.partial(gate_kernel, parts), in_specs=[HBM_SPEC]...  2.29 us
    pallas_call x1, Pallas kernels, far_conv(): pl.pallas_call(functools.partial(far_kernel, size, step), in_specs=[VMEM_...  1.9 us
    pallas_call x1, Pallas kernels, last_rows(): pl.pallas_call(last_rows_kernel, grid=(1,), in_specs=[block, block], out_...  1.16 us
    pallas_call x1, Pallas kernels, merge(): pl.pallas_call(functools.partial(merge_kernel, width), in_specs=[SMEM_SPE...  1.06 us
  transfers between devices with their start and end apart: 7, of which 5 were waited for; matrix products, arithmetic and copies ran while one was open for 3% of the time, Pallas kernels for 23%

profile of v13, /device:TPU:0, one launch (start us, length us, event | category | flops | bytes accessed | tf_op | source)
XLA Modules:
  0.0 44.1 jit_solution(11307946208124743860)
XLA Ops:
  0.0 2.3 %gate.1 = (bf16[512,128]{1,0:T(8,128)(2,1)S(1)}, bf16[768,128]{1,0:T(8,128)(2,1)S(1)}, bf16[768,128]{1,0:T(8,128)(2,1)S(1)}, bf16[512,128]{1,0:T(8,128)(2,1)S(1)...) custom-call(s32[4]{0:T(128)} %sources_in.1, s32[16]{0:T(128)} %owner_in.1, bf16[512,1024]{1,0:T(8,128)(2,1)} %key.1, ...), custom_call_target="tpu_custom_call" | custom-call | tf_op jit(solution)/shard_map/gate/pallas_call | solution.py:134
  2.3 4.7 %collective-permute-start.3 = (bf16[768,128]{1,0:T(8,128)(2,1)S(1)}, bf16[768,128]{1,0:T(8,128)(2,1)S(1)}, u32[]{:S(2)}, u32[]{:S(2)}) collective-permute-start(bf16[768,128]{1,0:T(8,128)(2,1)S(1)} %get-tuple-element.38), channel_id=1, source_target_pairs={{0,8},{4,12},{8,0},{12,4},{1,9},{5,13},{9,1},{13,5},{2,10},{6,14},... | collective-permute-start | bytes 589832 | tf_op jit(solution)/shard_map/ppermute | solution.py:959
  7.0 0.9 %collective-permute-start.6 = (bf16[512,128]{1,0:T(8,128)(2,1)S(1)}, bf16[512,128]{1,0:T(8,128)(2,1)S(1)}, u32[]{:S(2)}, u32[]{:S(2)}) collective-permute-start(bf16[512,128]{1,0:T(8,128)(2,1)S(1)} %get-tuple-element.45), channel_id=1, source_target_pairs={{0,12},{4,8},{8,4},{12,0},{1,13},{5,9},{9,5},{13,1},{2,14},{6,10},... | collective-permute-start | bytes 393224 | tf_op jit(solution)/shard_map/ppermute | solution.py:959
  7.9 0.6 %slice.26 = s32[1]{0:T(128)} slice(s32[23]{0:T(128)S(1)} %get-tuple-element.36.meta.meta_in), slice={[6:7]} | slice | bytes 8 | tf_op jit(solution)/shard_map/slice | solution.py:970
  9.2 0.7 %conditional.1 = (bf16[256,128]{1,0:T(8,128)(2,1)}, bf16[256,128]{1,0:T(8,128)(2,1)}, bf16[256,128]{1,0:T(8,128)(2,1)}, bf16[4,256,128]{2,1,0:T(8,128)(2,1)S(1)}, bf16[4,256,128]{2,1,0:T(8,128)(2,1)S(1)}) conditional(s32[]{:T(128)} %bitcast.6, bf16[4,256,128]{2,1,0:T(8,128)(2,1)S(1)} %get-tuple-element.40, ...), branch_computations={%region_0.0_spmd, %region_1.0_spmd} | conditional | bytes 1179808 | solution.py:970
  9.2 0.7 %slice_bitcast_fusion = (bf16[256,128]{1,0:T(8,128)(2,1)}, bf16[256,128]{1,0:T(8,128)(2,1)}, bf16[256,128]{1,0:T(8,128)(2,1)}) fusion(bf16[4,256,128]{2,1,0:T(8,128)(2,1)S(1)} %param), kind=kLoop, calls=%fused_computation | loop fusion | bytes 393216 | tf_op jit(solution)/shard_map/cond/branch_0_fun/squeeze | solution.py:968
  9.9 0.0 collective-permute-start.4
  9.9 9.8 %collective-permute-done.3.received.refs_1_ = bf16[768,128]{1,0:T(8,128)(2,1)S(1)} collective-permute-done((bf16[768,128]{1,0:T(8,128)(2,1)S(1)}, bf16[768,128]{1,0:T(8,128)(2,1)S(1)}, u32[]{:S(2)}, u32[]{:S(2)}) %collective-permute-start.3) | collective-permute-done | bytes 196640 | tf_op jit(solution)/shard_map/ppermute | solution.py:959
  19.7 0.1 collective-permute-start.5
  19.8 1.2 %last_rows.1.last = bf16[1024,128]{1,0:T(8,128)(2,1)S(1)} custom-call(bf16[512,1024]{1,0:T(8,128)(2,1)} %key.1, bf16[512,1024]{1,0:T(8,128)(2,1)} %value.1), custom_call_target="tpu_custom_call" | custom-call | tf_op jit(solution)/shard_map/last_rows/pallas_call | solution.py:715
  21.0 0.0 collective-permute-done.6.refs_3_
  21.0 3.0 %collective-permute-done.5.refs_3_ = bf16[256,128]{1,0:T(8,128)(2,1)S(1)} collective-permute-done((bf16[256,128]{1,0:T(8,128)(2,1)S(1)}, bf16[256,128]{1,0:T(8,128)(2,1)S(1)}, u32[]{:S(2)}, u32[]{:S(2)}) %collective-permute-start.5) | collective-permute-done | bytes 65568 | tf_op jit(solution)/shard_map/ppermute | solution.py:959
  24.0 0.0 collective-permute-done.4.refs_2_
  24.0 1.1 %merge.1.pieces = bf16[3,256,128]{2,1,0:T(8,128)(2,1)S(1)} custom-call(s32[23]{0:T(128)S(1)} %get-tuple-element.36.meta.meta_in, bf16[512,128]{1,0:T(8,128)(2,1)S(1)} %get-tuple-element.37.refs_0_, bf16[768,128]{1,0:T(8,128)(2,1)S(1)} %collective-permute-done.3.received.refs_1_, bf16[768,128]{1,0:T(8,128)(2,1)S(1)} %collective-permute-done.4.refs_2_, ...), custom_call_target="tpu_custom_call" | custom-call | tf_op jit(solution)/shard_map/merge/pallas_call | solution.py:589
  25.0 1.6 %collective-permute-start.7 = (bf16[3,256,128]{2,1,0:T(8,128)(2,1)S(1)}, bf16[3,256,128]{2,1,0:T(8,128)(2,1)S(1)}, u32[]{:S(2)}, u32[]{:S(2)}) collective-permute-start(bf16[3,256,128]{2,1,0:T(8,128)(2,1)S(1)} %merge.1.pieces), channel_id=1, source_target_pairs={{0,8},{4,12},{8,0},{12,4},{1,9},{5,13},{9,1},{13,5},{2,10},{6,14},... | collective-permute-start | bytes 589832 | tf_op jit(solution)/shard_map/ppermute | solution.py:959
  26.6 2.0 %collective-permute-start.9 = (bf16[3,256,128]{2,1,0:T(8,128)(2,1)S(1)}, bf16[3,256,128]{2,1,0:T(8,128)(2,1)S(1)}, u32[]{:S(2)}, u32[]{:S(2)}) collective-permute-start(bf16[3,256,128]{2,1,0:T(8,128)(2,1)S(1)} %merge.1.pieces), channel_id=1, source_target_pairs={{0,4},{4,0},{8,12},{12,8},{1,5},{5,1},{9,13},{13,9},{2,6},{6,2},{1... | collective-permute-start | bytes 589832 | tf_op jit(solution)/shard_map/ppermute | solution.py:959
  28.6 0.0 copy-done
  28.6 5.5 %open_conv.1 = (bf16[64,16,2304]{2,1,0:T(8,128)(2,1)S(1)}, f32[128,1024]{1,0:T(8,128)S(1)}, bf16[512,1024]{1,0:T(8,128)(2,1)}) custom-call(s32[23]{0:T(128)S(1)} %get-tuple-element.36.meta.meta_in, bf16[1024,128]{1,0:T(8,128)(2,1)S(1)} %last_rows.1.last, bf16[3,256,128]{2,1,0:T(8,128)(2,1)S(1)} %merge.1.pieces, bf16[512,1024]{1,0:T(8,128)(2,1)S(1)} %copy-done, ...), custom_call_target="tpu_custom_call" | custom-call | tf_op jit(solution)/shard_map/open_conv/pallas_call | solution.py:821
  34.1 1.8 %collective-permute-done.7.refs_1_ = bf16[3,256,128]{2,1,0:T(8,128)(2,1)S(1)} collective-permute-done((bf16[3,256,128]{2,1,0:T(8,128)(2,1)S(1)}, bf16[3,256,128]{2,1,0:T(8,128)(2,1)S(1)}, u32[]{:S(2)}, u32[]{:S(2)}) %collective-permute-start.7) | collective-permute-done | bytes 196640 | tf_op jit(solution)/shard_map/ppermute | solution.py:959
  35.9 0.0 collective-permute-start.8
  35.9 0.1 collective-permute-done.9.refs_0_
  36.0 3.4 %near_conv.1 = (bf16[512,1024]{1,0:T(8,128)(2,1)}, bf16[16,64,768]{2,1,0:T(8,128)(2,1)S(1)}) custom-call(s32[23]{0:T(128)S(1)} %get-tuple-element.36.meta.meta_in, bf16[64,16,2304]{2,1,0:T(8,128)(2,1)S(1)} %get-tuple-element.55.shifted, f32[128,1024]{1,0:T(8,128)S(1)} %get-tuple-element.56.term, ...), custom_call_target="tpu_custom_call", output_to_operand_aliasing={{0}: (4, {})} | custom-call | tf_op jit(solution)/shard_map/near_conv/pallas_call | solution.py:881
  39.4 2.8 %collective-permute-done.8.pieces = bf16[3,256,128]{2,1,0:T(8,128)(2,1)S(1)} collective-permute-done((bf16[3,256,128]{2,1,0:T(8,128)(2,1)S(1)}, bf16[3,256,128]{2,1,0:T(8,128)(2,1)S(1)}, u32[]{:S(2)}, u32[]{:S(2)}) %collective-permute-start.8) | collective-permute-done | bytes 196640 | tf_op jit(solution)/shard_map/ppermute | solution.py:959
  42.2 1.9 %far_conv.1 = bf16[512,1024]{1,0:T(8,128)(2,1)} custom-call(bf16[3,256,128]{2,1,0:T(8,128)(2,1)S(1)} %collective-permute-done.8.pieces, bf16[16,64,768]{2,1,0:T(8,128)(2,1)S(1)} %get-tuple-element.58.ready, f32[128,1024]{1,0:T(8,128)S(1)} %get-tuple-element.56.term, bf16[512,1024]{1,0:T(8,128)(2,1)S(1)} %copy-done, ...), custom_call_target="tpu_custom_call", output_to_operand_aliasing={{}: (4, {})} | custom-call | tf_op jit(solution)/shard_map/far_conv/pallas_call | solution.py:924
  (5 shorter events, 0.0 us)
Async XLA Ops:
  0.0 28.6 %copy-start.1 = (bf16[64,512]{1,0:T(8,128)(2,1)S(1)}, bf16[64,512]{1,0:T(8,128)(2,1)}, u32[]{:S(2)}) copy-start(bf16[64,512]{1,0:T(8,128)(2,1)} %refs_0_.1) | copy-start | bytes 196612
  0.0 28.6 %copy-start = (bf16[512,1024]{1,0:T(8,128)(2,1)S(1)}, bf16[512,1024]{1,0:T(8,128)(2,1)}, u32[]{:S(2)}) copy-start(bf16[512,1024]{1,0:T(8,128)(2,1)} %query.5) | copy-start | bytes 3145732
  2.3 17.4 %collective-permute-start.3 = (bf16[768,128]{1,0:T(8,128)(2,1)S(1)}, bf16[768,128]{1,0:T(8,128)(2,1)S(1)}, u32[]{:S(2)}, u32[]{:S(2)}) collective-permute-start(bf16[768,128]{1,0:T(8,128)(2,1)S(1)} %get-tuple-element.38), channel_id=1, source_target_pairs={{0,8},{4,12},{8,0},{12,4},{1,9},{5,13},{9,1},{13,5},{2,10},{6,14},... | collective-permute-start | bytes 589832 | tf_op jit(solution)/shard_map/ppermute | solution.py:959
  7.0 14.0 %collective-permute-start.6 = (bf16[512,128]{1,0:T(8,128)(2,1)S(1)}, bf16[512,128]{1,0:T(8,128)(2,1)S(1)}, u32[]{:S(2)}, u32[]{:S(2)}) collective-permute-start(bf16[512,128]{1,0:T(8,128)(2,1)S(1)} %get-tuple-element.45), channel_id=1, source_target_pairs={{0,12},{4,8},{8,4},{12,0},{1,13},{5,9},{9,5},{13,1},{2,14},{6,10},... | collective-permute-start | bytes 393224 | tf_op jit(solution)/shard_map/ppermute | solution.py:959
  9.9 14.1 %collective-permute-start.4 = (bf16[768,128]{1,0:T(8,128)(2,1)S(1)}, bf16[768,128]{1,0:T(8,128)(2,1)S(1)}, u32[]{:S(2)}, u32[]{:S(2)}) collective-permute-start(bf16[768,128]{1,0:T(8,128)(2,1)S(1)} %get-tuple-element.39), channel_id=1, source_target_pairs={{0,4},{4,0},{8,12},{12,8},{1,5},{5,1},{9,13},{13,9},{2,6},{6,2},{1... | collective-permute-start | bytes 589832 | tf_op jit(solution)/shard_map/ppermute | solution.py:959
  19.7 4.3 %collective-permute-start.5 = (bf16[256,128]{1,0:T(8,128)(2,1)S(1)}, bf16[256,128]{1,0:T(8,128)(2,1)S(1)}, u32[]{:S(2)}, u32[]{:S(2)}) collective-permute-start(bf16[256,128]{1,0:T(8,128)(2,1)S(1)} %pick.1), channel_id=1, source_target_pairs={{0,4},{4,0},{8,12},{12,8},{1,5},{5,1},{9,13},{13,9},{2,6},{6,2},{1... | collective-permute-start | bytes 196616 | tf_op jit(solution)/shard_map/ppermute | solution.py:959
  25.0 10.9 %collective-permute-start.7 = (bf16[3,256,128]{2,1,0:T(8,128)(2,1)S(1)}, bf16[3,256,128]{2,1,0:T(8,128)(2,1)S(1)}, u32[]{:S(2)}, u32[]{:S(2)}) collective-permute-start(bf16[3,256,128]{2,1,0:T(8,128)(2,1)S(1)} %merge.1.pieces), channel_id=1, source_target_pairs={{0,8},{4,12},{8,0},{12,4},{1,9},{5,13},{9,1},{13,5},{2,10},{6,14},... | collective-permute-start | bytes 589832 | tf_op jit(solution)/shard_map/ppermute | solution.py:959
  26.6 9.4 %collective-permute-start.9 = (bf16[3,256,128]{2,1,0:T(8,128)(2,1)S(1)}, bf16[3,256,128]{2,1,0:T(8,128)(2,1)S(1)}, u32[]{:S(2)}, u32[]{:S(2)}) collective-permute-start(bf16[3,256,128]{2,1,0:T(8,128)(2,1)S(1)} %merge.1.pieces), channel_id=1, source_target_pairs={{0,4},{4,0},{8,12},{12,8},{1,5},{5,1},{9,13},{13,9},{2,6},{6,2},{1... | collective-permute-start | bytes 589832 | tf_op jit(solution)/shard_map/ppermute | solution.py:959
  35.9 6.3 %collective-permute-start.8 = (bf16[3,256,128]{2,1,0:T(8,128)(2,1)S(1)}, bf16[3,256,128]{2,1,0:T(8,128)(2,1)S(1)}, u32[]{:S(2)}, u32[]{:S(2)}) collective-permute-start(bf16[3,256,128]{2,1,0:T(8,128)(2,1)S(1)} %collective-permute-done.7.refs_1_), channel_id=1, source_target_pairs={{0,4},{4,0},{8,12},{12,8},{1,5},{5,1},{9,13},{13,9},{2,6},{6,2},{1... | collective-permute-start | bytes 589832 | tf_op jit(solution)/shard_map/ppermute | solution.py:959

commit v14 on v10

--- a/solution.py
+++ b/solution.py
@@ -27,16 +27,7 @@
     return pltpu.CompilerParams(vmem_limit_bytes=VMEM_LIMIT)
 
 
-def steps_of(size):
-    return sorted(range(size), key=lambda step: (min(step, size - step), step))
-
-
-def partner(me, step, size):
-    return lax.rem(me + step, size)
-
-
-def sender(me, step, size):
-    return lax.rem(me + size - step, size)
+STEPS = (0, 2, 1, 3)
 
 
 PLACE = SENT
@@ -52,7 +43,7 @@
     return (rows_k * rows_v).astype(jnp.bfloat16).T
 
 
-def gate_kernel(size, parts, sources_in, owner_in, key_in, value_in, filters_in, *refs):
+def gate_kernel(parts, sources_in, owner_in, key_in, value_in, filters_in, *refs):
     sends = refs[:parts]
     extra, meta, sources, owner, key, value, filters, sems = refs[parts:]
     stretch_count = owner.shape[0]
@@ -102,7 +93,7 @@
             slot = lax.fori_loop(0, sources[w], count, 0)
             first = pl.multiple_of(slot * STRETCH, STRETCH)
             for step in range(parts):
-                part = partner(me, step, size) if parts > 1 else 0
+                part = me ^ step if parts > 1 else 0
                 base = part * width
 
                 def fill(target, offset, base=base):
@@ -124,18 +115,14 @@
 
     meta[MANY] = many
     group_count = filters.shape[0]
-    for send in sends:
-        rows = (send.shape[0] - SLOTS * width) * LANES // filters.shape[1]
-        groups = pl.ds(0, rows)
-        if 0 < rows < group_count:
-            groups = pl.ds(pl.multiple_of(lax.axis_index("rep") * rows, rows), rows)
-        for tile in range(filters.shape[1] // LANES if rows else 0):
-            send[pl.ds(SLOTS * width + tile * rows, rows), :] = filters[
-                groups, pl.ds(tile * LANES, LANES)
-            ]
-
-
-def gate(size, filter_rows, sources, owner, key_proj, value_proj, filters):
+    for tile in range(filters.shape[1] // LANES):
+        piece = filters[:, pl.ds(tile * LANES, LANES)]
+        for send in sends:
+            if send.shape[0] > SLOTS * width:
+                send[pl.ds(SLOTS * width + tile * group_count, group_count), :] = piece
+
+
+def gate(filter_rows, sources, owner, key_proj, value_proj, filters):
     row_count, channels = key_proj.shape
     slots = row_count // STRETCH
     parts = len(filter_rows)
@@ -145,7 +132,7 @@
         for operand in (sources, owner, key_proj, value_proj, filters)
     ]
     *sends, extra, meta = pl.pallas_call(
-        functools.partial(gate_kernel, size, parts),
+        functools.partial(gate_kernel, parts),
         in_specs=[HBM_SPEC] * 5,
         out_specs=[VMEM_SPEC] * (parts + 1) + [SMEM_SPEC],
         out_shape=[
@@ -169,54 +156,68 @@
     return sends, extra, meta
 
 
-def merge_kernel(size, width, meta, *refs):
-    received, extras, out = refs[:size], refs[size:-1], refs[-1]
+def third_kernel(meta, *refs):
+    arrived, out = refs[:-1], refs[-1]
     me = lax.axis_index("seq")
-
+    for block, step in zip(arrived, STEPS):
+
+        @pl.when(me ^ step == meta[SENT - 1])
+        def _(block=block):
+            out[...] = block[...]
+
+
+def third(meta, arrived):
+    return pl.pallas_call(
+        third_kernel,
+        in_specs=[SMEM_SPEC] + [VMEM_SPEC] * len(arrived),
+        out_specs=VMEM_SPEC,
+        out_shape=jax.ShapeDtypeStruct(arrived[0].shape, arrived[0].dtype),
+        compiler_params=params(),
+        name="third",
+    )(meta, *arrived)
+
+
+def merge_kernel(width, meta, late, *refs):
+    received, out = refs[:-1], refs[-1]
+    me = lax.axis_index("seq")
     for w in range(SENT):
         place = meta[PLACE + w]
         rows = pl.ds(pl.multiple_of(jnp.minimum(place, SLOTS - 1) * width, LANES), width)
-        for block, step in zip(received, steps_of(size)):
-
-            @pl.when(sender(me, step, size) == meta[w])
+        for block, step in zip(received, STEPS):
+
+            @pl.when(me ^ step == meta[w])
             def _(w=w, block=block, rows=rows):
                 out[w] = block[rows, :]
 
-    for w in range(SLOTS, SENT):
-        for step, extra in enumerate(extras):
-
-            @pl.when((sender(me, step, size) == meta[w]) & (meta[PLACE + w] >= SLOTS))
-            def _(w=w, extra=extra):
-                out[w] = extra[...]
-
-
-def merge(size, width, meta, received, extras=()):
+    @pl.when(meta[PLACE + SENT - 1] >= SLOTS)
+    def _():
+        out[SENT - 1] = late[...]
+
+
+def merge(width, meta, received, late):
     return pl.pallas_call(
-        functools.partial(merge_kernel, size, width),
-        in_specs=[SMEM_SPEC] + [VMEM_SPEC] * (size + len(extras)),
+        functools.partial(merge_kernel, width),
+        in_specs=[SMEM_SPEC] + [VMEM_SPEC] * (1 + len(received)),
         out_specs=VMEM_SPEC,
         out_shape=jax.ShapeDtypeStruct((SENT, width, LANES), received[0].dtype),
         compiler_params=params(),
         name="merge",
-    )(meta, *received, *extras)
-
-
-def pick_kernel(first, *refs):
-    received, out = refs[:-1], refs[-1]
-    for index, block in enumerate(received):
-        out[index] = block[pl.ds(first, out.shape[1]), :]
+    )(meta, late, *received)
+
+
+def pick_kernel(first, received, out):
+    out[...] = received[pl.ds(first, out.shape[0]), :]
 
 
 def pick(first, received):
-    rows = received[0].shape[0] - first
     return pl.pallas_call(
         functools.partial(pick_kernel, first),
-        in_specs=[VMEM_SPEC] * len(received),
+        in_specs=[VMEM_SPEC],
         out_specs=VMEM_SPEC,
-        out_shape=jax.ShapeDtypeStruct((len(received), rows, LANES), received[0].dtype),
+        out_shape=jax.ShapeDtypeStruct((received.shape[0] - first, LANES), received.dtype),
         compiler_params=params(),
         name="pick",
-    )(*received)
+    )(received)
 
 
 def lag_tiles(size, first, filters):
@@ -226,23 +227,17 @@
         for shard in range(size):
             for tile in range(first):
                 rows = pl.ds(tile * group_count, group_count)
-                yield pl.ds(0, group_count), shard * first + tile, blocks[shard, rows, :]
+                yield shard * first + tile, blocks[shard, rows, :]
         return
-    own, far, mine, other = filters
-    me, rep = lax.axis_index("seq"), lax.axis_index("rep")
+    own, far, near, cross = filters
+    me = lax.axis_index("seq")
     group_count = own.shape[0]
     tiles = own.shape[1] // LANES
-    half = group_count // 2
     for tile in range(tiles):
-        whole = pl.ds(0, group_count)
-        yield whole, me * tiles + tile, own[:, pl.ds(tile * LANES, LANES)]
-        rows = pl.ds(first + tile * group_count, group_count)
-        yield whole, sender(me, 2, size) * tiles + tile, far[rows, :]
-        for index, step in enumerate((1, size - 1)):
-            number = sender(me, step, size) * tiles + tile
-            for place, halves in ((rep, mine), (1 - rep, other)):
-                groups = pl.ds(pl.multiple_of(place * half, half), half)
-                yield groups, number, halves[index, pl.ds(tile * half, half), :]
+        yield me * tiles + tile, own[:, pl.ds(tile * LANES, LANES)]
+        for block, start, step in ((far, first, 2), (near, first, 1), (cross, 0, 3)):
+            rows = pl.ds(start + tile * group_count, group_count)
+            yield (me ^ step) * tiles + tile, block[rows, :]
 
 
 def build_shifted(size, first, filters, reverse, shifted):
@@ -251,11 +246,11 @@
     row = lax.broadcasted_iota(jnp.int32, (LANES, LANES), 0)
     column = lax.broadcasted_iota(jnp.int32, (LANES, LANES), 1)
     flip = jnp.where(row + column == LANES - 1, 1.0, 0.0).astype(jnp.bfloat16)
-    for groups, number, values in lag_tiles(size, first, filters):
+    for number, values in lag_tiles(size, first, filters):
         start = lag_count - LANES - number * LANES
         if not isinstance(start, int):
             start = pl.multiple_of(start, LANES)
-        reverse[groups, pl.ds(start, LANES)] = jnp.dot(
+        reverse[:, pl.ds(start, LANES)] = jnp.dot(
             values, flip, preferred_element_type=jnp.float32
         )
     reverse[:, pl.ds(lag_count, SPAN)] = jnp.zeros((group_count, SPAN), jnp.float32)
@@ -547,17 +542,17 @@
     )(pieces, ready, term, query_proj, before)
 
 
-def shards(size, reps, key_proj, value_proj, query_proj, filters, sources, owner):
+def shards(size, key_proj, value_proj, query_proj, filters, sources, owner):
     row_count, channels = key_proj.shape
     group_count, part = filters.shape
     lag_count = size * part
     tiles = part // LANES
-    by_parts = (size, reps) == (4, 2) and channels % (size * LANES) == 0
-    half = group_count // 2 * tiles
-    filter_rows = [0, half, 2 * half, half] if by_parts else [2 * half]
+    by_parts = size == 4 and channels % (size * LANES) == 0
+    block = group_count * tiles
+    filter_rows = [0, block, block, 0] if by_parts else [block]
     parts = len(filter_rows)
     width = channels // parts
-    sends, extra, meta = gate(size, filter_rows, sources, owner, key_proj, value_proj, filters)
+    sends, extra, meta = gate(filter_rows, sources, owner, key_proj, value_proj, filters)
     last = last_rows(key_proj, value_proj)
     first = SLOTS * width
     if not by_parts:
@@ -569,25 +564,24 @@
             size, tiles, meta, last, pieces, query_proj, group_count, lag_count, [blocks]
         )[2]
 
-    def shift(value, step):
-        return lax.ppermute(value, "seq", [(z, (z + step) % size) for z in range(size)])
-
-    up, down, far = (shift(sends[step], step) for step in (1, size - 1, 2))
-    mine = pick(first, [up, down])
-    other = lax.ppermute(mine, "rep", [(0, 1), (1, 0)])
-    last, other, far = lax.optimization_barrier((last, other, far))
-    received = [sends[0], up, down, far]
-
-    def merge_more(meta, received, extra):
-        more = [extra[0]] + [shift(extra[step], step) for step in range(1, size)]
-        return merge(size, width, meta, received, more)
-
-    def merge_plain(meta, received, extra):
-        return merge(size, width, meta, received)
-
-    merged = lax.cond(meta[MANY] > 0, merge_more, merge_plain, meta, received, extra)
-    far_part = lax.ppermute(merged, "seq", [(0, 2), (2, 0), (1, 3), (3, 1)])
-    near_part = lax.ppermute(merged, "seq", [(0, 1), (1, 0), (2, 3), (3, 2)])
+    def exchange(value, step):
+        return lax.ppermute(value, "seq", [(z, z ^ step) for z in range(size)])
+
+    far, near, cross = (exchange(sends[step], step) for step in STEPS[1:])
+    cross_filters = exchange(pick(first, far), 1)
+
+    def more(meta, extra):
+        arrived = [extra[0]] + [exchange(extra[step], step) for step in STEPS[1:]]
+        return third(meta, arrived)
+
+    def none(meta, extra):
+        return extra[0]
+
+    extra, far = lax.optimization_barrier((extra, far))
+    late = lax.cond(meta[MANY] > 0, more, none, meta, extra)
+    last, cross_filters, late, cross = lax.optimization_barrier((last, cross_filters, late, cross))
+    merged = merge(width, meta, [sends[0], far, near, cross], late)
+    far_part, near_part = exchange(merged, 2), exchange(merged, 1)
     shifted, term, out = open_conv(
         size,
         first,
@@ -597,10 +591,10 @@
         query_proj,
         group_count,
         lag_count,
-        [filters, far, mine, other],
+        [filters, far, near, cross_filters],
     )
     far_part, out = lax.optimization_barrier((far_part, out))
-    last_part = lax.ppermute(far_part, "seq", [(0, 1), (1, 0), (2, 3), (3, 2)])
+    last_part = exchange(far_part, 1)
     out, ready = near_conv(
         size, (1, 2), 3, meta, [near_part, far_part], shifted, term, query_proj, out
     )
@@ -609,7 +603,7 @@
 
 def solution(mesh):
     return jax.shard_map(
-        functools.partial(shards, mesh.shape["seq"], mesh.shape["rep"]),
+        functools.partial(shards, mesh.shape["seq"]),
         mesh=mesh,
         in_specs=(
             P(("rep", "seq"), "ch"),

time: 43.4 us -> 42.8 us (0.986)
  starting transfers between devices: 10.8 us -> 9.47 us
  waiting for transfers between devices: 16 us -> 16.9 us
    ppermute x7, starting transfers between devices: 10.8 us -> 9.47 us  [exchange(): return lax.ppermute(value, 'seq', [(z, z ^ step) for z in range(size)])]
    ppermute x7, waiting for transfers between devices: 16 us -> 16.9 us  [exchange(): return lax.ppermute(value, 'seq', [(z, z ^ step) for z in range(size)])]
where the time goes in v14:
time: 42.8 us; the launch traced here: 42.7 us
  waiting for transfers between devices  16.9 us (39%)
  Pallas kernels  15 us (35%)
  starting transfers between devices  9.47 us (22%)
  between operations  0.71 us (2%)
  local copies, waits for them, and re-layouts  0.59 us (1%)
    ppermute x7, waiting for transfers between devices, exchange(): return lax.ppermute(value, 'seq', [(z, z ^ step) for z in range(size)])  16.9 us
    ppermute x7, starting transfers between devices, exchange(): return lax.ppermute(value, 'seq', [(z, z ^ step) for z in range(size)])  9.47 us
    pallas_call x1, Pallas kernels, open_conv(): pl.pallas_call(functools.partial(open_kernel, size, first), in_specs=[ANY...  5.44 us
    pallas_call x1, Pallas kernels, near_conv(): pl.pallas_call(functools.partial(near_kernel, size, steps, next_step), in...  3.37 us
    pallas_call x1, Pallas kernels, gate(): pl.pallas_call(functools.partial(gate_kernel, parts), in_specs=[HBM_SPEC]...  2.48 us
    pallas_call x1, Pallas kernels, far_conv(): pl.pallas_call(functools.partial(far_kernel, size, step), in_specs=[VMEM_...  1.89 us
    pallas_call x1, Pallas kernels, last_rows(): pl.pallas_call(last_rows_kernel, grid=(1,), in_specs=[block, block], out_...  1.16 us
  transfers between devices with their start and end apart: 7, of which 6 were waited for; matrix products, arithmetic and copies ran while one was open for 1% of the time, Pallas kernels for 23%

profile of v14, /device:TPU:0, one launch (start us, length us, event | category | flops | bytes accessed | tf_op | source)
XLA Modules:
  0.0 42.7 jit_solution(13282157816677799136)
XLA Ops:
  0.0 0.0 copy-start.1
  0.0 2.5 %gate.1 = (bf16[512,128]{1,0:T(8,128)(2,1)S(1)}, bf16[768,128]{1,0:T(8,128)(2,1)S(1)}, bf16[768,128]{1,0:T(8,128)(2,1)S(1)}, bf16[512,128]{1,0:T(8,128)(2,1)S(1)...) custom-call(s32[4]{0:T(128)} %sources_in.1, s32[16]{0:T(128)} %owner_in.1, bf16[512,1024]{1,0:T(8,128)(2,1)} %key.1, ...), custom_call_target="tpu_custom_call" | custom-call | tf_op jit(solution)/shard_map/gate/pallas_call | solution.py:134
  2.5 4.3 %collective-permute-start.3 = (bf16[768,128]{1,0:T(8,128)(2,1)S(1)}, bf16[768,128]{1,0:T(8,128)(2,1)S(1)}, u32[]{:S(2)}, u32[]{:S(2)}) collective-permute-start(bf16[768,128]{1,0:T(8,128)(2,1)S(1)} %get-tuple-element.35), channel_id=1, source_target_pairs={{0,8},{4,12},{8,0},{12,4},{1,9},{5,13},{9,1},{13,5},{2,10},{6,14},... | collective-permute-start | bytes 589832 | tf_op jit(solution)/shard_map/ppermute | solution.py:568
  6.8 1.4 %collective-permute-start.6 = (bf16[768,128]{1,0:T(8,128)(2,1)S(1)}, bf16[768,128]{1,0:T(8,128)(2,1)S(1)}, u32[]{:S(2)}, u32[]{:S(2)}) collective-permute-start(bf16[768,128]{1,0:T(8,128)(2,1)S(1)} %get-tuple-element.42), channel_id=1, source_target_pairs={{0,4},{4,0},{8,12},{12,8},{1,5},{5,1},{9,13},{13,9},{2,6},{6,2},{1... | collective-permute-start | bytes 589832 | tf_op jit(solution)/shard_map/ppermute | solution.py:568
  8.2 0.1 collective-permute-start.5
  8.3 0.6 %slice.18 = s32[1]{0:T(128)} slice(s32[23]{0:T(128)S(1)} %get-tuple-element.34.meta.meta_in), slice={[6:7]} | slice | bytes 8 | tf_op jit(solution)/shard_map/slice | solution.py:581
  9.5 8.1 %collective-permute-done.3.received.refs_1_ = bf16[768,128]{1,0:T(8,128)(2,1)S(1)} collective-permute-done((bf16[768,128]{1,0:T(8,128)(2,1)S(1)}, bf16[768,128]{1,0:T(8,128)(2,1)S(1)}, u32[]{:S(2)}, u32[]{:S(2)}) %collective-permute-start.3) | collective-permute-done | bytes 196640 | tf_op jit(solution)/shard_map/ppermute | solution.py:568
  17.7 0.1 collective-permute-start.4
  17.8 1.2 %last_rows.1.last = bf16[1024,128]{1,0:T(8,128)(2,1)S(1)} custom-call(bf16[512,1024]{1,0:T(8,128)(2,1)} %key.1, bf16[512,1024]{1,0:T(8,128)(2,1)} %value.1), custom_call_target="tpu_custom_call" | custom-call | tf_op jit(solution)/shard_map/last_rows/pallas_call | solution.py:324
  18.9 0.8 %collective-permute-done.5.refs_3_ = bf16[512,128]{1,0:T(8,128)(2,1)S(1)} collective-permute-done((bf16[512,128]{1,0:T(8,128)(2,1)S(1)}, bf16[512,128]{1,0:T(8,128)(2,1)S(1)}, u32[]{:S(2)}, u32[]{:S(2)}) %collective-permute-start.5) | collective-permute-done | bytes 131104 | tf_op jit(solution)/shard_map/ppermute | solution.py:568
  19.7 2.3 %collective-permute-done.4.refs_3_ = bf16[256,128]{1,0:T(8,128)(2,1)S(1)} collective-permute-done((bf16[256,128]{1,0:T(8,128)(2,1)S(1)}, bf16[256,128]{1,0:T(8,128)(2,1)S(1)}, u32[]{:S(2)}, u32[]{:S(2)}) %collective-permute-start.4) | collective-permute-done | bytes 65568 | tf_op jit(solution)/shard_map/ppermute | solution.py:568
  22.0 0.0 collective-permute-done.6.refs_2_
  22.0 0.7 %merge.1.pieces = bf16[3,256,128]{2,1,0:T(8,128)(2,1)S(1)} custom-call(s32[23]{0:T(128)S(1)} %get-tuple-element.34.meta.meta_in, bf16[256,128]{1,0:T(8,128)(2,1)S(1)} %get-tuple-element.57.late, bf16[512,128]{1,0:T(8,128)(2,1)S(1)} %get-tuple-element.40.refs_0_, bf16[768,128]{1,0:T(8,128)(2,1)S(1)} %collective-permute-done.3.received.refs_1_, ...), custom_call_target="tpu_custom_call" | custom-call | tf_op jit(solution)/shard_map/merge/pallas_call | solution.py:198
  22.7 2.1 %collective-permute-start.7 = (bf16[3,256,128]{2,1,0:T(8,128)(2,1)S(1)}, bf16[3,256,128]{2,1,0:T(8,128)(2,1)S(1)}, u32[]{:S(2)}, u32[]{:S(2)}) collective-permute-start(bf16[3,256,128]{2,1,0:T(8,128)(2,1)S(1)} %merge.1.pieces), channel_id=1, source_target_pairs={{0,8},{4,12},{8,0},{12,4},{1,9},{5,13},{9,1},{13,5},{2,10},{6,14},... | collective-permute-start | bytes 589832 | tf_op jit(solution)/shard_map/ppermute | solution.py:568
  24.8 1.5 %collective-permute-start.9 = (bf16[3,256,128]{2,1,0:T(8,128)(2,1)S(1)}, bf16[3,256,128]{2,1,0:T(8,128)(2,1)S(1)}, u32[]{:S(2)}, u32[]{:S(2)}) collective-permute-start(bf16[3,256,128]{2,1,0:T(8,128)(2,1)S(1)} %merge.1.pieces), channel_id=1, source_target_pairs={{0,4},{4,0},{8,12},{12,8},{1,5},{5,1},{9,13},{13,9},{2,6},{6,2},{1... | collective-permute-start | bytes 589832 | tf_op jit(solution)/shard_map/ppermute | solution.py:568
  26.3 0.0 copy-done.1
  26.3 0.0 copy-done
  26.3 5.4 %open_conv.1 = (bf16[64,16,2304]{2,1,0:T(8,128)(2,1)S(1)}, f32[128,1024]{1,0:T(8,128)S(1)}, bf16[512,1024]{1,0:T(8,128)(2,1)}) custom-call(s32[23]{0:T(128)S(1)} %get-tuple-element.34.meta.meta_in, bf16[1024,128]{1,0:T(8,128)(2,1)S(1)} %last_rows.1.last, bf16[3,256,128]{2,1,0:T(8,128)(2,1)S(1)} %merge.1.pieces, bf16[512,1024]{1,0:T(8,128)(2,1)S(1)} %copy-done, ...), custom_call_target="tpu_custom_call" | custom-call | tf_op jit(solution)/shard_map/open_conv/pallas_call | solution.py:430
  31.7 2.4 %collective-permute-done.7.refs_1_ = bf16[3,256,128]{2,1,0:T(8,128)(2,1)S(1)} collective-permute-done((bf16[3,256,128]{2,1,0:T(8,128)(2,1)S(1)}, bf16[3,256,128]{2,1,0:T(8,128)(2,1)S(1)}, u32[]{:S(2)}, u32[]{:S(2)}) %collective-permute-start.7) | collective-permute-done | bytes 196640 | tf_op jit(solution)/shard_map/ppermute | solution.py:568
  34.2 0.0 collective-permute-start.8
  34.2 1.1 %collective-permute-done.9.refs_0_ = bf16[3,256,128]{2,1,0:T(8,128)(2,1)S(1)} collective-permute-done((bf16[3,256,128]{2,1,0:T(8,128)(2,1)S(1)}, bf16[3,256,128]{2,1,0:T(8,128)(2,1)S(1)}, u32[]{:S(2)}, u32[]{:S(2)}) %collective-permute-start.9) | collective-permute-done | bytes 196640 | tf_op jit(solution)/shard_map/ppermute | solution.py:568
  35.3 3.4 %near_conv.1 = (bf16[512,1024]{1,0:T(8,128)(2,1)}, bf16[16,64,768]{2,1,0:T(8,128)(2,1)S(1)}) custom-call(s32[23]{0:T(128)S(1)} %get-tuple-element.34.meta.meta_in, bf16[64,16,2304]{2,1,0:T(8,128)(2,1)S(1)} %get-tuple-element.48.shifted, f32[128,1024]{1,0:T(8,128)S(1)} %get-tuple-element.49.term, ...), custom_call_target="tpu_custom_call", output_to_operand_aliasing={{0}: (4, {})} | custom-call | tf_op jit(solution)/shard_map/near_conv/pallas_call | solution.py:490
  38.6 2.1 %collective-permute-done.8.pieces = bf16[3,256,128]{2,1,0:T(8,128)(2,1)S(1)} collective-permute-done((bf16[3,256,128]{2,1,0:T(8,128)(2,1)S(1)}, bf16[3,256,128]{2,1,0:T(8,128)(2,1)S(1)}, u32[]{:S(2)}, u32[]{:S(2)}) %collective-permute-start.8) | collective-permute-done | bytes 196640 | tf_op jit(solution)/shard_map/ppermute | solution.py:568
  40.8 1.9 %far_conv.1 = bf16[512,1024]{1,0:T(8,128)(2,1)} custom-call(bf16[3,256,128]{2,1,0:T(8,128)(2,1)S(1)} %collective-permute-done.8.pieces, bf16[16,64,768]{2,1,0:T(8,128)(2,1)S(1)} %get-tuple-element.51.ready, f32[128,1024]{1,0:T(8,128)S(1)} %get-tuple-element.49.term, bf16[512,1024]{1,0:T(8,128)(2,1)S(1)} %copy-done, ...), custom_call_target="tpu_custom_call", output_to_operand_aliasing={{}: (4, {})} | custom-call | tf_op jit(solution)/shard_map/far_conv/pallas_call | solution.py:533
  (4 shorter events, 0.0 us)
Async XLA Ops:
  0.0 26.3 %copy-start.1 = (bf16[64,512]{1,0:T(8,128)(2,1)S(1)}, bf16[64,512]{1,0:T(8,128)(2,1)}, u32[]{:S(2)}) copy-start(bf16[64,512]{1,0:T(8,128)(2,1)} %refs_0_.1) | copy-start | bytes 196612
  0.0 26.3 %copy-start = (bf16[512,1024]{1,0:T(8,128)(2,1)S(1)}, bf16[512,1024]{1,0:T(8,128)(2,1)}, u32[]{:S(2)}) copy-start(bf16[512,1024]{1,0:T(8,128)(2,1)} %query.5) | copy-start | bytes 3145732
  2.5 15.2 %collective-permute-start.3 = (bf16[768,128]{1,0:T(8,128)(2,1)S(1)}, bf16[768,128]{1,0:T(8,128)(2,1)S(1)}, u32[]{:S(2)}, u32[]{:S(2)}) collective-permute-start(bf16[768,128]{1,0:T(8,128)(2,1)S(1)} %get-tuple-element.35), channel_id=1, source_target_pairs={{0,8},{4,12},{8,0},{12,4},{1,9},{5,13},{9,1},{13,5},{2,10},{6,14},... | collective-permute-start | bytes 589832 | tf_op jit(solution)/shard_map/ppermute | solution.py:568
  6.8 15.3 %collective-permute-start.6 = (bf16[768,128]{1,0:T(8,128)(2,1)S(1)}, bf16[768,128]{1,0:T(8,128)(2,1)S(1)}, u32[]{:S(2)}, u32[]{:S(2)}) collective-permute-start(bf16[768,128]{1,0:T(8,128)(2,1)S(1)} %get-tuple-element.42), channel_id=1, source_target_pairs={{0,4},{4,0},{8,12},{12,8},{1,5},{5,1},{9,13},{13,9},{2,6},{6,2},{1... | collective-permute-start | bytes 589832 | tf_op jit(solution)/shard_map/ppermute | solution.py:568
  8.2 11.6 %collective-permute-start.5 = (bf16[512,128]{1,0:T(8,128)(2,1)S(1)}, bf16[512,128]{1,0:T(8,128)(2,1)S(1)}, u32[]{:S(2)}, u32[]{:S(2)}) collective-permute-start(bf16[512,128]{1,0:T(8,128)(2,1)S(1)} %get-tuple-element.38), channel_id=1, source_target_pairs={{0,12},{4,8},{8,4},{12,0},{1,13},{5,9},{9,5},{13,1},{2,14},{6,10},... | collective-permute-start | bytes 393224 | tf_op jit(solution)/shard_map/ppermute | solution.py:568
  17.7 4.3 %collective-permute-start.4 = (bf16[256,128]{1,0:T(8,128)(2,1)S(1)}, bf16[256,128]{1,0:T(8,128)(2,1)S(1)}, u32[]{:S(2)}, u32[]{:S(2)}) collective-permute-start(bf16[256,128]{1,0:T(8,128)(2,1)S(1)} %pick.1), channel_id=1, source_target_pairs={{0,4},{4,0},{8,12},{12,8},{1,5},{5,1},{9,13},{13,9},{2,6},{6,2},{1... | collective-permute-start | bytes 196616 | tf_op jit(solution)/shard_map/ppermute | solution.py:568
  22.7 11.5 %collective-permute-start.7 = (bf16[3,256,128]{2,1,0:T(8,128)(2,1)S(1)}, bf16[3,256,128]{2,1,0:T(8,128)(2,1)S(1)}, u32[]{:S(2)}, u32[]{:S(2)}) collective-permute-start(bf16[3,256,128]{2,1,0:T(8,128)(2,1)S(1)} %merge.1.pieces), channel_id=1, source_target_pairs={{0,8},{4,12},{8,0},{12,4},{1,9},{5,13},{9,1},{13,5},{2,10},{6,14},... | collective-permute-start | bytes 589832 | tf_op jit(solution)/shard_map/ppermute | solution.py:568
  24.8 10.4 %collective-permute-start.9 = (bf16[3,256,128]{2,1,0:T(8,128)(2,1)S(1)}, bf16[3,256,128]{2,1,0:T(8,128)(2,1)S(1)}, u32[]{:S(2)}, u32[]{:S(2)}) collective-permute-start(bf16[3,256,128]{2,1,0:T(8,128)(2,1)S(1)} %merge.1.pieces), channel_id=1, source_target_pairs={{0,4},{4,0},{8,12},{12,8},{1,5},{5,1},{9,13},{13,9},{2,6},{6,2},{1... | collective-permute-start | bytes 589832 | tf_op jit(solution)/shard_map/ppermute | solution.py:568
  34.2 6.6 %collective-permute-start.8 = (bf16[3,256,128]{2,1,0:T(8,128)(2,1)S(1)}, bf16[3,256,128]{2,1,0:T(8,128)(2,1)S(1)}, u32[]{:S(2)}, u32[]{:S(2)}) collective-permute-start(bf16[3,256,128]{2,1,0:T(8,128)(2,1)S(1)} %collective-permute-done.7.refs_1_), channel_id=1, source_target_pairs={{0,4},{4,0},{8,12},{12,8},{1,5},{5,1},{9,13},{13,9},{2,6},{6,2},{1... | collective-permute-start | bytes 589832 | tf_op jit(solution)/shard_map/ppermute | solution.py:568

commit v15 on v14

--- a/solution.py
+++ b/solution.py
@@ -579,7 +579,7 @@
 
     extra, far = lax.optimization_barrier((extra, far))
     late = lax.cond(meta[MANY] > 0, more, none, meta, extra)
-    last, cross_filters, late, cross = lax.optimization_barrier((last, cross_filters, late, cross))
+    last, late, cross = lax.optimization_barrier((last, late, cross))
     merged = merge(width, meta, [sends[0], far, near, cross], late)
     far_part, near_part = exchange(merged, 2), exchange(merged, 1)
     shifted, term, out = open_conv(

time: 42.8 us -> 45 us (1.051)
  starting transfers between devices: 9.47 us -> 14 us
  waiting for transfers between devices: 16.9 us -> 14 us
  Pallas kernels: 15 us -> 15.5 us
    ppermute x7, starting transfers between devices: 9.47 us -> 14 us  [exchange(): return lax.ppermute(value, 'seq', [(z, z ^ step) for z in range(size)])]
    ppermute x7, waiting for transfers between devices: 16.9 us -> 14 us  [exchange(): return lax.ppermute(value, 'seq', [(z, z ^ step) for z in range(size)])]
  transfers between devices with their start and end apart: 7 -> 7, of which waited for: 6 -> 4; matrix products, arithmetic and copies ran while one was open for 1% -> 1% of each run, Pallas kernels for 23% -> 22%
where the time goes in v15:
time: 45 us; the launch traced here: 44.8 us
  Pallas kernels  15.5 us (34%)
  starting transfers between devices  14 us (31%)
  waiting for transfers between devices  14 us (31%)
  between operations  0.71 us (2%)
  local copies, waits for them, and re-layouts  0.59 us (1%)
    ppermute x7, starting transfers between devices, exchange(): return lax.ppermute(value, 'seq', [(z, z ^ step) for z in range(size)])  14 us
    ppermute x7, waiting for transfers between devices, exchange(): return lax.ppermute(value, 'seq', [(z, z ^ step) for z in range(size)])  14 us
    pallas_call x1, Pallas kernels, open_conv(): pl.pallas_call(functools.partial(open_kernel, size, first), in_specs=[ANY...  5.46 us
    pallas_call x1, Pallas kernels, near_conv(): pl.pallas_call(functools.partial(near_kernel, size, steps, next_step), in...  3.43 us
    pallas_call x1, Pallas kernels, gate(): pl.pallas_call(functools.partial(gate_kernel, parts), in_specs=[HBM_SPEC]...  2.88 us
    pallas_call x1, Pallas kernels, far_conv(): pl.pallas_call(functools.partial(far_kernel, size, step), in_specs=[VMEM_...  1.89 us
    pallas_call x1, Pallas kernels, last_rows(): pl.pallas_call(last_rows_kernel, grid=(1,), in_specs=[block, block], out_...  1.16 us
  transfers between devices with their start and end apart: 7, of which 4 were waited for; matrix products, arithmetic and copies ran while one was open for 1% of the time, Pallas kernels for 22%

profile of v15, /device:TPU:0, one launch (start us, length us, event | category | flops | bytes accessed | tf_op | source)
XLA Modules:
  0.0 44.8 jit_solution(8446114954342677189)
XLA Ops:
  0.0 0.0 copy-start.1
  0.0 2.9 %gate.1 = (bf16[512,128]{1,0:T(8,128)(2,1)S(1)}, bf16[768,128]{1,0:T(8,128)(2,1)S(1)}, bf16[768,128]{1,0:T(8,128)(2,1)S(1)}, bf16[512,128]{1,0:T(8,128)(2,1)S(1)...) custom-call(s32[4]{0:T(128)} %sources_in.1, s32[16]{0:T(128)} %owner_in.1, bf16[512,1024]{1,0:T(8,128)(2,1)} %key.1, ...), custom_call_target="tpu_custom_call" | custom-call | tf_op jit(solution)/shard_map/gate/pallas_call | solution.py:134
  2.9 3.5 %collective-permute-start.3 = (bf16[768,128]{1,0:T(8,128)(2,1)S(1)}, bf16[768,128]{1,0:T(8,128)(2,1)S(1)}, u32[]{:S(2)}, u32[]{:S(2)}) collective-permute-start(bf16[768,128]{1,0:T(8,128)(2,1)S(1)} %get-tuple-element.35), channel_id=1, source_target_pairs={{0,8},{4,12},{8,0},{12,4},{1,9},{5,13},{9,1},{13,5},{2,10},{6,14},... | collective-permute-start | bytes 589832 | tf_op jit(solution)/shard_map/ppermute | solution.py:568
  6.4 1.8 %collective-permute-start.5 = (bf16[768,128]{1,0:T(8,128)(2,1)S(1)}, bf16[768,128]{1,0:T(8,128)(2,1)S(1)}, u32[]{:S(2)}, u32[]{:S(2)}) collective-permute-start(bf16[768,128]{1,0:T(8,128)(2,1)S(1)} %get-tuple-element.41), channel_id=1, source_target_pairs={{0,4},{4,0},{8,12},{12,8},{1,5},{5,1},{9,13},{13,9},{2,6},{6,2},{1... | collective-permute-start | bytes 589832 | tf_op jit(solution)/shard_map/ppermute | solution.py:568
  8.2 0.0 collective-permute-start.4
  8.2 1.2 %last_rows.1.last = bf16[1024,128]{1,0:T(8,128)(2,1)S(1)} custom-call(bf16[512,1024]{1,0:T(8,128)(2,1)} %key.1, bf16[512,1024]{1,0:T(8,128)(2,1)} %value.1), custom_call_target="tpu_custom_call" | custom-call | tf_op jit(solution)/shard_map/last_rows/pallas_call | solution.py:324
  9.3 0.6 %slice.18 = s32[1]{0:T(128)} slice(s32[23]{0:T(128)S(1)} %get-tuple-element.33.meta.meta_in), slice={[6:7]} | slice | bytes 8 | tf_op jit(solution)/shard_map/slice | solution.py:581
  10.6 6.4 %collective-permute-done.3.refs_1_.received = bf16[768,128]{1,0:T(8,128)(2,1)S(1)} collective-permute-done((bf16[768,128]{1,0:T(8,128)(2,1)S(1)}, bf16[768,128]{1,0:T(8,128)(2,1)S(1)}, u32[]{:S(2)}, u32[]{:S(2)}) %collective-permute-start.3) | collective-permute-done | bytes 196640 | tf_op jit(solution)/shard_map/ppermute | solution.py:568
  17.0 2.7 %collective-permute-done.4.refs_3_ = bf16[512,128]{1,0:T(8,128)(2,1)S(1)} collective-permute-done((bf16[512,128]{1,0:T(8,128)(2,1)S(1)}, bf16[512,128]{1,0:T(8,128)(2,1)S(1)}, u32[]{:S(2)}, u32[]{:S(2)}) %collective-permute-start.4) | collective-permute-done | bytes 131104 | tf_op jit(solution)/shard_map/ppermute | solution.py:568
  19.7 0.0 collective-permute-done.5.refs_2_
  19.7 0.7 %merge.1.pieces = bf16[3,256,128]{2,1,0:T(8,128)(2,1)S(1)} custom-call(s32[23]{0:T(128)S(1)} %get-tuple-element.33.meta.meta_in, bf16[256,128]{1,0:T(8,128)(2,1)S(1)} %get-tuple-element.55.late, bf16[512,128]{1,0:T(8,128)(2,1)S(1)} %get-tuple-element.39.refs_0_, bf16[768,128]{1,0:T(8,128)(2,1)S(1)} %collective-permute-done.3.refs_1_.received, ...), custom_call_target="tpu_custom_call" | custom-call | tf_op jit(solution)/shard_map/merge/pallas_call | solution.py:198
  20.4 4.2 %collective-permute-start.6 = (bf16[3,256,128]{2,1,0:T(8,128)(2,1)S(1)}, bf16[3,256,128]{2,1,0:T(8,128)(2,1)S(1)}, u32[]{:S(2)}, u32[]{:S(2)}) collective-permute-start(bf16[3,256,128]{2,1,0:T(8,128)(2,1)S(1)} %merge.1.pieces), channel_id=1, source_target_pairs={{0,8},{4,12},{8,0},{12,4},{1,9},{5,13},{9,1},{13,5},{2,10},{6,14},... | collective-permute-start | bytes 589832 | tf_op jit(solution)/shard_map/ppermute | solution.py:568
  24.5 0.0 collective-permute-start.7
  24.5 2.0 %collective-permute-start.9 = (bf16[3,256,128]{2,1,0:T(8,128)(2,1)S(1)}, bf16[3,256,128]{2,1,0:T(8,128)(2,1)S(1)}, u32[]{:S(2)}, u32[]{:S(2)}) collective-permute-start(bf16[3,256,128]{2,1,0:T(8,128)(2,1)S(1)} %merge.1.pieces), channel_id=1, source_target_pairs={{0,4},{4,0},{8,12},{12,8},{1,5},{5,1},{9,13},{13,9},{2,6},{6,2},{1... | collective-permute-start | bytes 589832 | tf_op jit(solution)/shard_map/ppermute | solution.py:568
  26.5 4.7 %collective-permute-done.7.refs_3_ = bf16[256,128]{1,0:T(8,128)(2,1)S(1)} collective-permute-done((bf16[256,128]{1,0:T(8,128)(2,1)S(1)}, bf16[256,128]{1,0:T(8,128)(2,1)S(1)}, u32[]{:S(2)}, u32[]{:S(2)}) %collective-permute-start.7) | collective-permute-done | bytes 65568 | tf_op jit(solution)/shard_map/ppermute | solution.py:568
  31.2 0.0 copy-done.1
  31.2 0.0 copy-done
  31.3 5.5 %open_conv.1 = (bf16[64,16,2304]{2,1,0:T(8,128)(2,1)S(1)}, f32[128,1024]{1,0:T(8,128)S(1)}, bf16[512,1024]{1,0:T(8,128)(2,1)}) custom-call(s32[23]{0:T(128)S(1)} %get-tuple-element.33.meta.meta_in, bf16[1024,128]{1,0:T(8,128)(2,1)S(1)} %last_rows.1.last, bf16[3,256,128]{2,1,0:T(8,128)(2,1)S(1)} %merge.1.pieces, bf16[512,1024]{1,0:T(8,128)(2,1)S(1)} %copy-done, ...), custom_call_target="tpu_custom_call" | custom-call | tf_op jit(solution)/shard_map/open_conv/pallas_call | solution.py:430
  36.7 0.0 collective-permute-done.6.refs_1_
  36.7 2.6 %collective-permute-start.8 = (bf16[3,256,128]{2,1,0:T(8,128)(2,1)S(1)}, bf16[3,256,128]{2,1,0:T(8,128)(2,1)S(1)}, u32[]{:S(2)}, u32[]{:S(2)}) collective-permute-start(bf16[3,256,128]{2,1,0:T(8,128)(2,1)S(1)} %collective-permute-done.6.refs_1_), channel_id=1, source_target_pairs={{0,4},{4,0},{8,12},{12,8},{1,5},{5,1},{9,13},{13,9},{2,6},{6,2},{1... | collective-permute-start | bytes 589832 | tf_op jit(solution)/shard_map/ppermute | solution.py:568
  39.3 0.0 collective-permute-done.9.refs_0_
  39.3 3.4 %near_conv.1 = (bf16[512,1024]{1,0:T(8,128)(2,1)}, bf16[16,64,768]{2,1,0:T(8,128)(2,1)S(1)}) custom-call(s32[23]{0:T(128)S(1)} %get-tuple-element.33.meta.meta_in, bf16[64,16,2304]{2,1,0:T(8,128)(2,1)S(1)} %get-tuple-element.46.shifted, f32[128,1024]{1,0:T(8,128)S(1)} %get-tuple-element.47.term, ...), custom_call_target="tpu_custom_call", output_to_operand_aliasing={{0}: (4, {})} | custom-call | tf_op jit(solution)/shard_map/near_conv/pallas_call | solution.py:490
  42.7 0.2 collective-permute-done.8.pieces
  42.9 1.9 %far_conv.1 = bf16[512,1024]{1,0:T(8,128)(2,1)} custom-call(bf16[3,256,128]{2,1,0:T(8,128)(2,1)S(1)} %collective-permute-done.8.pieces, bf16[16,64,768]{2,1,0:T(8,128)(2,1)S(1)} %get-tuple-element.49.ready, f32[128,1024]{1,0:T(8,128)S(1)} %get-tuple-element.47.term, bf16[512,1024]{1,0:T(8,128)(2,1)S(1)} %copy-done, ...), custom_call_target="tpu_custom_call", output_to_operand_aliasing={{}: (4, {})} | custom-call | tf_op jit(solution)/shard_map/far_conv/pallas_call | solution.py:533
  (4 shorter events, 0.0 us)
Async XLA Ops:
  0.0 31.2 %copy-start.1 = (bf16[64,512]{1,0:T(8,128)(2,1)S(1)}, bf16[64,512]{1,0:T(8,128)(2,1)}, u32[]{:S(2)}) copy-start(bf16[64,512]{1,0:T(8,128)(2,1)} %refs_0_.1) | copy-start | bytes 196612
  0.0 31.2 %copy-start = (bf16[512,1024]{1,0:T(8,128)(2,1)S(1)}, bf16[512,1024]{1,0:T(8,128)(2,1)}, u32[]{:S(2)}) copy-start(bf16[512,1024]{1,0:T(8,128)(2,1)} %query.5) | copy-start | bytes 3145732
  2.9 14.1 %collective-permute-start.3 = (bf16[768,128]{1,0:T(8,128)(2,1)S(1)}, bf16[768,128]{1,0:T(8,128)(2,1)S(1)}, u32[]{:S(2)}, u32[]{:S(2)}) collective-permute-start(bf16[768,128]{1,0:T(8,128)(2,1)S(1)} %get-tuple-element.35), channel_id=1, source_target_pairs={{0,8},{4,12},{8,0},{12,4},{1,9},{5,13},{9,1},{13,5},{2,10},{6,14},... | collective-permute-start | bytes 589832 | tf_op jit(solution)/shard_map/ppermute | solution.py:568
  6.4 13.3 %collective-permute-start.5 = (bf16[768,128]{1,0:T(8,128)(2,1)S(1)}, bf16[768,128]{1,0:T(8,128)(2,1)S(1)}, u32[]{:S(2)}, u32[]{:S(2)}) collective-permute-start(bf16[768,128]{1,0:T(8,128)(2,1)S(1)} %get-tuple-element.41), channel_id=1, source_target_pairs={{0,4},{4,0},{8,12},{12,8},{1,5},{5,1},{9,13},{13,9},{2,6},{6,2},{1... | collective-permute-start | bytes 589832 | tf_op jit(solution)/shard_map/ppermute | solution.py:568
  8.2 11.5 %collective-permute-start.4 = (bf16[512,128]{1,0:T(8,128)(2,1)S(1)}, bf16[512,128]{1,0:T(8,128)(2,1)S(1)}, u32[]{:S(2)}, u32[]{:S(2)}) collective-permute-start(bf16[512,128]{1,0:T(8,128)(2,1)S(1)} %get-tuple-element.37), channel_id=1, source_target_pairs={{0,12},{4,8},{8,4},{12,0},{1,13},{5,9},{9,5},{13,1},{2,14},{6,10},... | collective-permute-start | bytes 393224 | tf_op jit(solution)/shard_map/ppermute | solution.py:568
  20.4 16.4 %collective-permute-start.6 = (bf16[3,256,128]{2,1,0:T(8,128)(2,1)S(1)}, bf16[3,256,128]{2,1,0:T(8,128)(2,1)S(1)}, u32[]{:S(2)}, u32[]{:S(2)}) collective-permute-start(bf16[3,256,128]{2,1,0:T(8,128)(2,1)S(1)} %merge.1.pieces), channel_id=1, source_target_pairs={{0,8},{4,12},{8,0},{12,4},{1,9},{5,13},{9,1},{13,5},{2,10},{6,14},... | collective-permute-start | bytes 589832 | tf_op jit(solution)/shard_map/ppermute | solution.py:568
  24.5 6.7 %collective-permute-start.7 = (bf16[256,128]{1,0:T(8,128)(2,1)S(1)}, bf16[256,128]{1,0:T(8,128)(2,1)S(1)}, u32[]{:S(2)}, u32[]{:S(2)}) collective-permute-start(bf16[256,128]{1,0:T(8,128)(2,1)S(1)} %pick.1), channel_id=1, source_target_pairs={{0,4},{4,0},{8,12},{12,8},{1,5},{5,1},{9,13},{13,9},{2,6},{6,2},{1... | collective-permute-start | bytes 196616 | tf_op jit(solution)/shard_map/ppermute | solution.py:568
  24.5 14.8 %collective-permute-start.9 = (bf16[3,256,128]{2,1,0:T(8,128)(2,1)S(1)}, bf16[3,256,128]{2,1,0:T(8,128)(2,1)S(1)}, u32[]{:S(2)}, u32[]{:S(2)}) collective-permute-start(bf16[3,256,128]{2,1,0:T(8,128)(2,1)S(1)} %merge.1.pieces), channel_id=1, source_target_pairs={{0,4},{4,0},{8,12},{12,8},{1,5},{5,1},{9,13},{13,9},{2,6},{6,2},{1... | collective-permute-start | bytes 589832 | tf_op jit(solution)/shard_map/ppermute | solution.py:568
  36.7 6.2 %collective-permute-start.8 = (bf16[3,256,128]{2,1,0:T(8,128)(2,1)S(1)}, bf16[3,256,128]{2,1,0:T(8,128)(2,1)S(1)}, u32[]{:S(2)}, u32[]{:S(2)}) collective-permute-start(bf16[3,256,128]{2,1,0:T(8,128)(2,1)S(1)} %collective-permute-done.6.refs_1_), channel_id=1, source_target_pairs={{0,4},{4,0},{8,12},{12,8},{1,5},{5,1},{9,13},{13,9},{2,6},{6,2},{1... | collective-permute-start | bytes 589832 | tf_op jit(solution)/shard_map/ppermute | solution.py:568

commit v16 on v14

--- a/solution.py
+++ b/solution.py
@@ -34,6 +34,7 @@
 MANY = 2 * SENT
 WINDOWS = MANY + 1
 SLOTS = 2
+CHOICES = SENT * len(STEPS) * SLOTS
 
 
 def product(key, value, start, columns):
@@ -45,7 +46,7 @@
 
 def gate_kernel(parts, sources_in, owner_in, key_in, value_in, filters_in, *refs):
     sends = refs[:parts]
-    extra, meta, sources, owner, key, value, filters, sems = refs[parts:]
+    extra, choice, meta, sources, owner, key, value, filters, sems = refs[parts:]
     stretch_count = owner.shape[0]
     channels = key.shape[1]
     width = channels // parts
@@ -84,6 +85,11 @@
         meta[w] = holder
         meta[PLACE + w] = place
         many = many + jnp.where(place >= SLOTS, 1, 0)
+        for index, step in enumerate(STEPS):
+            for packed in range(SLOTS):
+                here = jnp.where((holder == me ^ step) & (place == packed), 1, 0)
+                mask = jnp.broadcast_to(here, choice.shape[1:]).astype(jnp.int16)
+                choice[(w * len(STEPS) + index) * SLOTS + packed] = mask
 
         @pl.when(holder == me)
         def _(w=w, holder=holder, place=place):
@@ -131,15 +137,16 @@
         pltpu.with_memory_space_constraint(operand, pltpu.HBM)
         for operand in (sources, owner, key_proj, value_proj, filters)
     ]
-    *sends, extra, meta = pl.pallas_call(
+    *sends, extra, choice, meta = pl.pallas_call(
         functools.partial(gate_kernel, parts),
         in_specs=[HBM_SPEC] * 5,
-        out_specs=[VMEM_SPEC] * (parts + 1) + [SMEM_SPEC],
+        out_specs=[VMEM_SPEC] * (parts + 2) + [SMEM_SPEC],
         out_shape=[
             jax.ShapeDtypeStruct((SLOTS * width + rows, LANES), jnp.bfloat16) for rows in filter_rows
         ]
         + [
             jax.ShapeDtypeStruct((parts, width, LANES), jnp.bfloat16),
+            jax.ShapeDtypeStruct((CHOICES, GROUP_CH, LANES), jnp.int16),
             jax.ShapeDtypeStruct((WINDOWS + slots * WIN,), jnp.int32),
         ],
         scratch_shapes=[
@@ -153,7 +160,7 @@
         compiler_params=params(),
         name="gate",
     )(*operands)
-    return sends, extra, meta
+    return sends, extra, choice, meta
 
 
 def third_kernel(meta, *refs):
@@ -177,32 +184,27 @@
     )(meta, *arrived)
 
 
-def merge_kernel(width, meta, late, *refs):
+def merge_kernel(width, choice, late, *refs):
     received, out = refs[:-1], refs[-1]
-    me = lax.axis_index("seq")
     for w in range(SENT):
-        place = meta[PLACE + w]
-        rows = pl.ds(pl.multiple_of(jnp.minimum(place, SLOTS - 1) * width, LANES), width)
-        for block, step in zip(received, STEPS):
-
-            @pl.when(me ^ step == meta[w])
-            def _(w=w, block=block, rows=rows):
-                out[w] = block[rows, :]
-
-    @pl.when(meta[PLACE + SENT - 1] >= SLOTS)
-    def _():
-        out[SENT - 1] = late[...]
-
-
-def merge(width, meta, received, late):
+        masks = [choice[w * len(STEPS) * SLOTS + number] != 0 for number in range(len(STEPS) * SLOTS)]
+        for start in range(0, width, GROUP_CH):
+            tile = late[pl.ds(start, GROUP_CH), :]
+            for number, mask in enumerate(masks):
+                rows = pl.ds(number % SLOTS * width + start, GROUP_CH)
+                tile = jnp.where(mask, received[number // SLOTS][rows, :], tile)
+            out[w, pl.ds(start, GROUP_CH), :] = tile
+
+
+def merge(width, choice, received, late):
     return pl.pallas_call(
         functools.partial(merge_kernel, width),
-        in_specs=[SMEM_SPEC] + [VMEM_SPEC] * (1 + len(received)),
+        in_specs=[VMEM_SPEC] * (2 + len(received)),
         out_specs=VMEM_SPEC,
         out_shape=jax.ShapeDtypeStruct((SENT, width, LANES), received[0].dtype),
         compiler_params=params(),
         name="merge",
-    )(meta, late, *received)
+    )(choice, late, *received)
 
 
 def pick_kernel(first, received, out):
@@ -552,7 +554,7 @@
     filter_rows = [0, block, block, 0] if by_parts else [block]
     parts = len(filter_rows)
     width = channels // parts
-    sends, extra, meta = gate(filter_rows, sources, owner, key_proj, value_proj, filters)
+    sends, extra, choice, meta = gate(filter_rows, sources, owner, key_proj, value_proj, filters)
     last = last_rows(key_proj, value_proj)
     first = SLOTS * width
     if not by_parts:
@@ -580,7 +582,7 @@
     extra, far = lax.optimization_barrier((extra, far))
     late = lax.cond(meta[MANY] > 0, more, none, meta, extra)
     last, cross_filters, late, cross = lax.optimization_barrier((last, cross_filters, late, cross))
-    merged = merge(width, meta, [sends[0], far, near, cross], late)
+    merged = merge(width, choice, [sends[0], far, near, cross], late)
     far_part, near_part = exchange(merged, 2), exchange(merged, 1)
     shifted, term, out = open_conv(
         size,

time: 42.8 us -> 42.3 us (0.988)
  Pallas kernels: 15 us -> 14.4 us
    pallas_call x1, Pallas kernels: 0.66 us -> 0.18 us  [merge(): pl.pallas_call(functools.partial(merge_kernel, width), in_specs=[VMEM_SPE...]
  transfers between devices with their start and end apart: 7 -> 7, of which waited for: 6 -> 6; matrix products, arithmetic and copies ran while one was open for 1% -> 1% of each run, Pallas kernels for 23% -> 24%
where the time goes in v16:
time: 42.3 us; the launch traced here: 42.2 us
  waiting for transfers between devices  16.9 us (40%)
  Pallas kernels  14.4 us (34%)
  starting transfers between devices  9.55 us (23%)
  between operations  0.7 us (2%)
  local copies, waits for them, and re-layouts  0.59 us (1%)
    ppermute x7, waiting for transfers between devices, exchange(): return lax.ppermute(value, 'seq', [(z, z ^ step) for z in range(size)])  16.9 us
    ppermute x7, starting transfers between devices, exchange(): return lax.ppermute(value, 'seq', [(z, z ^ step) for z in range(size)])  9.55 us
    pallas_call x1, Pallas kernels, open_conv(): pl.pallas_call(functools.partial(open_kernel, size, first), in_specs=[ANY...  5.45 us
    pallas_call x1, Pallas kernels, near_conv(): pl.pallas_call(functools.partial(near_kernel, size, steps, next_step), in...  3.43 us
    pallas_call x1, Pallas kernels, gate(): pl.pallas_call(functools.partial(gate_kernel, parts), in_specs=[HBM_SPEC]...  2.32 us
    pallas_call x1, Pallas kernels, far_conv(): pl.pallas_call(functools.partial(far_kernel, size, step), in_specs=[VMEM_...  1.89 us
    pallas_call x1, Pallas kernels, last_rows(): pl.pallas_call(last_rows_kernel, grid=(1,), in_specs=[block, block], out_...  1.16 us
  transfers between devices with their start and end apart: 7, of which 6 were waited for; matrix products, arithmetic and copies ran while one was open for 1% of the time, Pallas kernels for 24%

profile of v16, /device:TPU:0, one launch (start us, length us, event | category | flops | bytes accessed | tf_op | source)
XLA Modules:
  0.0 42.2 jit_solution(4924413002798527112)
XLA Ops:
  0.0 0.0 copy-start.1
  0.0 2.3 %gate.1 = (bf16[512,128]{1,0:T(8,128)(2,1)S(1)}, bf16[768,128]{1,0:T(8,128)(2,1)S(1)}, bf16[768,128]{1,0:T(8,128)(2,1)S(1)}, bf16[512,128]{1,0:T(8,128)(2,1)S(1)...) custom-call(s32[4]{0:T(128)} %sources_in.1, s32[16]{0:T(128)} %owner_in.1, ...), custom_call_target="tpu_custom_call" | custom-call | tf_op jit(solution)/shard_map/gate/pallas_call | solution.py:140
  2.3 4.5 %collective-permute-start.3 = (bf16[768,128]{1,0:T(8,128)(2,1)S(1)}, bf16[768,128]{1,0:T(8,128)(2,1)S(1)}, u32[]{:S(2)}, u32[]{:S(2)}) collective-permute-start(bf16[768,128]{1,0:T(8,128)(2,1)S(1)} %get-tuple-element.36), channel_id=1, source_target_pairs={{0,8},{4,12},{8,0},{12,4},{1,9},{5,13},{9,1},{13,5},{2,10},{6,14},... | collective-permute-start | bytes 589832 | tf_op jit(solution)/shard_map/ppermute | solution.py:570
  6.8 1.4 %collective-permute-start.6 = (bf16[768,128]{1,0:T(8,128)(2,1)S(1)}, bf16[768,128]{1,0:T(8,128)(2,1)S(1)}, u32[]{:S(2)}, u32[]{:S(2)}) collective-permute-start(bf16[768,128]{1,0:T(8,128)(2,1)S(1)} %get-tuple-element.44), channel_id=1, source_target_pairs={{0,4},{4,0},{8,12},{12,8},{1,5},{5,1},{9,13},{13,9},{2,6},{6,2},{1... | collective-permute-start | bytes 589832 | tf_op jit(solution)/shard_map/ppermute | solution.py:570
  8.2 0.2 collective-permute-start.5
  8.4 0.6 %slice.18 = s32[1]{0:T(128)} slice(s32[23]{0:T(128)S(1)} %get-tuple-element.37.meta_in), slice={[6:7]} | slice | bytes 8 | tf_op jit(solution)/shard_map/slice | solution.py:583
  9.6 8.3 %collective-permute-done.3.received.refs_1_ = bf16[768,128]{1,0:T(8,128)(2,1)S(1)} collective-permute-done((bf16[768,128]{1,0:T(8,128)(2,1)S(1)}, bf16[768,128]{1,0:T(8,128)(2,1)S(1)}, u32[]{:S(2)}, u32[]{:S(2)}) %collective-permute-start.3) | collective-permute-done | bytes 196640 | tf_op jit(solution)/shard_map/ppermute | solution.py:570
  17.9 0.1 collective-permute-start.4
  18.0 1.2 %last_rows.1.last = bf16[1024,128]{1,0:T(8,128)(2,1)S(1)} custom-call(bf16[512,1024]{1,0:T(8,128)(2,1)} %key.1, bf16[512,1024]{1,0:T(8,128)(2,1)} %value.1), custom_call_target="tpu_custom_call" | custom-call | tf_op jit(solution)/shard_map/last_rows/pallas_call | solution.py:326
  19.2 0.7 %collective-permute-done.5.refs_3_ = bf16[512,128]{1,0:T(8,128)(2,1)S(1)} collective-permute-done((bf16[512,128]{1,0:T(8,128)(2,1)S(1)}, bf16[512,128]{1,0:T(8,128)(2,1)S(1)}, u32[]{:S(2)}, u32[]{:S(2)}) %collective-permute-start.5) | collective-permute-done | bytes 131104 | tf_op jit(solution)/shard_map/ppermute | solution.py:570
  19.8 2.4 %collective-permute-done.4.refs_3_ = bf16[256,128]{1,0:T(8,128)(2,1)S(1)} collective-permute-done((bf16[256,128]{1,0:T(8,128)(2,1)S(1)}, bf16[256,128]{1,0:T(8,128)(2,1)S(1)}, u32[]{:S(2)}, u32[]{:S(2)}) %collective-permute-start.4) | collective-permute-done | bytes 65568 | tf_op jit(solution)/shard_map/ppermute | solution.py:570
  22.2 0.0 collective-permute-done.6.refs_2_
  22.2 0.2 merge.1.pieces
  22.4 1.9 %collective-permute-start.7 = (bf16[3,256,128]{2,1,0:T(8,128)(2,1)S(1)}, bf16[3,256,128]{2,1,0:T(8,128)(2,1)S(1)}, u32[]{:S(2)}, u32[]{:S(2)}) collective-permute-start(bf16[3,256,128]{2,1,0:T(8,128)(2,1)S(1)} %merge.1.pieces), channel_id=1, source_target_pairs={{0,8},{4,12},{8,0},{12,4},{1,9},{5,13},{9,1},{13,5},{2,10},{6,14},... | collective-permute-start | bytes 589832 | tf_op jit(solution)/shard_map/ppermute | solution.py:570
  24.4 1.5 %collective-permute-start.9 = (bf16[3,256,128]{2,1,0:T(8,128)(2,1)S(1)}, bf16[3,256,128]{2,1,0:T(8,128)(2,1)S(1)}, u32[]{:S(2)}, u32[]{:S(2)}) collective-permute-start(bf16[3,256,128]{2,1,0:T(8,128)(2,1)S(1)} %merge.1.pieces), channel_id=1, source_target_pairs={{0,4},{4,0},{8,12},{12,8},{1,5},{5,1},{9,13},{13,9},{2,6},{6,2},{1... | collective-permute-start | bytes 589832 | tf_op jit(solution)/shard_map/ppermute | solution.py:570
  25.9 0.0 copy-done.1
  25.9 0.0 copy-done
  25.9 5.4 %open_conv.1 = (bf16[64,16,2304]{2,1,0:T(8,128)(2,1)S(1)}, f32[128,1024]{1,0:T(8,128)S(1)}, bf16[512,1024]{1,0:T(8,128)(2,1)}) custom-call(s32[23]{0:T(128)S(1)} %get-tuple-element.37.meta_in, bf16[1024,128]{1,0:T(8,128)(2,1)S(1)} %last_rows.1.last, bf16[3,256,128]{2,1,0:T(8,128)(2,1)S(1)} %merge.1.pieces, bf16[512,1024]{1,0:T(8,128)(2,1)S(1)} %copy-done, ...), custom_call_target="tpu_custom_call" | custom-call | tf_op jit(solution)/shard_map/open_conv/pallas_call | solution.py:432
  31.3 2.4 %collective-permute-done.7.refs_1_ = bf16[3,256,128]{2,1,0:T(8,128)(2,1)S(1)} collective-permute-done((bf16[3,256,128]{2,1,0:T(8,128)(2,1)S(1)}, bf16[3,256,128]{2,1,0:T(8,128)(2,1)S(1)}, u32[]{:S(2)}, u32[]{:S(2)}) %collective-permute-start.7) | collective-permute-done | bytes 196640 | tf_op jit(solution)/shard_map/ppermute | solution.py:570
  33.7 0.0 collective-permute-start.8
  33.7 1.1 %collective-permute-done.9.refs_0_ = bf16[3,256,128]{2,1,0:T(8,128)(2,1)S(1)} collective-permute-done((bf16[3,256,128]{2,1,0:T(8,128)(2,1)S(1)}, bf16[3,256,128]{2,1,0:T(8,128)(2,1)S(1)}, u32[]{:S(2)}, u32[]{:S(2)}) %collective-permute-start.9) | collective-permute-done | bytes 196640 | tf_op jit(solution)/shard_map/ppermute | solution.py:570
  34.8 3.4 %near_conv.1 = (bf16[512,1024]{1,0:T(8,128)(2,1)}, bf16[16,64,768]{2,1,0:T(8,128)(2,1)S(1)}) custom-call(s32[23]{0:T(128)S(1)} %get-tuple-element.37.meta_in, bf16[64,16,2304]{2,1,0:T(8,128)(2,1)S(1)} %get-tuple-element.50.shifted, f32[128,1024]{1,0:T(8,128)S(1)} %get-tuple-element.51.term, ...), custom_call_target="tpu_custom_call", output_to_operand_aliasing={{0}: (4, {})} | custom-call | tf_op jit(solution)/shard_map/near_conv/pallas_call | solution.py:492
  38.2 2.1 %collective-permute-done.8.pieces = bf16[3,256,128]{2,1,0:T(8,128)(2,1)S(1)} collective-permute-done((bf16[3,256,128]{2,1,0:T(8,128)(2,1)S(1)}, bf16[3,256,128]{2,1,0:T(8,128)(2,1)S(1)}, u32[]{:S(2)}, u32[]{:S(2)}) %collective-permute-start.8) | collective-permute-done | bytes 196640 | tf_op jit(solution)/shard_map/ppermute | solution.py:570
  40.3 1.9 %far_conv.1 = bf16[512,1024]{1,0:T(8,128)(2,1)} custom-call(bf16[3,256,128]{2,1,0:T(8,128)(2,1)S(1)} %collective-permute-done.8.pieces, bf16[16,64,768]{2,1,0:T(8,128)(2,1)S(1)} %get-tuple-element.53.ready, f32[128,1024]{1,0:T(8,128)S(1)} %get-tuple-element.51.term, bf16[512,1024]{1,0:T(8,128)(2,1)S(1)} %copy-done, ...), custom_call_target="tpu_custom_call", output_to_operand_aliasing={{}: (4, {})} | custom-call | tf_op jit(solution)/shard_map/far_conv/pallas_call | solution.py:535
  (4 shorter events, 0.0 us)
Async XLA Ops:
  0.0 25.9 %copy-start.1 = (bf16[64,512]{1,0:T(8,128)(2,1)S(1)}, bf16[64,512]{1,0:T(8,128)(2,1)}, u32[]{:S(2)}) copy-start(bf16[64,512]{1,0:T(8,128)(2,1)} %refs_0_.1) | copy-start | bytes 196612
  0.0 25.9 %copy-start = (bf16[512,1024]{1,0:T(8,128)(2,1)S(1)}, bf16[512,1024]{1,0:T(8,128)(2,1)}, u32[]{:S(2)}) copy-start(bf16[512,1024]{1,0:T(8,128)(2,1)} %query.5) | copy-start | bytes 3145732
  2.3 15.6 %collective-permute-start.3 = (bf16[768,128]{1,0:T(8,128)(2,1)S(1)}, bf16[768,128]{1,0:T(8,128)(2,1)S(1)}, u32[]{:S(2)}, u32[]{:S(2)}) collective-permute-start(bf16[768,128]{1,0:T(8,128)(2,1)S(1)} %get-tuple-element.36), channel_id=1, source_target_pairs={{0,8},{4,12},{8,0},{12,4},{1,9},{5,13},{9,1},{13,5},{2,10},{6,14},... | collective-permute-start | bytes 589832 | tf_op jit(solution)/shard_map/ppermute | solution.py:570
  6.8 15.4 %collective-permute-start.6 = (bf16[768,128]{1,0:T(8,128)(2,1)S(1)}, bf16[768,128]{1,0:T(8,128)(2,1)S(1)}, u32[]{:S(2)}, u32[]{:S(2)}) collective-permute-start(bf16[768,128]{1,0:T(8,128)(2,1)S(1)} %get-tuple-element.44), channel_id=1, source_target_pairs={{0,4},{4,0},{8,12},{12,8},{1,5},{5,1},{9,13},{13,9},{2,6},{6,2},{1... | collective-permute-start | bytes 589832 | tf_op jit(solution)/shard_map/ppermute | solution.py:570
  8.2 11.6 %collective-permute-start.5 = (bf16[512,128]{1,0:T(8,128)(2,1)S(1)}, bf16[512,128]{1,0:T(8,128)(2,1)S(1)}, u32[]{:S(2)}, u32[]{:S(2)}) collective-permute-start(bf16[512,128]{1,0:T(8,128)(2,1)S(1)} %get-tuple-element.40), channel_id=1, source_target_pairs={{0,12},{4,8},{8,4},{12,0},{1,13},{5,9},{9,5},{13,1},{2,14},{6,10},... | collective-permute-start | bytes 393224 | tf_op jit(solution)/shard_map/ppermute | solution.py:570
  17.9 4.3 %collective-permute-start.4 = (bf16[256,128]{1,0:T(8,128)(2,1)S(1)}, bf16[256,128]{1,0:T(8,128)(2,1)S(1)}, u32[]{:S(2)}, u32[]{:S(2)}) collective-permute-start(bf16[256,128]{1,0:T(8,128)(2,1)S(1)} %pick.1), channel_id=1, source_target_pairs={{0,4},{4,0},{8,12},{12,8},{1,5},{5,1},{9,13},{13,9},{2,6},{6,2},{1... | collective-permute-start | bytes 196616 | tf_op jit(solution)/shard_map/ppermute | solution.py:570
  22.4 11.3 %collective-permute-start.7 = (bf16[3,256,128]{2,1,0:T(8,128)(2,1)S(1)}, bf16[3,256,128]{2,1,0:T(8,128)(2,1)S(1)}, u32[]{:S(2)}, u32[]{:S(2)}) collective-permute-start(bf16[3,256,128]{2,1,0:T(8,128)(2,1)S(1)} %merge.1.pieces), channel_id=1, source_target_pairs={{0,8},{4,12},{8,0},{12,4},{1,9},{5,13},{9,1},{13,5},{2,10},{6,14},... | collective-permute-start | bytes 589832 | tf_op jit(solution)/shard_map/ppermute | solution.py:570
  24.4 10.4 %collective-permute-start.9 = (bf16[3,256,128]{2,1,0:T(8,128)(2,1)S(1)}, bf16[3,256,128]{2,1,0:T(8,128)(2,1)S(1)}, u32[]{:S(2)}, u32[]{:S(2)}) collective-permute-start(bf16[3,256,128]{2,1,0:T(8,128)(2,1)S(1)} %merge.1.pieces), channel_id=1, source_target_pairs={{0,4},{4,0},{8,12},{12,8},{1,5},{5,1},{9,13},{13,9},{2,6},{6,2},{1... | collective-permute-start | bytes 589832 | tf_op jit(solution)/shard_map/ppermute | solution.py:570
  33.7 6.6 %collective-permute-start.8 = (bf16[3,256,128]{2,1,0:T(8,128)(2,1)S(1)}, bf16[3,256,128]{2,1,0:T(8,128)(2,1)S(1)}, u32[]{:S(2)}, u32[]{:S(2)}) collective-permute-start(bf16[3,256,128]{2,1,0:T(8,128)(2,1)S(1)} %collective-permute-done.7.refs_1_), channel_id=1, source_target_pairs={{0,4},{4,0},{8,12},{12,8},{1,5},{5,1},{9,13},{13,9},{2,6},{6,2},{1... | collective-permute-start | bytes 589832 | tf_op jit(solution)/shard_map/ppermute | solution.py:570
